TPU v7x, 32 devices: a whole 2x2x4 slice. The times are simulated.
32 devices in a mesh: seq: 8 (over z, y), batch: 4 (over x, core).
Axes of the slice: x: 2, y: 2, z: 4, core: 2. Of those that a mesh axis runs over, the one named last changes fastest.
Arguments:
- queries: bfloat16 [12288, 8192], P(('batch', 'seq')), parts along dimension 0, may hold values from -6 to 6
- keys: bfloat16 [12288, 8192], P(('batch', 'seq')), parts along dimension 0, may hold values from -6 to 6
- values: bfloat16 [12288, 8192], P(('batch', 'seq')), parts along dimension 0, may hold values from -6 to 6
- gain: float32 [8192], replicated, may hold values from 0.1 to 1.9
Outputs:
- mixed: bfloat16 [12288, 8192], P('batch', 'seq'), parts along dimension 0
There are 4 independent parts, one for each index of `batch`. A program takes and returns all parts, laid end to end along the dimension named above; an argument that names none is the same for every part. Nothing has to cross between parts.
All inputs are finite; a program needn't handle non-finite values.
Results may differ from a plain program's by a relative error of at most 0.005.
Values may be sent and summed in bfloat16 or wider, within the bound.
No kernel may reach another device: no remote copies, remote signals or barrier semaphores. Data moves between devices by JAX's collectives and lax.ppermute only.
A program may use at most 384 MiB of HBM per device.

v0:
```python
import functools

import jax
import jax.numpy as jnp
from jax import lax
from jax.experimental import pallas as pl
from jax.experimental.pallas import tpu as pltpu
from jax.sharding import PartitionSpec as P

HEADS = 64
HEAD = 128
LOCAL = (2, 6)
PREFIX = (1, 1, 2, 2, 2)
MIXED = (2, 2, 2, 2)
TILE = 256
VMEM = 48 * 1024 * 1024
ORDER = {}


def params():
    return pltpu.CompilerParams(vmem_limit_bytes=VMEM)


def column(place, row, side, n, low):
    col = place[1] if side == 0 else 1 - place[1]
    return pl.multiple_of(((2 * row + col) * (HEADS // n) + low) * HEAD, HEAD)


def local_body(n, low, widths, place, keys, values, *refs):
    outs, (kbuf, vbuf, sems) = refs[:-3], refs[-3:]
    total = sum(widths)
    copies = []
    for slot in range(n):
        cols = pl.ds(column(place, slot // 2, slot % 2, n, low), total * HEAD)
        copies.append(
            [
                pltpu.make_async_copy(source.at[:, cols], buf.at[slot], sems.at[which, slot])
                for which, (source, buf) in enumerate(((keys, kbuf), (values, vbuf)))
            ]
        )
    for pair in copies:
        for copy in pair:
            copy.start()
    for slot in range(n):
        for copy in copies[slot]:
            copy.wait()
        places = [(chunk, head) for chunk, width in enumerate(widths) for head in range(width)]
        for first in range(0, total, 2):
            size = min(2, total - first)
            cols = slice(first * HEAD, (first + size) * HEAD)
            both = lax.dot_general(
                kbuf[slot, :, cols],
                vbuf[slot, :, cols],
                (((0,), (0,)), ((), ())),
                preferred_element_type=jnp.float32,
            )
            for index in range(size):
                chunk, head = places[first + index]
                out = outs[2 * chunk + slot % 2]
                part = slice(index * HEAD, (index + 1) * HEAD)
                out[slot // 2, head] = both[part, part].astype(out.dtype)


def local_states(place, keys, values, n, low, widths):
    rows, m, total = keys.shape[0], n // 2, sum(widths)
    buf = pltpu.VMEM((n, rows, total * HEAD), keys.dtype)
    shapes = [
        jax.ShapeDtypeStruct((m, width, HEAD, HEAD), kind)
        for width in widths
        for kind in (jnp.float32, jnp.bfloat16)
    ]
    return pl.pallas_call(
        functools.partial(local_body, n, low, widths),
        in_specs=[pl.BlockSpec(memory_space=pltpu.SMEM)] + [pl.BlockSpec(memory_space=pl.ANY)] * 2,
        out_specs=[pl.BlockSpec(memory_space=pltpu.VMEM)] * len(shapes),
        out_shape=shapes,
        scratch_shapes=[buf, buf, pltpu.SemaphoreType.DMA((2, n))],
        compiler_params=params(),
        cost_estimate=pl.CostEstimate(
            flops=2 * n * total * rows * HEAD * HEAD, bytes_accessed=4 * rows * n * total * HEAD, transcendentals=0
        ),
        name="local",
    )(place, keys, values)


def masked_scores(query, key):
    rows = query.shape[0]
    tiles = []
    for low in range(0, rows, TILE):
        high = min(low + TILE, rows)
        part = lax.dot_general(
            query[low:], key[low:high], (((1,), (1,)), ((), ())), preferred_element_type=jnp.float32
        )
        size = high - low
        spot = lax.broadcasted_iota(jnp.int32, (size, size), 0)
        other = lax.broadcasted_iota(jnp.int32, (size, size), 1)
        pieces = [jnp.where(other <= spot, part[:size], 0.0).astype(jnp.bfloat16)]
        if low:
            pieces.insert(0, jnp.zeros((low, size), jnp.bfloat16))
        if high < rows:
            pieces.append(part[size:].astype(jnp.bfloat16))
        tiles.append(jnp.concatenate(pieces, axis=0) if len(pieces) > 1 else pieces[0])
    return tiles


def attend_body(n, low, spans, place, queries, keys, values, gain, *refs):
    states, outs = refs[: 2 * len(spans)], refs[2 * len(spans) :][:n]
    qbuf, kbuf, vbuf, sown, soth, gbuf, held, sems, extra = refs[-9:]
    width = sum(size for _, size in spans)
    m = n // 2
    wide = width * HEAD
    spots = [lax.rem(place[0] + row, m) for row in range(m)]
    small, start = [(gain, gbuf)], 0
    for chunk, (skip, size) in enumerate(spans):
        for source, buf in ((states[2 * chunk], sown), (states[2 * chunk + 1], soth)):
            small.append((source.at[:, skip : skip + size], buf.at[:, start : start + size]))
        start += size
    small = [pltpu.make_async_copy(source, buf, extra.at[which]) for which, (source, buf) in enumerate(small)]
    copies = []
    for slot in range(n):
        cols = pl.ds(column(place, spots[slot // 2], slot % 2, n, low), wide)
        copies.append(
            [
                pltpu.make_async_copy(source.at[:, cols], buf.at[slot], sems.at[which, slot])
                for which, (source, buf) in enumerate(((queries, qbuf), (keys, kbuf), (values, vbuf)))
            ]
        )
    for slot in range(n):
        for copy in copies[slot]:
            copy.start()
        if slot == 1:
            for copy in small:
                copy.start()
    sends = [pltpu.make_async_copy(held.at[slot], outs[slot], sems.at[3, slot]) for slot in range(n)]
    group = max(1, 4 // width)
    for first in range(0, n, group):
        slots = range(first, min(first + group, n))
        for slot in slots:
            for copy in copies[slot]:
                copy.wait()
        heads = [(slot, head, slice(head * HEAD, (head + 1) * HEAD)) for slot in slots for head in range(width)]
        scores = [masked_scores(qbuf[slot, :, cols], kbuf[slot, :, cols]) for slot, _, cols in heads]
        if first == 0:
            for copy in small:
                copy.wait()
        attended = []
        for (slot, head, cols), tiles in zip(heads, scores):
            state = (sown if slot % 2 == 0 else soth)[spots[slot // 2], head]
            left = jnp.concatenate([*tiles, qbuf[slot, :, cols]], axis=1)
            right = jnp.concatenate([vbuf[slot, :, cols], state], axis=0)
            attended.append(jnp.dot(left, right, preferred_element_type=jnp.float32))
        for (slot, head, cols), value in zip(heads, attended):
            square = jnp.mean(value * value, axis=-1, keepdims=True)
            start = column(place, spots[slot // 2], slot % 2, n, low + head)
            mixed = value * lax.rsqrt(square + 1e-05) * gbuf[:, pl.ds(start, HEAD)]
            held[slot, :, cols] = mixed.astype(held.dtype)
        for slot in slots:
            sends[slot].start()
    for copy in sends:
        copy.wait()


def attend(place, queries, keys, values, gain, states, spans, n, low):
    rows, m = queries.shape[0], n // 2
    width = sum(size for _, size in spans)
    wide = width * HEAD
    tokens = pltpu.VMEM((n, rows, wide), jnp.bfloat16)
    state = pltpu.VMEM((m, width, HEAD, HEAD), jnp.bfloat16)
    return pl.pallas_call(
        functools.partial(attend_body, n, low, spans),
        in_specs=[pl.BlockSpec(memory_space=pltpu.SMEM)] + [pl.BlockSpec(memory_space=pl.ANY)] * (4 + 2 * len(states)),
        out_specs=[pl.BlockSpec(memory_space=pl.ANY)] * n,
        out_shape=[jax.ShapeDtypeStruct((rows, wide), jnp.bfloat16)] * n,
        scratch_shapes=[
            tokens,
            tokens,
            tokens,
            state,
            state,
            pltpu.VMEM((1, HEADS * HEAD), jnp.float32),
            tokens,
            pltpu.SemaphoreType.DMA((4, n)),
            pltpu.SemaphoreType.DMA((1 + 2 * len(states),)),
        ],
        compiler_params=params(),
        cost_estimate=pl.CostEstimate(
            flops=2 * n * width * rows * HEAD * (2 * rows + HEAD),
            bytes_accessed=8 * rows * n * wide,
            transcendentals=n * width * rows,
        ),
        name="attend",
    )(place, queries, keys, values, gain, *(array for pair in states for array in pair))


def put_body(n, low, place, *refs):
    parts, out, again, sems = refs[:n], refs[-3], refs[-2], refs[-1]
    m = n // 2
    rows, wide = parts[0].shape
    copies = []
    for shift in range(n):
        row = lax.rem(place[0] + m - shift // 2, m)
        col = place[1] if shift % 2 == 0 else 1 - place[1]
        start = pl.multiple_of((2 * row + col) * rows, rows)
        copies.append(
            pltpu.make_async_copy(
                parts[shift], out.at[pl.ds(start, rows), pl.ds(low * HEAD, wide)], sems.at[shift]
            )
        )
    for copy in copies:
        copy.start()
    for index in range(2):
        again[index] = place[index]
    for copy in copies:
        copy.wait()


def put(place, parts, out, n, low):
    rows, first = parts[0].shape[0], out is None
    anywhere = pl.BlockSpec(memory_space=pl.ANY)
    return pl.pallas_call(
        functools.partial(put_body, n, low),
        in_specs=[pl.BlockSpec(memory_space=pltpu.SMEM)] + [anywhere] * (n if first else n + 1),
        out_specs=[anywhere, pl.BlockSpec(memory_space=pltpu.SMEM)],
        out_shape=[
            jax.ShapeDtypeStruct((n * rows, HEADS // n * HEAD), jnp.bfloat16),
            jax.ShapeDtypeStruct((2,), jnp.int32),
        ],
        scratch_shapes=[pltpu.SemaphoreType.DMA((n,))],
        input_output_aliases={} if first else {n + 1: 0},
        compiler_params=params(),
        name="put",
    )(place, *parts, *(() if first else (out,)))


def split(widths, per_dest):
    chunks, low = [], 0
    for width in widths:
        if low < per_dest:
            width = min(width, per_dest - low)
            chunks.append((low, width))
            low += width
    return chunks


def inside(chunks, low, width):
    return [c for c, (start, _) in enumerate(chunks) if low <= start < low + width]


class Plan:
    def __init__(self, n, queries, keys, values, gain):
        self.n, self.m = n, n // 2
        me = lax.axis_index("seq")
        self.col = me % 2
        self.place = jnp.stack([me // 2, self.col]).astype(jnp.int32)
        self.arrays = queries, keys, values
        self.gain = gain.reshape(1, HEADS * HEAD)
        self.groups, self.parts, self.chunks = (split(widths, HEADS // n) for widths in (LOCAL, PREFIX, MIXED))
        self.made = {}

    def has(self, key):
        limit = {"message": self.m, "prefix": self.m, "sent": self.n - 1}.get(key[0], 0)
        chunks = {"group": self.groups, "mixed": self.chunks, "sent": self.chunks}.get(key[0], self.parts)
        return key[1] < len(chunks) and (len(key) < 3 or key[2] <= limit)

    def get(self, *key):
        if key not in self.made:
            self.made[key] = getattr(self, key[0])(*key[1:])
        return self.made[key]

    def hold(self, value, *key):
        others = []
        for other in ORDER.get(key, ()):
            if self.has(other):
                result = self.get(*other)
                others.append(result[1] if other[0] == "mixed" else result)
        return lax.optimization_barrier((value, *others))[0] if others else value

    def group(self, g):
        low, width = self.groups[g]
        widths = tuple(self.parts[c][1] for c in inside(self.parts, low, width))
        _, keys, values = self.arrays
        return local_states(self.hold(self.place, "group", g), keys, values, self.n, low, widths)

    def local(self, c):
        for g, group in enumerate(self.groups):
            members = inside(self.parts, *group)
            if c in members:
                spot = 2 * members.index(c)
                return self.get("group", g)[spot : spot + 2]

    def both(self, c):
        return self.get("local", c)[0] + self.get("prefix", c, 0).astype(jnp.float32)

    def total(self, c):
        parts = [self.get("prefix", c, s) for s in range(1, self.m)]
        return sum(parts[1:], parts[0]).astype(jnp.float32)

    def message(self, c, s):
        if s == 0:
            value = self.get("local", c)[1]
        elif s < self.m:
            value = self.get("both", c)
            if s > 1:
                value = self.get("prefix", c, s - 1).astype(jnp.float32) + value
        else:
            value = self.get("total", c) + jnp.where(self.col == 0, self.get("local", c)[0], 0.0)
        return self.hold(value.astype(jnp.bfloat16), "message", c, s)

    def prefix(self, c, s):
        if s in (0, self.m):
            pairs = [(d, d ^ 1) for d in range(self.n)]
        else:
            pairs = [(2 * (s - 1) + y, 2 * s + y) for y in range(2)]
        return lax.ppermute(self.get("message", c, s), "seq", pairs)

    def states(self, c):
        near = self.get("prefix", c, 0).astype(jnp.float32)
        own = (self.get("total", c) + jnp.where(self.col == 1, near, 0.0)).astype(jnp.bfloat16)
        return own, self.get("prefix", c, self.m)

    def mixed(self, c):
        low, width = self.chunks[c]
        place = self.get("put", c - 3)[1] if c > 2 else self.place
        place = self.hold(place, "mixed", c)
        states, spans = [], []
        for part, (start, size) in enumerate(self.parts):
            first, last = max(low, start), min(low + width, start + size)
            if first < last:
                states.append(self.get("states", part))
                spans.append((first - start, last - first))
        return attend(place, *self.arrays, self.gain, states, tuple(spans), self.n, low)

    def sent(self, c, k):
        pairs = [
            (2 * z + y, 2 * ((z + k // 2) % self.m) + (y + k) % 2) for z in range(self.m) for y in range(2)
        ]
        return lax.ppermute(self.hold(self.get("mixed", c)[k], "sent", c, k), "seq", pairs)

    def put(self, c):
        parts = [self.get("mixed", c)[0]] + [self.get("sent", c, k) for k in range(1, self.n)]
        out = self.get("put", c - 1)[0] if c else None
        return put(self.place, parts, out, self.n, self.chunks[c][0])


def per_device(n, *arrays):
    plan = Plan(n, *arrays)
    return plan.get("put", len(plan.chunks) - 1)[0]


def solution(mesh):
    tokens = P(("batch", "seq"), None)
    return jax.shard_map(
        functools.partial(per_device, mesh.shape["seq"]),
        mesh=mesh,
        in_specs=(tokens, tokens, tokens, P()),
        out_specs=P("batch", "seq"),
        check_vma=False,
    )
```

profile of v0, /device:TPU:8, one launch (start us, length us, event | category | flops | bytes accessed | tf_op | source)
XLA Modules:
  0.0 216.0 jit_solution(655886621141357949)
XLA Ops:
  0.1 4.2 %local.2 = (f32[4,1,128,128]{3,2,1,0:T(8,128)S(1)}, bf16[4,1,128,128]{3,2,1,0:T(8,128)(2,1)S(1)}, f32[4,1,128,128]{3,2,1,0:T(8,128)S(1)}, bf16[4,1,128,128]{3,2,1,0:T(8,128)(2,1)S(1)}) custom-call(s32[2]{0:T(128)S(1)} %pad_add_fusion.place, bf16[384,8192]{1,0:T(8,128)(2,1)} %keys.11, bf16[384,8192]{1,0:T(8,128)(2,1)} %values.11), custom_call_target="tpu_custom_call" | custom-call | flops 201326592 | bytes 3145728 | tf_op jit(solution)/shard_map/local/pallas_call | solution.py:72
  4.2 1.6 collective-permute-start.5
  5.8 5.5 %local.3 = (f32[4,2,128,128]{3,2,1,0:T(8,128)S(1)}, bf16[4,2,128,128]{3,2,1,0:T(8,128)(2,1)S(1)}, f32[4,2,128,128]{3,2,1,0:T(8,128)S(1)}, bf16[4,2,128,128]{3,2,...) custom-call(s32[2]{0:T(128)S(1)} %pad_add_fusion.place, ...), custom_call_target="tpu_custom_call" | custom-call | flops 603979776 | bytes 9437184 | tf_op jit(solution)/shard_map/local/pallas_call | solution.py:72
  11.9 1.5 collective-permute-start
  13.9 1.5 collective-permute-start.17
  17.7 5.7 %collective-permute-done = bf16[4,1,128,128]{3,2,1,0:T(8,128)(2,1)S(1)} collective-permute-done((bf16[4,1,128,128]{3,2,1,0:T(8,128)(2,1)S(1)}, bf16[4,1,128,128]{3,2,1,0:T(8,128)(2,1)S(1)}, u32[]{:S(2)}, u32[]{:S(2)}) %collective-permute-start) | collective-permute-done | bytes 131104 | tf_op jit(solution)/shard_map/ppermute | solution.py:314
  28.1 2.3 %collective-permute-start.7 = (bf16[4,1,128,128]{3,2,1,0:T(8,128)(2,1)S(1)}, bf16[4,1,128,128]{3,2,1,0:T(8,128)(2,1)S(1)}, u32[]{:S(2)}, u32[]{:S(2)}) collective-permute-start(bf16[4,1,128,128]{3,2,1,0:T(8,128)(2,1)S(1)} %add_convert_fusion.7), channel_id=1, source_target_pairs={{8,16},{12,20},{9,17},{13,21},{10,18},{14,22},{11,19},{15,23}} | collective-permute-start | bytes 393224 | tf_op jit(solution)/shard_map/ppermute | solution.py:314
  30.3 1.5 collective-permute-done.1
  31.9 1.3 collective-permute-start.2
  40.3 4.1 %collective-permute-start.43 = (bf16[4,2,128,128]{3,2,1,0:T(8,128)(2,1)S(1)}, bf16[4,2,128,128]{3,2,1,0:T(8,128)(2,1)S(1)}, u32[]{:S(2)}, u32[]{:S(2)}) collective-permute-start(bf16[4,2,128,128]{3,2,1,0:T(8,128)(2,1)S(1)} %add_convert_fusion.1), channel_id=1, source_target_pairs={{8,16},{12,20},{9,17},{13,21},{10,18},{14,22},{11,19},{15,23}} | collective-permute-start | bytes 786440 | tf_op jit(solution)/shard_map/ppermute | solution.py:314
  46.1 1.6 collective-permute-start.4
  48.8 1.3 collective-permute-start.31
  50.2 1.3 collective-permute-start.19
  51.9 8.7 %attend.4 = (bf16[384,256]{1,0:T(8,128)(2,1)S(1)}, bf16[384,256]{1,0:T(8,128)(2,1)S(1)}, bf16[384,256]{1,0:T(8,128)(2,1)S(1)}, bf16[384,256]{1,0:T(8,128)(2,1)S(...) custom-call(s32[2]{0:T(128)S(1)} %pad_add_fusion.place, ...), custom_call_target="tpu_custom_call" | custom-call | flops 1409286144 | bytes 6291456 | tf_op jit(solution)/shard_map/attend/pallas_call | solution.py:169
  61.5 1.7 collective-permute-start.12
  65.9 4.0 %collective-permute-start.13 = (bf16[384,256]{1,0:T(8,128)(2,1)S(1)}, bf16[384,256]{1,0:T(8,128)(2,1)S(1)}, u32[]{:S(2)}, u32[]{:S(2)}) collective-permute-start(bf16[384,256]{1,0:T(8,128)(2,1)S(1)} %get-tuple-element.60), channel_id=1, source_target_pairs={{0,16},{4,20},{8,24},{12,28},{16,0},{20,4},{24,8},{28,12},{1,17},{... | collective-permute-start | bytes 589832 | tf_op jit(solution)/shard_map/ppermute | solution.py:337
  74.0 17.2 %collective-permute-start.14 = (bf16[384,256]{1,0:T(8,128)(2,1)S(1)}, bf16[384,256]{1,0:T(8,128)(2,1)S(1)}, u32[]{:S(2)}, u32[]{:S(2)}) collective-permute-start(bf16[384,256]{1,0:T(8,128)(2,1)S(1)} %get-tuple-element.61), channel_id=1, source_target_pairs={{0,20},{4,16},{8,28},{12,24},{16,4},{20,0},{24,12},{28,8},{1,21},{... | collective-permute-start | bytes 589832 | tf_op jit(solution)/shard_map/ppermute | solution.py:337
  91.4 2.7 %collective-permute-start.15 = (bf16[384,256]{1,0:T(8,128)(2,1)S(1)}, bf16[384,256]{1,0:T(8,128)(2,1)S(1)}, u32[]{:S(2)}, u32[]{:S(2)}) collective-permute-start(bf16[384,256]{1,0:T(8,128)(2,1)S(1)} %get-tuple-element.62), channel_id=1, source_target_pairs={{0,24},{4,28},{8,0},{12,4},{16,8},{20,12},{24,16},{28,20},{1,25},{... | collective-permute-start | bytes 589832 | tf_op jit(solution)/shard_map/ppermute | solution.py:337
  94.1 6.8 %collective-permute-start.16 = (bf16[384,256]{1,0:T(8,128)(2,1)S(1)}, bf16[384,256]{1,0:T(8,128)(2,1)S(1)}, u32[]{:S(2)}, u32[]{:S(2)}) collective-permute-start(bf16[384,256]{1,0:T(8,128)(2,1)S(1)} %get-tuple-element.63), channel_id=1, source_target_pairs={{0,28},{4,24},{8,4},{12,0},{16,12},{20,8},{24,20},{28,16},{1,29},{... | collective-permute-start | bytes 589832 | tf_op jit(solution)/shard_map/ppermute | solution.py:337
  100.9 2.0 collective-permute-start.33
  103.0 8.7 %attend.7 = (bf16[384,256]{1,0:T(8,128)(2,1)S(1)}, bf16[384,256]{1,0:T(8,128)(2,1)S(1)}, bf16[384,256]{1,0:T(8,128)(2,1)S(1)}, bf16[384,256]{1,0:T(8,128)(2,1)S(...) custom-call(s32[2]{0:T(128)S(1)} %pad_add_fusion.place, ...), custom_call_target="tpu_custom_call" | custom-call | flops 1409286144 | bytes 6291456 | tf_op jit(solution)/shard_map/attend/pallas_call | solution.py:169
  111.6 2.0 collective-permute-start.46
  113.7 5.5 %collective-permute-start.47 = (bf16[384,256]{1,0:T(8,128)(2,1)S(1)}, bf16[384,256]{1,0:T(8,128)(2,1)S(1)}, u32[]{:S(2)}, u32[]{:S(2)}) collective-permute-start(bf16[384,256]{1,0:T(8,128)(2,1)S(1)} %get-tuple-element.89), channel_id=1, source_target_pairs={{0,8},{4,12},{8,16},{12,20},{16,24},{20,28},{24,0},{28,4},{1,9},{5... | collective-permute-start | bytes 589832 | tf_op jit(solution)/shard_map/ppermute | solution.py:337
  119.2 4.7 %collective-permute-start.48 = (bf16[384,256]{1,0:T(8,128)(2,1)S(1)}, bf16[384,256]{1,0:T(8,128)(2,1)S(1)}, u32[]{:S(2)}, u32[]{:S(2)}) collective-permute-start(bf16[384,256]{1,0:T(8,128)(2,1)S(1)} %get-tuple-element.90), channel_id=1, source_target_pairs={{0,12},{4,8},{8,20},{12,16},{16,28},{20,24},{24,4},{28,0},{1,13},{... | collective-permute-start | bytes 589832 | tf_op jit(solution)/shard_map/ppermute | solution.py:337
  123.9 2.4 %collective-permute-start.50 = (bf16[384,256]{1,0:T(8,128)(2,1)S(1)}, bf16[384,256]{1,0:T(8,128)(2,1)S(1)}, u32[]{:S(2)}, u32[]{:S(2)}) collective-permute-start(bf16[384,256]{1,0:T(8,128)(2,1)S(1)} %get-tuple-element.92), channel_id=1, source_target_pairs={{0,20},{4,16},{8,28},{12,24},{16,4},{20,0},{24,12},{28,8},{1,21},{... | collective-permute-start | bytes 589832 | tf_op jit(solution)/shard_map/ppermute | solution.py:337
  126.3 8.7 %attend.6 = (bf16[384,256]{1,0:T(8,128)(2,1)S(1)}, bf16[384,256]{1,0:T(8,128)(2,1)S(1)}, bf16[384,256]{1,0:T(8,128)(2,1)S(1)}, bf16[384,256]{1,0:T(8,128)(2,1)S(...) custom-call(s32[2]{0:T(128)S(1)} %pad_add_fusion.place, ...), custom_call_target="tpu_custom_call" | custom-call | flops 1409286144 | bytes 6291456 | tf_op jit(solution)/shard_map/attend/pallas_call | solution.py:169
  135.0 2.9 %collective-permute-start.52 = (bf16[384,256]{1,0:T(8,128)(2,1)S(1)}, bf16[384,256]{1,0:T(8,128)(2,1)S(1)}, u32[]{:S(2)}, u32[]{:S(2)}) collective-permute-start(bf16[384,256]{1,0:T(8,128)(2,1)S(1)} %get-tuple-element.94), channel_id=1, source_target_pairs={{0,28},{4,24},{8,4},{12,0},{16,12},{20,8},{24,20},{28,16},{1,29},{... | collective-permute-start | bytes 589832 | tf_op jit(solution)/shard_map/ppermute | solution.py:337
  138.0 1.3 collective-permute-done.48.refs_3_
  139.3 2.1 collective-permute-start.34
  141.4 6.3 %collective-permute-done.49.refs_4_ = bf16[384,256]{1,0:T(8,128)(2,1)S(1)} collective-permute-done((bf16[384,256]{1,0:T(8,128)(2,1)S(1)}, bf16[384,256]{1,0:T(8,128)(2,1)S(1)}, u32[]{:S(2)}, u32[]{:S(2)}) %collective-permute-start.49) | collective-permute-done | bytes 196640 | tf_op jit(solution)/shard_map/ppermute | solution.py:337
  147.7 4.2 %collective-permute-done.50.refs_5_ = bf16[384,256]{1,0:T(8,128)(2,1)S(1)} collective-permute-done((bf16[384,256]{1,0:T(8,128)(2,1)S(1)}, bf16[384,256]{1,0:T(8,128)(2,1)S(1)}, u32[]{:S(2)}, u32[]{:S(2)}) %collective-permute-start.50) | collective-permute-done | bytes 196640 | tf_op jit(solution)/shard_map/ppermute | solution.py:337
  153.1 3.2 %collective-permute-start.37 = (bf16[384,256]{1,0:T(8,128)(2,1)S(1)}, bf16[384,256]{1,0:T(8,128)(2,1)S(1)}, u32[]{:S(2)}, u32[]{:S(2)}) collective-permute-start(bf16[384,256]{1,0:T(8,128)(2,1)S(1)} %get-tuple-element.81), channel_id=1, source_target_pairs={{0,16},{4,20},{8,24},{12,28},{16,0},{20,4},{24,8},{28,12},{1,17},{... | collective-permute-start | bytes 589832 | tf_op jit(solution)/shard_map/ppermute | solution.py:337
  156.3 2.3 %put.4 = (bf16[3072,1024]{1,0:T(8,128)(2,1)}, s32[2]{0:T(128)S(1)}) custom-call(s32[2]{0:T(128)S(1)} %pad_add_fusion.place, bf16[384,256]{1,0:T(8,128)(2,1)S(1)} %get-tuple-element.56.refs_0_, bf16[384,256]{1,0:T(8,128)(2,1)S(1)} %collective-permute-done.10.refs_1_, bf16[384,256]{1,0:T(8,128)(2,1)S(1)} %collective-permute-done.11.refs_2_, ...), custom_call_target="tpu_custom_call" | custom-call | tf_op jit(solution)/shard_map/put/pallas_call | solution.py:220
  158.7 8.7 %attend.5 = (bf16[384,256]{1,0:T(8,128)(2,1)S(1)}, bf16[384,256]{1,0:T(8,128)(2,1)S(1)}, bf16[384,256]{1,0:T(8,128)(2,1)S(1)}, bf16[384,256]{1,0:T(8,128)(2,1)S(...) custom-call(s32[2]{0:T(128)S(1)} %get-tuple-element.64.place, ...), custom_call_target="tpu_custom_call" | custom-call | flops 1409286144 | bytes 6291456 | tf_op jit(solution)/shard_map/attend/pallas_call | solution.py:169
  167.4 2.9 %collective-permute-start.39 = (bf16[384,256]{1,0:T(8,128)(2,1)S(1)}, bf16[384,256]{1,0:T(8,128)(2,1)S(1)}, u32[]{:S(2)}, u32[]{:S(2)}) collective-permute-start(bf16[384,256]{1,0:T(8,128)(2,1)S(1)} %get-tuple-element.83), channel_id=1, source_target_pairs={{0,24},{4,28},{8,0},{12,4},{16,8},{20,12},{24,16},{28,20},{1,25},{... | collective-permute-start | bytes 589832 | tf_op jit(solution)/shard_map/ppermute | solution.py:337
  170.4 2.3 %collective-permute-start.40 = (bf16[384,256]{1,0:T(8,128)(2,1)S(1)}, bf16[384,256]{1,0:T(8,128)(2,1)S(1)}, u32[]{:S(2)}, u32[]{:S(2)}) collective-permute-start(bf16[384,256]{1,0:T(8,128)(2,1)S(1)} %get-tuple-element.84), channel_id=1, source_target_pairs={{0,28},{4,24},{8,4},{12,0},{16,12},{20,8},{24,20},{28,16},{1,29},{... | collective-permute-start | bytes 589832 | tf_op jit(solution)/shard_map/ppermute | solution.py:337
  173.3 8.2 %collective-permute-done.37.refs_4_ = bf16[384,256]{1,0:T(8,128)(2,1)S(1)} collective-permute-done((bf16[384,256]{1,0:T(8,128)(2,1)S(1)}, bf16[384,256]{1,0:T(8,128)(2,1)S(1)}, u32[]{:S(2)}, u32[]{:S(2)}) %collective-permute-start.37) | collective-permute-done | bytes 196640 | tf_op jit(solution)/shard_map/ppermute | solution.py:337
  181.5 10.5 %collective-permute-done.38.refs_5_ = bf16[384,256]{1,0:T(8,128)(2,1)S(1)} collective-permute-done((bf16[384,256]{1,0:T(8,128)(2,1)S(1)}, bf16[384,256]{1,0:T(8,128)(2,1)S(1)}, u32[]{:S(2)}, u32[]{:S(2)}) %collective-permute-start.38) | collective-permute-done | bytes 196640 | tf_op jit(solution)/shard_map/ppermute | solution.py:337
  192.0 4.6 %collective-permute-start.25 = (bf16[384,256]{1,0:T(8,128)(2,1)S(1)}, bf16[384,256]{1,0:T(8,128)(2,1)S(1)}, u32[]{:S(2)}, u32[]{:S(2)}) collective-permute-start(bf16[384,256]{1,0:T(8,128)(2,1)S(1)} %get-tuple-element.71), channel_id=1, source_target_pairs={{0,16},{4,20},{8,24},{12,28},{16,0},{20,4},{24,8},{28,12},{1,17},{... | collective-permute-start | bytes 589832 | tf_op jit(solution)/shard_map/ppermute | solution.py:337
  196.6 3.0 %collective-permute-start.27 = (bf16[384,256]{1,0:T(8,128)(2,1)S(1)}, bf16[384,256]{1,0:T(8,128)(2,1)S(1)}, u32[]{:S(2)}, u32[]{:S(2)}) collective-permute-start(bf16[384,256]{1,0:T(8,128)(2,1)S(1)} %get-tuple-element.73), channel_id=1, source_target_pairs={{0,24},{4,28},{8,0},{12,4},{16,8},{20,12},{24,16},{28,20},{1,25},{... | collective-permute-start | bytes 589832 | tf_op jit(solution)/shard_map/ppermute | solution.py:337
  199.6 2.3 %collective-permute-start.28 = (bf16[384,256]{1,0:T(8,128)(2,1)S(1)}, bf16[384,256]{1,0:T(8,128)(2,1)S(1)}, u32[]{:S(2)}, u32[]{:S(2)}) collective-permute-start(bf16[384,256]{1,0:T(8,128)(2,1)S(1)} %get-tuple-element.74), channel_id=1, source_target_pairs={{0,28},{4,24},{8,4},{12,0},{16,12},{20,8},{24,20},{28,16},{1,29},{... | collective-permute-start | bytes 589832 | tf_op jit(solution)/shard_map/ppermute | solution.py:337
  201.9 2.3 %put.5 = (bf16[3072,1024]{1,0:T(8,128)(2,1)}, s32[2]{0:T(128)}) custom-call(s32[2]{0:T(128)S(1)} %pad_add_fusion.place, bf16[384,256]{1,0:T(8,128)(2,1)S(1)} %get-tuple-element.87.refs_0_, bf16[384,256]{1,0:T(8,128)(2,1)S(1)} %collective-permute-done.46.refs_1_, ...), custom_call_target="tpu_custom_call", output_to_operand_aliasing={{0}: (9, {})} | custom-call | tf_op jit(solution)/shard_map/put/pallas_call | solution.py:220
  204.2 2.3 %put.6 = (bf16[3072,1024]{1,0:T(8,128)(2,1)}, s32[2]{0:T(128)}) custom-call(s32[2]{0:T(128)S(1)} %pad_add_fusion.place, bf16[384,256]{1,0:T(8,128)(2,1)S(1)} %get-tuple-element.77.refs_0_, bf16[384,256]{1,0:T(8,128)(2,1)S(1)} %collective-permute-done.34.refs_1_, ...), custom_call_target="tpu_custom_call", output_to_operand_aliasing={{0}: (9, {})} | custom-call | tf_op jit(solution)/shard_map/put/pallas_call | solution.py:220
  206.5 1.4 collective-permute-done.24.refs_3_
  207.9 2.1 collective-permute-done.25.refs_4_
  210.0 2.1 collective-permute-done.26.refs_5_
  212.1 1.5 collective-permute-done.28.refs_7_
  213.5 2.3 %put.7 = (bf16[3072,1024]{1,0:T(8,128)(2,1)}, s32[2]{0:T(128)}) custom-call(s32[2]{0:T(128)S(1)} %pad_add_fusion.place, bf16[384,256]{1,0:T(8,128)(2,1)S(1)} %get-tuple-element.67.refs_0_, bf16[384,256]{1,0:T(8,128)(2,1)S(1)} %collective-permute-done.22.refs_1_, ...), custom_call_target="tpu_custom_call", output_to_operand_aliasing={{0}: (9, {})} | custom-call | tf_op jit(solution)/shard_map/put/pallas_call | solution.py:220
  (91 shorter events, 28.1 us)
Async XLA Ops:
  4.2 11.2 %collective-permute-start.5 = (bf16[4,1,128,128]{3,2,1,0:T(8,128)(2,1)S(1)}, bf16[4,1,128,128]{3,2,1,0:T(8,128)(2,1)}, u32[]{:S(2)}, u32[]{:S(2)}) collective-permute-start(bf16[4,1,128,128]{3,2,1,0:T(8,128)(2,1)S(1)} %get-tuple-element.55), channel_id=1, source_target_pairs={{0,4},{4,0},{8,12},{12,8},{16,20},{20,16},{24,28},{28,24},{1,5},{5... | collective-permute-start | bytes 393224 | tf_op jit(solution)/shard_map/ppermute | solution.py:314
  11.3 13.4 %collective-permute-start.41 = (bf16[4,2,128,128]{3,2,1,0:T(8,128)(2,1)S(1)}, bf16[4,2,128,128]{3,2,1,0:T(8,128)(2,1)}, u32[]{:S(2)}, u32[]{:S(2)}) collective-permute-start(bf16[4,2,128,128]{3,2,1,0:T(8,128)(2,1)S(1)} %get-tuple-element.86), channel_id=1, source_target_pairs={{0,4},{4,0},{8,12},{12,8},{16,20},{20,16},{24,28},{28,24},{1,5},{5... | collective-permute-start | bytes 786440 | tf_op jit(solution)/shard_map/ppermute | solution.py:314
  11.9 11.5 %collective-permute-start = (bf16[4,1,128,128]{3,2,1,0:T(8,128)(2,1)S(1)}, bf16[4,1,128,128]{3,2,1,0:T(8,128)(2,1)S(1)}, u32[]{:S(2)}, u32[]{:S(2)}) collective-permute-start(bf16[4,1,128,128]{3,2,1,0:T(8,128)(2,1)S(1)} %get-tuple-element.53), channel_id=1, source_target_pairs={{0,4},{4,0},{8,12},{12,8},{16,20},{20,16},{24,28},{28,24},{1,5},{5... | collective-permute-start | bytes 393224 | tf_op jit(solution)/shard_map/ppermute | solution.py:314
  13.4 19.7 %collective-permute-start.29 = (bf16[4,2,128,128]{3,2,1,0:T(8,128)(2,1)S(1)}, bf16[4,2,128,128]{3,2,1,0:T(8,128)(2,1)}, u32[]{:S(2)}, u32[]{:S(2)}) collective-permute-start(bf16[4,2,128,128]{3,2,1,0:T(8,128)(2,1)S(1)} %get-tuple-element.76), channel_id=1, source_target_pairs={{0,4},{4,0},{8,12},{12,8},{16,20},{20,16},{24,28},{28,24},{1,5},{5... | collective-permute-start | bytes 786440 | tf_op jit(solution)/shard_map/ppermute | solution.py:314
  13.9 21.5 %collective-permute-start.17 = (bf16[4,2,128,128]{3,2,1,0:T(8,128)(2,1)S(1)}, bf16[4,2,128,128]{3,2,1,0:T(8,128)(2,1)S(1)}, u32[]{:S(2)}, u32[]{:S(2)}) collective-permute-start(bf16[4,2,128,128]{3,2,1,0:T(8,128)(2,1)S(1)} %get-tuple-element.66), channel_id=1, source_target_pairs={{0,4},{4,0},{8,12},{12,8},{16,20},{20,16},{24,28},{28,24},{1,5},{5... | collective-permute-start | bytes 786440 | tf_op jit(solution)/shard_map/ppermute | solution.py:314
  16.4 10.7 %collective-permute-start.6 = (bf16[4,1,128,128]{3,2,1,0:T(8,128)(2,1)S(1)}, bf16[4,1,128,128]{3,2,1,0:T(8,128)(2,1)S(1)}, u32[]{:S(2)}, u32[]{:S(2)}) collective-permute-start(bf16[4,1,128,128]{3,2,1,0:T(8,128)(2,1)S(1)} %fusion.14), channel_id=1, source_target_pairs={{0,8},{4,12},{1,9},{5,13},{2,10},{6,14},{3,11},{7,15}} | collective-permute-start | bytes 393224 | tf_op jit(solution)/shard_map/ppermute | solution.py:314
  23.5 8.3 %collective-permute-start.1 = (bf16[4,1,128,128]{3,2,1,0:T(8,128)(2,1)S(1)}, bf16[4,1,128,128]{3,2,1,0:T(8,128)(2,1)S(1)}, u32[]{:S(2)}, u32[]{:S(2)}) collective-permute-start(bf16[4,1,128,128]{3,2,1,0:T(8,128)(2,1)S(1)} %fusion.13), channel_id=1, source_target_pairs={{0,8},{4,12},{1,9},{5,13},{2,10},{6,14},{3,11},{7,15}} | collective-permute-start | bytes 393224 | tf_op jit(solution)/shard_map/ppermute | solution.py:314
  25.8 13.5 %collective-permute-start.42 = (bf16[4,2,128,128]{3,2,1,0:T(8,128)(2,1)S(1)}, bf16[4,2,128,128]{3,2,1,0:T(8,128)(2,1)S(1)}, u32[]{:S(2)}, u32[]{:S(2)}) collective-permute-start(bf16[4,2,128,128]{3,2,1,0:T(8,128)(2,1)S(1)} %fusion.12), channel_id=1, source_target_pairs={{0,8},{4,12},{1,9},{5,13},{2,10},{6,14},{3,11},{7,15}} | collective-permute-start | bytes 786440 | tf_op jit(solution)/shard_map/ppermute | solution.py:314
  28.1 8.8 %collective-permute-start.7 = (bf16[4,1,128,128]{3,2,1,0:T(8,128)(2,1)S(1)}, bf16[4,1,128,128]{3,2,1,0:T(8,128)(2,1)S(1)}, u32[]{:S(2)}, u32[]{:S(2)}) collective-permute-start(bf16[4,1,128,128]{3,2,1,0:T(8,128)(2,1)S(1)} %add_convert_fusion.7), channel_id=1, source_target_pairs={{8,16},{12,20},{9,17},{13,21},{10,18},{14,22},{11,19},{15,23}} | collective-permute-start | bytes 393224 | tf_op jit(solution)/shard_map/ppermute | solution.py:314
  31.9 6.7 %collective-permute-start.2 = (bf16[4,1,128,128]{3,2,1,0:T(8,128)(2,1)S(1)}, bf16[4,1,128,128]{3,2,1,0:T(8,128)(2,1)S(1)}, u32[]{:S(2)}, u32[]{:S(2)}) collective-permute-start(bf16[4,1,128,128]{3,2,1,0:T(8,128)(2,1)S(1)} %add_convert_fusion.9), channel_id=1, source_target_pairs={{8,16},{12,20},{9,17},{13,21},{10,18},{14,22},{11,19},{15,23}} | collective-permute-start | bytes 393224 | tf_op jit(solution)/shard_map/ppermute | solution.py:314
  34.2 13.5 %collective-permute-start.30 = (bf16[4,2,128,128]{3,2,1,0:T(8,128)(2,1)S(1)}, bf16[4,2,128,128]{3,2,1,0:T(8,128)(2,1)S(1)}, u32[]{:S(2)}, u32[]{:S(2)}) collective-permute-start(bf16[4,2,128,128]{3,2,1,0:T(8,128)(2,1)S(1)} %fusion.11), channel_id=1, source_target_pairs={{0,8},{4,12},{1,9},{5,13},{2,10},{6,14},{3,11},{7,15}} | collective-permute-start | bytes 786440 | tf_op jit(solution)/shard_map/ppermute | solution.py:314
  35.6 14.5 %collective-permute-start.18 = (bf16[4,2,128,128]{3,2,1,0:T(8,128)(2,1)S(1)}, bf16[4,2,128,128]{3,2,1,0:T(8,128)(2,1)S(1)}, u32[]{:S(2)}, u32[]{:S(2)}) collective-permute-start(bf16[4,2,128,128]{3,2,1,0:T(8,128)(2,1)S(1)} %fusion.10), channel_id=1, source_target_pairs={{0,8},{4,12},{1,9},{5,13},{2,10},{6,14},{3,11},{7,15}} | collective-permute-start | bytes 786440 | tf_op jit(solution)/shard_map/ppermute | solution.py:314
  38.6 7.4 %collective-permute-start.3 = (bf16[4,1,128,128]{3,2,1,0:T(8,128)(2,1)S(1)}, bf16[4,1,128,128]{3,2,1,0:T(8,128)(2,1)S(1)}, u32[]{:S(2)}, u32[]{:S(2)}) collective-permute-start(bf16[4,1,128,128]{3,2,1,0:T(8,128)(2,1)S(1)} %add_convert_fusion.8), channel_id=1, source_target_pairs={{16,24},{20,28},{17,25},{21,29},{18,26},{22,30},{19,27},{23,31}} | collective-permute-start | bytes 393224 | tf_op jit(solution)/shard_map/ppermute | solution.py:314
  40.3 21.1 %collective-permute-start.43 = (bf16[4,2,128,128]{3,2,1,0:T(8,128)(2,1)S(1)}, bf16[4,2,128,128]{3,2,1,0:T(8,128)(2,1)S(1)}, u32[]{:S(2)}, u32[]{:S(2)}) collective-permute-start(bf16[4,2,128,128]{3,2,1,0:T(8,128)(2,1)S(1)} %add_convert_fusion.1), channel_id=1, source_target_pairs={{8,16},{12,20},{9,17},{13,21},{10,18},{14,22},{11,19},{15,23}} | collective-permute-start | bytes 786440 | tf_op jit(solution)/shard_map/ppermute | solution.py:314
  48.8 15.4 %collective-permute-start.31 = (bf16[4,2,128,128]{3,2,1,0:T(8,128)(2,1)S(1)}, bf16[4,2,128,128]{3,2,1,0:T(8,128)(2,1)S(1)}, u32[]{:S(2)}, u32[]{:S(2)}) collective-permute-start(bf16[4,2,128,128]{3,2,1,0:T(8,128)(2,1)S(1)} %add_convert_fusion.3), channel_id=1, source_target_pairs={{8,16},{12,20},{9,17},{13,21},{10,18},{14,22},{11,19},{15,23}} | collective-permute-start | bytes 786440 | tf_op jit(solution)/shard_map/ppermute | solution.py:314
  50.2 15.7 %collective-permute-start.19 = (bf16[4,2,128,128]{3,2,1,0:T(8,128)(2,1)S(1)}, bf16[4,2,128,128]{3,2,1,0:T(8,128)(2,1)S(1)}, u32[]{:S(2)}, u32[]{:S(2)}) collective-permute-start(bf16[4,2,128,128]{3,2,1,0:T(8,128)(2,1)S(1)} %add_convert_fusion.5), channel_id=1, source_target_pairs={{8,16},{12,20},{9,17},{13,21},{10,18},{14,22},{11,19},{15,23}} | collective-permute-start | bytes 786440 | tf_op jit(solution)/shard_map/ppermute | solution.py:314
  60.5 13.4 %collective-permute-start.10 = (bf16[384,256]{1,0:T(8,128)(2,1)S(1)}, bf16[384,256]{1,0:T(8,128)(2,1)S(1)}, u32[]{:S(2)}, u32[]{:S(2)}) collective-permute-start(bf16[384,256]{1,0:T(8,128)(2,1)S(1)} %get-tuple-element.57), channel_id=1, source_target_pairs={{0,4},{4,0},{8,12},{12,8},{16,20},{20,16},{24,28},{28,24},{1,5},{5... | collective-permute-start | bytes 589832 | tf_op jit(solution)/shard_map/ppermute | solution.py:337
  61.5 29.9 %collective-permute-start.11 = (bf16[384,256]{1,0:T(8,128)(2,1)S(1)}, bf16[384,256]{1,0:T(8,128)(2,1)S(1)}, u32[]{:S(2)}, u32[]{:S(2)}) collective-permute-start(bf16[384,256]{1,0:T(8,128)(2,1)S(1)} %get-tuple-element.58), channel_id=1, source_target_pairs={{0,8},{4,12},{8,16},{12,20},{16,24},{20,28},{24,0},{28,4},{1,9},{5... | collective-permute-start | bytes 589832 | tf_op jit(solution)/shard_map/ppermute | solution.py:337
  61.5 32.6 %collective-permute-start.12 = (bf16[384,256]{1,0:T(8,128)(2,1)S(1)}, bf16[384,256]{1,0:T(8,128)(2,1)S(1)}, u32[]{:S(2)}, u32[]{:S(2)}) collective-permute-start(bf16[384,256]{1,0:T(8,128)(2,1)S(1)} %get-tuple-element.59), channel_id=1, source_target_pairs={{0,12},{4,8},{8,20},{12,16},{16,28},{20,24},{24,4},{28,0},{1,13},{... | collective-permute-start | bytes 589832 | tf_op jit(solution)/shard_map/ppermute | solution.py:337
  65.9 34.9 %collective-permute-start.13 = (bf16[384,256]{1,0:T(8,128)(2,1)S(1)}, bf16[384,256]{1,0:T(8,128)(2,1)S(1)}, u32[]{:S(2)}, u32[]{:S(2)}) collective-permute-start(bf16[384,256]{1,0:T(8,128)(2,1)S(1)} %get-tuple-element.60), channel_id=1, source_target_pairs={{0,16},{4,20},{8,24},{12,28},{16,0},{20,4},{24,8},{28,12},{1,17},{... | collective-permute-start | bytes 589832 | tf_op jit(solution)/shard_map/ppermute | solution.py:337
  71.9 19.2 %collective-permute-start.20 = (bf16[4,2,128,128]{3,2,1,0:T(8,128)(2,1)S(1)}, bf16[4,2,128,128]{3,2,1,0:T(8,128)(2,1)S(1)}, u32[]{:S(2)}, u32[]{:S(2)}) collective-permute-start(bf16[4,2,128,128]{3,2,1,0:T(8,128)(2,1)S(1)} %add_convert_fusion.4), channel_id=1, source_target_pairs={{16,24},{20,28},{17,25},{21,29},{18,26},{22,30},{19,27},{23,31}} | collective-permute-start | bytes 786440 | tf_op jit(solution)/shard_map/ppermute | solution.py:314
  74.0 37.6 %collective-permute-start.14 = (bf16[384,256]{1,0:T(8,128)(2,1)S(1)}, bf16[384,256]{1,0:T(8,128)(2,1)S(1)}, u32[]{:S(2)}, u32[]{:S(2)}) collective-permute-start(bf16[384,256]{1,0:T(8,128)(2,1)S(1)} %get-tuple-element.61), channel_id=1, source_target_pairs={{0,20},{4,16},{8,28},{12,24},{16,4},{20,0},{24,12},{28,8},{1,21},{... | collective-permute-start | bytes 589832 | tf_op jit(solution)/shard_map/ppermute | solution.py:337
  91.2 11.7 %collective-permute-start.45 = (bf16[4,2,128,128]{3,2,1,0:T(8,128)(2,1)S(1)}, bf16[4,2,128,128]{3,2,1,0:T(8,128)(2,1)S(1)}, u32[]{:S(2)}, u32[]{:S(2)}) collective-permute-start(bf16[4,2,128,128]{3,2,1,0:T(8,128)(2,1)S(1)} %get-tuple-element.99), channel_id=1, source_target_pairs={{0,4},{4,0},{8,12},{12,8},{16,20},{20,16},{24,28},{28,24},{1,5},{5... | collective-permute-start | bytes 786440 | tf_op jit(solution)/shard_map/ppermute | solution.py:314
  91.4 22.3 %collective-permute-start.15 = (bf16[384,256]{1,0:T(8,128)(2,1)S(1)}, bf16[384,256]{1,0:T(8,128)(2,1)S(1)}, u32[]{:S(2)}, u32[]{:S(2)}) collective-permute-start(bf16[384,256]{1,0:T(8,128)(2,1)S(1)} %get-tuple-element.62), channel_id=1, source_target_pairs={{0,24},{4,28},{8,0},{12,4},{16,8},{20,12},{24,16},{28,20},{1,25},{... | collective-permute-start | bytes 589832 | tf_op jit(solution)/shard_map/ppermute | solution.py:337
  94.1 25.1 %collective-permute-start.16 = (bf16[384,256]{1,0:T(8,128)(2,1)S(1)}, bf16[384,256]{1,0:T(8,128)(2,1)S(1)}, u32[]{:S(2)}, u32[]{:S(2)}) collective-permute-start(bf16[384,256]{1,0:T(8,128)(2,1)S(1)} %get-tuple-element.63), channel_id=1, source_target_pairs={{0,28},{4,24},{8,4},{12,0},{16,12},{20,8},{24,20},{28,16},{1,29},{... | collective-permute-start | bytes 589832 | tf_op jit(solution)/shard_map/ppermute | solution.py:337
  100.9 23.0 %collective-permute-start.33 = (bf16[4,2,128,128]{3,2,1,0:T(8,128)(2,1)S(1)}, bf16[4,2,128,128]{3,2,1,0:T(8,128)(2,1)S(1)}, u32[]{:S(2)}, u32[]{:S(2)}) collective-permute-start(bf16[4,2,128,128]{3,2,1,0:T(8,128)(2,1)S(1)} %get-tuple-element.101), channel_id=1, source_target_pairs={{0,4},{4,0},{8,12},{12,8},{16,20},{20,16},{24,28},{28,24},{1,5},{5... | collective-permute-start | bytes 786440 | tf_op jit(solution)/shard_map/ppermute | solution.py:314
  102.9 21.0 %collective-permute-start.21 = (bf16[4,2,128,128]{3,2,1,0:T(8,128)(2,1)S(1)}, bf16[4,2,128,128]{3,2,1,0:T(8,128)(2,1)S(1)}, u32[]{:S(2)}, u32[]{:S(2)}) collective-permute-start(bf16[4,2,128,128]{3,2,1,0:T(8,128)(2,1)S(1)} %get-tuple-element.103), channel_id=1, source_target_pairs={{0,4},{4,0},{8,12},{12,8},{16,20},{20,16},{24,28},{28,24},{1,5},{5... | collective-permute-start | bytes 786440 | tf_op jit(solution)/shard_map/ppermute | solution.py:314
  111.6 14.7 %collective-permute-start.46 = (bf16[384,256]{1,0:T(8,128)(2,1)S(1)}, bf16[384,256]{1,0:T(8,128)(2,1)S(1)}, u32[]{:S(2)}, u32[]{:S(2)}) collective-permute-start(bf16[384,256]{1,0:T(8,128)(2,1)S(1)} %get-tuple-element.88), channel_id=1, source_target_pairs={{0,4},{4,0},{8,12},{12,8},{16,20},{20,16},{24,28},{28,24},{1,5},{5... | collective-permute-start | bytes 589832 | tf_op jit(solution)/shard_map/ppermute | solution.py:337
  113.7 21.3 %collective-permute-start.47 = (bf16[384,256]{1,0:T(8,128)(2,1)S(1)}, bf16[384,256]{1,0:T(8,128)(2,1)S(1)}, u32[]{:S(2)}, u32[]{:S(2)}) collective-permute-start(bf16[384,256]{1,0:T(8,128)(2,1)S(1)} %get-tuple-element.89), channel_id=1, source_target_pairs={{0,8},{4,12},{8,16},{12,20},{16,24},{20,28},{24,0},{28,4},{1,9},{5... | collective-permute-start | bytes 589832 | tf_op jit(solution)/shard_map/ppermute | solution.py:337
  119.2 20.1 %collective-permute-start.48 = (bf16[384,256]{1,0:T(8,128)(2,1)S(1)}, bf16[384,256]{1,0:T(8,128)(2,1)S(1)}, u32[]{:S(2)}, u32[]{:S(2)}) collective-permute-start(bf16[384,256]{1,0:T(8,128)(2,1)S(1)} %get-tuple-element.90), channel_id=1, source_target_pairs={{0,12},{4,8},{8,20},{12,16},{16,28},{20,24},{24,4},{28,0},{1,13},{... | collective-permute-start | bytes 589832 | tf_op jit(solution)/shard_map/ppermute | solution.py:337
  123.9 23.9 %collective-permute-start.49 = (bf16[384,256]{1,0:T(8,128)(2,1)S(1)}, bf16[384,256]{1,0:T(8,128)(2,1)S(1)}, u32[]{:S(2)}, u32[]{:S(2)}) collective-permute-start(bf16[384,256]{1,0:T(8,128)(2,1)S(1)} %get-tuple-element.91), channel_id=1, source_target_pairs={{0,16},{4,20},{8,24},{12,28},{16,0},{20,4},{24,8},{28,12},{1,17},{... | collective-permute-start | bytes 589832 | tf_op jit(solution)/shard_map/ppermute | solution.py:337
  123.9 28.1 %collective-permute-start.50 = (bf16[384,256]{1,0:T(8,128)(2,1)S(1)}, bf16[384,256]{1,0:T(8,128)(2,1)S(1)}, u32[]{:S(2)}, u32[]{:S(2)}) collective-permute-start(bf16[384,256]{1,0:T(8,128)(2,1)S(1)} %get-tuple-element.92), channel_id=1, source_target_pairs={{0,20},{4,16},{8,28},{12,24},{16,4},{20,0},{24,12},{28,8},{1,21},{... | collective-permute-start | bytes 589832 | tf_op jit(solution)/shard_map/ppermute | solution.py:337
  126.3 26.8 %collective-permute-start.51 = (bf16[384,256]{1,0:T(8,128)(2,1)S(1)}, bf16[384,256]{1,0:T(8,128)(2,1)S(1)}, u32[]{:S(2)}, u32[]{:S(2)}) collective-permute-start(bf16[384,256]{1,0:T(8,128)(2,1)S(1)} %get-tuple-element.93), channel_id=1, source_target_pairs={{0,24},{4,28},{8,0},{12,4},{16,8},{20,12},{24,16},{28,20},{1,25},{... | collective-permute-start | bytes 589832 | tf_op jit(solution)/shard_map/ppermute | solution.py:337
  135.0 32.3 %collective-permute-start.52 = (bf16[384,256]{1,0:T(8,128)(2,1)S(1)}, bf16[384,256]{1,0:T(8,128)(2,1)S(1)}, u32[]{:S(2)}, u32[]{:S(2)}) collective-permute-start(bf16[384,256]{1,0:T(8,128)(2,1)S(1)} %get-tuple-element.94), channel_id=1, source_target_pairs={{0,28},{4,24},{8,4},{12,0},{16,12},{20,8},{24,20},{28,16},{1,29},{... | collective-permute-start | bytes 589832 | tf_op jit(solution)/shard_map/ppermute | solution.py:337
  139.3 28.1 %collective-permute-start.34 = (bf16[384,256]{1,0:T(8,128)(2,1)S(1)}, bf16[384,256]{1,0:T(8,128)(2,1)S(1)}, u32[]{:S(2)}, u32[]{:S(2)}) collective-permute-start(bf16[384,256]{1,0:T(8,128)(2,1)S(1)} %get-tuple-element.78), channel_id=1, source_target_pairs={{0,4},{4,0},{8,12},{12,8},{16,20},{20,16},{24,28},{28,24},{1,5},{5... | collective-permute-start | bytes 589832 | tf_op jit(solution)/shard_map/ppermute | solution.py:337
  147.7 22.6 %collective-permute-start.35 = (bf16[384,256]{1,0:T(8,128)(2,1)S(1)}, bf16[384,256]{1,0:T(8,128)(2,1)S(1)}, u32[]{:S(2)}, u32[]{:S(2)}) collective-permute-start(bf16[384,256]{1,0:T(8,128)(2,1)S(1)} %get-tuple-element.79), channel_id=1, source_target_pairs={{0,8},{4,12},{8,16},{12,20},{16,24},{20,28},{24,0},{28,4},{1,9},{5... | collective-permute-start | bytes 589832 | tf_op jit(solution)/shard_map/ppermute | solution.py:337
  152.0 20.8 %collective-permute-start.36 = (bf16[384,256]{1,0:T(8,128)(2,1)S(1)}, bf16[384,256]{1,0:T(8,128)(2,1)S(1)}, u32[]{:S(2)}, u32[]{:S(2)}) collective-permute-start(bf16[384,256]{1,0:T(8,128)(2,1)S(1)} %get-tuple-element.80), channel_id=1, source_target_pairs={{0,12},{4,8},{8,20},{12,16},{16,28},{20,24},{24,4},{28,0},{1,13},{... | collective-permute-start | bytes 589832 | tf_op jit(solution)/shard_map/ppermute | solution.py:337
  153.1 28.4 %collective-permute-start.37 = (bf16[384,256]{1,0:T(8,128)(2,1)S(1)}, bf16[384,256]{1,0:T(8,128)(2,1)S(1)}, u32[]{:S(2)}, u32[]{:S(2)}) collective-permute-start(bf16[384,256]{1,0:T(8,128)(2,1)S(1)} %get-tuple-element.81), channel_id=1, source_target_pairs={{0,16},{4,20},{8,24},{12,28},{16,0},{20,4},{24,8},{28,12},{1,17},{... | collective-permute-start | bytes 589832 | tf_op jit(solution)/shard_map/ppermute | solution.py:337
  167.3 24.6 %collective-permute-start.38 = (bf16[384,256]{1,0:T(8,128)(2,1)S(1)}, bf16[384,256]{1,0:T(8,128)(2,1)S(1)}, u32[]{:S(2)}, u32[]{:S(2)}) collective-permute-start(bf16[384,256]{1,0:T(8,128)(2,1)S(1)} %get-tuple-element.82), channel_id=1, source_target_pairs={{0,20},{4,16},{8,28},{12,24},{16,4},{20,0},{24,12},{28,8},{1,21},{... | collective-permute-start | bytes 589832 | tf_op jit(solution)/shard_map/ppermute | solution.py:337
  167.4 24.6 %collective-permute-start.39 = (bf16[384,256]{1,0:T(8,128)(2,1)S(1)}, bf16[384,256]{1,0:T(8,128)(2,1)S(1)}, u32[]{:S(2)}, u32[]{:S(2)}) collective-permute-start(bf16[384,256]{1,0:T(8,128)(2,1)S(1)} %get-tuple-element.83), channel_id=1, source_target_pairs={{0,24},{4,28},{8,0},{12,4},{16,8},{20,12},{24,16},{28,20},{1,25},{... | collective-permute-start | bytes 589832 | tf_op jit(solution)/shard_map/ppermute | solution.py:337
  170.4 26.3 %collective-permute-start.40 = (bf16[384,256]{1,0:T(8,128)(2,1)S(1)}, bf16[384,256]{1,0:T(8,128)(2,1)S(1)}, u32[]{:S(2)}, u32[]{:S(2)}) collective-permute-start(bf16[384,256]{1,0:T(8,128)(2,1)S(1)} %get-tuple-element.84), channel_id=1, source_target_pairs={{0,28},{4,24},{8,4},{12,0},{16,12},{20,8},{24,20},{28,16},{1,29},{... | collective-permute-start | bytes 589832 | tf_op jit(solution)/shard_map/ppermute | solution.py:337
  172.7 23.9 %collective-permute-start.22 = (bf16[384,256]{1,0:T(8,128)(2,1)S(1)}, bf16[384,256]{1,0:T(8,128)(2,1)S(1)}, u32[]{:S(2)}, u32[]{:S(2)}) collective-permute-start(bf16[384,256]{1,0:T(8,128)(2,1)S(1)} %get-tuple-element.68), channel_id=1, source_target_pairs={{0,4},{4,0},{8,12},{12,8},{16,20},{20,16},{24,28},{28,24},{1,5},{5... | collective-permute-start | bytes 589832 | tf_op jit(solution)/shard_map/ppermute | solution.py:337
  181.4 18.2 %collective-permute-start.23 = (bf16[384,256]{1,0:T(8,128)(2,1)S(1)}, bf16[384,256]{1,0:T(8,128)(2,1)S(1)}, u32[]{:S(2)}, u32[]{:S(2)}) collective-permute-start(bf16[384,256]{1,0:T(8,128)(2,1)S(1)} %get-tuple-element.69), channel_id=1, source_target_pairs={{0,8},{4,12},{8,16},{12,20},{16,24},{20,28},{24,0},{28,4},{1,9},{5... | collective-permute-start | bytes 589832 | tf_op jit(solution)/shard_map/ppermute | solution.py:337
  192.0 15.9 %collective-permute-start.24 = (bf16[384,256]{1,0:T(8,128)(2,1)S(1)}, bf16[384,256]{1,0:T(8,128)(2,1)S(1)}, u32[]{:S(2)}, u32[]{:S(2)}) collective-permute-start(bf16[384,256]{1,0:T(8,128)(2,1)S(1)} %get-tuple-element.70), channel_id=1, source_target_pairs={{0,12},{4,8},{8,20},{12,16},{16,28},{20,24},{24,4},{28,0},{1,13},{... | collective-permute-start | bytes 589832 | tf_op jit(solution)/shard_map/ppermute | solution.py:337
  192.0 18.0 %collective-permute-start.25 = (bf16[384,256]{1,0:T(8,128)(2,1)S(1)}, bf16[384,256]{1,0:T(8,128)(2,1)S(1)}, u32[]{:S(2)}, u32[]{:S(2)}) collective-permute-start(bf16[384,256]{1,0:T(8,128)(2,1)S(1)} %get-tuple-element.71), channel_id=1, source_target_pairs={{0,16},{4,20},{8,24},{12,28},{16,0},{20,4},{24,8},{28,12},{1,17},{... | collective-permute-start | bytes 589832 | tf_op jit(solution)/shard_map/ppermute | solution.py:337
  196.6 15.5 %collective-permute-start.26 = (bf16[384,256]{1,0:T(8,128)(2,1)S(1)}, bf16[384,256]{1,0:T(8,128)(2,1)S(1)}, u32[]{:S(2)}, u32[]{:S(2)}) collective-permute-start(bf16[384,256]{1,0:T(8,128)(2,1)S(1)} %get-tuple-element.72), channel_id=1, source_target_pairs={{0,20},{4,16},{8,28},{12,24},{16,4},{20,0},{24,12},{28,8},{1,21},{... | collective-permute-start | bytes 589832 | tf_op jit(solution)/shard_map/ppermute | solution.py:337
  196.6 15.4 %collective-permute-start.27 = (bf16[384,256]{1,0:T(8,128)(2,1)S(1)}, bf16[384,256]{1,0:T(8,128)(2,1)S(1)}, u32[]{:S(2)}, u32[]{:S(2)}) collective-permute-start(bf16[384,256]{1,0:T(8,128)(2,1)S(1)} %get-tuple-element.73), channel_id=1, source_target_pairs={{0,24},{4,28},{8,0},{12,4},{16,8},{20,12},{24,16},{28,20},{1,25},{... | collective-permute-start | bytes 589832 | tf_op jit(solution)/shard_map/ppermute | solution.py:337
  199.6 13.9 %collective-permute-start.28 = (bf16[384,256]{1,0:T(8,128)(2,1)S(1)}, bf16[384,256]{1,0:T(8,128)(2,1)S(1)}, u32[]{:S(2)}, u32[]{:S(2)}) collective-permute-start(bf16[384,256]{1,0:T(8,128)(2,1)S(1)} %get-tuple-element.74), channel_id=1, source_target_pairs={{0,28},{4,24},{8,4},{12,0},{16,12},{20,8},{24,20},{28,16},{1,29},{... | collective-permute-start | bytes 589832 | tf_op jit(solution)/shard_map/ppermute | solution.py:337
  (6 other events, 61.6 us)
where the time goes:
time: 217 us; the launch traced here: 216 us
  starting transfers between devices  103 us (47%)
  Pallas kernels  53.5 us (25%)
  waiting for transfers between devices  45.3 us (21%)
  other arithmetic  13.3 us (6%)
    ppermute x28, starting transfers between devices, sent(): lax.ppermute(self.hold(self.get('mixed', c)[k], 'sent', c, k), 'seq', pairs)  73.1 us
    ppermute x28, waiting for transfers between devices, sent(): lax.ppermute(self.hold(self.get('mixed', c)[k], 'sent', c, k), 'seq', pairs)  37.7 us
    pallas_call x4, Pallas kernels, attend(): pl.pallas_call(functools.partial(attend_body, n, low, spans), in_specs=[p...  34.7 us
    ppermute x25, starting transfers between devices, prefix(): return lax.ppermute(self.get('message', c, s), 'seq', pairs)  30.2 us
    convert_element_type x20, other arithmetic, message(): return self.hold(value.astype(jnp.bfloat16), 'message', c, s)  13.2 us
    pallas_call x2, Pallas kernels, local_states(): pl.pallas_call(functools.partial(local_body, n, low, widths), in_specs=[p...  9.67 us
    pallas_call x4, Pallas kernels, put(): pl.pallas_call(functools.partial(put_body, n, low), in_specs=[pl.BlockSpe...  9.14 us
    ppermute x25, waiting for transfers between devices, prefix(): return lax.ppermute(self.get('message', c, s), 'seq', pairs)  7.6 us
  transfers between devices with their start and end apart: 53, of which 12 were waited for; matrix products, arithmetic and copies ran while one was open for 6% of the time, Pallas kernels for 22%

commit v1 on v0

--- a/solution.py
+++ b/solution.py
@@ -13,12 +13,17 @@
 PREFIX = (1, 1, 2, 2, 2)
 MIXED = (2, 2, 2, 2)
 TILE = 256
-VMEM = 48 * 1024 * 1024
-ORDER = {}
-
-
-def params():
-    return pltpu.CompilerParams(vmem_limit_bytes=VMEM)
+SPARE = 8 * 1024 * 1024
+ORDER = {
+    ("message", 2, 0): [("message", 0, 1), ("message", 1, 1)],
+    ("message", 3, 0): [("message", 0, 1), ("message", 1, 1)],
+    ("message", 4, 0): [("message", 0, 1), ("message", 1, 1)],
+    ("mixed", 0): [("message", 2, 4), ("message", 3, 3), ("message", 4, 2)],
+}
+
+
+def params(buffers=0):
+    return pltpu.CompilerParams(vmem_limit_bytes=buffers + SPARE)
 
 
 def column(place, row, side, n, low):
@@ -75,7 +80,7 @@
         out_specs=[pl.BlockSpec(memory_space=pltpu.VMEM)] * len(shapes),
         out_shape=shapes,
         scratch_shapes=[buf, buf, pltpu.SemaphoreType.DMA((2, n))],
-        compiler_params=params(),
+        compiler_params=params(4 * n * rows * total * HEAD + 3 * n * total * HEAD * HEAD),
         cost_estimate=pl.CostEstimate(
             flops=2 * n * total * rows * HEAD * HEAD, bytes_accessed=4 * rows * n * total * HEAD, transcendentals=0
         ),
@@ -182,7 +187,7 @@
             pltpu.SemaphoreType.DMA((4, n)),
             pltpu.SemaphoreType.DMA((1 + 2 * len(states),)),
         ],
-        compiler_params=params(),
+        compiler_params=params(8 * n * rows * wide + 2 * n * width * HEAD * HEAD + 4 * HEADS * HEAD),
         cost_estimate=pl.CostEstimate(
             flops=2 * n * width * rows * HEAD * (2 * rows + HEAD),
             bytes_accessed=8 * rows * n * wide,

time: 217 us -> 224 us (1.032)
  waiting for transfers between devices: 45.3 us -> 92.6 us
  starting transfers between devices: 103 us -> 66.7 us
  other arithmetic: 13.3 us -> 1.96 us
  local copies, waits for them, and re-layouts: 0.01 us -> 11.2 us
  Pallas kernels: 53.5 us -> 50.1 us
    ppermute x28, starting transfers between devices: 73.1 us -> 38.1 us  [sent(): lax.ppermute(self.hold(self.get('mixed', c)[k], 'sent', c, k), 'seq', pairs)]
    ppermute x28, waiting for transfers between devices: 37.7 us -> 63.5 us  [sent(): lax.ppermute(self.hold(self.get('mixed', c)[k], 'sent', c, k), 'seq', pairs)]
    ppermute x25, waiting for transfers between devices: 7.6 us -> 29.2 us  [prefix(): return lax.ppermute(self.get('message', c, s), 'seq', pairs)]
    convert_element_type x20 -> x19, other arithmetic: 13.2 us -> 1.66 us  [message(): return self.hold(value.astype(jnp.bfloat16), 'message', c, s)]
    unnamed x2 -> x22, local copies, waits for them, and re-layouts: 0.01 us -> 11.2 us
    pallas_call x4, Pallas kernels: 34.7 us -> 32.2 us  [attend(): pl.pallas_call(functools.partial(attend_body, n, low, spans), in_specs=[p...]
  transfers between devices with their start and end apart: 53 -> 53, of which waited for: 12 -> 25; matrix products, arithmetic and copies ran while one was open for 6% -> 1% of each run, Pallas kernels for 22% -> 20%
where the time goes in v1:
time: 224 us; the launch traced here: 223 us
  waiting for transfers between devices  92.6 us (41%)
  starting transfers between devices  66.7 us (30%)
  Pallas kernels  50.1 us (22%)
  local copies, waits for them, and re-layouts  11.2 us (5%)
    ppermute x28, waiting for transfers between devices, sent(): lax.ppermute(self.hold(self.get('mixed', c)[k], 'sent', c, k), 'seq', pairs)  63.5 us
    ppermute x28, starting transfers between devices, sent(): lax.ppermute(self.hold(self.get('mixed', c)[k], 'sent', c, k), 'seq', pairs)  38.1 us
    pallas_call x4, Pallas kernels, attend(): pl.pallas_call(functools.partial(attend_body, n, low, spans), in_specs=[p...  32.2 us
    ppermute x25, waiting for transfers between devices, prefix(): return lax.ppermute(self.get('message', c, s), 'seq', pairs)  29.2 us
    ppermute x25, starting transfers between devices, prefix(): return lax.ppermute(self.get('message', c, s), 'seq', pairs)  28.6 us
    unnamed x22, local copies, waits for them, and re-layouts  11.2 us
    pallas_call x4, Pallas kernels, put(): pl.pallas_call(functools.partial(put_body, n, low), in_specs=[pl.BlockSpe...  9.14 us
    pallas_call x2, Pallas kernels, local_states(): pl.pallas_call(functools.partial(local_body, n, low, widths), in_specs=[p...  8.82 us
  transfers between devices with their start and end apart: 53, of which 25 were waited for; matrix products, arithmetic and copies ran while one was open for 1% of the time, Pallas kernels for 20%

profile of v1, /device:TPU:8, one launch (start us, length us, event | category | flops | bytes accessed | tf_op | source)
XLA Modules:
  0.0 223.3 jit_solution(15478410851533417152)
XLA Ops:
  0.1 2.8 %copy-done = bf16[384,8192]{1,0:T(8,128)(2,1)S(1)} copy-done((bf16[384,8192]{1,0:T(8,128)(2,1)S(1)}, bf16[384,8192]{1,0:T(8,128)(2,1)}, u32[]{:S(2)}) %copy-start) | copy-done | bytes 6291480
  2.9 2.8 %copy-done.2 = bf16[384,8192]{1,0:T(8,128)(2,1)S(1)} copy-done((bf16[384,8192]{1,0:T(8,128)(2,1)S(1)}, bf16[384,8192]{1,0:T(8,128)(2,1)}, u32[]{:S(2)}) %copy-start.2) | copy-done | bytes 6291480
  5.6 3.6 %local.3 = (f32[4,1,128,128]{3,2,1,0:T(8,128)S(1)}, bf16[4,1,128,128]{3,2,1,0:T(8,128)(2,1)S(1)}, f32[4,1,128,128]{3,2,1,0:T(8,128)S(1)}, bf16[4,1,128,128]{3,2,1,0:T(8,128)(2,1)S(1)}) custom-call(s32[2]{0:T(128)S(1)} %pad_add_fusion.place, bf16[384,8192]{1,0:T(8,128)(2,1)S(1)} %copy-done, bf16[384,8192]{1,0:T(8,128)(2,1)S(1)} %copy-done.2), custom_call_target="tpu_custom_call" | custom-call | flops 201326592 | bytes 3145728 | tf_op jit(solution)/shard_map/local/pallas_call | solution.py:77
  9.3 1.6 collective-permute-start.1
  11.4 2.8 %copy-done.1 = bf16[384,8192]{1,0:T(8,128)(2,1)S(1)} copy-done((bf16[384,8192]{1,0:T(8,128)(2,1)S(1)}, bf16[384,8192]{1,0:T(8,128)(2,1)}, u32[]{:S(2)}) %copy-start.1) | copy-done | bytes 6291480
  14.2 2.8 %copy-done.3 = bf16[384,8192]{1,0:T(8,128)(2,1)S(1)} copy-done((bf16[384,8192]{1,0:T(8,128)(2,1)S(1)}, bf16[384,8192]{1,0:T(8,128)(2,1)}, u32[]{:S(2)}) %copy-start.3) | copy-done | bytes 6291480
  16.9 5.2 %local.2 = (f32[4,2,128,128]{3,2,1,0:T(8,128)S(1)}, bf16[4,2,128,128]{3,2,1,0:T(8,128)(2,1)S(1)}, f32[4,2,128,128]{3,2,1,0:T(8,128)S(1)}, bf16[4,2,128,128]{3,2,...) custom-call(s32[2]{0:T(128)S(1)} %pad_add_fusion.place, ...), custom_call_target="tpu_custom_call" | custom-call | flops 603979776 | bytes 9437184 | tf_op jit(solution)/shard_map/local/pallas_call | solution.py:77
  24.8 1.6 collective-permute-start.9
  28.5 1.7 collective-permute-done.15
  41.1 2.5 %collective-permute-done.2 = bf16[4,2,128,128]{3,2,1,0:T(8,128)(2,1)S(1)} collective-permute-done((bf16[4,2,128,128]{3,2,1,0:T(8,128)(2,1)S(1)}, bf16[4,2,128,128]{3,2,1,0:T(8,128)(2,1)S(1)}, u32[]{:S(2)}, u32[]{:S(2)}) %collective-permute-start.2) | collective-permute-done | bytes 262176 | tf_op jit(solution)/shard_map/ppermute | solution.py:319
  45.1 1.6 collective-permute-start.18
  47.4 8.2 %collective-permute-done.3 = bf16[4,2,128,128]{3,2,1,0:T(8,128)(2,1)S(1)} collective-permute-done((bf16[4,2,128,128]{3,2,1,0:T(8,128)(2,1)S(1)}, bf16[4,2,128,128]{3,2,1,0:T(8,128)(2,1)S(1)}, u32[]{:S(2)}, u32[]{:S(2)}) %collective-permute-start.3) | collective-permute-done | bytes 262176 | tf_op jit(solution)/shard_map/ppermute | solution.py:319
  60.0 3.9 %collective-permute-done.4 = bf16[4,2,128,128]{3,2,1,0:T(8,128)(2,1)S(1)} collective-permute-done((bf16[4,2,128,128]{3,2,1,0:T(8,128)(2,1)S(1)}, bf16[4,2,128,128]{3,2,1,0:T(8,128)(2,1)S(1)}, u32[]{:S(2)}, u32[]{:S(2)}) %collective-permute-start.4) | collective-permute-done | bytes 262176 | tf_op jit(solution)/shard_map/ppermute | solution.py:319
  64.7 3.6 %collective-permute-done.8 = bf16[4,2,128,128]{3,2,1,0:T(8,128)(2,1)S(1)} collective-permute-done((bf16[4,2,128,128]{3,2,1,0:T(8,128)(2,1)S(1)}, bf16[4,2,128,128]{3,2,1,0:T(8,128)(2,1)S(1)}, u32[]{:S(2)}, u32[]{:S(2)}) %collective-permute-start.8) | collective-permute-done | bytes 262176 | tf_op jit(solution)/shard_map/ppermute | solution.py:319
  69.1 2.0 collective-permute-done.26
  74.0 8.2 %attend.4 = (bf16[384,256]{1,0:T(8,128)(2,1)S(1)}, bf16[384,256]{1,0:T(8,128)(2,1)S(1)}, bf16[384,256]{1,0:T(8,128)(2,1)S(1)}, bf16[384,256]{1,0:T(8,128)(2,1)S(...) custom-call(s32[2]{0:T(128)S(1)} %pad_add_fusion.place, ...), custom_call_target="tpu_custom_call" | custom-call | flops 1409286144 | bytes 6291456 | tf_op jit(solution)/shard_map/attend/pallas_call | solution.py:174
  82.8 3.1 %collective-permute-start.20 = (bf16[384,256]{1,0:T(8,128)(2,1)S(1)}, bf16[384,256]{1,0:T(8,128)(2,1)S(1)}, u32[]{:S(2)}, u32[]{:S(2)}) collective-permute-start(bf16[384,256]{1,0:T(8,128)(2,1)S(1)} %get-tuple-element.72), channel_id=1, source_target_pairs={{0,8},{4,12},{8,16},{12,20},{16,24},{20,28},{24,0},{28,4},{1,9},{5... | collective-permute-start | bytes 589832 | tf_op jit(solution)/shard_map/ppermute | solution.py:342
  88.8 2.1 collective-permute-start.23
  91.2 14.3 %collective-permute-done.20.refs_2_ = bf16[384,256]{1,0:T(8,128)(2,1)S(1)} collective-permute-done((bf16[384,256]{1,0:T(8,128)(2,1)S(1)}, bf16[384,256]{1,0:T(8,128)(2,1)S(1)}, u32[]{:S(2)}, u32[]{:S(2)}) %collective-permute-start.20) | collective-permute-done | bytes 196640 | tf_op jit(solution)/shard_map/ppermute | solution.py:342
  105.5 3.4 %collective-permute-done.21.refs_3_ = bf16[384,256]{1,0:T(8,128)(2,1)S(1)} collective-permute-done((bf16[384,256]{1,0:T(8,128)(2,1)S(1)}, bf16[384,256]{1,0:T(8,128)(2,1)S(1)}, u32[]{:S(2)}, u32[]{:S(2)}) %collective-permute-start.21) | collective-permute-done | bytes 196640 | tf_op jit(solution)/shard_map/ppermute | solution.py:342
  108.9 2.1 collective-permute-done.22.refs_4_
  113.0 8.0 %attend.7 = (bf16[384,256]{1,0:T(8,128)(2,1)S(1)}, bf16[384,256]{1,0:T(8,128)(2,1)S(1)}, bf16[384,256]{1,0:T(8,128)(2,1)S(1)}, bf16[384,256]{1,0:T(8,128)(2,1)S(...) custom-call(s32[2]{0:T(128)S(1)} %pad_add_fusion.place, ...), custom_call_target="tpu_custom_call" | custom-call | flops 1409286144 | bytes 6291456 | tf_op jit(solution)/shard_map/attend/pallas_call | solution.py:174
  121.0 1.6 collective-permute-start.46
  123.1 3.5 %collective-permute-start.48 = (bf16[384,256]{1,0:T(8,128)(2,1)S(1)}, bf16[384,256]{1,0:T(8,128)(2,1)S(1)}, u32[]{:S(2)}, u32[]{:S(2)}) collective-permute-start(bf16[384,256]{1,0:T(8,128)(2,1)S(1)} %get-tuple-element.98), channel_id=1, source_target_pairs={{0,12},{4,8},{8,20},{12,16},{16,28},{20,24},{24,4},{28,0},{1,13},{... | collective-permute-start | bytes 589832 | tf_op jit(solution)/shard_map/ppermute | solution.py:342
  127.5 3.7 %collective-permute-done.28.refs_1_ = bf16[4,2,128,128]{3,2,1,0:T(8,128)(2,1)S(1)} collective-permute-done((bf16[4,2,128,128]{3,2,1,0:T(8,128)(2,1)S(1)}, bf16[4,2,128,128]{3,2,1,0:T(8,128)(2,1)S(1)}, u32[]{:S(2)}, u32[]{:S(2)}) %collective-permute-start.28) | collective-permute-done | bytes 262176 | tf_op jit(solution)/shard_map/ppermute | solution.py:319
  131.6 1.7 collective-permute-done.46.refs_1_
  133.3 8.0 %attend.6 = (bf16[384,256]{1,0:T(8,128)(2,1)S(1)}, bf16[384,256]{1,0:T(8,128)(2,1)S(1)}, bf16[384,256]{1,0:T(8,128)(2,1)S(1)}, bf16[384,256]{1,0:T(8,128)(2,1)S(...) custom-call(s32[2]{0:T(128)S(1)} %pad_add_fusion.place, ...), custom_call_target="tpu_custom_call" | custom-call | flops 1409286144 | bytes 6291456 | tf_op jit(solution)/shard_map/attend/pallas_call | solution.py:174
  141.3 3.2 %collective-permute-start.52 = (bf16[384,256]{1,0:T(8,128)(2,1)S(1)}, bf16[384,256]{1,0:T(8,128)(2,1)S(1)}, u32[]{:S(2)}, u32[]{:S(2)}) collective-permute-start(bf16[384,256]{1,0:T(8,128)(2,1)S(1)} %get-tuple-element.102), channel_id=1, source_target_pairs={{0,28},{4,24},{8,4},{12,0},{16,12},{20,8},{24,20},{28,16},{1,29},{... | collective-permute-start | bytes 589832 | tf_op jit(solution)/shard_map/ppermute | solution.py:342
  144.9 1.8 collective-permute-start.38
  146.7 4.5 %collective-permute-done.49.refs_4_ = bf16[384,256]{1,0:T(8,128)(2,1)S(1)} collective-permute-done((bf16[384,256]{1,0:T(8,128)(2,1)S(1)}, bf16[384,256]{1,0:T(8,128)(2,1)S(1)}, u32[]{:S(2)}, u32[]{:S(2)}) %collective-permute-start.49) | collective-permute-done | bytes 196640 | tf_op jit(solution)/shard_map/ppermute | solution.py:342
  151.2 6.3 %collective-permute-done.50.refs_5_ = bf16[384,256]{1,0:T(8,128)(2,1)S(1)} collective-permute-done((bf16[384,256]{1,0:T(8,128)(2,1)S(1)}, bf16[384,256]{1,0:T(8,128)(2,1)S(1)}, u32[]{:S(2)}, u32[]{:S(2)}) %collective-permute-start.50) | collective-permute-done | bytes 196640 | tf_op jit(solution)/shard_map/ppermute | solution.py:342
  157.5 2.6 %collective-permute-start.41 = (bf16[384,256]{1,0:T(8,128)(2,1)S(1)}, bf16[384,256]{1,0:T(8,128)(2,1)S(1)}, u32[]{:S(2)}, u32[]{:S(2)}) collective-permute-start(bf16[384,256]{1,0:T(8,128)(2,1)S(1)} %get-tuple-element.91), channel_id=1, source_target_pairs={{0,16},{4,20},{8,24},{12,28},{16,0},{20,4},{24,8},{28,12},{1,17},{... | collective-permute-start | bytes 589832 | tf_op jit(solution)/shard_map/ppermute | solution.py:342
  160.2 2.3 %put.4 = (bf16[3072,1024]{1,0:T(8,128)(2,1)}, s32[2]{0:T(128)S(1)}) custom-call(s32[2]{0:T(128)S(1)} %pad_add_fusion.place, bf16[384,256]{1,0:T(8,128)(2,1)S(1)} %get-tuple-element.70.refs_0_, bf16[384,256]{1,0:T(8,128)(2,1)S(1)} %collective-permute-done.19.refs_1_, bf16[384,256]{1,0:T(8,128)(2,1)S(1)} %collective-permute-done.20.refs_2_, ...), custom_call_target="tpu_custom_call" | custom-call | tf_op jit(solution)/shard_map/put/pallas_call | solution.py:225
  162.5 8.0 %attend.5 = (bf16[384,256]{1,0:T(8,128)(2,1)S(1)}, bf16[384,256]{1,0:T(8,128)(2,1)S(1)}, bf16[384,256]{1,0:T(8,128)(2,1)S(1)}, bf16[384,256]{1,0:T(8,128)(2,1)S(...) custom-call(s32[2]{0:T(128)S(1)} %get-tuple-element.78.place, ...), custom_call_target="tpu_custom_call" | custom-call | flops 1409286144 | bytes 6291456 | tf_op jit(solution)/shard_map/attend/pallas_call | solution.py:174
  170.5 1.8 collective-permute-start.42
  172.3 2.1 collective-permute-start.43
  175.9 2.3 %collective-permute-start.29 = (bf16[384,256]{1,0:T(8,128)(2,1)S(1)}, bf16[384,256]{1,0:T(8,128)(2,1)S(1)}, u32[]{:S(2)}, u32[]{:S(2)}) collective-permute-start(bf16[384,256]{1,0:T(8,128)(2,1)S(1)} %get-tuple-element.80), channel_id=1, source_target_pairs={{0,4},{4,0},{8,12},{12,8},{16,20},{20,16},{24,28},{28,24},{1,5},{5... | collective-permute-start | bytes 589832 | tf_op jit(solution)/shard_map/ppermute | solution.py:342
  178.2 7.3 %collective-permute-done.42.refs_5_ = bf16[384,256]{1,0:T(8,128)(2,1)S(1)} collective-permute-done((bf16[384,256]{1,0:T(8,128)(2,1)S(1)}, bf16[384,256]{1,0:T(8,128)(2,1)S(1)}, u32[]{:S(2)}, u32[]{:S(2)}) %collective-permute-start.42) | collective-permute-done | bytes 196640 | tf_op jit(solution)/shard_map/ppermute | solution.py:342
  185.5 2.6 %collective-permute-start.31 = (bf16[384,256]{1,0:T(8,128)(2,1)S(1)}, bf16[384,256]{1,0:T(8,128)(2,1)S(1)}, u32[]{:S(2)}, u32[]{:S(2)}) collective-permute-start(bf16[384,256]{1,0:T(8,128)(2,1)S(1)} %get-tuple-element.82), channel_id=1, source_target_pairs={{0,12},{4,8},{8,20},{12,16},{16,28},{20,24},{24,4},{28,0},{1,13},{... | collective-permute-start | bytes 589832 | tf_op jit(solution)/shard_map/ppermute | solution.py:342
  188.1 11.2 %collective-permute-done.43.refs_6_ = bf16[384,256]{1,0:T(8,128)(2,1)S(1)} collective-permute-done((bf16[384,256]{1,0:T(8,128)(2,1)S(1)}, bf16[384,256]{1,0:T(8,128)(2,1)S(1)}, u32[]{:S(2)}, u32[]{:S(2)}) %collective-permute-start.43) | collective-permute-done | bytes 196640 | tf_op jit(solution)/shard_map/ppermute | solution.py:342
  199.3 3.6 %collective-permute-done.44.refs_7_ = bf16[384,256]{1,0:T(8,128)(2,1)S(1)} collective-permute-done((bf16[384,256]{1,0:T(8,128)(2,1)S(1)}, bf16[384,256]{1,0:T(8,128)(2,1)S(1)}, u32[]{:S(2)}, u32[]{:S(2)}) %collective-permute-start.44) | collective-permute-done | bytes 196640 | tf_op jit(solution)/shard_map/ppermute | solution.py:342
  203.9 4.3 %collective-permute-start.35 = (bf16[384,256]{1,0:T(8,128)(2,1)S(1)}, bf16[384,256]{1,0:T(8,128)(2,1)S(1)}, u32[]{:S(2)}, u32[]{:S(2)}) collective-permute-start(bf16[384,256]{1,0:T(8,128)(2,1)S(1)} %get-tuple-element.86), channel_id=1, source_target_pairs={{0,28},{4,24},{8,4},{12,0},{16,12},{20,8},{24,20},{28,16},{1,29},{... | collective-permute-start | bytes 589832 | tf_op jit(solution)/shard_map/ppermute | solution.py:342
  208.2 2.3 %put.5 = (bf16[3072,1024]{1,0:T(8,128)(2,1)}, s32[2]{0:T(128)}) custom-call(s32[2]{0:T(128)S(1)} %pad_add_fusion.place, bf16[384,256]{1,0:T(8,128)(2,1)S(1)} %get-tuple-element.95.refs_0_, bf16[384,256]{1,0:T(8,128)(2,1)S(1)} %collective-permute-done.46.refs_1_, ...), custom_call_target="tpu_custom_call", output_to_operand_aliasing={{0}: (9, {})} | custom-call | tf_op jit(solution)/shard_map/put/pallas_call | solution.py:225
  210.4 2.3 %put.6 = (bf16[3072,1024]{1,0:T(8,128)(2,1)}, s32[2]{0:T(128)}) custom-call(s32[2]{0:T(128)S(1)} %pad_add_fusion.place, bf16[384,256]{1,0:T(8,128)(2,1)S(1)} %get-tuple-element.87.refs_0_, bf16[384,256]{1,0:T(8,128)(2,1)S(1)} %collective-permute-done.38.refs_1_, ...), custom_call_target="tpu_custom_call", output_to_operand_aliasing={{0}: (9, {})} | custom-call | tf_op jit(solution)/shard_map/put/pallas_call | solution.py:225
  212.7 2.3 %collective-permute-done.32.refs_4_ = bf16[384,256]{1,0:T(8,128)(2,1)S(1)} collective-permute-done((bf16[384,256]{1,0:T(8,128)(2,1)S(1)}, bf16[384,256]{1,0:T(8,128)(2,1)S(1)}, u32[]{:S(2)}, u32[]{:S(2)}) %collective-permute-start.32) | collective-permute-done | bytes 196640 | tf_op jit(solution)/shard_map/ppermute | solution.py:342
  215.0 3.2 %collective-permute-done.33.refs_5_ = bf16[384,256]{1,0:T(8,128)(2,1)S(1)} collective-permute-done((bf16[384,256]{1,0:T(8,128)(2,1)S(1)}, bf16[384,256]{1,0:T(8,128)(2,1)S(1)}, u32[]{:S(2)}, u32[]{:S(2)}) %collective-permute-start.33) | collective-permute-done | bytes 196640 | tf_op jit(solution)/shard_map/ppermute | solution.py:342
  218.8 2.1 collective-permute-done.35.refs_7_
  220.9 2.3 %put.7 = (bf16[3072,1024]{1,0:T(8,128)(2,1)}, s32[2]{0:T(128)}) custom-call(s32[2]{0:T(128)S(1)} %pad_add_fusion.place, bf16[384,256]{1,0:T(8,128)(2,1)S(1)} %get-tuple-element.79.refs_0_, bf16[384,256]{1,0:T(8,128)(2,1)S(1)} %collective-permute-done.29.refs_1_, ...), custom_call_target="tpu_custom_call", output_to_operand_aliasing={{0}: (9, {})} | custom-call | tf_op jit(solution)/shard_map/put/pallas_call | solution.py:225
  (114 shorter events, 37.9 us)
Async XLA Ops:
  9.3 12.9 %collective-permute-start.1 = (bf16[4,1,128,128]{3,2,1,0:T(8,128)(2,1)S(1)}, bf16[4,1,128,128]{3,2,1,0:T(8,128)(2,1)S(1)}, u32[]{:S(2)}, u32[]{:S(2)}) collective-permute-start(bf16[4,1,128,128]{3,2,1,0:T(8,128)(2,1)S(1)} %get-tuple-element.61), channel_id=1, source_target_pairs={{0,4},{4,0},{8,12},{12,8},{16,20},{20,16},{24,28},{28,24},{1,5},{5... | collective-permute-start | bytes 393224 | tf_op jit(solution)/shard_map/ppermute | solution.py:319
  10.9 12.6 %collective-permute-start = (bf16[4,1,128,128]{3,2,1,0:T(8,128)(2,1)S(1)}, bf16[4,1,128,128]{3,2,1,0:T(8,128)(2,1)S(1)}, u32[]{:S(2)}, u32[]{:S(2)}) collective-permute-start(bf16[4,1,128,128]{3,2,1,0:T(8,128)(2,1)S(1)} %get-tuple-element.59), channel_id=1, source_target_pairs={{0,4},{4,0},{8,12},{12,8},{16,20},{20,16},{24,28},{28,24},{1,5},{5... | collective-permute-start | bytes 393224 | tf_op jit(solution)/shard_map/ppermute | solution.py:319
  23.5 8.3 %collective-permute-start.11 = (bf16[4,1,128,128]{3,2,1,0:T(8,128)(2,1)S(1)}, bf16[4,1,128,128]{3,2,1,0:T(8,128)(2,1)S(1)}, u32[]{:S(2)}, u32[]{:S(2)}) collective-permute-start(bf16[4,1,128,128]{3,2,1,0:T(8,128)(2,1)S(1)} %fusion.13), channel_id=1, source_target_pairs={{0,8},{4,12},{1,9},{5,13},{2,10},{6,14},{3,11},{7,15}} | collective-permute-start | bytes 393224 | tf_op jit(solution)/shard_map/ppermute | solution.py:319
  24.8 11.8 %collective-permute-start.9 = (bf16[4,2,128,128]{3,2,1,0:T(8,128)(2,1)S(1)}, bf16[4,2,128,128]{3,2,1,0:T(8,128)(2,1)S(1)}, u32[]{:S(2)}, u32[]{:S(2)}) collective-permute-start(bf16[4,2,128,128]{3,2,1,0:T(8,128)(2,1)S(1)} %get-tuple-element.68), channel_id=1, source_target_pairs={{0,4},{4,0},{8,12},{12,8},{16,20},{20,16},{24,28},{28,24},{1,5},{5... | collective-permute-start | bytes 786440 | tf_op jit(solution)/shard_map/ppermute | solution.py:319
  26.4 13.3 %collective-permute-start.6 = (bf16[4,2,128,128]{3,2,1,0:T(8,128)(2,1)S(1)}, bf16[4,2,128,128]{3,2,1,0:T(8,128)(2,1)S(1)}, u32[]{:S(2)}, u32[]{:S(2)}) collective-permute-start(bf16[4,2,128,128]{3,2,1,0:T(8,128)(2,1)S(1)} %get-tuple-element.65), channel_id=1, source_target_pairs={{0,4},{4,0},{8,12},{12,8},{16,20},{20,16},{24,28},{28,24},{1,5},{5... | collective-permute-start | bytes 786440 | tf_op jit(solution)/shard_map/ppermute | solution.py:319
  26.9 16.7 %collective-permute-start.2 = (bf16[4,2,128,128]{3,2,1,0:T(8,128)(2,1)S(1)}, bf16[4,2,128,128]{3,2,1,0:T(8,128)(2,1)S(1)}, u32[]{:S(2)}, u32[]{:S(2)}) collective-permute-start(bf16[4,2,128,128]{3,2,1,0:T(8,128)(2,1)S(1)} %get-tuple-element.62), channel_id=1, source_target_pairs={{0,4},{4,0},{8,12},{12,8},{16,20},{20,16},{24,28},{28,24},{1,5},{5... | collective-permute-start | bytes 786440 | tf_op jit(solution)/shard_map/ppermute | solution.py:319
  34.5 10.5 %collective-permute-start.17 = (bf16[4,1,128,128]{3,2,1,0:T(8,128)(2,1)S(1)}, bf16[4,1,128,128]{3,2,1,0:T(8,128)(2,1)S(1)}, u32[]{:S(2)}, u32[]{:S(2)}) collective-permute-start(bf16[4,1,128,128]{3,2,1,0:T(8,128)(2,1)S(1)} %add_convert_fusion.6), channel_id=1, source_target_pairs={{16,24},{20,28},{17,25},{21,29},{18,26},{22,30},{19,27},{23,31}} | collective-permute-start | bytes 393224 | tf_op jit(solution)/shard_map/ppermute | solution.py:319
  35.9 10.8 %collective-permute-start.13 = (bf16[4,1,128,128]{3,2,1,0:T(8,128)(2,1)S(1)}, bf16[4,1,128,128]{3,2,1,0:T(8,128)(2,1)S(1)}, u32[]{:S(2)}, u32[]{:S(2)}) collective-permute-start(bf16[4,1,128,128]{3,2,1,0:T(8,128)(2,1)S(1)} %add_convert_fusion.8), channel_id=1, source_target_pairs={{16,24},{20,28},{17,25},{21,29},{18,26},{22,30},{19,27},{23,31}} | collective-permute-start | bytes 393224 | tf_op jit(solution)/shard_map/ppermute | solution.py:319
  36.7 21.9 %collective-permute-start.10 = (bf16[4,2,128,128]{3,2,1,0:T(8,128)(2,1)S(1)}, bf16[4,2,128,128]{3,2,1,0:T(8,128)(2,1)S(1)}, u32[]{:S(2)}, u32[]{:S(2)}) collective-permute-start(bf16[4,2,128,128]{3,2,1,0:T(8,128)(2,1)S(1)} %fusion.12), channel_id=1, source_target_pairs={{0,8},{4,12},{1,9},{5,13},{2,10},{6,14},{3,11},{7,15}} | collective-permute-start | bytes 786440 | tf_op jit(solution)/shard_map/ppermute | solution.py:319
  39.8 17.4 %collective-permute-start.7 = (bf16[4,2,128,128]{3,2,1,0:T(8,128)(2,1)S(1)}, bf16[4,2,128,128]{3,2,1,0:T(8,128)(2,1)S(1)}, u32[]{:S(2)}, u32[]{:S(2)}) collective-permute-start(bf16[4,2,128,128]{3,2,1,0:T(8,128)(2,1)S(1)} %fusion.11), channel_id=1, source_target_pairs={{0,8},{4,12},{1,9},{5,13},{2,10},{6,14},{3,11},{7,15}} | collective-permute-start | bytes 786440 | tf_op jit(solution)/shard_map/ppermute | solution.py:319
  43.7 11.9 %collective-permute-start.3 = (bf16[4,2,128,128]{3,2,1,0:T(8,128)(2,1)S(1)}, bf16[4,2,128,128]{3,2,1,0:T(8,128)(2,1)S(1)}, u32[]{:S(2)}, u32[]{:S(2)}) collective-permute-start(bf16[4,2,128,128]{3,2,1,0:T(8,128)(2,1)S(1)} %fusion.10), channel_id=1, source_target_pairs={{0,8},{4,12},{1,9},{5,13},{2,10},{6,14},{3,11},{7,15}} | collective-permute-start | bytes 786440 | tf_op jit(solution)/shard_map/ppermute | solution.py:319
  45.1 28.7 %collective-permute-start.18 = (bf16[4,1,128,128]{3,2,1,0:T(8,128)(2,1)S(1)}, bf16[4,1,128,128]{3,2,1,0:T(8,128)(2,1)S(1)}, u32[]{:S(2)}, u32[]{:S(2)}) collective-permute-start(bf16[4,1,128,128]{3,2,1,0:T(8,128)(2,1)S(1)} %get-tuple-element.113), channel_id=1, source_target_pairs={{0,4},{4,0},{8,12},{12,8},{16,20},{20,16},{24,28},{28,24},{1,5},{5... | collective-permute-start | bytes 393224 | tf_op jit(solution)/shard_map/ppermute | solution.py:319
  46.9 27.0 %collective-permute-start.14 = (bf16[4,1,128,128]{3,2,1,0:T(8,128)(2,1)S(1)}, bf16[4,1,128,128]{3,2,1,0:T(8,128)(2,1)S(1)}, u32[]{:S(2)}, u32[]{:S(2)}) collective-permute-start(bf16[4,1,128,128]{3,2,1,0:T(8,128)(2,1)S(1)} %get-tuple-element.115), channel_id=1, source_target_pairs={{0,4},{4,0},{8,12},{12,8},{16,20},{20,16},{24,28},{28,24},{1,5},{5... | collective-permute-start | bytes 393224 | tf_op jit(solution)/shard_map/ppermute | solution.py:319
  55.8 8.2 %collective-permute-start.4 = (bf16[4,2,128,128]{3,2,1,0:T(8,128)(2,1)S(1)}, bf16[4,2,128,128]{3,2,1,0:T(8,128)(2,1)S(1)}, u32[]{:S(2)}, u32[]{:S(2)}) collective-permute-start(bf16[4,2,128,128]{3,2,1,0:T(8,128)(2,1)S(1)} %add_convert_fusion.5), channel_id=1, source_target_pairs={{8,16},{12,20},{9,17},{13,21},{10,18},{14,22},{11,19},{15,23}} | collective-permute-start | bytes 786440 | tf_op jit(solution)/shard_map/ppermute | solution.py:319
  57.3 11.0 %collective-permute-start.8 = (bf16[4,2,128,128]{3,2,1,0:T(8,128)(2,1)S(1)}, bf16[4,2,128,128]{3,2,1,0:T(8,128)(2,1)S(1)}, u32[]{:S(2)}, u32[]{:S(2)}) collective-permute-start(bf16[4,2,128,128]{3,2,1,0:T(8,128)(2,1)S(1)} %add_convert_fusion.3), channel_id=1, source_target_pairs={{8,16},{12,20},{9,17},{13,21},{10,18},{14,22},{11,19},{15,23}} | collective-permute-start | bytes 786440 | tf_op jit(solution)/shard_map/ppermute | solution.py:319
  58.7 12.4 %collective-permute-start.26 = (bf16[4,2,128,128]{3,2,1,0:T(8,128)(2,1)S(1)}, bf16[4,2,128,128]{3,2,1,0:T(8,128)(2,1)S(1)}, u32[]{:S(2)}, u32[]{:S(2)}) collective-permute-start(bf16[4,2,128,128]{3,2,1,0:T(8,128)(2,1)S(1)} %add_convert_fusion.1), channel_id=1, source_target_pairs={{8,16},{12,20},{9,17},{13,21},{10,18},{14,22},{11,19},{15,23}} | collective-permute-start | bytes 786440 | tf_op jit(solution)/shard_map/ppermute | solution.py:319
  68.4 17.5 %collective-permute-start.36 = (bf16[4,2,128,128]{3,2,1,0:T(8,128)(2,1)S(1)}, bf16[4,2,128,128]{3,2,1,0:T(8,128)(2,1)S(1)}, u32[]{:S(2)}, u32[]{:S(2)}) collective-permute-start(bf16[4,2,128,128]{3,2,1,0:T(8,128)(2,1)S(1)} %add_convert_fusion.2), channel_id=1, source_target_pairs={{16,24},{20,28},{17,25},{21,29},{18,26},{22,30},{19,27},{23,31}} | collective-permute-start | bytes 786440 | tf_op jit(solution)/shard_map/ppermute | solution.py:319
  71.2 15.9 %collective-permute-start.27 = (bf16[4,2,128,128]{3,2,1,0:T(8,128)(2,1)S(1)}, bf16[4,2,128,128]{3,2,1,0:T(8,128)(2,1)S(1)}, u32[]{:S(2)}, u32[]{:S(2)}) collective-permute-start(bf16[4,2,128,128]{3,2,1,0:T(8,128)(2,1)S(1)} %add_convert_fusion), channel_id=1, source_target_pairs={{16,24},{20,28},{17,25},{21,29},{18,26},{22,30},{19,27},{23,31}} | collective-permute-start | bytes 786440 | tf_op jit(solution)/shard_map/ppermute | solution.py:319
  72.3 40.2 %collective-permute-start.45 = (bf16[4,2,128,128]{3,2,1,0:T(8,128)(2,1)S(1)}, bf16[4,2,128,128]{3,2,1,0:T(8,128)(2,1)S(1)}, u32[]{:S(2)}, u32[]{:S(2)}) collective-permute-start(bf16[4,2,128,128]{3,2,1,0:T(8,128)(2,1)S(1)} %get-tuple-element.108), channel_id=1, source_target_pairs={{0,4},{4,0},{8,12},{12,8},{16,20},{20,16},{24,28},{28,24},{1,5},{5... | collective-permute-start | bytes 786440 | tf_op jit(solution)/shard_map/ppermute | solution.py:319
  82.8 22.7 %collective-permute-start.20 = (bf16[384,256]{1,0:T(8,128)(2,1)S(1)}, bf16[384,256]{1,0:T(8,128)(2,1)S(1)}, u32[]{:S(2)}, u32[]{:S(2)}) collective-permute-start(bf16[384,256]{1,0:T(8,128)(2,1)S(1)} %get-tuple-element.72), channel_id=1, source_target_pairs={{0,8},{4,12},{8,16},{12,20},{16,24},{20,28},{24,0},{28,4},{1,9},{5... | collective-permute-start | bytes 589832 | tf_op jit(solution)/shard_map/ppermute | solution.py:342
  85.9 23.0 %collective-permute-start.21 = (bf16[384,256]{1,0:T(8,128)(2,1)S(1)}, bf16[384,256]{1,0:T(8,128)(2,1)S(1)}, u32[]{:S(2)}, u32[]{:S(2)}) collective-permute-start(bf16[384,256]{1,0:T(8,128)(2,1)S(1)} %get-tuple-element.73), channel_id=1, source_target_pairs={{0,12},{4,8},{8,20},{12,16},{16,28},{20,24},{24,4},{28,0},{1,13},{... | collective-permute-start | bytes 589832 | tf_op jit(solution)/shard_map/ppermute | solution.py:342
  87.1 23.9 %collective-permute-start.22 = (bf16[384,256]{1,0:T(8,128)(2,1)S(1)}, bf16[384,256]{1,0:T(8,128)(2,1)S(1)}, u32[]{:S(2)}, u32[]{:S(2)}) collective-permute-start(bf16[384,256]{1,0:T(8,128)(2,1)S(1)} %get-tuple-element.74), channel_id=1, source_target_pairs={{0,16},{4,20},{8,24},{12,28},{16,0},{20,4},{24,8},{28,12},{1,17},{... | collective-permute-start | bytes 589832 | tf_op jit(solution)/shard_map/ppermute | solution.py:342
  88.8 32.2 %collective-permute-start.23 = (bf16[384,256]{1,0:T(8,128)(2,1)S(1)}, bf16[384,256]{1,0:T(8,128)(2,1)S(1)}, u32[]{:S(2)}, u32[]{:S(2)}) collective-permute-start(bf16[384,256]{1,0:T(8,128)(2,1)S(1)} %get-tuple-element.75), channel_id=1, source_target_pairs={{0,20},{4,16},{8,28},{12,24},{16,4},{20,0},{24,12},{28,8},{1,21},{... | collective-permute-start | bytes 589832 | tf_op jit(solution)/shard_map/ppermute | solution.py:342
  105.5 17.2 %collective-permute-start.24 = (bf16[384,256]{1,0:T(8,128)(2,1)S(1)}, bf16[384,256]{1,0:T(8,128)(2,1)S(1)}, u32[]{:S(2)}, u32[]{:S(2)}) collective-permute-start(bf16[384,256]{1,0:T(8,128)(2,1)S(1)} %get-tuple-element.76), channel_id=1, source_target_pairs={{0,24},{4,28},{8,0},{12,4},{16,8},{20,12},{24,16},{28,20},{1,25},{... | collective-permute-start | bytes 589832 | tf_op jit(solution)/shard_map/ppermute | solution.py:342
  108.9 14.1 %collective-permute-start.25 = (bf16[384,256]{1,0:T(8,128)(2,1)S(1)}, bf16[384,256]{1,0:T(8,128)(2,1)S(1)}, u32[]{:S(2)}, u32[]{:S(2)}) collective-permute-start(bf16[384,256]{1,0:T(8,128)(2,1)S(1)} %get-tuple-element.77), channel_id=1, source_target_pairs={{0,28},{4,24},{8,4},{12,0},{16,12},{20,8},{24,20},{28,16},{1,29},{... | collective-permute-start | bytes 589832 | tf_op jit(solution)/shard_map/ppermute | solution.py:342
  111.0 15.5 %collective-permute-start.37 = (bf16[4,2,128,128]{3,2,1,0:T(8,128)(2,1)S(1)}, bf16[4,2,128,128]{3,2,1,0:T(8,128)(2,1)S(1)}, u32[]{:S(2)}, u32[]{:S(2)}) collective-permute-start(bf16[4,2,128,128]{3,2,1,0:T(8,128)(2,1)S(1)} %get-tuple-element.109), channel_id=1, source_target_pairs={{0,4},{4,0},{8,12},{12,8},{16,20},{20,16},{24,28},{28,24},{1,5},{5... | collective-permute-start | bytes 786440 | tf_op jit(solution)/shard_map/ppermute | solution.py:319
  112.5 18.6 %collective-permute-start.28 = (bf16[4,2,128,128]{3,2,1,0:T(8,128)(2,1)S(1)}, bf16[4,2,128,128]{3,2,1,0:T(8,128)(2,1)S(1)}, u32[]{:S(2)}, u32[]{:S(2)}) collective-permute-start(bf16[4,2,128,128]{3,2,1,0:T(8,128)(2,1)S(1)} %get-tuple-element.111), channel_id=1, source_target_pairs={{0,4},{4,0},{8,12},{12,8},{16,20},{20,16},{24,28},{28,24},{1,5},{5... | collective-permute-start | bytes 786440 | tf_op jit(solution)/shard_map/ppermute | solution.py:319
  121.0 12.2 %collective-permute-start.46 = (bf16[384,256]{1,0:T(8,128)(2,1)S(1)}, bf16[384,256]{1,0:T(8,128)(2,1)S(1)}, u32[]{:S(2)}, u32[]{:S(2)}) collective-permute-start(bf16[384,256]{1,0:T(8,128)(2,1)S(1)} %get-tuple-element.96), channel_id=1, source_target_pairs={{0,4},{4,0},{8,12},{12,8},{16,20},{20,16},{24,28},{28,24},{1,5},{5... | collective-permute-start | bytes 589832 | tf_op jit(solution)/shard_map/ppermute | solution.py:342
  122.6 18.6 %collective-permute-start.47 = (bf16[384,256]{1,0:T(8,128)(2,1)S(1)}, bf16[384,256]{1,0:T(8,128)(2,1)S(1)}, u32[]{:S(2)}, u32[]{:S(2)}) collective-permute-start(bf16[384,256]{1,0:T(8,128)(2,1)S(1)} %get-tuple-element.97), channel_id=1, source_target_pairs={{0,8},{4,12},{8,16},{12,20},{16,24},{20,28},{24,0},{28,4},{1,9},{5... | collective-permute-start | bytes 589832 | tf_op jit(solution)/shard_map/ppermute | solution.py:342
  123.1 21.8 %collective-permute-start.48 = (bf16[384,256]{1,0:T(8,128)(2,1)S(1)}, bf16[384,256]{1,0:T(8,128)(2,1)S(1)}, u32[]{:S(2)}, u32[]{:S(2)}) collective-permute-start(bf16[384,256]{1,0:T(8,128)(2,1)S(1)} %get-tuple-element.98), channel_id=1, source_target_pairs={{0,12},{4,8},{8,20},{12,16},{16,28},{20,24},{24,4},{28,0},{1,13},{... | collective-permute-start | bytes 589832 | tf_op jit(solution)/shard_map/ppermute | solution.py:342
  126.5 24.7 %collective-permute-start.49 = (bf16[384,256]{1,0:T(8,128)(2,1)S(1)}, bf16[384,256]{1,0:T(8,128)(2,1)S(1)}, u32[]{:S(2)}, u32[]{:S(2)}) collective-permute-start(bf16[384,256]{1,0:T(8,128)(2,1)S(1)} %get-tuple-element.99), channel_id=1, source_target_pairs={{0,16},{4,20},{8,24},{12,28},{16,0},{20,4},{24,8},{28,12},{1,17},{... | collective-permute-start | bytes 589832 | tf_op jit(solution)/shard_map/ppermute | solution.py:342
  131.2 26.4 %collective-permute-start.50 = (bf16[384,256]{1,0:T(8,128)(2,1)S(1)}, bf16[384,256]{1,0:T(8,128)(2,1)S(1)}, u32[]{:S(2)}, u32[]{:S(2)}) collective-permute-start(bf16[384,256]{1,0:T(8,128)(2,1)S(1)} %get-tuple-element.100), channel_id=1, source_target_pairs={{0,20},{4,16},{8,28},{12,24},{16,4},{20,0},{24,12},{28,8},{1,21},{... | collective-permute-start | bytes 589832 | tf_op jit(solution)/shard_map/ppermute | solution.py:342
  133.3 24.3 %collective-permute-start.51 = (bf16[384,256]{1,0:T(8,128)(2,1)S(1)}, bf16[384,256]{1,0:T(8,128)(2,1)S(1)}, u32[]{:S(2)}, u32[]{:S(2)}) collective-permute-start(bf16[384,256]{1,0:T(8,128)(2,1)S(1)} %get-tuple-element.101), channel_id=1, source_target_pairs={{0,24},{4,28},{8,0},{12,4},{16,8},{20,12},{24,16},{28,20},{1,25},{... | collective-permute-start | bytes 589832 | tf_op jit(solution)/shard_map/ppermute | solution.py:342
  141.3 29.2 %collective-permute-start.52 = (bf16[384,256]{1,0:T(8,128)(2,1)S(1)}, bf16[384,256]{1,0:T(8,128)(2,1)S(1)}, u32[]{:S(2)}, u32[]{:S(2)}) collective-permute-start(bf16[384,256]{1,0:T(8,128)(2,1)S(1)} %get-tuple-element.102), channel_id=1, source_target_pairs={{0,28},{4,24},{8,4},{12,0},{16,12},{20,8},{24,20},{28,16},{1,29},{... | collective-permute-start | bytes 589832 | tf_op jit(solution)/shard_map/ppermute | solution.py:342
  144.9 27.4 %collective-permute-start.38 = (bf16[384,256]{1,0:T(8,128)(2,1)S(1)}, bf16[384,256]{1,0:T(8,128)(2,1)S(1)}, u32[]{:S(2)}, u32[]{:S(2)}) collective-permute-start(bf16[384,256]{1,0:T(8,128)(2,1)S(1)} %get-tuple-element.88), channel_id=1, source_target_pairs={{0,4},{4,0},{8,12},{12,8},{16,20},{20,16},{24,28},{28,24},{1,5},{5... | collective-permute-start | bytes 589832 | tf_op jit(solution)/shard_map/ppermute | solution.py:342
  151.2 23.2 %collective-permute-start.39 = (bf16[384,256]{1,0:T(8,128)(2,1)S(1)}, bf16[384,256]{1,0:T(8,128)(2,1)S(1)}, u32[]{:S(2)}, u32[]{:S(2)}) collective-permute-start(bf16[384,256]{1,0:T(8,128)(2,1)S(1)} %get-tuple-element.89), channel_id=1, source_target_pairs={{0,8},{4,12},{8,16},{12,20},{16,24},{20,28},{24,0},{28,4},{1,9},{5... | collective-permute-start | bytes 589832 | tf_op jit(solution)/shard_map/ppermute | solution.py:342
  157.5 18.3 %collective-permute-start.40 = (bf16[384,256]{1,0:T(8,128)(2,1)S(1)}, bf16[384,256]{1,0:T(8,128)(2,1)S(1)}, u32[]{:S(2)}, u32[]{:S(2)}) collective-permute-start(bf16[384,256]{1,0:T(8,128)(2,1)S(1)} %get-tuple-element.90), channel_id=1, source_target_pairs={{0,12},{4,8},{8,20},{12,16},{16,28},{20,24},{24,4},{28,0},{1,13},{... | collective-permute-start | bytes 589832 | tf_op jit(solution)/shard_map/ppermute | solution.py:342
  157.5 20.6 %collective-permute-start.41 = (bf16[384,256]{1,0:T(8,128)(2,1)S(1)}, bf16[384,256]{1,0:T(8,128)(2,1)S(1)}, u32[]{:S(2)}, u32[]{:S(2)}) collective-permute-start(bf16[384,256]{1,0:T(8,128)(2,1)S(1)} %get-tuple-element.91), channel_id=1, source_target_pairs={{0,16},{4,20},{8,24},{12,28},{16,0},{20,4},{24,8},{28,12},{1,17},{... | collective-permute-start | bytes 589832 | tf_op jit(solution)/shard_map/ppermute | solution.py:342
  170.5 15.0 %collective-permute-start.42 = (bf16[384,256]{1,0:T(8,128)(2,1)S(1)}, bf16[384,256]{1,0:T(8,128)(2,1)S(1)}, u32[]{:S(2)}, u32[]{:S(2)}) collective-permute-start(bf16[384,256]{1,0:T(8,128)(2,1)S(1)} %get-tuple-element.92), channel_id=1, source_target_pairs={{0,20},{4,16},{8,28},{12,24},{16,4},{20,0},{24,12},{28,8},{1,21},{... | collective-permute-start | bytes 589832 | tf_op jit(solution)/shard_map/ppermute | solution.py:342
  172.3 27.0 %collective-permute-start.43 = (bf16[384,256]{1,0:T(8,128)(2,1)S(1)}, bf16[384,256]{1,0:T(8,128)(2,1)S(1)}, u32[]{:S(2)}, u32[]{:S(2)}) collective-permute-start(bf16[384,256]{1,0:T(8,128)(2,1)S(1)} %get-tuple-element.93), channel_id=1, source_target_pairs={{0,24},{4,28},{8,0},{12,4},{16,8},{20,12},{24,16},{28,20},{1,25},{... | collective-permute-start | bytes 589832 | tf_op jit(solution)/shard_map/ppermute | solution.py:342
  174.4 28.5 %collective-permute-start.44 = (bf16[384,256]{1,0:T(8,128)(2,1)S(1)}, bf16[384,256]{1,0:T(8,128)(2,1)S(1)}, u32[]{:S(2)}, u32[]{:S(2)}) collective-permute-start(bf16[384,256]{1,0:T(8,128)(2,1)S(1)} %get-tuple-element.94), channel_id=1, source_target_pairs={{0,28},{4,24},{8,4},{12,0},{16,12},{20,8},{24,20},{28,16},{1,29},{... | collective-permute-start | bytes 589832 | tf_op jit(solution)/shard_map/ppermute | solution.py:342
  175.9 27.0 %collective-permute-start.29 = (bf16[384,256]{1,0:T(8,128)(2,1)S(1)}, bf16[384,256]{1,0:T(8,128)(2,1)S(1)}, u32[]{:S(2)}, u32[]{:S(2)}) collective-permute-start(bf16[384,256]{1,0:T(8,128)(2,1)S(1)} %get-tuple-element.80), channel_id=1, source_target_pairs={{0,4},{4,0},{8,12},{12,8},{16,20},{20,16},{24,28},{28,24},{1,5},{5... | collective-permute-start | bytes 589832 | tf_op jit(solution)/shard_map/ppermute | solution.py:342
  178.2 25.7 %collective-permute-start.30 = (bf16[384,256]{1,0:T(8,128)(2,1)S(1)}, bf16[384,256]{1,0:T(8,128)(2,1)S(1)}, u32[]{:S(2)}, u32[]{:S(2)}) collective-permute-start(bf16[384,256]{1,0:T(8,128)(2,1)S(1)} %get-tuple-element.81), channel_id=1, source_target_pairs={{0,8},{4,12},{8,16},{12,20},{16,24},{20,28},{24,0},{28,4},{1,9},{5... | collective-permute-start | bytes 589832 | tf_op jit(solution)/shard_map/ppermute | solution.py:342
  185.5 27.2 %collective-permute-start.31 = (bf16[384,256]{1,0:T(8,128)(2,1)S(1)}, bf16[384,256]{1,0:T(8,128)(2,1)S(1)}, u32[]{:S(2)}, u32[]{:S(2)}) collective-permute-start(bf16[384,256]{1,0:T(8,128)(2,1)S(1)} %get-tuple-element.82), channel_id=1, source_target_pairs={{0,12},{4,8},{8,20},{12,16},{16,28},{20,24},{24,4},{28,0},{1,13},{... | collective-permute-start | bytes 589832 | tf_op jit(solution)/shard_map/ppermute | solution.py:342
  199.3 15.7 %collective-permute-start.32 = (bf16[384,256]{1,0:T(8,128)(2,1)S(1)}, bf16[384,256]{1,0:T(8,128)(2,1)S(1)}, u32[]{:S(2)}, u32[]{:S(2)}) collective-permute-start(bf16[384,256]{1,0:T(8,128)(2,1)S(1)} %get-tuple-element.83), channel_id=1, source_target_pairs={{0,16},{4,20},{8,24},{12,28},{16,0},{20,4},{24,8},{28,12},{1,17},{... | collective-permute-start | bytes 589832 | tf_op jit(solution)/shard_map/ppermute | solution.py:342
  202.9 15.3 %collective-permute-start.33 = (bf16[384,256]{1,0:T(8,128)(2,1)S(1)}, bf16[384,256]{1,0:T(8,128)(2,1)S(1)}, u32[]{:S(2)}, u32[]{:S(2)}) collective-permute-start(bf16[384,256]{1,0:T(8,128)(2,1)S(1)} %get-tuple-element.84), channel_id=1, source_target_pairs={{0,20},{4,16},{8,28},{12,24},{16,4},{20,0},{24,12},{28,8},{1,21},{... | collective-permute-start | bytes 589832 | tf_op jit(solution)/shard_map/ppermute | solution.py:342
  202.9 15.9 %collective-permute-start.34 = (bf16[384,256]{1,0:T(8,128)(2,1)S(1)}, bf16[384,256]{1,0:T(8,128)(2,1)S(1)}, u32[]{:S(2)}, u32[]{:S(2)}) collective-permute-start(bf16[384,256]{1,0:T(8,128)(2,1)S(1)} %get-tuple-element.85), channel_id=1, source_target_pairs={{0,24},{4,28},{8,0},{12,4},{16,8},{20,12},{24,16},{28,20},{1,25},{... | collective-permute-start | bytes 589832 | tf_op jit(solution)/shard_map/ppermute | solution.py:342
  203.9 17.0 %collective-permute-start.35 = (bf16[384,256]{1,0:T(8,128)(2,1)S(1)}, bf16[384,256]{1,0:T(8,128)(2,1)S(1)}, u32[]{:S(2)}, u32[]{:S(2)}) collective-permute-start(bf16[384,256]{1,0:T(8,128)(2,1)S(1)} %get-tuple-element.86), channel_id=1, source_target_pairs={{0,28},{4,24},{8,4},{12,0},{16,12},{20,8},{24,20},{28,16},{1,29},{... | collective-permute-start | bytes 589832 | tf_op jit(solution)/shard_map/ppermute | solution.py:342
  (16 other events, 323.8 us)

commit v2 on v1

--- a/solution.py
+++ b/solution.py
@@ -15,9 +15,26 @@
 TILE = 256
 SPARE = 8 * 1024 * 1024
 ORDER = {
-    ("message", 2, 0): [("message", 0, 1), ("message", 1, 1)],
-    ("message", 3, 0): [("message", 0, 1), ("message", 1, 1)],
-    ("message", 4, 0): [("message", 0, 1), ("message", 1, 1)],
+    ("message", 1, 0): [("message", 0, 0)],
+    ("message", 2, 0): [("message", 1, 0)],
+    ("message", 3, 0): [("message", 2, 0)],
+    ("message", 4, 0): [("message", 3, 0)],
+    ("message", 1, 1): [("message", 0, 1)],
+    ("message", 1, 2): [("message", 0, 2)],
+    ("message", 1, 3): [("message", 0, 3)],
+    ("message", 1, 4): [("message", 0, 4)],
+    ("message", 2, 1): [("message", 1, 1)],
+    ("message", 2, 2): [("message", 1, 2)],
+    ("message", 2, 3): [("message", 1, 3)],
+    ("message", 2, 4): [("message", 1, 4)],
+    ("message", 3, 1): [("message", 2, 1)],
+    ("message", 3, 2): [("message", 2, 2)],
+    ("message", 3, 3): [("message", 2, 3)],
+    ("message", 3, 4): [("message", 2, 4)],
+    ("message", 4, 1): [("message", 3, 1)],
+    ("message", 4, 2): [("message", 3, 2)],
+    ("message", 4, 3): [("message", 3, 3)],
+    ("message", 4, 4): [("message", 3, 4)],
     ("mixed", 0): [("message", 2, 4), ("message", 3, 3), ("message", 4, 2)],
 }
 
@@ -76,7 +93,7 @@
     ]
     return pl.pallas_call(
         functools.partial(local_body, n, low, widths),
-        in_specs=[pl.BlockSpec(memory_space=pltpu.SMEM)] + [pl.BlockSpec(memory_space=pl.ANY)] * 2,
+        in_specs=[pl.BlockSpec(memory_space=pltpu.SMEM)] + [pl.BlockSpec(memory_space=pltpu.HBM)] * 2,
         out_specs=[pl.BlockSpec(memory_space=pltpu.VMEM)] * len(shapes),
         out_shape=shapes,
         scratch_shapes=[buf, buf, pltpu.SemaphoreType.DMA((2, n))],
@@ -173,8 +190,10 @@
     state = pltpu.VMEM((m, width, HEAD, HEAD), jnp.bfloat16)
     return pl.pallas_call(
         functools.partial(attend_body, n, low, spans),
-        in_specs=[pl.BlockSpec(memory_space=pltpu.SMEM)] + [pl.BlockSpec(memory_space=pl.ANY)] * (4 + 2 * len(states)),
-        out_specs=[pl.BlockSpec(memory_space=pl.ANY)] * n,
+        in_specs=[pl.BlockSpec(memory_space=pltpu.SMEM)]
+        + [pl.BlockSpec(memory_space=pltpu.HBM)] * 3
+        + [pl.BlockSpec(memory_space=pl.ANY)] * (1 + 2 * len(states)),
+        out_specs=[pl.BlockSpec(memory_space=pltpu.HBM)] * n,
         out_shape=[jax.ShapeDtypeStruct((rows, wide), jnp.bfloat16)] * n,
         scratch_shapes=[
             tokens,
@@ -221,7 +240,7 @@
 
 def put(place, parts, out, n, low):
     rows, first = parts[0].shape[0], out is None
-    anywhere = pl.BlockSpec(memory_space=pl.ANY)
+    anywhere = pl.BlockSpec(memory_space=pltpu.HBM)
     return pl.pallas_call(
         functools.partial(put_body, n, low),
         in_specs=[pl.BlockSpec(memory_space=pltpu.SMEM)] + [anywhere] * (n if first else n + 1),
@@ -257,7 +276,7 @@
         me = lax.axis_index("seq")
         self.col = me % 2
         self.place = jnp.stack([me // 2, self.col]).astype(jnp.int32)
-        self.arrays = queries, keys, values
+        self.arrays = tuple(pltpu.with_memory_space_constraint(x, pltpu.HBM) for x in (queries, keys, values))
         self.gain = gain.reshape(1, HEADS * HEAD)
         self.groups, self.parts, self.chunks = (split(widths, HEADS // n) for widths in (LOCAL, PREFIX, MIXED))
         self.made = {}

time: 224 us -> 215 us (0.960)
  waiting for transfers between devices: 92.6 us -> 73 us
  local copies, waits for them, and re-layouts: 11.2 us -> 0.01 us
  other arithmetic: 1.96 us -> 12.4 us
  starting transfers between devices: 66.7 us -> 74.7 us
  Pallas kernels: 50.1 us -> 53.5 us
    ppermute x25, waiting for transfers between devices: 29.2 us -> 12.5 us  [prefix(): return lax.ppermute(self.get('message', c, s), 'seq', pairs)]
    unnamed x22 -> x2, local copies, waits for them, and re-layouts: 11.2 us -> 0.01 us
    convert_element_type x19 -> x15, other arithmetic: 1.66 us -> 8.85 us  [message(): return self.hold(value.astype(jnp.bfloat16), 'message', c, s)]
    ppermute x28, starting transfers between devices: 38.1 us -> 43 us  [sent(): lax.ppermute(self.hold(self.get('mixed', c)[k], 'sent', c, k), 'seq', pairs)]
    convert_element_type x1 -> x4, other arithmetic: 0.22 us -> 3.47 us  [states(): (self.get('total', c) + jnp.where(self.col == 1, near, 0.0)).astype(jnp.b...]
    ppermute x25, starting transfers between devices: 28.6 us -> 31.6 us  [prefix(): return lax.ppermute(self.get('message', c, s), 'seq', pairs)]
    ppermute x28, waiting for transfers between devices: 63.5 us -> 60.5 us  [sent(): lax.ppermute(self.hold(self.get('mixed', c)[k], 'sent', c, k), 'seq', pairs)]
    pallas_call x4, Pallas kernels: 32.2 us -> 34.7 us  [attend(): pl.pallas_call(functools.partial(attend_body, n, low, spans), in_specs=[p...]
  transfers between devices with their start and end apart: 53 -> 53, of which waited for: 25 -> 20; matrix products, arithmetic and copies ran while one was open for 1% -> 6% of each run, Pallas kernels for 20% -> 22%
where the time goes in v2:
time: 215 us; the launch traced here: 214 us
  starting transfers between devices  74.7 us (35%)
  waiting for transfers between devices  73 us (34%)
  Pallas kernels  53.5 us (25%)
  other arithmetic  12.4 us (6%)
    ppermute x28, waiting for transfers between devices, sent(): lax.ppermute(self.hold(self.get('mixed', c)[k], 'sent', c, k), 'seq', pairs)  60.5 us
    ppermute x28, starting transfers between devices, sent(): lax.ppermute(self.hold(self.get('mixed', c)[k], 'sent', c, k), 'seq', pairs)  43 us
    pallas_call x4, Pallas kernels, attend(): pl.pallas_call(functools.partial(attend_body, n, low, spans), in_specs=[p...  34.7 us
    ppermute x25, starting transfers between devices, prefix(): return lax.ppermute(self.get('message', c, s), 'seq', pairs)  31.6 us
    ppermute x25, waiting for transfers between devices, prefix(): return lax.ppermute(self.get('message', c, s), 'seq', pairs)  12.5 us
    pallas_call x2, Pallas kernels, local_states(): pl.pallas_call(functools.partial(local_body, n, low, widths), in_specs=[p...  9.67 us
    pallas_call x4, Pallas kernels, put(): pl.pallas_call(functools.partial(put_body, n, low), in_specs=[pl.BlockSpe...  9.14 us
    convert_element_type x15, other arithmetic, message(): return self.hold(value.astype(jnp.bfloat16), 'message', c, s)  8.85 us
  transfers between devices with their start and end apart: 53, of which 20 were waited for; matrix products, arithmetic and copies ran while one was open for 6% of the time, Pallas kernels for 22%

profile of v2, /device:TPU:8, one launch (start us, length us, event | category | flops | bytes accessed | tf_op | source)
XLA Modules:
  0.0 214.2 jit_solution(6000219288014010862)
XLA Ops:
  0.1 4.2 %local.3 = (f32[4,1,128,128]{3,2,1,0:T(8,128)S(1)}, bf16[4,1,128,128]{3,2,1,0:T(8,128)(2,1)S(1)}, f32[4,1,128,128]{3,2,1,0:T(8,128)S(1)}, bf16[4,1,128,128]{3,2,1,0:T(8,128)(2,1)S(1)}) custom-call(s32[2]{0:T(128)S(1)} %pad_add_fusion.place, bf16[384,8192]{1,0:T(8,128)(2,1)} %keys.11, bf16[384,8192]{1,0:T(8,128)(2,1)} %values.11), custom_call_target="tpu_custom_call" | custom-call | flops 201326592 | bytes 3145728 | tf_op jit(solution)/shard_map/local/pallas_call | solution.py:94
  4.2 1.6 collective-permute-start.2
  6.3 5.5 %local.2 = (f32[4,2,128,128]{3,2,1,0:T(8,128)S(1)}, bf16[4,2,128,128]{3,2,1,0:T(8,128)(2,1)S(1)}, f32[4,2,128,128]{3,2,1,0:T(8,128)S(1)}, bf16[4,2,128,128]{3,2,...) custom-call(s32[2]{0:T(128)S(1)} %pad_add_fusion.place, ...), custom_call_target="tpu_custom_call" | custom-call | flops 603979776 | bytes 9437184 | tf_op jit(solution)/shard_map/local/pallas_call | solution.py:94
  11.9 1.6 collective-permute-start
  13.9 1.5 collective-permute-start.15
  19.1 4.5 %collective-permute-done.5 = bf16[4,1,128,128]{3,2,1,0:T(8,128)(2,1)S(1)} collective-permute-done((bf16[4,1,128,128]{3,2,1,0:T(8,128)(2,1)S(1)}, bf16[4,1,128,128]{3,2,1,0:T(8,128)(2,1)S(1)}, u32[]{:S(2)}, u32[]{:S(2)}) %collective-permute-start.5) | collective-permute-done | bytes 131104 | tf_op jit(solution)/shard_map/ppermute | solution.py:338
  24.5 1.3 collective-permute-start.8
  25.9 1.3 collective-permute-start.7
  38.1 1.4 collective-permute-done.3
  40.6 5.8 %collective-permute-start.6 = (bf16[4,2,128,128]{3,2,1,0:T(8,128)(2,1)S(1)}, bf16[4,2,128,128]{3,2,1,0:T(8,128)(2,1)S(1)}, u32[]{:S(2)}, u32[]{:S(2)}) collective-permute-start(bf16[4,2,128,128]{3,2,1,0:T(8,128)(2,1)S(1)} %add_convert_fusion.5), channel_id=1, source_target_pairs={{8,16},{12,20},{9,17},{13,21},{10,18},{14,22},{11,19},{15,23}} | collective-permute-start | bytes 786440 | tf_op jit(solution)/shard_map/ppermute | solution.py:338
  47.5 1.3 collective-permute-start.14
  48.9 1.3 collective-permute-start.26
  50.2 2.9 %collective-permute-done.6 = bf16[4,2,128,128]{3,2,1,0:T(8,128)(2,1)S(1)} collective-permute-done((bf16[4,2,128,128]{3,2,1,0:T(8,128)(2,1)S(1)}, bf16[4,2,128,128]{3,2,1,0:T(8,128)(2,1)S(1)}, u32[]{:S(2)}, u32[]{:S(2)}) %collective-permute-start.6) | collective-permute-done | bytes 262176 | tf_op jit(solution)/shard_map/ppermute | solution.py:338
  54.8 2.5 %collective-permute-done.14 = bf16[4,2,128,128]{3,2,1,0:T(8,128)(2,1)S(1)} collective-permute-done((bf16[4,2,128,128]{3,2,1,0:T(8,128)(2,1)S(1)}, bf16[4,2,128,128]{3,2,1,0:T(8,128)(2,1)S(1)}, u32[]{:S(2)}, u32[]{:S(2)}) %collective-permute-start.14) | collective-permute-done | bytes 262176 | tf_op jit(solution)/shard_map/ppermute | solution.py:338
  62.1 1.5 collective-permute-start.45
  63.7 8.7 %attend.4 = (bf16[384,256]{1,0:T(8,128)(2,1)S(1)}, bf16[384,256]{1,0:T(8,128)(2,1)S(1)}, bf16[384,256]{1,0:T(8,128)(2,1)S(1)}, bf16[384,256]{1,0:T(8,128)(2,1)S(...) custom-call(s32[2]{0:T(128)S(1)} %pad_add_fusion.place, ...), custom_call_target="tpu_custom_call" | custom-call | flops 1409286144 | bytes 6291456 | tf_op jit(solution)/shard_map/attend/pallas_call | solution.py:191
  73.0 3.1 %collective-permute-start.20 = (bf16[384,256]{1,0:T(8,128)(2,1)S(1)}, bf16[384,256]{1,0:T(8,128)(2,1)S(1)}, u32[]{:S(2)}, u32[]{:S(2)}) collective-permute-start(bf16[384,256]{1,0:T(8,128)(2,1)S(1)} %get-tuple-element.103), channel_id=1, source_target_pairs={{0,8},{4,12},{8,16},{12,20},{16,24},{20,28},{24,0},{28,4},{1,9},{5... | collective-permute-start | bytes 589832 | tf_op jit(solution)/shard_map/ppermute | solution.py:361
  76.1 2.7 %collective-permute-start.21 = (bf16[384,256]{1,0:T(8,128)(2,1)S(1)}, bf16[384,256]{1,0:T(8,128)(2,1)S(1)}, u32[]{:S(2)}, u32[]{:S(2)}) collective-permute-start(bf16[384,256]{1,0:T(8,128)(2,1)S(1)} %get-tuple-element.104), channel_id=1, source_target_pairs={{0,12},{4,8},{8,20},{12,16},{16,28},{20,24},{24,4},{28,0},{1,13},{... | collective-permute-start | bytes 589832 | tf_op jit(solution)/shard_map/ppermute | solution.py:361
  79.2 2.4 %collective-permute-done.19.refs_1_ = bf16[384,256]{1,0:T(8,128)(2,1)S(1)} collective-permute-done((bf16[384,256]{1,0:T(8,128)(2,1)S(1)}, bf16[384,256]{1,0:T(8,128)(2,1)S(1)}, u32[]{:S(2)}, u32[]{:S(2)}) %collective-permute-start.19) | collective-permute-done | bytes 196640 | tf_op jit(solution)/shard_map/ppermute | solution.py:361
  81.5 2.6 %collective-permute-start.23 = (bf16[384,256]{1,0:T(8,128)(2,1)S(1)}, bf16[384,256]{1,0:T(8,128)(2,1)S(1)}, u32[]{:S(2)}, u32[]{:S(2)}) collective-permute-start(bf16[384,256]{1,0:T(8,128)(2,1)S(1)} %get-tuple-element.106), channel_id=1, source_target_pairs={{0,20},{4,16},{8,28},{12,24},{16,4},{20,0},{24,12},{28,8},{1,21},{... | collective-permute-start | bytes 589832 | tf_op jit(solution)/shard_map/ppermute | solution.py:361
  85.4 3.7 %collective-permute-done.20.refs_2_ = bf16[384,256]{1,0:T(8,128)(2,1)S(1)} collective-permute-done((bf16[384,256]{1,0:T(8,128)(2,1)S(1)}, bf16[384,256]{1,0:T(8,128)(2,1)S(1)}, u32[]{:S(2)}, u32[]{:S(2)}) %collective-permute-start.20) | collective-permute-done | bytes 196640 | tf_op jit(solution)/shard_map/ppermute | solution.py:361
  89.1 3.6 %collective-permute-done.21.refs_3_ = bf16[384,256]{1,0:T(8,128)(2,1)S(1)} collective-permute-done((bf16[384,256]{1,0:T(8,128)(2,1)S(1)}, bf16[384,256]{1,0:T(8,128)(2,1)S(1)}, u32[]{:S(2)}, u32[]{:S(2)}) %collective-permute-start.21) | collective-permute-done | bytes 196640 | tf_op jit(solution)/shard_map/ppermute | solution.py:361
  92.7 1.4 collective-permute-start.29
  94.1 5.0 %collective-permute-done.22.refs_4_ = bf16[384,256]{1,0:T(8,128)(2,1)S(1)} collective-permute-done((bf16[384,256]{1,0:T(8,128)(2,1)S(1)}, bf16[384,256]{1,0:T(8,128)(2,1)S(1)}, u32[]{:S(2)}, u32[]{:S(2)}) %collective-permute-start.22) | collective-permute-done | bytes 196640 | tf_op jit(solution)/shard_map/ppermute | solution.py:361
  99.0 5.6 %collective-permute-start.25 = (bf16[384,256]{1,0:T(8,128)(2,1)S(1)}, bf16[384,256]{1,0:T(8,128)(2,1)S(1)}, u32[]{:S(2)}, u32[]{:S(2)}) collective-permute-start(bf16[384,256]{1,0:T(8,128)(2,1)S(1)} %get-tuple-element.108), channel_id=1, source_target_pairs={{0,28},{4,24},{8,4},{12,0},{16,12},{20,8},{24,20},{28,16},{1,29},{... | collective-permute-start | bytes 589832 | tf_op jit(solution)/shard_map/ppermute | solution.py:361
  104.6 8.6 %attend.7 = (bf16[384,256]{1,0:T(8,128)(2,1)S(1)}, bf16[384,256]{1,0:T(8,128)(2,1)S(1)}, bf16[384,256]{1,0:T(8,128)(2,1)S(1)}, bf16[384,256]{1,0:T(8,128)(2,1)S(...) custom-call(s32[2]{0:T(128)S(1)} %pad_add_fusion.place, ...), custom_call_target="tpu_custom_call" | custom-call | flops 1409286144 | bytes 6291456 | tf_op jit(solution)/shard_map/attend/pallas_call | solution.py:191
  114.1 5.1 %collective-permute-start.49 = (bf16[384,256]{1,0:T(8,128)(2,1)S(1)}, bf16[384,256]{1,0:T(8,128)(2,1)S(1)}, u32[]{:S(2)}, u32[]{:S(2)}) collective-permute-start(bf16[384,256]{1,0:T(8,128)(2,1)S(1)} %get-tuple-element.133), channel_id=1, source_target_pairs={{0,16},{4,20},{8,24},{12,28},{16,0},{20,4},{24,8},{28,12},{1,17},{... | collective-permute-start | bytes 589832 | tf_op jit(solution)/shard_map/ppermute | solution.py:361
  120.0 8.7 %attend.6 = (bf16[384,256]{1,0:T(8,128)(2,1)S(1)}, bf16[384,256]{1,0:T(8,128)(2,1)S(1)}, bf16[384,256]{1,0:T(8,128)(2,1)S(1)}, bf16[384,256]{1,0:T(8,128)(2,1)S(...) custom-call(s32[2]{0:T(128)S(1)} %pad_add_fusion.place, ...), custom_call_target="tpu_custom_call" | custom-call | flops 1409286144 | bytes 6291456 | tf_op jit(solution)/shard_map/attend/pallas_call | solution.py:191
  128.7 4.6 %collective-permute-start.52 = (bf16[384,256]{1,0:T(8,128)(2,1)S(1)}, bf16[384,256]{1,0:T(8,128)(2,1)S(1)}, u32[]{:S(2)}, u32[]{:S(2)}) collective-permute-start(bf16[384,256]{1,0:T(8,128)(2,1)S(1)} %get-tuple-element.136), channel_id=1, source_target_pairs={{0,28},{4,24},{8,4},{12,0},{16,12},{20,8},{24,20},{28,16},{1,29},{... | collective-permute-start | bytes 589832 | tf_op jit(solution)/shard_map/ppermute | solution.py:361
  133.3 5.0 %collective-permute-done.48.refs_3_ = bf16[384,256]{1,0:T(8,128)(2,1)S(1)} collective-permute-done((bf16[384,256]{1,0:T(8,128)(2,1)S(1)}, bf16[384,256]{1,0:T(8,128)(2,1)S(1)}, u32[]{:S(2)}, u32[]{:S(2)}) %collective-permute-start.48) | collective-permute-done | bytes 196640 | tf_op jit(solution)/shard_map/ppermute | solution.py:361
  138.3 1.3 collective-permute-start.38
  139.6 2.9 %collective-permute-done.49.refs_4_ = bf16[384,256]{1,0:T(8,128)(2,1)S(1)} collective-permute-done((bf16[384,256]{1,0:T(8,128)(2,1)S(1)}, bf16[384,256]{1,0:T(8,128)(2,1)S(1)}, u32[]{:S(2)}, u32[]{:S(2)}) %collective-permute-start.49) | collective-permute-done | bytes 196640 | tf_op jit(solution)/shard_map/ppermute | solution.py:361
  142.5 6.3 %collective-permute-done.50.refs_5_ = bf16[384,256]{1,0:T(8,128)(2,1)S(1)} collective-permute-done((bf16[384,256]{1,0:T(8,128)(2,1)S(1)}, bf16[384,256]{1,0:T(8,128)(2,1)S(1)}, u32[]{:S(2)}, u32[]{:S(2)}) %collective-permute-start.50) | collective-permute-done | bytes 196640 | tf_op jit(solution)/shard_map/ppermute | solution.py:361
  148.8 4.1 %collective-permute-start.41 = (bf16[384,256]{1,0:T(8,128)(2,1)S(1)}, bf16[384,256]{1,0:T(8,128)(2,1)S(1)}, u32[]{:S(2)}, u32[]{:S(2)}) collective-permute-start(bf16[384,256]{1,0:T(8,128)(2,1)S(1)} %get-tuple-element.125), channel_id=1, source_target_pairs={{0,16},{4,20},{8,24},{12,28},{16,0},{20,4},{24,8},{28,12},{1,17},{... | collective-permute-start | bytes 589832 | tf_op jit(solution)/shard_map/ppermute | solution.py:361
  153.0 2.3 %put.4 = (bf16[3072,1024]{1,0:T(8,128)(2,1)}, s32[2]{0:T(128)S(1)}) custom-call(s32[2]{0:T(128)S(1)} %pad_add_fusion.place, bf16[384,256]{1,0:T(8,128)(2,1)S(1)} %get-tuple-element.101.refs_0_, bf16[384,256]{1,0:T(8,128)(2,1)S(1)} %collective-permute-done.19.refs_1_, bf16[384,256]{1,0:T(8,128)(2,1)S(1)} %collective-permute-done.20.refs_2_, ...), custom_call_target="tpu_custom_call" | custom-call | tf_op jit(solution)/shard_map/put/pallas_call | solution.py:244
  155.3 8.7 %attend.5 = (bf16[384,256]{1,0:T(8,128)(2,1)S(1)}, bf16[384,256]{1,0:T(8,128)(2,1)S(1)}, bf16[384,256]{1,0:T(8,128)(2,1)S(1)}, bf16[384,256]{1,0:T(8,128)(2,1)S(...) custom-call(s32[2]{0:T(128)S(1)} %get-tuple-element.109.place, ...), custom_call_target="tpu_custom_call" | custom-call | flops 1409286144 | bytes 6291456 | tf_op jit(solution)/shard_map/attend/pallas_call | solution.py:191
  164.2 2.8 %collective-permute-start.43 = (bf16[384,256]{1,0:T(8,128)(2,1)S(1)}, bf16[384,256]{1,0:T(8,128)(2,1)S(1)}, u32[]{:S(2)}, u32[]{:S(2)}) collective-permute-start(bf16[384,256]{1,0:T(8,128)(2,1)S(1)} %get-tuple-element.127), channel_id=1, source_target_pairs={{0,24},{4,28},{8,0},{12,4},{16,8},{20,12},{24,16},{28,20},{1,25},{... | collective-permute-start | bytes 589832 | tf_op jit(solution)/shard_map/ppermute | solution.py:361
  167.0 2.3 %collective-permute-start.44 = (bf16[384,256]{1,0:T(8,128)(2,1)S(1)}, bf16[384,256]{1,0:T(8,128)(2,1)S(1)}, u32[]{:S(2)}, u32[]{:S(2)}) collective-permute-start(bf16[384,256]{1,0:T(8,128)(2,1)S(1)} %get-tuple-element.128), channel_id=1, source_target_pairs={{0,28},{4,24},{8,4},{12,0},{16,12},{20,8},{24,20},{28,16},{1,29},{... | collective-permute-start | bytes 589832 | tf_op jit(solution)/shard_map/ppermute | solution.py:361
  170.1 1.7 collective-permute-done.41.refs_4_
  171.8 12.2 %collective-permute-done.42.refs_5_ = bf16[384,256]{1,0:T(8,128)(2,1)S(1)} collective-permute-done((bf16[384,256]{1,0:T(8,128)(2,1)S(1)}, bf16[384,256]{1,0:T(8,128)(2,1)S(1)}, u32[]{:S(2)}, u32[]{:S(2)}) %collective-permute-start.42) | collective-permute-done | bytes 196640 | tf_op jit(solution)/shard_map/ppermute | solution.py:361
  184.0 1.7 collective-permute-done.43.refs_6_
  186.0 11.1 %collective-permute-done.44.refs_7_ = bf16[384,256]{1,0:T(8,128)(2,1)S(1)} collective-permute-done((bf16[384,256]{1,0:T(8,128)(2,1)S(1)}, bf16[384,256]{1,0:T(8,128)(2,1)S(1)}, u32[]{:S(2)}, u32[]{:S(2)}) %collective-permute-start.44) | collective-permute-done | bytes 196640 | tf_op jit(solution)/shard_map/ppermute | solution.py:361
  198.2 4.3 %collective-permute-start.36 = (bf16[384,256]{1,0:T(8,128)(2,1)S(1)}, bf16[384,256]{1,0:T(8,128)(2,1)S(1)}, u32[]{:S(2)}, u32[]{:S(2)}) collective-permute-start(bf16[384,256]{1,0:T(8,128)(2,1)S(1)} %get-tuple-element.120), channel_id=1, source_target_pairs={{0,28},{4,24},{8,4},{12,0},{16,12},{20,8},{24,20},{28,16},{1,29},{... | collective-permute-start | bytes 589832 | tf_op jit(solution)/shard_map/ppermute | solution.py:361
  202.5 2.3 %put.5 = (bf16[3072,1024]{1,0:T(8,128)(2,1)}, s32[2]{0:T(128)}) custom-call(s32[2]{0:T(128)S(1)} %pad_add_fusion.place, bf16[384,256]{1,0:T(8,128)(2,1)S(1)} %get-tuple-element.129.refs_0_, bf16[384,256]{1,0:T(8,128)(2,1)S(1)} %collective-permute-done.46.refs_1_, ...), custom_call_target="tpu_custom_call", output_to_operand_aliasing={{0}: (9, {})} | custom-call | tf_op jit(solution)/shard_map/put/pallas_call | solution.py:244
  204.7 2.3 %put.6 = (bf16[3072,1024]{1,0:T(8,128)(2,1)}, s32[2]{0:T(128)}) custom-call(s32[2]{0:T(128)S(1)} %pad_add_fusion.place, bf16[384,256]{1,0:T(8,128)(2,1)S(1)} %get-tuple-element.121.refs_0_, bf16[384,256]{1,0:T(8,128)(2,1)S(1)} %collective-permute-done.38.refs_1_, ...), custom_call_target="tpu_custom_call", output_to_operand_aliasing={{0}: (9, {})} | custom-call | tf_op jit(solution)/shard_map/put/pallas_call | solution.py:244
  207.9 2.1 collective-permute-done.34.refs_5_
  210.0 1.7 collective-permute-done.36.refs_7_
  211.8 2.3 %put.7 = (bf16[3072,1024]{1,0:T(8,128)(2,1)}, s32[2]{0:T(128)}) custom-call(s32[2]{0:T(128)S(1)} %pad_add_fusion.place, bf16[384,256]{1,0:T(8,128)(2,1)S(1)} %get-tuple-element.113.refs_0_, bf16[384,256]{1,0:T(8,128)(2,1)S(1)} %collective-permute-done.30.refs_1_, ...), custom_call_target="tpu_custom_call", output_to_operand_aliasing={{0}: (9, {})} | custom-call | tf_op jit(solution)/shard_map/put/pallas_call | solution.py:244
  (90 shorter events, 32.0 us)
Async XLA Ops:
  4.2 11.2 %collective-permute-start.2 = (bf16[4,1,128,128]{3,2,1,0:T(8,128)(2,1)S(1)}, bf16[4,1,128,128]{3,2,1,0:T(8,128)(2,1)}, u32[]{:S(2)}, u32[]{:S(2)}) collective-permute-start(bf16[4,1,128,128]{3,2,1,0:T(8,128)(2,1)S(1)} %get-tuple-element.76), channel_id=1, source_target_pairs={{0,4},{4,0},{8,12},{12,8},{16,20},{20,16},{24,28},{28,24},{1,5},{5... | collective-permute-start | bytes 393224 | tf_op jit(solution)/shard_map/ppermute | solution.py:338
  5.8 11.9 %collective-permute-start.1 = (bf16[4,1,128,128]{3,2,1,0:T(8,128)(2,1)S(1)}, bf16[4,1,128,128]{3,2,1,0:T(8,128)(2,1)S(1)}, u32[]{:S(2)}, u32[]{:S(2)}) collective-permute-start(bf16[4,1,128,128]{3,2,1,0:T(8,128)(2,1)S(1)} %get-tuple-element.77), channel_id=1, source_target_pairs={{0,4},{4,0},{8,12},{12,8},{16,20},{20,16},{24,28},{28,24},{1,5},{5... | collective-permute-start | bytes 393224 | tf_op jit(solution)/shard_map/ppermute | solution.py:338
  11.9 15.3 %collective-permute-start = (bf16[4,2,128,128]{3,2,1,0:T(8,128)(2,1)S(1)}, bf16[4,2,128,128]{3,2,1,0:T(8,128)(2,1)}, u32[]{:S(2)}, u32[]{:S(2)}) collective-permute-start(bf16[4,2,128,128]{3,2,1,0:T(8,128)(2,1)S(1)} %get-tuple-element.78), channel_id=1, source_target_pairs={{0,4},{4,0},{8,12},{12,8},{16,20},{20,16},{24,28},{28,24},{1,5},{5... | collective-permute-start | bytes 786440 | tf_op jit(solution)/shard_map/ppermute | solution.py:338
  13.4 13.7 %collective-permute-start.12 = (bf16[4,2,128,128]{3,2,1,0:T(8,128)(2,1)S(1)}, bf16[4,2,128,128]{3,2,1,0:T(8,128)(2,1)}, u32[]{:S(2)}, u32[]{:S(2)}) collective-permute-start(bf16[4,2,128,128]{3,2,1,0:T(8,128)(2,1)S(1)} %get-tuple-element.91), channel_id=1, source_target_pairs={{0,4},{4,0},{8,12},{12,8},{16,20},{20,16},{24,28},{28,24},{1,5},{5... | collective-permute-start | bytes 786440 | tf_op jit(solution)/shard_map/ppermute | solution.py:338
  13.9 17.0 %collective-permute-start.15 = (bf16[4,2,128,128]{3,2,1,0:T(8,128)(2,1)S(1)}, bf16[4,2,128,128]{3,2,1,0:T(8,128)(2,1)S(1)}, u32[]{:S(2)}, u32[]{:S(2)}) collective-permute-start(bf16[4,2,128,128]{3,2,1,0:T(8,128)(2,1)S(1)} %get-tuple-element.97), channel_id=1, source_target_pairs={{0,4},{4,0},{8,12},{12,8},{16,20},{20,16},{24,28},{28,24},{1,5},{5... | collective-permute-start | bytes 786440 | tf_op jit(solution)/shard_map/ppermute | solution.py:338
  17.8 8.1 %collective-permute-start.4 = (bf16[4,1,128,128]{3,2,1,0:T(8,128)(2,1)S(1)}, bf16[4,1,128,128]{3,2,1,0:T(8,128)(2,1)S(1)}, u32[]{:S(2)}, u32[]{:S(2)}) collective-permute-start(bf16[4,1,128,128]{3,2,1,0:T(8,128)(2,1)S(1)} %fusion.13), channel_id=1, source_target_pairs={{0,8},{4,12},{1,9},{5,13},{2,10},{6,14},{3,11},{7,15}} | collective-permute-start | bytes 393224 | tf_op jit(solution)/shard_map/ppermute | solution.py:338
  24.5 7.9 %collective-permute-start.8 = (bf16[4,1,128,128]{3,2,1,0:T(8,128)(2,1)S(1)}, bf16[4,1,128,128]{3,2,1,0:T(8,128)(2,1)S(1)}, u32[]{:S(2)}, u32[]{:S(2)}) collective-permute-start(bf16[4,1,128,128]{3,2,1,0:T(8,128)(2,1)S(1)} %add_convert_fusion.8), channel_id=1, source_target_pairs={{8,16},{12,20},{9,17},{13,21},{10,18},{14,22},{11,19},{15,23}} | collective-permute-start | bytes 393224 | tf_op jit(solution)/shard_map/ppermute | solution.py:338
  25.9 8.2 %collective-permute-start.7 = (bf16[4,1,128,128]{3,2,1,0:T(8,128)(2,1)S(1)}, bf16[4,1,128,128]{3,2,1,0:T(8,128)(2,1)S(1)}, u32[]{:S(2)}, u32[]{:S(2)}) collective-permute-start(bf16[4,1,128,128]{3,2,1,0:T(8,128)(2,1)S(1)} %add_convert_fusion.9), channel_id=1, source_target_pairs={{8,16},{12,20},{9,17},{13,21},{10,18},{14,22},{11,19},{15,23}} | collective-permute-start | bytes 393224 | tf_op jit(solution)/shard_map/ppermute | solution.py:338
  28.4 11.1 %collective-permute-start.3 = (bf16[4,2,128,128]{3,2,1,0:T(8,128)(2,1)S(1)}, bf16[4,2,128,128]{3,2,1,0:T(8,128)(2,1)S(1)}, u32[]{:S(2)}, u32[]{:S(2)}) collective-permute-start(bf16[4,2,128,128]{3,2,1,0:T(8,128)(2,1)S(1)} %get-tuple-element.82), channel_id=1, source_target_pairs={{0,8},{4,12},{1,9},{5,13},{2,10},{6,14},{3,11},{7,15}} | collective-permute-start | bytes 786440 | tf_op jit(solution)/shard_map/ppermute | solution.py:338
  29.7 16.7 %collective-permute-start.13 = (bf16[4,2,128,128]{3,2,1,0:T(8,128)(2,1)S(1)}, bf16[4,2,128,128]{3,2,1,0:T(8,128)(2,1)S(1)}, u32[]{:S(2)}, u32[]{:S(2)}) collective-permute-start(bf16[4,2,128,128]{3,2,1,0:T(8,128)(2,1)S(1)} %get-tuple-element.92), channel_id=1, source_target_pairs={{0,8},{4,12},{1,9},{5,13},{2,10},{6,14},{3,11},{7,15}} | collective-permute-start | bytes 786440 | tf_op jit(solution)/shard_map/ppermute | solution.py:338
  31.1 17.7 %collective-permute-start.16 = (bf16[4,2,128,128]{3,2,1,0:T(8,128)(2,1)S(1)}, bf16[4,2,128,128]{3,2,1,0:T(8,128)(2,1)S(1)}, u32[]{:S(2)}, u32[]{:S(2)}) collective-permute-start(bf16[4,2,128,128]{3,2,1,0:T(8,128)(2,1)S(1)} %fusion.12), channel_id=1, source_target_pairs={{0,8},{4,12},{1,9},{5,13},{2,10},{6,14},{3,11},{7,15}} | collective-permute-start | bytes 786440 | tf_op jit(solution)/shard_map/ppermute | solution.py:338
  35.8 27.9 %collective-permute-start.17 = (bf16[4,1,128,128]{3,2,1,0:T(8,128)(2,1)S(1)}, bf16[4,1,128,128]{3,2,1,0:T(8,128)(2,1)S(1)}, u32[]{:S(2)}, u32[]{:S(2)}) collective-permute-start(bf16[4,1,128,128]{3,2,1,0:T(8,128)(2,1)S(1)} %get-tuple-element.150), channel_id=1, source_target_pairs={{0,4},{4,0},{8,12},{12,8},{16,20},{20,16},{24,28},{28,24},{1,5},{5... | collective-permute-start | bytes 393224 | tf_op jit(solution)/shard_map/ppermute | solution.py:338
  37.2 26.5 %collective-permute-start.18 = (bf16[4,1,128,128]{3,2,1,0:T(8,128)(2,1)S(1)}, bf16[4,1,128,128]{3,2,1,0:T(8,128)(2,1)S(1)}, u32[]{:S(2)}, u32[]{:S(2)}) collective-permute-start(bf16[4,1,128,128]{3,2,1,0:T(8,128)(2,1)S(1)} %get-tuple-element.87), channel_id=1, source_target_pairs={{0,4},{4,0},{8,12},{12,8},{16,20},{20,16},{24,28},{28,24},{1,5},{5... | collective-permute-start | bytes 393224 | tf_op jit(solution)/shard_map/ppermute | solution.py:338
  40.6 12.5 %collective-permute-start.6 = (bf16[4,2,128,128]{3,2,1,0:T(8,128)(2,1)S(1)}, bf16[4,2,128,128]{3,2,1,0:T(8,128)(2,1)S(1)}, u32[]{:S(2)}, u32[]{:S(2)}) collective-permute-start(bf16[4,2,128,128]{3,2,1,0:T(8,128)(2,1)S(1)} %add_convert_fusion.5), channel_id=1, source_target_pairs={{8,16},{12,20},{9,17},{13,21},{10,18},{14,22},{11,19},{15,23}} | collective-permute-start | bytes 786440 | tf_op jit(solution)/shard_map/ppermute | solution.py:338
  47.5 9.9 %collective-permute-start.14 = (bf16[4,2,128,128]{3,2,1,0:T(8,128)(2,1)S(1)}, bf16[4,2,128,128]{3,2,1,0:T(8,128)(2,1)S(1)}, u32[]{:S(2)}, u32[]{:S(2)}) collective-permute-start(bf16[4,2,128,128]{3,2,1,0:T(8,128)(2,1)S(1)} %add_convert_fusion.3), channel_id=1, source_target_pairs={{8,16},{12,20},{9,17},{13,21},{10,18},{14,22},{11,19},{15,23}} | collective-permute-start | bytes 786440 | tf_op jit(solution)/shard_map/ppermute | solution.py:338
  48.9 11.3 %collective-permute-start.26 = (bf16[4,2,128,128]{3,2,1,0:T(8,128)(2,1)S(1)}, bf16[4,2,128,128]{3,2,1,0:T(8,128)(2,1)S(1)}, u32[]{:S(2)}, u32[]{:S(2)}) collective-permute-start(bf16[4,2,128,128]{3,2,1,0:T(8,128)(2,1)S(1)} %add_convert_fusion.1), channel_id=1, source_target_pairs={{8,16},{12,20},{9,17},{13,21},{10,18},{14,22},{11,19},{15,23}} | collective-permute-start | bytes 786440 | tf_op jit(solution)/shard_map/ppermute | solution.py:338
  58.4 20.7 %collective-permute-start.28 = (bf16[4,2,128,128]{3,2,1,0:T(8,128)(2,1)S(1)}, bf16[4,2,128,128]{3,2,1,0:T(8,128)(2,1)S(1)}, u32[]{:S(2)}, u32[]{:S(2)}) collective-permute-start(bf16[4,2,128,128]{3,2,1,0:T(8,128)(2,1)S(1)} %add_convert_fusion.2), channel_id=1, source_target_pairs={{16,24},{20,28},{17,25},{21,29},{18,26},{22,30},{19,27},{23,31}} | collective-permute-start | bytes 786440 | tf_op jit(solution)/shard_map/ppermute | solution.py:338
  60.3 15.9 %collective-permute-start.27 = (bf16[4,2,128,128]{3,2,1,0:T(8,128)(2,1)S(1)}, bf16[4,2,128,128]{3,2,1,0:T(8,128)(2,1)S(1)}, u32[]{:S(2)}, u32[]{:S(2)}) collective-permute-start(bf16[4,2,128,128]{3,2,1,0:T(8,128)(2,1)S(1)} %add_convert_fusion), channel_id=1, source_target_pairs={{16,24},{20,28},{17,25},{21,29},{18,26},{22,30},{19,27},{23,31}} | collective-permute-start | bytes 786440 | tf_op jit(solution)/shard_map/ppermute | solution.py:338
  62.1 36.9 %collective-permute-start.45 = (bf16[4,2,128,128]{3,2,1,0:T(8,128)(2,1)S(1)}, bf16[4,2,128,128]{3,2,1,0:T(8,128)(2,1)S(1)}, u32[]{:S(2)}, u32[]{:S(2)}) collective-permute-start(bf16[4,2,128,128]{3,2,1,0:T(8,128)(2,1)S(1)} %get-tuple-element.88), channel_id=1, source_target_pairs={{0,4},{4,0},{8,12},{12,8},{16,20},{20,16},{24,28},{28,24},{1,5},{5... | collective-permute-start | bytes 786440 | tf_op jit(solution)/shard_map/ppermute | solution.py:338
  72.4 9.2 %collective-permute-start.19 = (bf16[384,256]{1,0:T(8,128)(2,1)S(1)}, bf16[384,256]{1,0:T(8,128)(2,1)S(1)}, u32[]{:S(2)}, u32[]{:S(2)}) collective-permute-start(bf16[384,256]{1,0:T(8,128)(2,1)S(1)} %get-tuple-element.102), channel_id=1, source_target_pairs={{0,4},{4,0},{8,12},{12,8},{16,20},{20,16},{24,28},{28,24},{1,5},{5... | collective-permute-start | bytes 589832 | tf_op jit(solution)/shard_map/ppermute | solution.py:361
  73.0 16.0 %collective-permute-start.20 = (bf16[384,256]{1,0:T(8,128)(2,1)S(1)}, bf16[384,256]{1,0:T(8,128)(2,1)S(1)}, u32[]{:S(2)}, u32[]{:S(2)}) collective-permute-start(bf16[384,256]{1,0:T(8,128)(2,1)S(1)} %get-tuple-element.103), channel_id=1, source_target_pairs={{0,8},{4,12},{8,16},{12,20},{16,24},{20,28},{24,0},{28,4},{1,9},{5... | collective-permute-start | bytes 589832 | tf_op jit(solution)/shard_map/ppermute | solution.py:361
  76.1 16.6 %collective-permute-start.21 = (bf16[384,256]{1,0:T(8,128)(2,1)S(1)}, bf16[384,256]{1,0:T(8,128)(2,1)S(1)}, u32[]{:S(2)}, u32[]{:S(2)}) collective-permute-start(bf16[384,256]{1,0:T(8,128)(2,1)S(1)} %get-tuple-element.104), channel_id=1, source_target_pairs={{0,12},{4,8},{8,20},{12,16},{16,28},{20,24},{24,4},{28,0},{1,13},{... | collective-permute-start | bytes 589832 | tf_op jit(solution)/shard_map/ppermute | solution.py:361
  79.1 19.9 %collective-permute-start.22 = (bf16[384,256]{1,0:T(8,128)(2,1)S(1)}, bf16[384,256]{1,0:T(8,128)(2,1)S(1)}, u32[]{:S(2)}, u32[]{:S(2)}) collective-permute-start(bf16[384,256]{1,0:T(8,128)(2,1)S(1)} %get-tuple-element.105), channel_id=1, source_target_pairs={{0,16},{4,20},{8,24},{12,28},{16,0},{20,4},{24,8},{28,12},{1,17},{... | collective-permute-start | bytes 589832 | tf_op jit(solution)/shard_map/ppermute | solution.py:361
  81.5 31.8 %collective-permute-start.23 = (bf16[384,256]{1,0:T(8,128)(2,1)S(1)}, bf16[384,256]{1,0:T(8,128)(2,1)S(1)}, u32[]{:S(2)}, u32[]{:S(2)}) collective-permute-start(bf16[384,256]{1,0:T(8,128)(2,1)S(1)} %get-tuple-element.106), channel_id=1, source_target_pairs={{0,20},{4,16},{8,28},{12,24},{16,4},{20,0},{24,12},{28,8},{1,21},{... | collective-permute-start | bytes 589832 | tf_op jit(solution)/shard_map/ppermute | solution.py:361
  89.1 30.2 %collective-permute-start.37 = (bf16[4,2,128,128]{3,2,1,0:T(8,128)(2,1)S(1)}, bf16[4,2,128,128]{3,2,1,0:T(8,128)(2,1)S(1)}, u32[]{:S(2)}, u32[]{:S(2)}) collective-permute-start(bf16[4,2,128,128]{3,2,1,0:T(8,128)(2,1)S(1)} %get-tuple-element.111), channel_id=1, source_target_pairs={{0,4},{4,0},{8,12},{12,8},{16,20},{20,16},{24,28},{28,24},{1,5},{5... | collective-permute-start | bytes 786440 | tf_op jit(solution)/shard_map/ppermute | solution.py:338
  92.7 21.5 %collective-permute-start.29 = (bf16[4,2,128,128]{3,2,1,0:T(8,128)(2,1)S(1)}, bf16[4,2,128,128]{3,2,1,0:T(8,128)(2,1)S(1)}, u32[]{:S(2)}, u32[]{:S(2)}) collective-permute-start(bf16[4,2,128,128]{3,2,1,0:T(8,128)(2,1)S(1)} %get-tuple-element.112), channel_id=1, source_target_pairs={{0,4},{4,0},{8,12},{12,8},{16,20},{20,16},{24,28},{28,24},{1,5},{5... | collective-permute-start | bytes 786440 | tf_op jit(solution)/shard_map/ppermute | solution.py:338
  99.0 15.0 %collective-permute-start.24 = (bf16[384,256]{1,0:T(8,128)(2,1)S(1)}, bf16[384,256]{1,0:T(8,128)(2,1)S(1)}, u32[]{:S(2)}, u32[]{:S(2)}) collective-permute-start(bf16[384,256]{1,0:T(8,128)(2,1)S(1)} %get-tuple-element.107), channel_id=1, source_target_pairs={{0,24},{4,28},{8,0},{12,4},{16,8},{20,12},{24,16},{28,20},{1,25},{... | collective-permute-start | bytes 589832 | tf_op jit(solution)/shard_map/ppermute | solution.py:361
  99.0 15.0 %collective-permute-start.25 = (bf16[384,256]{1,0:T(8,128)(2,1)S(1)}, bf16[384,256]{1,0:T(8,128)(2,1)S(1)}, u32[]{:S(2)}, u32[]{:S(2)}) collective-permute-start(bf16[384,256]{1,0:T(8,128)(2,1)S(1)} %get-tuple-element.108), channel_id=1, source_target_pairs={{0,28},{4,24},{8,4},{12,0},{16,12},{20,8},{24,20},{28,16},{1,29},{... | collective-permute-start | bytes 589832 | tf_op jit(solution)/shard_map/ppermute | solution.py:361
  114.1 14.6 %collective-permute-start.47 = (bf16[384,256]{1,0:T(8,128)(2,1)S(1)}, bf16[384,256]{1,0:T(8,128)(2,1)S(1)}, u32[]{:S(2)}, u32[]{:S(2)}) collective-permute-start(bf16[384,256]{1,0:T(8,128)(2,1)S(1)} %get-tuple-element.131), channel_id=1, source_target_pairs={{0,8},{4,12},{8,16},{12,20},{16,24},{20,28},{24,0},{28,4},{1,9},{5... | collective-permute-start | bytes 589832 | tf_op jit(solution)/shard_map/ppermute | solution.py:361
  114.1 24.2 %collective-permute-start.48 = (bf16[384,256]{1,0:T(8,128)(2,1)S(1)}, bf16[384,256]{1,0:T(8,128)(2,1)S(1)}, u32[]{:S(2)}, u32[]{:S(2)}) collective-permute-start(bf16[384,256]{1,0:T(8,128)(2,1)S(1)} %get-tuple-element.132), channel_id=1, source_target_pairs={{0,12},{4,8},{8,20},{12,16},{16,28},{20,24},{24,4},{28,0},{1,13},{... | collective-permute-start | bytes 589832 | tf_op jit(solution)/shard_map/ppermute | solution.py:361
  114.1 28.4 %collective-permute-start.49 = (bf16[384,256]{1,0:T(8,128)(2,1)S(1)}, bf16[384,256]{1,0:T(8,128)(2,1)S(1)}, u32[]{:S(2)}, u32[]{:S(2)}) collective-permute-start(bf16[384,256]{1,0:T(8,128)(2,1)S(1)} %get-tuple-element.133), channel_id=1, source_target_pairs={{0,16},{4,20},{8,24},{12,28},{16,0},{20,4},{24,8},{28,12},{1,17},{... | collective-permute-start | bytes 589832 | tf_op jit(solution)/shard_map/ppermute | solution.py:361
  119.2 29.6 %collective-permute-start.50 = (bf16[384,256]{1,0:T(8,128)(2,1)S(1)}, bf16[384,256]{1,0:T(8,128)(2,1)S(1)}, u32[]{:S(2)}, u32[]{:S(2)}) collective-permute-start(bf16[384,256]{1,0:T(8,128)(2,1)S(1)} %get-tuple-element.134), channel_id=1, source_target_pairs={{0,20},{4,16},{8,28},{12,24},{16,4},{20,0},{24,12},{28,8},{1,21},{... | collective-permute-start | bytes 589832 | tf_op jit(solution)/shard_map/ppermute | solution.py:361
  119.6 29.2 %collective-permute-start.51 = (bf16[384,256]{1,0:T(8,128)(2,1)S(1)}, bf16[384,256]{1,0:T(8,128)(2,1)S(1)}, u32[]{:S(2)}, u32[]{:S(2)}) collective-permute-start(bf16[384,256]{1,0:T(8,128)(2,1)S(1)} %get-tuple-element.135), channel_id=1, source_target_pairs={{0,24},{4,28},{8,0},{12,4},{16,8},{20,12},{24,16},{28,20},{1,25},{... | collective-permute-start | bytes 589832 | tf_op jit(solution)/shard_map/ppermute | solution.py:361
  128.7 35.3 %collective-permute-start.52 = (bf16[384,256]{1,0:T(8,128)(2,1)S(1)}, bf16[384,256]{1,0:T(8,128)(2,1)S(1)}, u32[]{:S(2)}, u32[]{:S(2)}) collective-permute-start(bf16[384,256]{1,0:T(8,128)(2,1)S(1)} %get-tuple-element.136), channel_id=1, source_target_pairs={{0,28},{4,24},{8,4},{12,0},{16,12},{20,8},{24,20},{28,16},{1,29},{... | collective-permute-start | bytes 589832 | tf_op jit(solution)/shard_map/ppermute | solution.py:361
  138.3 25.9 %collective-permute-start.38 = (bf16[384,256]{1,0:T(8,128)(2,1)S(1)}, bf16[384,256]{1,0:T(8,128)(2,1)S(1)}, u32[]{:S(2)}, u32[]{:S(2)}) collective-permute-start(bf16[384,256]{1,0:T(8,128)(2,1)S(1)} %get-tuple-element.122), channel_id=1, source_target_pairs={{0,4},{4,0},{8,12},{12,8},{16,20},{20,16},{24,28},{28,24},{1,5},{5... | collective-permute-start | bytes 589832 | tf_op jit(solution)/shard_map/ppermute | solution.py:361
  142.5 24.5 %collective-permute-start.39 = (bf16[384,256]{1,0:T(8,128)(2,1)S(1)}, bf16[384,256]{1,0:T(8,128)(2,1)S(1)}, u32[]{:S(2)}, u32[]{:S(2)}) collective-permute-start(bf16[384,256]{1,0:T(8,128)(2,1)S(1)} %get-tuple-element.123), channel_id=1, source_target_pairs={{0,8},{4,12},{8,16},{12,20},{16,24},{20,28},{24,0},{28,4},{1,9},{5... | collective-permute-start | bytes 589832 | tf_op jit(solution)/shard_map/ppermute | solution.py:361
  148.8 20.6 %collective-permute-start.40 = (bf16[384,256]{1,0:T(8,128)(2,1)S(1)}, bf16[384,256]{1,0:T(8,128)(2,1)S(1)}, u32[]{:S(2)}, u32[]{:S(2)}) collective-permute-start(bf16[384,256]{1,0:T(8,128)(2,1)S(1)} %get-tuple-element.124), channel_id=1, source_target_pairs={{0,12},{4,8},{8,20},{12,16},{16,28},{20,24},{24,4},{28,0},{1,13},{... | collective-permute-start | bytes 589832 | tf_op jit(solution)/shard_map/ppermute | solution.py:361
  148.8 22.9 %collective-permute-start.41 = (bf16[384,256]{1,0:T(8,128)(2,1)S(1)}, bf16[384,256]{1,0:T(8,128)(2,1)S(1)}, u32[]{:S(2)}, u32[]{:S(2)}) collective-permute-start(bf16[384,256]{1,0:T(8,128)(2,1)S(1)} %get-tuple-element.125), channel_id=1, source_target_pairs={{0,16},{4,20},{8,24},{12,28},{16,0},{20,4},{24,8},{28,12},{1,17},{... | collective-permute-start | bytes 589832 | tf_op jit(solution)/shard_map/ppermute | solution.py:361
  164.0 20.0 %collective-permute-start.42 = (bf16[384,256]{1,0:T(8,128)(2,1)S(1)}, bf16[384,256]{1,0:T(8,128)(2,1)S(1)}, u32[]{:S(2)}, u32[]{:S(2)}) collective-permute-start(bf16[384,256]{1,0:T(8,128)(2,1)S(1)} %get-tuple-element.126), channel_id=1, source_target_pairs={{0,20},{4,16},{8,28},{12,24},{16,4},{20,0},{24,12},{28,8},{1,21},{... | collective-permute-start | bytes 589832 | tf_op jit(solution)/shard_map/ppermute | solution.py:361
  164.2 21.5 %collective-permute-start.43 = (bf16[384,256]{1,0:T(8,128)(2,1)S(1)}, bf16[384,256]{1,0:T(8,128)(2,1)S(1)}, u32[]{:S(2)}, u32[]{:S(2)}) collective-permute-start(bf16[384,256]{1,0:T(8,128)(2,1)S(1)} %get-tuple-element.127), channel_id=1, source_target_pairs={{0,24},{4,28},{8,0},{12,4},{16,8},{20,12},{24,16},{28,20},{1,25},{... | collective-permute-start | bytes 589832 | tf_op jit(solution)/shard_map/ppermute | solution.py:361
  167.0 30.1 %collective-permute-start.44 = (bf16[384,256]{1,0:T(8,128)(2,1)S(1)}, bf16[384,256]{1,0:T(8,128)(2,1)S(1)}, u32[]{:S(2)}, u32[]{:S(2)}) collective-permute-start(bf16[384,256]{1,0:T(8,128)(2,1)S(1)} %get-tuple-element.128), channel_id=1, source_target_pairs={{0,28},{4,24},{8,4},{12,0},{16,12},{20,8},{24,20},{28,16},{1,29},{... | collective-permute-start | bytes 589832 | tf_op jit(solution)/shard_map/ppermute | solution.py:361
  169.4 27.8 %collective-permute-start.30 = (bf16[384,256]{1,0:T(8,128)(2,1)S(1)}, bf16[384,256]{1,0:T(8,128)(2,1)S(1)}, u32[]{:S(2)}, u32[]{:S(2)}) collective-permute-start(bf16[384,256]{1,0:T(8,128)(2,1)S(1)} %get-tuple-element.114), channel_id=1, source_target_pairs={{0,4},{4,0},{8,12},{12,8},{16,20},{20,16},{24,28},{28,24},{1,5},{5... | collective-permute-start | bytes 589832 | tf_op jit(solution)/shard_map/ppermute | solution.py:361
  171.8 26.4 %collective-permute-start.31 = (bf16[384,256]{1,0:T(8,128)(2,1)S(1)}, bf16[384,256]{1,0:T(8,128)(2,1)S(1)}, u32[]{:S(2)}, u32[]{:S(2)}) collective-permute-start(bf16[384,256]{1,0:T(8,128)(2,1)S(1)} %get-tuple-element.115), channel_id=1, source_target_pairs={{0,8},{4,12},{8,16},{12,20},{16,24},{20,28},{24,0},{28,4},{1,9},{5... | collective-permute-start | bytes 589832 | tf_op jit(solution)/shard_map/ppermute | solution.py:361
  184.0 23.0 %collective-permute-start.32 = (bf16[384,256]{1,0:T(8,128)(2,1)S(1)}, bf16[384,256]{1,0:T(8,128)(2,1)S(1)}, u32[]{:S(2)}, u32[]{:S(2)}) collective-permute-start(bf16[384,256]{1,0:T(8,128)(2,1)S(1)} %get-tuple-element.116), channel_id=1, source_target_pairs={{0,12},{4,8},{8,20},{12,16},{16,28},{20,24},{24,4},{28,0},{1,13},{... | collective-permute-start | bytes 589832 | tf_op jit(solution)/shard_map/ppermute | solution.py:361
  185.7 22.2 %collective-permute-start.33 = (bf16[384,256]{1,0:T(8,128)(2,1)S(1)}, bf16[384,256]{1,0:T(8,128)(2,1)S(1)}, u32[]{:S(2)}, u32[]{:S(2)}) collective-permute-start(bf16[384,256]{1,0:T(8,128)(2,1)S(1)} %get-tuple-element.117), channel_id=1, source_target_pairs={{0,16},{4,20},{8,24},{12,28},{16,0},{20,4},{24,8},{28,12},{1,17},{... | collective-permute-start | bytes 589832 | tf_op jit(solution)/shard_map/ppermute | solution.py:361
  197.2 12.9 %collective-permute-start.34 = (bf16[384,256]{1,0:T(8,128)(2,1)S(1)}, bf16[384,256]{1,0:T(8,128)(2,1)S(1)}, u32[]{:S(2)}, u32[]{:S(2)}) collective-permute-start(bf16[384,256]{1,0:T(8,128)(2,1)S(1)} %get-tuple-element.118), channel_id=1, source_target_pairs={{0,20},{4,16},{8,28},{12,24},{16,4},{20,0},{24,12},{28,8},{1,21},{... | collective-permute-start | bytes 589832 | tf_op jit(solution)/shard_map/ppermute | solution.py:361
  197.2 12.9 %collective-permute-start.35 = (bf16[384,256]{1,0:T(8,128)(2,1)S(1)}, bf16[384,256]{1,0:T(8,128)(2,1)S(1)}, u32[]{:S(2)}, u32[]{:S(2)}) collective-permute-start(bf16[384,256]{1,0:T(8,128)(2,1)S(1)} %get-tuple-element.119), channel_id=1, source_target_pairs={{0,24},{4,28},{8,0},{12,4},{16,8},{20,12},{24,16},{28,20},{1,25},{... | collective-permute-start | bytes 589832 | tf_op jit(solution)/shard_map/ppermute | solution.py:361
  198.2 13.6 %collective-permute-start.36 = (bf16[384,256]{1,0:T(8,128)(2,1)S(1)}, bf16[384,256]{1,0:T(8,128)(2,1)S(1)}, u32[]{:S(2)}, u32[]{:S(2)}) collective-permute-start(bf16[384,256]{1,0:T(8,128)(2,1)S(1)} %get-tuple-element.120), channel_id=1, source_target_pairs={{0,28},{4,24},{8,4},{12,0},{16,12},{20,8},{24,20},{28,16},{1,29},{... | collective-permute-start | bytes 589832 | tf_op jit(solution)/shard_map/ppermute | solution.py:361
  (6 other events, 54.9 us)

commit v3 on v2

v3 whole, which is shorter than its diff:
```python
import functools

import jax
import jax.numpy as jnp
from jax import lax
from jax.experimental import pallas as pl
from jax.experimental.pallas import tpu as pltpu
from jax.sharding import PartitionSpec as P

HEADS = 64
HEAD = 128
LOCAL = (2, 6)
SWAP = (1, 1, 3, 3)
PREFIX = (1, 1, 3, 3)
MIXED = (2, 3, 3)
TILE = 256
SPARE = 8 * 1024 * 1024
ORDER = {
    ("message", 1, 1): [("message", 0, 1)],
    ("message", 1, 2): [("message", 0, 2)],
    ("message", 1, 3): [("message", 0, 3)],
    ("message", 1, 4): [("message", 0, 4)],
    ("message", 3, 1): [("message", 2, 1)],
    ("message", 3, 2): [("message", 2, 2)],
    ("message", 3, 3): [("message", 2, 3)],
    ("message", 3, 4): [("message", 2, 4)],
    ("message", 2, 1): [("message", 1, 2)],
    ("mixed", 0): [("message", 2, 2), ("message", 3, 1)],
}


def params(buffers=0):
    return pltpu.CompilerParams(vmem_limit_bytes=buffers + SPARE)


def column(place, row, side, n):
    col = place[1] if side == 0 else 1 - place[1]
    return pl.multiple_of(((2 * row + col) * (HEADS // n) + place[2]) * HEAD, HEAD)


def local_body(n, widths, swaps, place, low, keys, values, *refs):
    outs, (kbuf, vbuf, sems) = refs[:-3], refs[-3:]
    total = sum(widths)
    here = place[0], place[1], low[0]

    def copies(row, side):
        cols = pl.ds(column(here, row, side, n), total * HEAD)
        slot = 2 * row + side
        return [
            pltpu.make_async_copy(source.at[:, cols], buf.at[slot], sems.at[which, slot])
            for which, (source, buf) in enumerate(((keys, kbuf), (values, vbuf)))
        ]

    def fetch(row, carry):
        for side in range(2):
            for copy in copies(row, side):
                copy.start()
        return carry

    def work(row, carry):
        for side in range(2):
            for copy in copies(row, side):
                copy.wait()
        places = [
            [(out, head) for out, width in zip(arrays, sizes) for head in range(width)]
            for arrays, sizes in ((outs[: len(widths)], widths), (outs[len(widths) :], swaps))
        ]
        for side in range(2):
            for first in range(0, total, 2):
                size = min(2, total - first)
                cols = slice(first * HEAD, (first + size) * HEAD)
                both = lax.dot_general(
                    kbuf[2 * row + side, :, cols],
                    vbuf[2 * row + side, :, cols],
                    (((0,), (0,)), ((), ())),
                    preferred_element_type=jnp.float32,
                )
                for index in range(first, first + size):
                    part = slice((index - first) * HEAD, (index - first + 1) * HEAD)
                    out, head = places[side][index]
                    out[row, head] = both[part, part].astype(out.dtype)
        return carry

    lax.fori_loop(0, n // 2, fetch, 0)
    lax.fori_loop(0, n // 2, work, 0)


def local_states(place, keys, values, n, low, widths, swaps):
    rows, m, total = keys.shape[0], n // 2, sum(widths)
    buf = pltpu.VMEM((n, rows, total * HEAD), keys.dtype)
    shapes = [jax.ShapeDtypeStruct((m, width, HEAD, HEAD), jnp.float32) for width in widths]
    shapes += [jax.ShapeDtypeStruct((m, width, HEAD, HEAD), jnp.bfloat16) for width in swaps]
    return pl.pallas_call(
        functools.partial(local_body, n, widths, swaps),
        in_specs=[pl.BlockSpec(memory_space=pltpu.SMEM)] * 2 + [pl.BlockSpec(memory_space=pltpu.HBM)] * 2,
        out_specs=[pl.BlockSpec(memory_space=pltpu.VMEM)] * len(shapes),
        out_shape=shapes,
        scratch_shapes=[buf, buf, pltpu.SemaphoreType.DMA((2, n))],
        compiler_params=params(4 * n * rows * total * HEAD + 3 * n * total * HEAD * HEAD),
        cost_estimate=pl.CostEstimate(
            flops=2 * n * total * rows * HEAD * HEAD, bytes_accessed=4 * rows * n * total * HEAD, transcendentals=0
        ),
        name="local",
    )(place, jnp.full((1,), low, jnp.int32), keys, values)


def masked_scores(query, key):
    rows = query.shape[0]
    tiles = []
    for low in range(0, rows, TILE):
        high = min(low + TILE, rows)
        part = lax.dot_general(
            query[low:], key[low:high], (((1,), (1,)), ((), ())), preferred_element_type=jnp.float32
        )
        size = high - low
        spot = lax.broadcasted_iota(jnp.int32, (size, size), 0)
        other = lax.broadcasted_iota(jnp.int32, (size, size), 1)
        pieces = [jnp.where(other <= spot, part[:size], 0.0).astype(jnp.bfloat16)]
        if low:
            pieces.insert(0, jnp.zeros((low, size), jnp.bfloat16))
        if high < rows:
            pieces.append(part[size:].astype(jnp.bfloat16))
        tiles.append(jnp.concatenate(pieces, axis=0) if len(pieces) > 1 else pieces[0])
    return tiles


def attend_body(n, spans, place, low, queries, keys, values, gain, *refs):
    states, outs = refs[: 2 * len(spans)], refs[2 * len(spans) :][:n]
    qbuf, kbuf, vbuf, sown, soth, gbuf, held, sems, extra = refs[-9:]
    width = sum(size for _, size in spans)
    m, wide = n // 2, width * HEAD
    here = place[0], place[1], low[0]
    small, start = [(gain, gbuf)], 0
    for chunk, (skip, size) in enumerate(spans):
        for source, buf in ((states[2 * chunk], sown), (states[2 * chunk + 1], soth)):
            small.append((source.at[:, skip : skip + size], buf.at[:, start : start + size]))
        start += size
    small = [pltpu.make_async_copy(source, buf, extra.at[which]) for which, (source, buf) in enumerate(small)]

    def copies(step, side):
        cols = pl.ds(column(here, lax.rem(here[0] + step, m), side, n), wide)
        slot = 2 * step + side
        return [
            pltpu.make_async_copy(source.at[:, cols], buf.at[slot], sems.at[which, slot])
            for which, (source, buf) in enumerate(((queries, qbuf), (keys, kbuf), (values, vbuf)))
        ]

    def sends(step):
        return [
            pltpu.make_async_copy(held.at[slot], outs[slot], sems.at[3, slot])
            for slot in (2 * step, 2 * step + 1)
        ]

    def fetch(step, carry):
        for side in range(2):
            for copy in copies(step, side):
                copy.start()
        return carry

    def work(step, carry):
        for side in range(2):
            for copy in copies(step, side):
                copy.wait()
        row = lax.rem(here[0] + step, m)
        heads = [(side, head, slice(head * HEAD, (head + 1) * HEAD)) for side in range(2) for head in range(width)]
        scores = [masked_scores(qbuf[2 * step + side, :, cols], kbuf[2 * step + side, :, cols]) for side, _, cols in heads]
        attended = []
        for (side, head, cols), tiles in zip(heads, scores):
            slot = 2 * step + side
            state = (sown if side == 0 else soth)[row, head]
            left = jnp.concatenate([*tiles, qbuf[slot, :, cols]], axis=1)
            right = jnp.concatenate([vbuf[slot, :, cols], state], axis=0)
            attended.append(jnp.dot(left, right, preferred_element_type=jnp.float32))
        for (side, head, cols), value in zip(heads, attended):
            square = jnp.mean(value * value, axis=-1, keepdims=True)
            begin = pl.multiple_of(column(here, row, side, n) + head * HEAD, HEAD)
            mixed = value * lax.rsqrt(square + 1e-05) * gbuf[:, pl.ds(begin, HEAD)]
            held[2 * step + side, :, cols] = mixed.astype(held.dtype)
        for fixed in range(m):

            @pl.when(step == fixed)
            def _(fixed=fixed):
                for copy in sends(fixed):
                    copy.start()

        return carry

    lax.fori_loop(0, 1, fetch, 0)
    for copy in small:
        copy.start()
    lax.fori_loop(1, m, fetch, 0)
    for copy in small:
        copy.wait()
    lax.fori_loop(0, m, work, 0)
    for step in range(m):
        for copy in sends(step):
            copy.wait()


def attend(place, queries, keys, values, gain, states, spans, n, low):
    rows, m = queries.shape[0], n // 2
    width = sum(size for _, size in spans)
    wide = width * HEAD
    tokens = pltpu.VMEM((n, rows, wide), jnp.bfloat16)
    state = pltpu.VMEM((m, width, HEAD, HEAD), jnp.bfloat16)
    return pl.pallas_call(
        functools.partial(attend_body, n, spans),
        in_specs=[pl.BlockSpec(memory_space=pltpu.SMEM)] * 2
        + [pl.BlockSpec(memory_space=pltpu.HBM)] * 3
        + [pl.BlockSpec(memory_space=pl.ANY)] * (1 + 2 * len(states)),
        out_specs=[pl.BlockSpec(memory_space=pltpu.HBM)] * n,
        out_shape=[jax.ShapeDtypeStruct((rows, wide), jnp.bfloat16)] * n,
        scratch_shapes=[
            tokens,
            tokens,
            tokens,
            state,
            state,
            pltpu.VMEM((1, HEADS * HEAD), jnp.float32),
            tokens,
            pltpu.SemaphoreType.DMA((4, n)),
            pltpu.SemaphoreType.DMA((1 + 2 * len(states),)),
        ],
        compiler_params=params(8 * n * rows * wide + 2 * n * width * HEAD * HEAD + 4 * HEADS * HEAD),
        cost_estimate=pl.CostEstimate(
            flops=2 * n * width * rows * HEAD * (2 * rows + HEAD),
            bytes_accessed=8 * rows * n * wide,
            transcendentals=n * width * rows,
        ),
        name="attend",
    )(place, jnp.full((1,), low, jnp.int32), queries, keys, values, gain, *(array for pair in states for array in pair))


def put_body(n, place, low, *refs):
    parts, out, again, sems = refs[:n], refs[-3], refs[-2], refs[-1]
    m = n // 2
    rows, wide = parts[0].shape
    cols = pl.ds(pl.multiple_of(low[0] * HEAD, HEAD), wide)
    copies = []
    for shift in range(n):
        row = lax.rem(place[0] + m - shift // 2, m)
        col = place[1] if shift % 2 == 0 else 1 - place[1]
        start = pl.multiple_of((2 * row + col) * rows, rows)
        copies.append(
            pltpu.make_async_copy(parts[shift], out.at[pl.ds(start, rows), cols], sems.at[shift])
        )
    for copy in copies:
        copy.start()
    for index in range(2):
        again[index] = place[index]
    for copy in copies:
        copy.wait()


def put(place, parts, out, n, low):
    rows, first = parts[0].shape[0], out is None
    anywhere = pl.BlockSpec(memory_space=pltpu.HBM)
    return pl.pallas_call(
        functools.partial(put_body, n),
        in_specs=[pl.BlockSpec(memory_space=pltpu.SMEM)] * 2 + [anywhere] * (n if first else n + 1),
        out_specs=[anywhere, pl.BlockSpec(memory_space=pltpu.SMEM)],
        out_shape=[
            jax.ShapeDtypeStruct((n * rows, HEADS // n * HEAD), jnp.bfloat16),
            jax.ShapeDtypeStruct((2,), jnp.int32),
        ],
        scratch_shapes=[pltpu.SemaphoreType.DMA((n,))],
        input_output_aliases={} if first else {n + 2: 0},
        compiler_params=params(),
        name="put",
    )(place, jnp.full((1,), low, jnp.int32), *parts, *(() if first else (out,)))


def split(widths, per_dest):
    chunks, low = [], 0
    for width in widths:
        if low < per_dest:
            width = min(width, per_dest - low)
            chunks.append((low, width))
            low += width
    return chunks


def inside(chunks, low, width):
    return [c for c, (start, _) in enumerate(chunks) if low <= start < low + width]


class Plan:
    def __init__(self, n, queries, keys, values, gain):
        self.n, self.m = n, n // 2
        me = lax.axis_index("seq")
        self.col = me % 2
        self.place = jnp.stack([me // 2, self.col]).astype(jnp.int32)
        self.arrays = tuple(pltpu.with_memory_space_constraint(x, pltpu.HBM) for x in (queries, keys, values))
        self.gain = gain.reshape(1, HEADS * HEAD)
        self.groups, self.swaps, self.parts, self.chunks = (
            split(widths, HEADS // n) for widths in (LOCAL, SWAP, PREFIX, MIXED)
        )
        self.made = {}

    def has(self, key):
        limit = {"message": self.m, "prefix": self.m, "sent": self.n - 1}.get(key[0], 0)
        chunks = {"group": self.groups, "swap": self.swaps, "mixed": self.chunks, "sent": self.chunks}
        chunks = chunks.get(key[0], self.parts)
        return key[1] < len(chunks) and (len(key) < 3 or key[2] <= limit)

    def get(self, *key):
        if key not in self.made:
            self.made[key] = getattr(self, key[0])(*key[1:])
        return self.made[key]

    def hold(self, value, *key):
        others = []
        for other in ORDER.get(key, ()):
            if self.has(other):
                result = self.get(*other)
                while isinstance(result, (list, tuple)):
                    result = result[-1]
                others.append(result)
        return lax.optimization_barrier((value, *others))[0] if others else value

    def group(self, g):
        low, width = self.groups[g]
        widths = tuple(self.parts[c][1] for c in inside(self.parts, low, width))
        swaps = tuple(self.swaps[c][1] for c in inside(self.swaps, low, width))
        _, keys, values = self.arrays
        place = self.hold(self.place, "group", g)
        arrays = local_states(place, keys, values, self.n, low, widths, swaps)
        return arrays[: len(widths)], arrays[len(widths) :]

    def around(self, chunks, low):
        return next(c for c, (start, width) in enumerate(chunks) if start <= low < start + width)

    def swap(self, w):
        g = self.around(self.groups, self.swaps[w][0])
        spot = inside(self.swaps, *self.groups[g]).index(w)
        other = self.hold(self.get("group", g)[1][spot], "swap", w)
        return lax.ppermute(other, "seq", [(d, d ^ 1) for d in range(self.n)])

    def local(self, c):
        low, width = self.parts[c]
        g, w = self.around(self.groups, low), self.around(self.swaps, low)
        near = self.get("swap", w)[:, low - self.swaps[w][0] :][:, :width].astype(jnp.float32)
        return self.get("group", g)[0][inside(self.parts, *self.groups[g]).index(c)], near

    def total(self, c):
        parts = [self.get("prefix", c, s) for s in range(1, self.m)]
        return sum(parts[1:], parts[0]).astype(jnp.float32)

    def message(self, c, s):
        own, near = self.get("local", c)
        if s == self.m:
            value = self.get("total", c) + jnp.where(self.col == 0, own, 0.0)
        else:
            value = own + near
            if s > 1:
                value = self.get("prefix", c, s - 1).astype(jnp.float32) + value
        return self.hold(value.astype(jnp.bfloat16), "message", c, s)

    def prefix(self, c, s):
        if s == self.m:
            pairs = [(d, d ^ 1) for d in range(self.n)]
        else:
            pairs = [(2 * (s - 1) + y, 2 * s + y) for y in range(2)]
        return lax.ppermute(self.get("message", c, s), "seq", pairs)

    def states(self, c):
        _, near = self.get("local", c)
        own = (self.get("total", c) + jnp.where(self.col == 1, near, 0.0)).astype(jnp.bfloat16)
        return own, self.get("prefix", c, self.m)

    def mixed(self, c):
        low, width = self.chunks[c]
        place = self.get("put", c - 3)[1] if c > 2 else self.place
        place = self.hold(place, "mixed", c)
        states, spans = [], []
        for part, (start, size) in enumerate(self.parts):
            first, last = max(low, start), min(low + width, start + size)
            if first < last:
                states.append(self.get("states", part))
                spans.append((first - start, last - first))
        return attend(place, *self.arrays, self.gain, states, tuple(spans), self.n, low)

    def sent(self, c, k):
        pairs = [
            (2 * z + y, 2 * ((z + k // 2) % self.m) + (y + k) % 2) for z in range(self.m) for y in range(2)
        ]
        return lax.ppermute(self.hold(self.get("mixed", c)[k], "sent", c, k), "seq", pairs)

    def put(self, c):
        parts = [self.get("mixed", c)[0]] + [self.get("sent", c, k) for k in range(1, self.n)]
        out = self.get("put", c - 1)[0] if c else None
        return put(self.place, parts, out, self.n, self.chunks[c][0])


def per_device(n, *arrays):
    plan = Plan(n, *arrays)
    return plan.get("put", len(plan.chunks) - 1)[0]


def solution(mesh):
    tokens = P(("batch", "seq"), None)
    return jax.shard_map(
        functools.partial(per_device, mesh.shape["seq"]),
        mesh=mesh,
        in_specs=(tokens, tokens, tokens, P()),
        out_specs=P("batch", "seq"),
        check_vma=False,
    )
```

time: 215 us -> 213 us (level)
  waiting for transfers between devices: 73 us -> 107 us
  starting transfers between devices: 74.7 us -> 50.2 us
  Pallas kernels: 53.5 us -> 40.8 us
    ppermute x25 -> x16, waiting for transfers between devices: 12.5 us -> 32.7 us  [prefix(): return lax.ppermute(self.get('message', c, s), 'seq', pairs)]
    ppermute x28 -> x21, starting transfers between devices: 43 us -> 27.5 us  [sent(): lax.ppermute(self.hold(self.get('mixed', c)[k], 'sent', c, k), 'seq', pairs)]
    ppermute x28 -> x21, waiting for transfers between devices: 60.5 us -> 74.7 us  [sent(): lax.ppermute(self.hold(self.get('mixed', c)[k], 'sent', c, k), 'seq', pairs)]
    ppermute x25 -> x16, starting transfers between devices: 31.6 us -> 18.4 us  [prefix(): return lax.ppermute(self.get('message', c, s), 'seq', pairs)]
    pallas_call x10 -> x8, Pallas kernels: 53.5 us -> 40.8 us  [the longest x3 25.1 us: attend(): pl.pallas_call(functools.partial(attend_body, n, spans), in_specs=[pl.Blo...]
    ppermute x0 -> x4, starting transfers between devices: none -> 4.18 us  [swap(): return lax.ppermute(other, 'seq', [(d, d ^ 1) for d in range(self.n)])]
    convert_element_type x15, other arithmetic: 8.85 us -> 11.9 us  [message(): return self.hold(value.astype(jnp.bfloat16), 'message', c, s)]
  transfers between devices with their start and end apart: 53 -> 41, of which waited for: 20 -> 15; matrix products, arithmetic and copies ran while one was open for 6% -> 6% of each run, Pallas kernels for 22% -> 16%
where the time goes in v3:
time: 213 us; the launch traced here: 212 us
  waiting for transfers between devices  107 us (50%)
  starting transfers between devices  50.2 us (24%)
  Pallas kernels  40.8 us (19%)
  other arithmetic  13.3 us (6%)
    ppermute x21, waiting for transfers between devices, sent(): lax.ppermute(self.hold(self.get('mixed', c)[k], 'sent', c, k), 'seq', pairs)  74.7 us
    ppermute x16, waiting for transfers between devices, prefix(): return lax.ppermute(self.get('message', c, s), 'seq', pairs)  32.7 us
    ppermute x21, starting transfers between devices, sent(): lax.ppermute(self.hold(self.get('mixed', c)[k], 'sent', c, k), 'seq', pairs)  27.5 us
    pallas_call x3, Pallas kernels, attend(): pl.pallas_call(functools.partial(attend_body, n, spans), in_specs=[pl.Blo...  25.1 us
    ppermute x16, starting transfers between devices, prefix(): return lax.ppermute(self.get('message', c, s), 'seq', pairs)  18.4 us
    convert_element_type x15, other arithmetic, message(): return self.hold(value.astype(jnp.bfloat16), 'message', c, s)  11.9 us
    pallas_call x2, Pallas kernels, local_states(): pl.pallas_call(functools.partial(local_body, n, widths, swaps), in_specs=...  8.32 us
    pallas_call x3, Pallas kernels, put(): pl.pallas_call(functools.partial(put_body, n), in_specs=[pl.BlockSpec(mem...  7.33 us
  transfers between devices with their start and end apart: 41, of which 15 were waited for; matrix products, arithmetic and copies ran while one was open for 6% of the time, Pallas kernels for 16%

profile of v3, /device:TPU:8, one launch (start us, length us, event | category | flops | bytes accessed | tf_op | source)
XLA Modules:
  0.0 212.0 jit_solution(10695663888591017701)
XLA Ops:
  0.1 3.3 %local.3 = (f32[4,1,128,128]{3,2,1,0:T(8,128)S(1)}, f32[4,1,128,128]{3,2,1,0:T(8,128)S(1)}, bf16[4,1,128,128]{3,2,1,0:T(8,128)(2,1)S(1)}, bf16[4,1,128,128]{3,2,1,0:T(8,128)(2,1)S(1)}) custom-call(s32[2]{0:T(128)S(1)} %pad_add_fusion.place, s32[1]{0:T(128)} %constant.38.clone.1.low, bf16[384,8192]{1,0:T(8,128)(2,1)} %keys.9, bf16[384,8192]{1,0:T(8,128)(2,1)} %values.9), custom_call_target="tpu_custom_call" | custom-call | flops 201326592 | bytes 3145728 | tf_op jit(solution)/shard_map/local/pallas_call | solution.py:93
  3.4 1.6 collective-permute-start.3
  5.5 5.0 %local.2 = (f32[4,3,128,128]{3,2,1,0:T(8,128)S(1)}, f32[4,3,128,128]{3,2,1,0:T(8,128)S(1)}, bf16[4,3,128,128]{3,2,1,0:T(8,128)(2,1)S(1)}, bf16[4,3,128,128]{3,2,1,0:T(8,128)(2,1)S(1)}) custom-call(s32[2]{0:T(128)S(1)} %pad_add_fusion.place, s32[1]{0:T(128)} %constant.37.clone.1.low, bf16[384,8192]{1,0:T(8,128)(2,1)} %keys.9, bf16[384,8192]{1,0:T(8,128)(2,1)} %values.9), custom_call_target="tpu_custom_call" | custom-call | flops 603979776 | bytes 9437184 | tf_op jit(solution)/shard_map/local/pallas_call | solution.py:93
  10.5 1.6 collective-permute-start
  13.5 1.3 collective-permute-start.5
  15.8 1.3 collective-permute-start.4
  17.1 4.7 %collective-permute-done.5 = bf16[4,1,128,128]{3,2,1,0:T(8,128)(2,1)S(1)} collective-permute-done((bf16[4,1,128,128]{3,2,1,0:T(8,128)(2,1)S(1)}, bf16[4,1,128,128]{3,2,1,0:T(8,128)(2,1)S(1)}, u32[]{:S(2)}, u32[]{:S(2)}) %collective-permute-start.5) | collective-permute-done | bytes 131104 | tf_op jit(solution)/shard_map/ppermute | solution.py:364
  22.8 1.3 collective-permute-start.28
  25.0 1.3 collective-permute-start.31
  30.7 1.1 fusion.5
  31.8 1.3 collective-permute-start.7
  33.2 1.3 collective-permute-start.6
  35.5 1.6 collective-permute-start.30
  37.1 8.6 %collective-permute-done.7 = bf16[4,3,128,128]{3,2,1,0:T(8,128)(2,1)S(1)} collective-permute-done((bf16[4,3,128,128]{3,2,1,0:T(8,128)(2,1)S(1)}, bf16[4,3,128,128]{3,2,1,0:T(8,128)(2,1)S(1)}, u32[]{:S(2)}, u32[]{:S(2)}) %collective-permute-start.7) | collective-permute-done | bytes 393248 | tf_op jit(solution)/shard_map/ppermute | solution.py:364
  45.7 1.1 add_convert_fusion.2
  46.8 1.3 collective-permute-start.9
  48.2 2.9 %collective-permute-done.6 = bf16[4,3,128,128]{3,2,1,0:T(8,128)(2,1)S(1)} collective-permute-done((bf16[4,3,128,128]{3,2,1,0:T(8,128)(2,1)S(1)}, bf16[4,3,128,128]{3,2,1,0:T(8,128)(2,1)S(1)}, u32[]{:S(2)}, u32[]{:S(2)}) %collective-permute-start.6) | collective-permute-done | bytes 393248 | tf_op jit(solution)/shard_map/ppermute | solution.py:364
  51.2 1.3 collective-permute-start.8
  52.5 1.0 fusion.9
  53.6 1.6 collective-permute-start.33
  55.2 1.8 collective-permute-done.9
  57.0 1.1 add_convert_fusion
  58.8 3.0 %collective-permute-done.8 = bf16[4,3,128,128]{3,2,1,0:T(8,128)(2,1)S(1)} collective-permute-done((bf16[4,3,128,128]{3,2,1,0:T(8,128)(2,1)S(1)}, bf16[4,3,128,128]{3,2,1,0:T(8,128)(2,1)S(1)}, u32[]{:S(2)}, u32[]{:S(2)}) %collective-permute-start.8) | collective-permute-done | bytes 393248 | tf_op jit(solution)/shard_map/ppermute | solution.py:364
  62.7 8.7 %attend.5 = (bf16[384,256]{1,0:T(8,128)(2,1)S(1)}, bf16[384,256]{1,0:T(8,128)(2,1)S(1)}, bf16[384,256]{1,0:T(8,128)(2,1)S(1)}, bf16[384,256]{1,0:T(8,128)(2,1)S(...) custom-call(s32[2]{0:T(128)S(1)} %pad_add_fusion.place, ...), custom_call_target="tpu_custom_call" | custom-call | flops 1409286144 | bytes 6291456 | tf_op jit(solution)/shard_map/attend/pallas_call | solution.py:206
  71.4 1.6 collective-permute-start.34
  73.0 3.1 %collective-permute-start.35 = (bf16[384,256]{1,0:T(8,128)(2,1)S(1)}, bf16[384,256]{1,0:T(8,128)(2,1)S(1)}, u32[]{:S(2)}, u32[]{:S(2)}) collective-permute-start(bf16[384,256]{1,0:T(8,128)(2,1)S(1)} %get-tuple-element.86), channel_id=1, source_target_pairs={{0,8},{4,12},{8,16},{12,20},{16,24},{20,28},{24,0},{28,4},{1,9},{5... | collective-permute-start | bytes 589832 | tf_op jit(solution)/shard_map/ppermute | solution.py:387
  76.1 1.3 fusion.3
  78.3 1.6 collective-permute-start.12
  80.3 2.4 %collective-permute-start.37 = (bf16[384,256]{1,0:T(8,128)(2,1)S(1)}, bf16[384,256]{1,0:T(8,128)(2,1)S(1)}, u32[]{:S(2)}, u32[]{:S(2)}) collective-permute-start(bf16[384,256]{1,0:T(8,128)(2,1)S(1)} %get-tuple-element.88), channel_id=1, source_target_pairs={{0,16},{4,20},{8,24},{12,28},{16,0},{20,4},{24,8},{28,12},{1,17},{... | collective-permute-start | bytes 589832 | tf_op jit(solution)/shard_map/ppermute | solution.py:387
  82.7 2.4 %collective-permute-done.35.refs_2_ = bf16[384,256]{1,0:T(8,128)(2,1)S(1)} collective-permute-done((bf16[384,256]{1,0:T(8,128)(2,1)S(1)}, bf16[384,256]{1,0:T(8,128)(2,1)S(1)}, u32[]{:S(2)}, u32[]{:S(2)}) %collective-permute-start.35) | collective-permute-done | bytes 196640 | tf_op jit(solution)/shard_map/ppermute | solution.py:387
  85.2 10.7 %collective-permute-done.20.refs_1_ = bf16[4,3,128,128]{3,2,1,0:T(8,128)(2,1)S(1)} collective-permute-done((bf16[4,3,128,128]{3,2,1,0:T(8,128)(2,1)S(1)}, bf16[4,3,128,128]{3,2,1,0:T(8,128)(2,1)S(1)}, u32[]{:S(2)}, u32[]{:S(2)}) %collective-permute-start.20) | collective-permute-done | bytes 393248 | tf_op jit(solution)/shard_map/ppermute | solution.py:364
  95.9 8.2 %attend.4 = (bf16[384,384]{1,0:T(8,128)(2,1)S(1)}, bf16[384,384]{1,0:T(8,128)(2,1)S(1)}, bf16[384,384]{1,0:T(8,128)(2,1)S(1)}, bf16[384,384]{1,0:T(8,128)(2,1)S(...) custom-call(s32[2]{0:T(128)S(1)} %pad_add_fusion.place, ...), custom_call_target="tpu_custom_call" | custom-call | flops 2113929216 | bytes 9437184 | tf_op jit(solution)/shard_map/attend/pallas_call | solution.py:206
  104.1 1.8 collective-permute-start.21
  105.9 2.1 collective-permute-start.22
  108.0 1.7 collective-permute-start.23
  109.7 4.4 %collective-permute-done.39.refs_6_ = bf16[384,256]{1,0:T(8,128)(2,1)S(1)} collective-permute-done((bf16[384,256]{1,0:T(8,128)(2,1)S(1)}, bf16[384,256]{1,0:T(8,128)(2,1)S(1)}, u32[]{:S(2)}, u32[]{:S(2)}) %collective-permute-start.39) | collective-permute-done | bytes 196640 | tf_op jit(solution)/shard_map/ppermute | solution.py:387
  114.1 8.2 %attend.3 = (bf16[384,384]{1,0:T(8,128)(2,1)S(1)}, bf16[384,384]{1,0:T(8,128)(2,1)S(1)}, bf16[384,384]{1,0:T(8,128)(2,1)S(1)}, bf16[384,384]{1,0:T(8,128)(2,1)S(...) custom-call(s32[2]{0:T(128)S(1)} %pad_add_fusion.place, ...), custom_call_target="tpu_custom_call" | custom-call | flops 2113929216 | bytes 9437184 | tf_op jit(solution)/shard_map/attend/pallas_call | solution.py:206
  122.4 10.7 %collective-permute-done.40.refs_7_ = bf16[384,256]{1,0:T(8,128)(2,1)S(1)} collective-permute-done((bf16[384,256]{1,0:T(8,128)(2,1)S(1)}, bf16[384,256]{1,0:T(8,128)(2,1)S(1)}, u32[]{:S(2)}, u32[]{:S(2)}) %collective-permute-start.40) | collective-permute-done | bytes 196640 | tf_op jit(solution)/shard_map/ppermute | solution.py:387
  134.1 4.3 %collective-permute-start.27 = (bf16[384,384]{1,0:T(8,128)(2,1)S(1)}, bf16[384,384]{1,0:T(8,128)(2,1)S(1)}, u32[]{:S(2)}, u32[]{:S(2)}) collective-permute-start(bf16[384,384]{1,0:T(8,128)(2,1)S(1)} %get-tuple-element.80), channel_id=1, source_target_pairs={{0,28},{4,24},{8,4},{12,0},{16,12},{20,8},{24,20},{28,16},{1,29},{... | collective-permute-start | bytes 884744 | tf_op jit(solution)/shard_map/ppermute | solution.py:387
  138.8 20.3 %collective-permute-done.25.refs_5_ = bf16[384,384]{1,0:T(8,128)(2,1)S(1)} collective-permute-done((bf16[384,384]{1,0:T(8,128)(2,1)S(1)}, bf16[384,384]{1,0:T(8,128)(2,1)S(1)}, u32[]{:S(2)}, u32[]{:S(2)}) %collective-permute-start.25) | collective-permute-done | bytes 294944 | tf_op jit(solution)/shard_map/ppermute | solution.py:387
  159.1 3.4 %collective-permute-start.16 = (bf16[384,384]{1,0:T(8,128)(2,1)S(1)}, bf16[384,384]{1,0:T(8,128)(2,1)S(1)}, u32[]{:S(2)}, u32[]{:S(2)}) collective-permute-start(bf16[384,384]{1,0:T(8,128)(2,1)S(1)} %get-tuple-element.69), channel_id=1, source_target_pairs={{0,16},{4,20},{8,24},{12,28},{16,0},{20,4},{24,8},{28,12},{1,17},{... | collective-permute-start | bytes 884744 | tf_op jit(solution)/shard_map/ppermute | solution.py:387
  162.5 15.9 %collective-permute-done.27.refs_7_ = bf16[384,384]{1,0:T(8,128)(2,1)S(1)} collective-permute-done((bf16[384,384]{1,0:T(8,128)(2,1)S(1)}, bf16[384,384]{1,0:T(8,128)(2,1)S(1)}, u32[]{:S(2)}, u32[]{:S(2)}) %collective-permute-start.27) | collective-permute-done | bytes 294944 | tf_op jit(solution)/shard_map/ppermute | solution.py:387
  179.4 4.3 %collective-permute-start.19 = (bf16[384,384]{1,0:T(8,128)(2,1)S(1)}, bf16[384,384]{1,0:T(8,128)(2,1)S(1)}, u32[]{:S(2)}, u32[]{:S(2)}) collective-permute-start(bf16[384,384]{1,0:T(8,128)(2,1)S(1)} %get-tuple-element.72), channel_id=1, source_target_pairs={{0,28},{4,24},{8,4},{12,0},{16,12},{20,8},{24,20},{28,16},{1,29},{... | collective-permute-start | bytes 884744 | tf_op jit(solution)/shard_map/ppermute | solution.py:387
  183.7 2.3 %put.3 = (bf16[3072,1024]{1,0:T(8,128)(2,1)}, s32[2]{0:T(128)}) custom-call(s32[2]{0:T(128)S(1)} %pad_add_fusion.place, s32[1]{0:T(128)} %constant.38.clone.1.low, bf16[384,256]{1,0:T(8,128)(2,1)S(1)} %get-tuple-element.84.refs_0_, bf16[384,256]{1,0:T(8,128)(2,1)S(1)} %collective-permute-done.34.refs_1_, ...), custom_call_target="tpu_custom_call" | custom-call | tf_op jit(solution)/shard_map/put/pallas_call | solution.py:258
  185.9 2.5 %put.4 = (bf16[3072,1024]{1,0:T(8,128)(2,1)}, s32[2]{0:T(128)}) custom-call(s32[2]{0:T(128)S(1)} %pad_add_fusion.place, s32[1]{0:T(128)} %constant.37.clone.1.low, bf16[384,384]{1,0:T(8,128)(2,1)S(1)} %get-tuple-element.73.refs_0_, bf16[384,384]{1,0:T(8,128)(2,1)S(1)} %collective-permute-done.21.refs_1_, ...), custom_call_target="tpu_custom_call", output_to_operand_aliasing={{0}: (10, {})} | custom-call | tf_op jit(solution)/shard_map/put/pallas_call | solution.py:258
  188.5 14.8 %collective-permute-done.16.refs_4_ = bf16[384,384]{1,0:T(8,128)(2,1)S(1)} collective-permute-done((bf16[384,384]{1,0:T(8,128)(2,1)S(1)}, bf16[384,384]{1,0:T(8,128)(2,1)S(1)}, u32[]{:S(2)}, u32[]{:S(2)}) %collective-permute-start.16) | collective-permute-done | bytes 294944 | tf_op jit(solution)/shard_map/ppermute | solution.py:387
  203.3 6.1 %collective-permute-done.17.refs_5_ = bf16[384,384]{1,0:T(8,128)(2,1)S(1)} collective-permute-done((bf16[384,384]{1,0:T(8,128)(2,1)S(1)}, bf16[384,384]{1,0:T(8,128)(2,1)S(1)}, u32[]{:S(2)}, u32[]{:S(2)}) %collective-permute-start.17) | collective-permute-done | bytes 294944 | tf_op jit(solution)/shard_map/ppermute | solution.py:387
  209.5 2.5 %put.5 = (bf16[3072,1024]{1,0:T(8,128)(2,1)}, s32[2]{0:T(128)}) custom-call(s32[2]{0:T(128)S(1)} %pad_add_fusion.place, s32[1]{0:T(128)} %constant.36.clone.1.low, bf16[384,384]{1,0:T(8,128)(2,1)S(1)} %get-tuple-element.65.refs_0_, bf16[384,384]{1,0:T(8,128)(2,1)S(1)} %collective-permute-done.13.refs_1_, ...), custom_call_target="tpu_custom_call", output_to_operand_aliasing={{0}: (10, {})} | custom-call | tf_op jit(solution)/shard_map/put/pallas_call | solution.py:258
  (61 shorter events, 15.9 us)
Async XLA Ops:
  3.4 9.2 %collective-permute-start.3 = (bf16[4,1,128,128]{3,2,1,0:T(8,128)(2,1)S(1)}, bf16[4,1,128,128]{3,2,1,0:T(8,128)(2,1)}, u32[]{:S(2)}, u32[]{:S(2)}) collective-permute-start(bf16[4,1,128,128]{3,2,1,0:T(8,128)(2,1)S(1)} %get-tuple-element.57), channel_id=1, source_target_pairs={{0,4},{4,0},{8,12},{12,8},{16,20},{20,16},{24,28},{28,24},{1,5},{5... | collective-permute-start | bytes 393224 | tf_op jit(solution)/shard_map/ppermute | solution.py:337
  5.0 9.9 %collective-permute-start.2 = (bf16[4,1,128,128]{3,2,1,0:T(8,128)(2,1)S(1)}, bf16[4,1,128,128]{3,2,1,0:T(8,128)(2,1)}, u32[]{:S(2)}, u32[]{:S(2)}) collective-permute-start(bf16[4,1,128,128]{3,2,1,0:T(8,128)(2,1)S(1)} %get-tuple-element.55), channel_id=1, source_target_pairs={{0,4},{4,0},{8,12},{12,8},{16,20},{20,16},{24,28},{28,24},{1,5},{5... | collective-permute-start | bytes 393224 | tf_op jit(solution)/shard_map/ppermute | solution.py:337
  10.5 22.6 %collective-permute-start = (bf16[4,3,128,128]{3,2,1,0:T(8,128)(2,1)S(1)}, bf16[4,3,128,128]{3,2,1,0:T(8,128)(2,1)S(1)}, u32[]{:S(2)}, u32[]{:S(2)}) collective-permute-start(bf16[4,3,128,128]{3,2,1,0:T(8,128)(2,1)S(1)} %get-tuple-element.51), channel_id=1, source_target_pairs={{0,4},{4,0},{8,12},{12,8},{16,20},{20,16},{24,28},{28,24},{1,5},{5... | collective-permute-start | bytes 1179656 | tf_op jit(solution)/shard_map/ppermute | solution.py:337
  12.1 18.5 %collective-permute-start.1 = (bf16[4,3,128,128]{3,2,1,0:T(8,128)(2,1)S(1)}, bf16[4,3,128,128]{3,2,1,0:T(8,128)(2,1)}, u32[]{:S(2)}, u32[]{:S(2)}) collective-permute-start(bf16[4,3,128,128]{3,2,1,0:T(8,128)(2,1)S(1)} %get-tuple-element.53), channel_id=1, source_target_pairs={{0,4},{4,0},{8,12},{12,8},{16,20},{20,16},{24,28},{28,24},{1,5},{5... | collective-permute-start | bytes 1179656 | tf_op jit(solution)/shard_map/ppermute | solution.py:337
  13.5 8.3 %collective-permute-start.5 = (bf16[4,1,128,128]{3,2,1,0:T(8,128)(2,1)S(1)}, bf16[4,1,128,128]{3,2,1,0:T(8,128)(2,1)S(1)}, u32[]{:S(2)}, u32[]{:S(2)}) collective-permute-start(bf16[4,1,128,128]{3,2,1,0:T(8,128)(2,1)S(1)} %fusion.11), channel_id=1, source_target_pairs={{0,8},{4,12},{1,9},{5,13},{2,10},{6,14},{3,11},{7,15}} | collective-permute-start | bytes 393224 | tf_op jit(solution)/shard_map/ppermute | solution.py:364
  15.8 8.3 %collective-permute-start.4 = (bf16[4,1,128,128]{3,2,1,0:T(8,128)(2,1)S(1)}, bf16[4,1,128,128]{3,2,1,0:T(8,128)(2,1)S(1)}, u32[]{:S(2)}, u32[]{:S(2)}) collective-permute-start(bf16[4,1,128,128]{3,2,1,0:T(8,128)(2,1)S(1)} %fusion.10), channel_id=1, source_target_pairs={{0,8},{4,12},{1,9},{5,13},{2,10},{6,14},{3,11},{7,15}} | collective-permute-start | bytes 393224 | tf_op jit(solution)/shard_map/ppermute | solution.py:364
  22.8 4.6 %collective-permute-start.28 = (bf16[4,1,128,128]{3,2,1,0:T(8,128)(2,1)S(1)}, bf16[4,1,128,128]{3,2,1,0:T(8,128)(2,1)S(1)}, u32[]{:S(2)}, u32[]{:S(2)}) collective-permute-start(bf16[4,1,128,128]{3,2,1,0:T(8,128)(2,1)S(1)} %add_convert_fusion.6), channel_id=1, source_target_pairs={{8,16},{12,20},{9,17},{13,21},{10,18},{14,22},{11,19},{15,23}} | collective-permute-start | bytes 393224 | tf_op jit(solution)/shard_map/ppermute | solution.py:364
  25.0 4.0 %collective-permute-start.31 = (bf16[4,1,128,128]{3,2,1,0:T(8,128)(2,1)S(1)}, bf16[4,1,128,128]{3,2,1,0:T(8,128)(2,1)S(1)}, u32[]{:S(2)}, u32[]{:S(2)}) collective-permute-start(bf16[4,1,128,128]{3,2,1,0:T(8,128)(2,1)S(1)} %add_convert_fusion.7), channel_id=1, source_target_pairs={{8,16},{12,20},{9,17},{13,21},{10,18},{14,22},{11,19},{15,23}} | collective-permute-start | bytes 393224 | tf_op jit(solution)/shard_map/ppermute | solution.py:364
  28.3 6.2 %collective-permute-start.29 = (bf16[4,1,128,128]{3,2,1,0:T(8,128)(2,1)S(1)}, bf16[4,1,128,128]{3,2,1,0:T(8,128)(2,1)S(1)}, u32[]{:S(2)}, u32[]{:S(2)}) collective-permute-start(bf16[4,1,128,128]{3,2,1,0:T(8,128)(2,1)S(1)} %add_convert_fusion.5), channel_id=1, source_target_pairs={{16,24},{20,28},{17,25},{21,29},{18,26},{22,30},{19,27},{23,31}} | collective-permute-start | bytes 393224 | tf_op jit(solution)/shard_map/ppermute | solution.py:364
  30.0 22.6 %collective-permute-start.32 = (bf16[4,1,128,128]{3,2,1,0:T(8,128)(2,1)S(1)}, bf16[4,1,128,128]{3,2,1,0:T(8,128)(2,1)S(1)}, u32[]{:S(2)}, u32[]{:S(2)}) collective-permute-start(bf16[4,1,128,128]{3,2,1,0:T(8,128)(2,1)S(1)} %add_convert_fusion.4), channel_id=1, source_target_pairs={{16,24},{20,28},{17,25},{21,29},{18,26},{22,30},{19,27},{23,31}} | collective-permute-start | bytes 393224 | tf_op jit(solution)/shard_map/ppermute | solution.py:364
  30.6 32.1 %copy-start = (f32[8192]{0:T(1024)S(1)}, f32[8192]{0:T(1024)}, u32[]{:S(2)}) copy-start(f32[8192]{0:T(1024)} %param.7) | copy-start | bytes 98308
  31.8 13.9 %collective-permute-start.7 = (bf16[4,3,128,128]{3,2,1,0:T(8,128)(2,1)S(1)}, bf16[4,3,128,128]{3,2,1,0:T(8,128)(2,1)S(1)}, u32[]{:S(2)}, u32[]{:S(2)}) collective-permute-start(bf16[4,3,128,128]{3,2,1,0:T(8,128)(2,1)S(1)} %fusion.5), channel_id=1, source_target_pairs={{0,8},{4,12},{1,9},{5,13},{2,10},{6,14},{3,11},{7,15}} | collective-permute-start | bytes 1179656 | tf_op jit(solution)/shard_map/ppermute | solution.py:364
  33.2 17.9 %collective-permute-start.6 = (bf16[4,3,128,128]{3,2,1,0:T(8,128)(2,1)S(1)}, bf16[4,3,128,128]{3,2,1,0:T(8,128)(2,1)S(1)}, u32[]{:S(2)}, u32[]{:S(2)}) collective-permute-start(bf16[4,3,128,128]{3,2,1,0:T(8,128)(2,1)S(1)} %fusion.4), channel_id=1, source_target_pairs={{0,8},{4,12},{1,9},{5,13},{2,10},{6,14},{3,11},{7,15}} | collective-permute-start | bytes 1179656 | tf_op jit(solution)/shard_map/ppermute | solution.py:364
  35.5 27.2 %collective-permute-start.30 = (bf16[4,1,128,128]{3,2,1,0:T(8,128)(2,1)S(1)}, bf16[4,1,128,128]{3,2,1,0:T(8,128)(2,1)S(1)}, u32[]{:S(2)}, u32[]{:S(2)}) collective-permute-start(bf16[4,1,128,128]{3,2,1,0:T(8,128)(2,1)S(1)} %get-tuple-element.101), channel_id=1, source_target_pairs={{0,4},{4,0},{8,12},{12,8},{16,20},{20,16},{24,28},{28,24},{1,5},{5... | collective-permute-start | bytes 393224 | tf_op jit(solution)/shard_map/ppermute | solution.py:364
  46.8 10.1 %collective-permute-start.9 = (bf16[4,3,128,128]{3,2,1,0:T(8,128)(2,1)S(1)}, bf16[4,3,128,128]{3,2,1,0:T(8,128)(2,1)S(1)}, u32[]{:S(2)}, u32[]{:S(2)}) collective-permute-start(bf16[4,3,128,128]{3,2,1,0:T(8,128)(2,1)S(1)} %add_convert_fusion.2), channel_id=1, source_target_pairs={{8,16},{12,20},{9,17},{13,21},{10,18},{14,22},{11,19},{15,23}} | collective-permute-start | bytes 1179656 | tf_op jit(solution)/shard_map/ppermute | solution.py:364
  51.2 10.6 %collective-permute-start.8 = (bf16[4,3,128,128]{3,2,1,0:T(8,128)(2,1)S(1)}, bf16[4,3,128,128]{3,2,1,0:T(8,128)(2,1)S(1)}, u32[]{:S(2)}, u32[]{:S(2)}) collective-permute-start(bf16[4,3,128,128]{3,2,1,0:T(8,128)(2,1)S(1)} %add_convert_fusion.3), channel_id=1, source_target_pairs={{8,16},{12,20},{9,17},{13,21},{10,18},{14,22},{11,19},{15,23}} | collective-permute-start | bytes 1179656 | tf_op jit(solution)/shard_map/ppermute | solution.py:364
  53.6 9.1 %collective-permute-start.33 = (bf16[4,1,128,128]{3,2,1,0:T(8,128)(2,1)S(1)}, bf16[4,1,128,128]{3,2,1,0:T(8,128)(2,1)S(1)}, u32[]{:S(2)}, u32[]{:S(2)}) collective-permute-start(bf16[4,1,128,128]{3,2,1,0:T(8,128)(2,1)S(1)} %get-tuple-element.83), channel_id=1, source_target_pairs={{0,4},{4,0},{8,12},{12,8},{16,20},{20,16},{24,28},{28,24},{1,5},{5... | collective-permute-start | bytes 393224 | tf_op jit(solution)/shard_map/ppermute | solution.py:364
  58.1 18.0 %collective-permute-start.11 = (bf16[4,3,128,128]{3,2,1,0:T(8,128)(2,1)S(1)}, bf16[4,3,128,128]{3,2,1,0:T(8,128)(2,1)S(1)}, u32[]{:S(2)}, u32[]{:S(2)}) collective-permute-start(bf16[4,3,128,128]{3,2,1,0:T(8,128)(2,1)S(1)} %add_convert_fusion), channel_id=1, source_target_pairs={{16,24},{20,28},{17,25},{21,29},{18,26},{22,30},{19,27},{23,31}} | collective-permute-start | bytes 1179656 | tf_op jit(solution)/shard_map/ppermute | solution.py:364
  62.0 16.0 %collective-permute-start.10 = (bf16[4,3,128,128]{3,2,1,0:T(8,128)(2,1)S(1)}, bf16[4,3,128,128]{3,2,1,0:T(8,128)(2,1)S(1)}, u32[]{:S(2)}, u32[]{:S(2)}) collective-permute-start(bf16[4,3,128,128]{3,2,1,0:T(8,128)(2,1)S(1)} %add_convert_fusion.1), channel_id=1, source_target_pairs={{16,24},{20,28},{17,25},{21,29},{18,26},{22,30},{19,27},{23,31}} | collective-permute-start | bytes 1179656 | tf_op jit(solution)/shard_map/ppermute | solution.py:364
  71.4 8.9 %collective-permute-start.34 = (bf16[384,256]{1,0:T(8,128)(2,1)S(1)}, bf16[384,256]{1,0:T(8,128)(2,1)S(1)}, u32[]{:S(2)}, u32[]{:S(2)}) collective-permute-start(bf16[384,256]{1,0:T(8,128)(2,1)S(1)} %get-tuple-element.85), channel_id=1, source_target_pairs={{0,4},{4,0},{8,12},{12,8},{16,20},{20,16},{24,28},{28,24},{1,5},{5... | collective-permute-start | bytes 589832 | tf_op jit(solution)/shard_map/ppermute | solution.py:387
  73.0 12.2 %collective-permute-start.35 = (bf16[384,256]{1,0:T(8,128)(2,1)S(1)}, bf16[384,256]{1,0:T(8,128)(2,1)S(1)}, u32[]{:S(2)}, u32[]{:S(2)}) collective-permute-start(bf16[384,256]{1,0:T(8,128)(2,1)S(1)} %get-tuple-element.86), channel_id=1, source_target_pairs={{0,8},{4,12},{8,16},{12,20},{16,24},{20,28},{24,0},{28,4},{1,9},{5... | collective-permute-start | bytes 589832 | tf_op jit(solution)/shard_map/ppermute | solution.py:387
  77.4 18.4 %collective-permute-start.20 = (bf16[4,3,128,128]{3,2,1,0:T(8,128)(2,1)S(1)}, bf16[4,3,128,128]{3,2,1,0:T(8,128)(2,1)S(1)}, u32[]{:S(2)}, u32[]{:S(2)}) collective-permute-start(bf16[4,3,128,128]{3,2,1,0:T(8,128)(2,1)S(1)} %get-tuple-element.96), channel_id=1, source_target_pairs={{0,4},{4,0},{8,12},{12,8},{16,20},{20,16},{24,28},{28,24},{1,5},{5... | collective-permute-start | bytes 1179656 | tf_op jit(solution)/shard_map/ppermute | solution.py:364
  78.3 35.8 %collective-permute-start.12 = (bf16[4,3,128,128]{3,2,1,0:T(8,128)(2,1)S(1)}, bf16[4,3,128,128]{3,2,1,0:T(8,128)(2,1)S(1)}, u32[]{:S(2)}, u32[]{:S(2)}) collective-permute-start(bf16[4,3,128,128]{3,2,1,0:T(8,128)(2,1)S(1)} %get-tuple-element.64), channel_id=1, source_target_pairs={{0,4},{4,0},{8,12},{12,8},{16,20},{20,16},{24,28},{28,24},{1,5},{5... | collective-permute-start | bytes 1179656 | tf_op jit(solution)/shard_map/ppermute | solution.py:364
  79.9 24.2 %collective-permute-start.36 = (bf16[384,256]{1,0:T(8,128)(2,1)S(1)}, bf16[384,256]{1,0:T(8,128)(2,1)S(1)}, u32[]{:S(2)}, u32[]{:S(2)}) collective-permute-start(bf16[384,256]{1,0:T(8,128)(2,1)S(1)} %get-tuple-element.87), channel_id=1, source_target_pairs={{0,12},{4,8},{8,20},{12,16},{16,28},{20,24},{24,4},{28,0},{1,13},{... | collective-permute-start | bytes 589832 | tf_op jit(solution)/shard_map/ppermute | solution.py:387
  80.3 25.6 %collective-permute-start.37 = (bf16[384,256]{1,0:T(8,128)(2,1)S(1)}, bf16[384,256]{1,0:T(8,128)(2,1)S(1)}, u32[]{:S(2)}, u32[]{:S(2)}) collective-permute-start(bf16[384,256]{1,0:T(8,128)(2,1)S(1)} %get-tuple-element.88), channel_id=1, source_target_pairs={{0,16},{4,20},{8,24},{12,28},{16,0},{20,4},{24,8},{28,12},{1,17},{... | collective-permute-start | bytes 589832 | tf_op jit(solution)/shard_map/ppermute | solution.py:387
  85.2 22.8 %collective-permute-start.38 = (bf16[384,256]{1,0:T(8,128)(2,1)S(1)}, bf16[384,256]{1,0:T(8,128)(2,1)S(1)}, u32[]{:S(2)}, u32[]{:S(2)}) collective-permute-start(bf16[384,256]{1,0:T(8,128)(2,1)S(1)} %get-tuple-element.89), channel_id=1, source_target_pairs={{0,20},{4,16},{8,28},{12,24},{16,4},{20,0},{24,12},{28,8},{1,21},{... | collective-permute-start | bytes 589832 | tf_op jit(solution)/shard_map/ppermute | solution.py:387
  95.9 18.2 %collective-permute-start.39 = (bf16[384,256]{1,0:T(8,128)(2,1)S(1)}, bf16[384,256]{1,0:T(8,128)(2,1)S(1)}, u32[]{:S(2)}, u32[]{:S(2)}) collective-permute-start(bf16[384,256]{1,0:T(8,128)(2,1)S(1)} %get-tuple-element.90), channel_id=1, source_target_pairs={{0,24},{4,28},{8,0},{12,4},{16,8},{20,12},{24,16},{28,20},{1,25},{... | collective-permute-start | bytes 589832 | tf_op jit(solution)/shard_map/ppermute | solution.py:387
  104.1 28.9 %collective-permute-start.21 = (bf16[384,384]{1,0:T(8,128)(2,1)S(1)}, bf16[384,384]{1,0:T(8,128)(2,1)S(1)}, u32[]{:S(2)}, u32[]{:S(2)}) collective-permute-start(bf16[384,384]{1,0:T(8,128)(2,1)S(1)} %get-tuple-element.74), channel_id=1, source_target_pairs={{0,4},{4,0},{8,12},{12,8},{16,20},{20,16},{24,28},{28,24},{1,5},{5... | collective-permute-start | bytes 884744 | tf_op jit(solution)/shard_map/ppermute | solution.py:387
  105.9 28.2 %collective-permute-start.22 = (bf16[384,384]{1,0:T(8,128)(2,1)S(1)}, bf16[384,384]{1,0:T(8,128)(2,1)S(1)}, u32[]{:S(2)}, u32[]{:S(2)}) collective-permute-start(bf16[384,384]{1,0:T(8,128)(2,1)S(1)} %get-tuple-element.75), channel_id=1, source_target_pairs={{0,8},{4,12},{8,16},{12,20},{16,24},{20,28},{24,0},{28,4},{1,9},{5... | collective-permute-start | bytes 884744 | tf_op jit(solution)/shard_map/ppermute | solution.py:387
  108.0 30.4 %collective-permute-start.23 = (bf16[384,384]{1,0:T(8,128)(2,1)S(1)}, bf16[384,384]{1,0:T(8,128)(2,1)S(1)}, u32[]{:S(2)}, u32[]{:S(2)}) collective-permute-start(bf16[384,384]{1,0:T(8,128)(2,1)S(1)} %get-tuple-element.76), channel_id=1, source_target_pairs={{0,12},{4,8},{8,20},{12,16},{16,28},{20,24},{24,4},{28,0},{1,13},{... | collective-permute-start | bytes 884744 | tf_op jit(solution)/shard_map/ppermute | solution.py:387
  114.1 24.7 %collective-permute-start.24 = (bf16[384,384]{1,0:T(8,128)(2,1)S(1)}, bf16[384,384]{1,0:T(8,128)(2,1)S(1)}, u32[]{:S(2)}, u32[]{:S(2)}) collective-permute-start(bf16[384,384]{1,0:T(8,128)(2,1)S(1)} %get-tuple-element.77), channel_id=1, source_target_pairs={{0,16},{4,20},{8,24},{12,28},{16,0},{20,4},{24,8},{28,12},{1,17},{... | collective-permute-start | bytes 884744 | tf_op jit(solution)/shard_map/ppermute | solution.py:387
  114.1 18.9 %collective-permute-start.40 = (bf16[384,256]{1,0:T(8,128)(2,1)S(1)}, bf16[384,256]{1,0:T(8,128)(2,1)S(1)}, u32[]{:S(2)}, u32[]{:S(2)}) collective-permute-start(bf16[384,256]{1,0:T(8,128)(2,1)S(1)} %get-tuple-element.91), channel_id=1, source_target_pairs={{0,28},{4,24},{8,4},{12,0},{16,12},{20,8},{24,20},{28,16},{1,29},{... | collective-permute-start | bytes 589832 | tf_op jit(solution)/shard_map/ppermute | solution.py:387
  133.0 26.0 %collective-permute-start.25 = (bf16[384,384]{1,0:T(8,128)(2,1)S(1)}, bf16[384,384]{1,0:T(8,128)(2,1)S(1)}, u32[]{:S(2)}, u32[]{:S(2)}) collective-permute-start(bf16[384,384]{1,0:T(8,128)(2,1)S(1)} %get-tuple-element.78), channel_id=1, source_target_pairs={{0,20},{4,16},{8,28},{12,24},{16,4},{20,0},{24,12},{28,8},{1,21},{... | collective-permute-start | bytes 884744 | tf_op jit(solution)/shard_map/ppermute | solution.py:387
  133.1 26.0 %collective-permute-start.26 = (bf16[384,384]{1,0:T(8,128)(2,1)S(1)}, bf16[384,384]{1,0:T(8,128)(2,1)S(1)}, u32[]{:S(2)}, u32[]{:S(2)}) collective-permute-start(bf16[384,384]{1,0:T(8,128)(2,1)S(1)} %get-tuple-element.79), channel_id=1, source_target_pairs={{0,24},{4,28},{8,0},{12,4},{16,8},{20,12},{24,16},{28,20},{1,25},{... | collective-permute-start | bytes 884744 | tf_op jit(solution)/shard_map/ppermute | solution.py:387
  134.1 44.3 %collective-permute-start.27 = (bf16[384,384]{1,0:T(8,128)(2,1)S(1)}, bf16[384,384]{1,0:T(8,128)(2,1)S(1)}, u32[]{:S(2)}, u32[]{:S(2)}) collective-permute-start(bf16[384,384]{1,0:T(8,128)(2,1)S(1)} %get-tuple-element.80), channel_id=1, source_target_pairs={{0,28},{4,24},{8,4},{12,0},{16,12},{20,8},{24,20},{28,16},{1,29},{... | collective-permute-start | bytes 884744 | tf_op jit(solution)/shard_map/ppermute | solution.py:387
  138.3 40.0 %collective-permute-start.13 = (bf16[384,384]{1,0:T(8,128)(2,1)S(1)}, bf16[384,384]{1,0:T(8,128)(2,1)S(1)}, u32[]{:S(2)}, u32[]{:S(2)}) collective-permute-start(bf16[384,384]{1,0:T(8,128)(2,1)S(1)} %get-tuple-element.66), channel_id=1, source_target_pairs={{0,4},{4,0},{8,12},{12,8},{16,20},{20,16},{24,28},{28,24},{1,5},{5... | collective-permute-start | bytes 884744 | tf_op jit(solution)/shard_map/ppermute | solution.py:387
  138.8 40.6 %collective-permute-start.14 = (bf16[384,384]{1,0:T(8,128)(2,1)S(1)}, bf16[384,384]{1,0:T(8,128)(2,1)S(1)}, u32[]{:S(2)}, u32[]{:S(2)}) collective-permute-start(bf16[384,384]{1,0:T(8,128)(2,1)S(1)} %get-tuple-element.67), channel_id=1, source_target_pairs={{0,8},{4,12},{8,16},{12,20},{16,24},{20,28},{24,0},{28,4},{1,9},{5... | collective-permute-start | bytes 884744 | tf_op jit(solution)/shard_map/ppermute | solution.py:387
  159.1 29.4 %collective-permute-start.15 = (bf16[384,384]{1,0:T(8,128)(2,1)S(1)}, bf16[384,384]{1,0:T(8,128)(2,1)S(1)}, u32[]{:S(2)}, u32[]{:S(2)}) collective-permute-start(bf16[384,384]{1,0:T(8,128)(2,1)S(1)} %get-tuple-element.68), channel_id=1, source_target_pairs={{0,12},{4,8},{8,20},{12,16},{16,28},{20,24},{24,4},{28,0},{1,13},{... | collective-permute-start | bytes 884744 | tf_op jit(solution)/shard_map/ppermute | solution.py:387
  159.1 44.2 %collective-permute-start.16 = (bf16[384,384]{1,0:T(8,128)(2,1)S(1)}, bf16[384,384]{1,0:T(8,128)(2,1)S(1)}, u32[]{:S(2)}, u32[]{:S(2)}) collective-permute-start(bf16[384,384]{1,0:T(8,128)(2,1)S(1)} %get-tuple-element.69), channel_id=1, source_target_pairs={{0,16},{4,20},{8,24},{12,28},{16,0},{20,4},{24,8},{28,12},{1,17},{... | collective-permute-start | bytes 884744 | tf_op jit(solution)/shard_map/ppermute | solution.py:387
  178.4 31.0 %collective-permute-start.17 = (bf16[384,384]{1,0:T(8,128)(2,1)S(1)}, bf16[384,384]{1,0:T(8,128)(2,1)S(1)}, u32[]{:S(2)}, u32[]{:S(2)}) collective-permute-start(bf16[384,384]{1,0:T(8,128)(2,1)S(1)} %get-tuple-element.70), channel_id=1, source_target_pairs={{0,20},{4,16},{8,28},{12,24},{16,4},{20,0},{24,12},{28,8},{1,21},{... | collective-permute-start | bytes 884744 | tf_op jit(solution)/shard_map/ppermute | solution.py:387
  178.4 31.0 %collective-permute-start.18 = (bf16[384,384]{1,0:T(8,128)(2,1)S(1)}, bf16[384,384]{1,0:T(8,128)(2,1)S(1)}, u32[]{:S(2)}, u32[]{:S(2)}) collective-permute-start(bf16[384,384]{1,0:T(8,128)(2,1)S(1)} %get-tuple-element.71), channel_id=1, source_target_pairs={{0,24},{4,28},{8,0},{12,4},{16,8},{20,12},{24,16},{28,20},{1,25},{... | collective-permute-start | bytes 884744 | tf_op jit(solution)/shard_map/ppermute | solution.py:387
  179.4 30.1 %collective-permute-start.19 = (bf16[384,384]{1,0:T(8,128)(2,1)S(1)}, bf16[384,384]{1,0:T(8,128)(2,1)S(1)}, u32[]{:S(2)}, u32[]{:S(2)}) collective-permute-start(bf16[384,384]{1,0:T(8,128)(2,1)S(1)} %get-tuple-element.72), channel_id=1, source_target_pairs={{0,28},{4,24},{8,4},{12,0},{16,12},{20,8},{24,20},{28,16},{1,29},{... | collective-permute-start | bytes 884744 | tf_op jit(solution)/shard_map/ppermute | solution.py:387

commit v4 on v3

--- a/solution.py
+++ b/solution.py
@@ -10,22 +10,21 @@
 HEADS = 64
 HEAD = 128
 LOCAL = (2, 6)
-SWAP = (1, 1, 3, 3)
-PREFIX = (1, 1, 3, 3)
+SWAP = (2, 3, 3)
+PREFIX = (2, 3, 3)
 MIXED = (2, 3, 3)
 TILE = 256
 SPARE = 8 * 1024 * 1024
 ORDER = {
-    ("message", 1, 1): [("message", 0, 1)],
-    ("message", 1, 2): [("message", 0, 2)],
-    ("message", 1, 3): [("message", 0, 3)],
-    ("message", 1, 4): [("message", 0, 4)],
-    ("message", 3, 1): [("message", 2, 1)],
-    ("message", 3, 2): [("message", 2, 2)],
-    ("message", 3, 3): [("message", 2, 3)],
-    ("message", 3, 4): [("message", 2, 4)],
+    ("message", 0, 1): [("group", 1)],
+    ("message", 1, 1): [("message", 0, 2)],
+    ("message", 1, 2): [("message", 0, 3)],
+    ("message", 1, 3): [("message", 0, 4)],
     ("message", 2, 1): [("message", 1, 2)],
-    ("mixed", 0): [("message", 2, 2), ("message", 3, 1)],
+    ("message", 2, 2): [("message", 1, 3)],
+    ("message", 2, 3): [("message", 1, 4), ("mixed", 0)],
+    ("mixed", 0): [("message", 1, 3), ("message", 2, 2)],
+    ("message", 1, 4): [("mixed", 0)],
 }
 
 

time: 213 us -> 203 us (0.953)
  other arithmetic: 13.3 us -> 7.65 us
  waiting for transfers between devices: 107 us -> 103 us
    ppermute x16 -> x12, waiting for transfers between devices: 32.7 us -> 25.1 us  [prefix(): return lax.ppermute(self.get('message', c, s), 'seq', pairs)]
    convert_element_type x15 -> x10, other arithmetic: 11.9 us -> 4.88 us  [message(): return self.hold(value.astype(jnp.bfloat16), 'message', c, s)]
    ppermute x16 -> x12, starting transfers between devices: 18.4 us -> 14.7 us  [prefix(): return lax.ppermute(self.get('message', c, s), 'seq', pairs)]
    ppermute x21, starting transfers between devices: 27.5 us -> 30.9 us  [sent(): lax.ppermute(self.hold(self.get('mixed', c)[k], 'sent', c, k), 'seq', pairs)]
    ppermute x4 -> x3, starting transfers between devices: 4.18 us -> 4.76 us  [swap(): return lax.ppermute(other, 'seq', [(d, d ^ 1) for d in range(self.n)])]
  transfers between devices with their start and end apart: 41 -> 36, of which waited for: 15 -> 13; matrix products, arithmetic and copies ran while one was open for 6% -> 4% of each run, Pallas kernels for 16% -> 17%
where the time goes in v4:
time: 203 us; the launch traced here: 202 us
  waiting for transfers between devices  103 us (51%)
  starting transfers between devices  50.4 us (25%)
  Pallas kernels  40.8 us (20%)
  other arithmetic  7.65 us (4%)
    ppermute x21, waiting for transfers between devices, sent(): lax.ppermute(self.hold(self.get('mixed', c)[k], 'sent', c, k), 'seq', pairs)  76.2 us
    ppermute x21, starting transfers between devices, sent(): lax.ppermute(self.hold(self.get('mixed', c)[k], 'sent', c, k), 'seq', pairs)  30.9 us
    pallas_call x3, Pallas kernels, attend(): pl.pallas_call(functools.partial(attend_body, n, spans), in_specs=[pl.Blo...  25.2 us
    ppermute x12, waiting for transfers between devices, prefix(): return lax.ppermute(self.get('message', c, s), 'seq', pairs)  25.1 us
    ppermute x12, starting transfers between devices, prefix(): return lax.ppermute(self.get('message', c, s), 'seq', pairs)  14.7 us
    pallas_call x2, Pallas kernels, local_states(): pl.pallas_call(functools.partial(local_body, n, widths, swaps), in_specs=...  8.32 us
    pallas_call x3, Pallas kernels, put(): pl.pallas_call(functools.partial(put_body, n), in_specs=[pl.BlockSpec(mem...  7.33 us
    convert_element_type x10, other arithmetic, message(): return self.hold(value.astype(jnp.bfloat16), 'message', c, s)  4.88 us
  transfers between devices with their start and end apart: 36, of which 13 were waited for; matrix products, arithmetic and copies ran while one was open for 4% of the time, Pallas kernels for 17%

profile of v4, /device:TPU:8, one launch (start us, length us, event | category | flops | bytes accessed | tf_op | source)
XLA Modules:
  0.0 201.9 jit_solution(11238084108274473226)
XLA Ops:
  0.1 3.3 %local.3 = (f32[4,2,128,128]{3,2,1,0:T(8,128)S(1)}, bf16[4,2,128,128]{3,2,1,0:T(8,128)(2,1)S(1)}) custom-call(s32[2]{0:T(128)S(1)} %pad_add_fusion.place, s32[1]{0:T(128)} %constant.38.clone.1.low, bf16[384,8192]{1,0:T(8,128)(2,1)} %keys.9, bf16[384,8192]{1,0:T(8,128)(2,1)} %values.9), custom_call_target="tpu_custom_call" | custom-call | flops 201326592 | bytes 3145728 | tf_op jit(solution)/shard_map/local/pallas_call | solution.py:92
  3.4 1.6 collective-permute-start.2
  5.0 5.0 %local.2 = (f32[4,3,128,128]{3,2,1,0:T(8,128)S(1)}, f32[4,3,128,128]{3,2,1,0:T(8,128)S(1)}, bf16[4,3,128,128]{3,2,1,0:T(8,128)(2,1)S(1)}, bf16[4,3,128,128]{3,2,1,0:T(8,128)(2,1)S(1)}) custom-call(s32[2]{0:T(128)S(1)} %pad_add_fusion.place, s32[1]{0:T(128)} %constant.37.clone.1.low, bf16[384,8192]{1,0:T(8,128)(2,1)} %keys.9, bf16[384,8192]{1,0:T(8,128)(2,1)} %values.9), custom_call_target="tpu_custom_call" | custom-call | flops 603979776 | bytes 9437184 | tf_op jit(solution)/shard_map/local/pallas_call | solution.py:92
  10.0 1.5 collective-permute-done.2
  11.5 1.3 collective-permute-start.3
  12.8 1.6 collective-permute-start.1
  14.4 6.2 %collective-permute-done.3 = bf16[4,2,128,128]{3,2,1,0:T(8,128)(2,1)S(1)} collective-permute-done((bf16[4,2,128,128]{3,2,1,0:T(8,128)(2,1)S(1)}, bf16[4,2,128,128]{3,2,1,0:T(8,128)(2,1)S(1)}, u32[]{:S(2)}, u32[]{:S(2)}) %collective-permute-start.3) | collective-permute-done | bytes 262176 | tf_op jit(solution)/shard_map/ppermute | solution.py:363
  21.4 2.1 %collective-permute-start.5 = (bf16[4,2,128,128]{3,2,1,0:T(8,128)(2,1)}, bf16[4,2,128,128]{3,2,1,0:T(8,128)(2,1)}, u32[]{:S(2)}, u32[]{:S(2)}) collective-permute-start(bf16[4,2,128,128]{3,2,1,0:T(8,128)(2,1)} %add_convert_fusion.5), channel_id=1, source_target_pairs={{8,16},{12,20},{9,17},{13,21},{10,18},{14,22},{11,19},{15,23}} | collective-permute-start | bytes 786440 | tf_op jit(solution)/shard_map/ppermute | solution.py:363
  23.5 0.8 fusion.7
  24.4 1.3 collective-permute-start.4
  25.7 1.6 collective-permute-start
  27.3 1.1 add_convert_fusion.4
  29.1 6.5 %collective-permute-done.4 = bf16[4,3,128,128]{3,2,1,0:T(8,128)(2,1)} collective-permute-done((bf16[4,3,128,128]{3,2,1,0:T(8,128)(2,1)}, bf16[4,3,128,128]{3,2,1,0:T(8,128)(2,1)}, u32[]{:S(2)}, u32[]{:S(2)}) %collective-permute-start.4) | collective-permute-done | bytes 393248 | tf_op jit(solution)/shard_map/ppermute | solution.py:363
  35.6 1.2 add_convert_fusion.3
  36.8 1.3 collective-permute-start.7
  38.2 1.3 collective-permute-start.6
  39.6 1.4 fusion.5
  40.9 1.6 collective-permute-start.11
  42.5 1.5 collective-permute-done.7
  44.9 3.4 %collective-permute-done.6 = bf16[4,3,128,128]{3,2,1,0:T(8,128)(2,1)S(1)} collective-permute-done((bf16[4,3,128,128]{3,2,1,0:T(8,128)(2,1)S(1)}, bf16[4,3,128,128]{3,2,1,0:T(8,128)(2,1)S(1)}, u32[]{:S(2)}, u32[]{:S(2)}) %collective-permute-start.6) | collective-permute-done | bytes 393248 | tf_op jit(solution)/shard_map/ppermute | solution.py:363
  48.4 1.6 collective-permute-start.9
  50.1 8.6 %attend.3 = (bf16[384,256]{1,0:T(8,128)(2,1)S(1)}, bf16[384,256]{1,0:T(8,128)(2,1)S(1)}, bf16[384,256]{1,0:T(8,128)(2,1)S(1)}, bf16[384,256]{1,0:T(8,128)(2,1)S(...) custom-call(s32[2]{0:T(128)S(1)} %pad_add_fusion.place, ...), custom_call_target="tpu_custom_call" | custom-call | flops 1409286144 | bytes 6291456 | tf_op jit(solution)/shard_map/attend/pallas_call | solution.py:205
  58.8 1.3 fusion.1
  60.9 1.6 collective-permute-start.29
  63.4 1.6 collective-permute-start.13
  65.0 7.7 %collective-permute-start.31 = (bf16[384,256]{1,0:T(8,128)(2,1)S(1)}, bf16[384,256]{1,0:T(8,128)(2,1)S(1)}, u32[]{:S(2)}, u32[]{:S(2)}) collective-permute-start(bf16[384,256]{1,0:T(8,128)(2,1)S(1)} %get-tuple-element.82), channel_id=1, source_target_pairs={{0,12},{4,8},{8,20},{12,16},{16,28},{20,24},{24,4},{28,0},{1,13},{... | collective-permute-start | bytes 589832 | tf_op jit(solution)/shard_map/ppermute | solution.py:386
  72.7 2.9 %collective-permute-start.32 = (bf16[384,256]{1,0:T(8,128)(2,1)S(1)}, bf16[384,256]{1,0:T(8,128)(2,1)S(1)}, u32[]{:S(2)}, u32[]{:S(2)}) collective-permute-start(bf16[384,256]{1,0:T(8,128)(2,1)S(1)} %get-tuple-element.83), channel_id=1, source_target_pairs={{0,16},{4,20},{8,24},{12,28},{16,0},{20,4},{24,8},{28,12},{1,17},{... | collective-permute-start | bytes 589832 | tf_op jit(solution)/shard_map/ppermute | solution.py:386
  75.7 2.0 collective-permute-start.33
  77.6 7.5 %collective-permute-done.21.refs_1_ = bf16[4,3,128,128]{3,2,1,0:T(8,128)(2,1)S(1)} collective-permute-done((bf16[4,3,128,128]{3,2,1,0:T(8,128)(2,1)S(1)}, bf16[4,3,128,128]{3,2,1,0:T(8,128)(2,1)S(1)}, u32[]{:S(2)}, u32[]{:S(2)}) %collective-permute-start.21) | collective-permute-done | bytes 393248 | tf_op jit(solution)/shard_map/ppermute | solution.py:363
  85.1 8.3 %attend.5 = (bf16[384,384]{1,0:T(8,128)(2,1)S(1)}, bf16[384,384]{1,0:T(8,128)(2,1)S(1)}, bf16[384,384]{1,0:T(8,128)(2,1)S(1)}, bf16[384,384]{1,0:T(8,128)(2,1)S(...) custom-call(s32[2]{0:T(128)S(1)} %pad_add_fusion.place, ...), custom_call_target="tpu_custom_call" | custom-call | flops 2113929216 | bytes 9437184 | tf_op jit(solution)/shard_map/attend/pallas_call | solution.py:205
  94.0 2.0 collective-permute-start.23
  95.9 1.1 collective-permute-start.24
  97.0 14.6 %collective-permute-done.34.refs_6_ = bf16[384,256]{1,0:T(8,128)(2,1)S(1)} collective-permute-done((bf16[384,256]{1,0:T(8,128)(2,1)S(1)}, bf16[384,256]{1,0:T(8,128)(2,1)S(1)}, u32[]{:S(2)}, u32[]{:S(2)}) %collective-permute-start.34) | collective-permute-done | bytes 196640 | tf_op jit(solution)/shard_map/ppermute | solution.py:386
  112.3 8.3 %attend.4 = (bf16[384,384]{1,0:T(8,128)(2,1)S(1)}, bf16[384,384]{1,0:T(8,128)(2,1)S(1)}, bf16[384,384]{1,0:T(8,128)(2,1)S(1)}, bf16[384,384]{1,0:T(8,128)(2,1)S(...) custom-call(s32[2]{0:T(128)S(1)} %pad_add_fusion.place, ...), custom_call_target="tpu_custom_call" | custom-call | flops 2113929216 | bytes 9437184 | tf_op jit(solution)/shard_map/attend/pallas_call | solution.py:205
  120.6 8.2 %collective-permute-done.35.refs_7_ = bf16[384,256]{1,0:T(8,128)(2,1)S(1)} collective-permute-done((bf16[384,256]{1,0:T(8,128)(2,1)S(1)}, bf16[384,256]{1,0:T(8,128)(2,1)S(1)}, u32[]{:S(2)}, u32[]{:S(2)}) %collective-permute-start.35) | collective-permute-done | bytes 196640 | tf_op jit(solution)/shard_map/ppermute | solution.py:386
  128.8 1.0 collective-permute-start.27
  129.8 4.3 %collective-permute-start.28 = (bf16[384,384]{1,0:T(8,128)(2,1)S(1)}, bf16[384,384]{1,0:T(8,128)(2,1)S(1)}, u32[]{:S(2)}, u32[]{:S(2)}) collective-permute-start(bf16[384,384]{1,0:T(8,128)(2,1)S(1)} %get-tuple-element.78), channel_id=1, source_target_pairs={{0,28},{4,24},{8,4},{12,0},{16,12},{20,8},{24,20},{28,16},{1,29},{... | collective-permute-start | bytes 884744 | tf_op jit(solution)/shard_map/ppermute | solution.py:386
  134.1 1.8 collective-permute-start.14
  135.8 11.3 %collective-permute-done.26.refs_5_ = bf16[384,384]{1,0:T(8,128)(2,1)S(1)} collective-permute-done((bf16[384,384]{1,0:T(8,128)(2,1)S(1)}, bf16[384,384]{1,0:T(8,128)(2,1)S(1)}, u32[]{:S(2)}, u32[]{:S(2)}) %collective-permute-start.26) | collective-permute-done | bytes 294944 | tf_op jit(solution)/shard_map/ppermute | solution.py:386
  147.1 14.7 %collective-permute-done.27.refs_6_ = bf16[384,384]{1,0:T(8,128)(2,1)S(1)} collective-permute-done((bf16[384,384]{1,0:T(8,128)(2,1)S(1)}, bf16[384,384]{1,0:T(8,128)(2,1)S(1)}, u32[]{:S(2)}, u32[]{:S(2)}) %collective-permute-start.27) | collective-permute-done | bytes 294944 | tf_op jit(solution)/shard_map/ppermute | solution.py:386
  161.8 12.3 %collective-permute-done.28.refs_7_ = bf16[384,384]{1,0:T(8,128)(2,1)S(1)} collective-permute-done((bf16[384,384]{1,0:T(8,128)(2,1)S(1)}, bf16[384,384]{1,0:T(8,128)(2,1)S(1)}, u32[]{:S(2)}, u32[]{:S(2)}) %collective-permute-start.28) | collective-permute-done | bytes 294944 | tf_op jit(solution)/shard_map/ppermute | solution.py:386
  174.1 1.0 collective-permute-start.19
  175.2 4.3 %collective-permute-start.20 = (bf16[384,384]{1,0:T(8,128)(2,1)S(1)}, bf16[384,384]{1,0:T(8,128)(2,1)S(1)}, u32[]{:S(2)}, u32[]{:S(2)}) collective-permute-start(bf16[384,384]{1,0:T(8,128)(2,1)S(1)} %get-tuple-element.70), channel_id=1, source_target_pairs={{0,28},{4,24},{8,4},{12,0},{16,12},{20,8},{24,20},{28,16},{1,29},{... | collective-permute-start | bytes 884744 | tf_op jit(solution)/shard_map/ppermute | solution.py:386
  179.4 2.3 %put.3 = (bf16[3072,1024]{1,0:T(8,128)(2,1)}, s32[2]{0:T(128)}) custom-call(s32[2]{0:T(128)S(1)} %pad_add_fusion.place, s32[1]{0:T(128)} %constant.38.clone.1.low, bf16[384,256]{1,0:T(8,128)(2,1)S(1)} %get-tuple-element.79.refs_0_, bf16[384,256]{1,0:T(8,128)(2,1)S(1)} %collective-permute-done.29.refs_1_, ...), custom_call_target="tpu_custom_call" | custom-call | tf_op jit(solution)/shard_map/put/pallas_call | solution.py:257
  181.7 2.5 %put.4 = (bf16[3072,1024]{1,0:T(8,128)(2,1)}, s32[2]{0:T(128)}) custom-call(s32[2]{0:T(128)S(1)} %pad_add_fusion.place, s32[1]{0:T(128)} %constant.37.clone.1.low, bf16[384,384]{1,0:T(8,128)(2,1)S(1)} %get-tuple-element.71.refs_0_, bf16[384,384]{1,0:T(8,128)(2,1)S(1)} %collective-permute-done.22.refs_1_, ...), custom_call_target="tpu_custom_call", output_to_operand_aliasing={{0}: (10, {})} | custom-call | tf_op jit(solution)/shard_map/put/pallas_call | solution.py:257
  184.3 9.4 %collective-permute-done.17.refs_4_ = bf16[384,384]{1,0:T(8,128)(2,1)S(1)} collective-permute-done((bf16[384,384]{1,0:T(8,128)(2,1)S(1)}, bf16[384,384]{1,0:T(8,128)(2,1)S(1)}, u32[]{:S(2)}, u32[]{:S(2)}) %collective-permute-start.17) | collective-permute-done | bytes 294944 | tf_op jit(solution)/shard_map/ppermute | solution.py:386
  193.6 5.7 %collective-permute-done.18.refs_5_ = bf16[384,384]{1,0:T(8,128)(2,1)S(1)} collective-permute-done((bf16[384,384]{1,0:T(8,128)(2,1)S(1)}, bf16[384,384]{1,0:T(8,128)(2,1)S(1)}, u32[]{:S(2)}, u32[]{:S(2)}) %collective-permute-start.18) | collective-permute-done | bytes 294944 | tf_op jit(solution)/shard_map/ppermute | solution.py:386
  199.4 2.5 %put.5 = (bf16[3072,1024]{1,0:T(8,128)(2,1)}, s32[2]{0:T(128)}) custom-call(s32[2]{0:T(128)S(1)} %pad_add_fusion.place, s32[1]{0:T(128)} %constant.36.clone.1.low, bf16[384,384]{1,0:T(8,128)(2,1)S(1)} %get-tuple-element.63.refs_0_, bf16[384,384]{1,0:T(8,128)(2,1)S(1)} %collective-permute-done.14.refs_1_, ...), custom_call_target="tpu_custom_call", output_to_operand_aliasing={{0}: (10, {})} | custom-call | tf_op jit(solution)/shard_map/put/pallas_call | solution.py:257
  (51 shorter events, 5.7 us)
Async XLA Ops:
  3.4 8.1 %collective-permute-start.2 = (bf16[4,2,128,128]{3,2,1,0:T(8,128)(2,1)S(1)}, bf16[4,2,128,128]{3,2,1,0:T(8,128)(2,1)S(1)}, u32[]{:S(2)}, u32[]{:S(2)}) collective-permute-start(bf16[4,2,128,128]{3,2,1,0:T(8,128)(2,1)S(1)} %get-tuple-element.52), channel_id=1, source_target_pairs={{0,4},{4,0},{8,12},{12,8},{16,20},{20,16},{24,28},{28,24},{1,5},{5... | collective-permute-start | bytes 786440 | tf_op jit(solution)/shard_map/ppermute | solution.py:336
  11.5 12.9 %copy-start.1 = (bf16[4,2,128,128]{3,2,1,0:T(8,128)(2,1)}, bf16[4,2,128,128]{3,2,1,0:T(8,128)(2,1)S(1)}, u32[]{:S(2)}) copy-start(bf16[4,2,128,128]{3,2,1,0:T(8,128)(2,1)S(1)} %collective-permute-done.2) | copy-start | bytes 786436
  11.5 9.1 %collective-permute-start.3 = (bf16[4,2,128,128]{3,2,1,0:T(8,128)(2,1)S(1)}, bf16[4,2,128,128]{3,2,1,0:T(8,128)(2,1)S(1)}, u32[]{:S(2)}, u32[]{:S(2)}) collective-permute-start(bf16[4,2,128,128]{3,2,1,0:T(8,128)(2,1)S(1)} %fusion.8), channel_id=1, source_target_pairs={{0,8},{4,12},{1,9},{5,13},{2,10},{6,14},{3,11},{7,15}} | collective-permute-start | bytes 786440 | tf_op jit(solution)/shard_map/ppermute | solution.py:363
  12.8 10.7 %collective-permute-start.1 = (bf16[4,3,128,128]{3,2,1,0:T(8,128)(2,1)S(1)}, bf16[4,3,128,128]{3,2,1,0:T(8,128)(2,1)S(1)}, u32[]{:S(2)}, u32[]{:S(2)}) collective-permute-start(bf16[4,3,128,128]{3,2,1,0:T(8,128)(2,1)S(1)} %get-tuple-element.50), channel_id=1, source_target_pairs={{0,4},{4,0},{8,12},{12,8},{16,20},{20,16},{24,28},{28,24},{1,5},{5... | collective-permute-start | bytes 1179656 | tf_op jit(solution)/shard_map/ppermute | solution.py:336
  20.6 2.9 %copy-start.2 = (bf16[4,2,128,128]{3,2,1,0:T(8,128)(2,1)}, bf16[4,2,128,128]{3,2,1,0:T(8,128)(2,1)S(1)}, u32[]{:S(2)}) copy-start(bf16[4,2,128,128]{3,2,1,0:T(8,128)(2,1)S(1)} %collective-permute-done.3) | copy-start | bytes 786436
  21.4 28.7 %copy-start = (f32[8192]{0:T(1024)S(1)}, f32[8192]{0:T(1024)}, u32[]{:S(2)}) copy-start(f32[8192]{0:T(1024)} %param.7) | copy-start | bytes 98308
  21.4 5.9 %collective-permute-start.5 = (bf16[4,2,128,128]{3,2,1,0:T(8,128)(2,1)}, bf16[4,2,128,128]{3,2,1,0:T(8,128)(2,1)}, u32[]{:S(2)}, u32[]{:S(2)}) collective-permute-start(bf16[4,2,128,128]{3,2,1,0:T(8,128)(2,1)} %add_convert_fusion.5), channel_id=1, source_target_pairs={{8,16},{12,20},{9,17},{13,21},{10,18},{14,22},{11,19},{15,23}} | collective-permute-start | bytes 786440 | tf_op jit(solution)/shard_map/ppermute | solution.py:363
  24.4 11.3 %collective-permute-start.4 = (bf16[4,3,128,128]{3,2,1,0:T(8,128)(2,1)}, bf16[4,3,128,128]{3,2,1,0:T(8,128)(2,1)}, u32[]{:S(2)}, u32[]{:S(2)}) collective-permute-start(bf16[4,3,128,128]{3,2,1,0:T(8,128)(2,1)} %fusion.7), channel_id=1, source_target_pairs={{0,8},{4,12},{1,9},{5,13},{2,10},{6,14},{3,11},{7,15}} | collective-permute-start | bytes 1179656 | tf_op jit(solution)/shard_map/ppermute | solution.py:363
  25.7 12.5 %collective-permute-start = (bf16[4,3,128,128]{3,2,1,0:T(8,128)(2,1)S(1)}, bf16[4,3,128,128]{3,2,1,0:T(8,128)(2,1)S(1)}, u32[]{:S(2)}, u32[]{:S(2)}) collective-permute-start(bf16[4,3,128,128]{3,2,1,0:T(8,128)(2,1)S(1)} %get-tuple-element.48), channel_id=1, source_target_pairs={{0,4},{4,0},{8,12},{12,8},{16,20},{20,16},{24,28},{28,24},{1,5},{5... | collective-permute-start | bytes 1179656 | tf_op jit(solution)/shard_map/ppermute | solution.py:336
  28.4 11.1 %collective-permute-start.8 = (bf16[4,2,128,128]{3,2,1,0:T(8,128)(2,1)S(1)}, bf16[4,2,128,128]{3,2,1,0:T(8,128)(2,1)S(1)}, u32[]{:S(2)}, u32[]{:S(2)}) collective-permute-start(bf16[4,2,128,128]{3,2,1,0:T(8,128)(2,1)S(1)} %add_convert_fusion.4), channel_id=1, source_target_pairs={{16,24},{20,28},{17,25},{21,29},{18,26},{22,30},{19,27},{23,31}} | collective-permute-start | bytes 786440 | tf_op jit(solution)/shard_map/ppermute | solution.py:363
  36.8 7.2 %collective-permute-start.7 = (bf16[4,3,128,128]{3,2,1,0:T(8,128)(2,1)S(1)}, bf16[4,3,128,128]{3,2,1,0:T(8,128)(2,1)S(1)}, u32[]{:S(2)}, u32[]{:S(2)}) collective-permute-start(bf16[4,3,128,128]{3,2,1,0:T(8,128)(2,1)S(1)} %add_convert_fusion.3), channel_id=1, source_target_pairs={{8,16},{12,20},{9,17},{13,21},{10,18},{14,22},{11,19},{15,23}} | collective-permute-start | bytes 1179656 | tf_op jit(solution)/shard_map/ppermute | solution.py:363
  38.2 10.0 %collective-permute-start.6 = (bf16[4,3,128,128]{3,2,1,0:T(8,128)(2,1)S(1)}, bf16[4,3,128,128]{3,2,1,0:T(8,128)(2,1)S(1)}, u32[]{:S(2)}, u32[]{:S(2)}) collective-permute-start(bf16[4,3,128,128]{3,2,1,0:T(8,128)(2,1)S(1)} %fusion.6), channel_id=1, source_target_pairs={{0,8},{4,12},{1,9},{5,13},{2,10},{6,14},{3,11},{7,15}} | collective-permute-start | bytes 1179656 | tf_op jit(solution)/shard_map/ppermute | solution.py:363
  40.9 9.2 %collective-permute-start.11 = (bf16[4,2,128,128]{3,2,1,0:T(8,128)(2,1)S(1)}, bf16[4,2,128,128]{3,2,1,0:T(8,128)(2,1)S(1)}, u32[]{:S(2)}, u32[]{:S(2)}) collective-permute-start(bf16[4,2,128,128]{3,2,1,0:T(8,128)(2,1)S(1)} %get-tuple-element.94), channel_id=1, source_target_pairs={{0,4},{4,0},{8,12},{12,8},{16,20},{20,16},{24,28},{28,24},{1,5},{5... | collective-permute-start | bytes 786440 | tf_op jit(solution)/shard_map/ppermute | solution.py:363
  44.2 14.6 %collective-permute-start.10 = (bf16[4,3,128,128]{3,2,1,0:T(8,128)(2,1)S(1)}, bf16[4,3,128,128]{3,2,1,0:T(8,128)(2,1)S(1)}, u32[]{:S(2)}, u32[]{:S(2)}) collective-permute-start(bf16[4,3,128,128]{3,2,1,0:T(8,128)(2,1)S(1)} %add_convert_fusion.1), channel_id=1, source_target_pairs={{16,24},{20,28},{17,25},{21,29},{18,26},{22,30},{19,27},{23,31}} | collective-permute-start | bytes 1179656 | tf_op jit(solution)/shard_map/ppermute | solution.py:363
  48.4 11.7 %collective-permute-start.9 = (bf16[4,3,128,128]{3,2,1,0:T(8,128)(2,1)S(1)}, bf16[4,3,128,128]{3,2,1,0:T(8,128)(2,1)S(1)}, u32[]{:S(2)}, u32[]{:S(2)}) collective-permute-start(bf16[4,3,128,128]{3,2,1,0:T(8,128)(2,1)S(1)} %add_convert_fusion.2), channel_id=1, source_target_pairs={{8,16},{12,20},{9,17},{13,21},{10,18},{14,22},{11,19},{15,23}} | collective-permute-start | bytes 1179656 | tf_op jit(solution)/shard_map/ppermute | solution.py:363
  60.3 2.8 %collective-permute-start.12 = (bf16[4,3,128,128]{3,2,1,0:T(8,128)(2,1)S(1)}, bf16[4,3,128,128]{3,2,1,0:T(8,128)(2,1)S(1)}, u32[]{:S(2)}, u32[]{:S(2)}) collective-permute-start(bf16[4,3,128,128]{3,2,1,0:T(8,128)(2,1)S(1)} %add_convert_fusion), channel_id=1, source_target_pairs={{16,24},{20,28},{17,25},{21,29},{18,26},{22,30},{19,27},{23,31}} | collective-permute-start | bytes 1179656 | tf_op jit(solution)/shard_map/ppermute | solution.py:363
  60.9 11.8 %collective-permute-start.29 = (bf16[384,256]{1,0:T(8,128)(2,1)S(1)}, bf16[384,256]{1,0:T(8,128)(2,1)S(1)}, u32[]{:S(2)}, u32[]{:S(2)}) collective-permute-start(bf16[384,256]{1,0:T(8,128)(2,1)S(1)} %get-tuple-element.80), channel_id=1, source_target_pairs={{0,4},{4,0},{8,12},{12,8},{16,20},{20,16},{24,28},{28,24},{1,5},{5... | collective-permute-start | bytes 589832 | tf_op jit(solution)/shard_map/ppermute | solution.py:386
  62.5 13.1 %collective-permute-start.30 = (bf16[384,256]{1,0:T(8,128)(2,1)S(1)}, bf16[384,256]{1,0:T(8,128)(2,1)S(1)}, u32[]{:S(2)}, u32[]{:S(2)}) collective-permute-start(bf16[384,256]{1,0:T(8,128)(2,1)S(1)} %get-tuple-element.81), channel_id=1, source_target_pairs={{0,8},{4,12},{8,16},{12,20},{16,24},{20,28},{24,0},{28,4},{1,9},{5... | collective-permute-start | bytes 589832 | tf_op jit(solution)/shard_map/ppermute | solution.py:386
  62.6 22.5 %collective-permute-start.21 = (bf16[4,3,128,128]{3,2,1,0:T(8,128)(2,1)S(1)}, bf16[4,3,128,128]{3,2,1,0:T(8,128)(2,1)S(1)}, u32[]{:S(2)}, u32[]{:S(2)}) collective-permute-start(bf16[4,3,128,128]{3,2,1,0:T(8,128)(2,1)S(1)} %get-tuple-element.61), channel_id=1, source_target_pairs={{0,4},{4,0},{8,12},{12,8},{16,20},{20,16},{24,28},{28,24},{1,5},{5... | collective-permute-start | bytes 1179656 | tf_op jit(solution)/shard_map/ppermute | solution.py:363
  63.4 48.2 %collective-permute-start.13 = (bf16[4,3,128,128]{3,2,1,0:T(8,128)(2,1)S(1)}, bf16[4,3,128,128]{3,2,1,0:T(8,128)(2,1)S(1)}, u32[]{:S(2)}, u32[]{:S(2)}) collective-permute-start(bf16[4,3,128,128]{3,2,1,0:T(8,128)(2,1)S(1)} %get-tuple-element.91), channel_id=1, source_target_pairs={{0,4},{4,0},{8,12},{12,8},{16,20},{20,16},{24,28},{28,24},{1,5},{5... | collective-permute-start | bytes 1179656 | tf_op jit(solution)/shard_map/ppermute | solution.py:363
  65.0 28.4 %collective-permute-start.31 = (bf16[384,256]{1,0:T(8,128)(2,1)S(1)}, bf16[384,256]{1,0:T(8,128)(2,1)S(1)}, u32[]{:S(2)}, u32[]{:S(2)}) collective-permute-start(bf16[384,256]{1,0:T(8,128)(2,1)S(1)} %get-tuple-element.82), channel_id=1, source_target_pairs={{0,12},{4,8},{8,20},{12,16},{16,28},{20,24},{24,4},{28,0},{1,13},{... | collective-permute-start | bytes 589832 | tf_op jit(solution)/shard_map/ppermute | solution.py:386
  72.7 21.2 %collective-permute-start.32 = (bf16[384,256]{1,0:T(8,128)(2,1)S(1)}, bf16[384,256]{1,0:T(8,128)(2,1)S(1)}, u32[]{:S(2)}, u32[]{:S(2)}) collective-permute-start(bf16[384,256]{1,0:T(8,128)(2,1)S(1)} %get-tuple-element.83), channel_id=1, source_target_pairs={{0,16},{4,20},{8,24},{12,28},{16,0},{20,4},{24,8},{28,12},{1,17},{... | collective-permute-start | bytes 589832 | tf_op jit(solution)/shard_map/ppermute | solution.py:386
  75.7 20.3 %collective-permute-start.33 = (bf16[384,256]{1,0:T(8,128)(2,1)S(1)}, bf16[384,256]{1,0:T(8,128)(2,1)S(1)}, u32[]{:S(2)}, u32[]{:S(2)}) collective-permute-start(bf16[384,256]{1,0:T(8,128)(2,1)S(1)} %get-tuple-element.84), channel_id=1, source_target_pairs={{0,20},{4,16},{8,28},{12,24},{16,4},{20,0},{24,12},{28,8},{1,21},{... | collective-permute-start | bytes 589832 | tf_op jit(solution)/shard_map/ppermute | solution.py:386
  85.1 26.5 %collective-permute-start.34 = (bf16[384,256]{1,0:T(8,128)(2,1)S(1)}, bf16[384,256]{1,0:T(8,128)(2,1)S(1)}, u32[]{:S(2)}, u32[]{:S(2)}) collective-permute-start(bf16[384,256]{1,0:T(8,128)(2,1)S(1)} %get-tuple-element.85), channel_id=1, source_target_pairs={{0,24},{4,28},{8,0},{12,4},{16,8},{20,12},{24,16},{28,20},{1,25},{... | collective-permute-start | bytes 589832 | tf_op jit(solution)/shard_map/ppermute | solution.py:386
  93.4 35.4 %collective-permute-start.22 = (bf16[384,384]{1,0:T(8,128)(2,1)S(1)}, bf16[384,384]{1,0:T(8,128)(2,1)S(1)}, u32[]{:S(2)}, u32[]{:S(2)}) collective-permute-start(bf16[384,384]{1,0:T(8,128)(2,1)S(1)} %get-tuple-element.72), channel_id=1, source_target_pairs={{0,4},{4,0},{8,12},{12,8},{16,20},{20,16},{24,28},{28,24},{1,5},{5... | collective-permute-start | bytes 884744 | tf_op jit(solution)/shard_map/ppermute | solution.py:386
  94.0 35.8 %collective-permute-start.23 = (bf16[384,384]{1,0:T(8,128)(2,1)S(1)}, bf16[384,384]{1,0:T(8,128)(2,1)S(1)}, u32[]{:S(2)}, u32[]{:S(2)}) collective-permute-start(bf16[384,384]{1,0:T(8,128)(2,1)S(1)} %get-tuple-element.73), channel_id=1, source_target_pairs={{0,8},{4,12},{8,16},{12,20},{16,24},{20,28},{24,0},{28,4},{1,9},{5... | collective-permute-start | bytes 884744 | tf_op jit(solution)/shard_map/ppermute | solution.py:386
  95.9 38.1 %collective-permute-start.24 = (bf16[384,384]{1,0:T(8,128)(2,1)S(1)}, bf16[384,384]{1,0:T(8,128)(2,1)S(1)}, u32[]{:S(2)}, u32[]{:S(2)}) collective-permute-start(bf16[384,384]{1,0:T(8,128)(2,1)S(1)} %get-tuple-element.74), channel_id=1, source_target_pairs={{0,12},{4,8},{8,20},{12,16},{16,28},{20,24},{24,4},{28,0},{1,13},{... | collective-permute-start | bytes 884744 | tf_op jit(solution)/shard_map/ppermute | solution.py:386
  111.6 24.2 %collective-permute-start.25 = (bf16[384,384]{1,0:T(8,128)(2,1)S(1)}, bf16[384,384]{1,0:T(8,128)(2,1)S(1)}, u32[]{:S(2)}, u32[]{:S(2)}) collective-permute-start(bf16[384,384]{1,0:T(8,128)(2,1)S(1)} %get-tuple-element.75), channel_id=1, source_target_pairs={{0,16},{4,20},{8,24},{12,28},{16,0},{20,4},{24,8},{28,12},{1,17},{... | collective-permute-start | bytes 884744 | tf_op jit(solution)/shard_map/ppermute | solution.py:386
  111.6 17.1 %collective-permute-start.35 = (bf16[384,256]{1,0:T(8,128)(2,1)S(1)}, bf16[384,256]{1,0:T(8,128)(2,1)S(1)}, u32[]{:S(2)}, u32[]{:S(2)}) collective-permute-start(bf16[384,256]{1,0:T(8,128)(2,1)S(1)} %get-tuple-element.60), channel_id=1, source_target_pairs={{0,28},{4,24},{8,4},{12,0},{16,12},{20,8},{24,20},{28,16},{1,29},{... | collective-permute-start | bytes 589832 | tf_op jit(solution)/shard_map/ppermute | solution.py:386
  128.8 18.3 %collective-permute-start.26 = (bf16[384,384]{1,0:T(8,128)(2,1)S(1)}, bf16[384,384]{1,0:T(8,128)(2,1)S(1)}, u32[]{:S(2)}, u32[]{:S(2)}) collective-permute-start(bf16[384,384]{1,0:T(8,128)(2,1)S(1)} %get-tuple-element.76), channel_id=1, source_target_pairs={{0,20},{4,16},{8,28},{12,24},{16,4},{20,0},{24,12},{28,8},{1,21},{... | collective-permute-start | bytes 884744 | tf_op jit(solution)/shard_map/ppermute | solution.py:386
  128.8 33.0 %collective-permute-start.27 = (bf16[384,384]{1,0:T(8,128)(2,1)S(1)}, bf16[384,384]{1,0:T(8,128)(2,1)S(1)}, u32[]{:S(2)}, u32[]{:S(2)}) collective-permute-start(bf16[384,384]{1,0:T(8,128)(2,1)S(1)} %get-tuple-element.77), channel_id=1, source_target_pairs={{0,24},{4,28},{8,0},{12,4},{16,8},{20,12},{24,16},{28,20},{1,25},{... | collective-permute-start | bytes 884744 | tf_op jit(solution)/shard_map/ppermute | solution.py:386
  129.8 44.4 %collective-permute-start.28 = (bf16[384,384]{1,0:T(8,128)(2,1)S(1)}, bf16[384,384]{1,0:T(8,128)(2,1)S(1)}, u32[]{:S(2)}, u32[]{:S(2)}) collective-permute-start(bf16[384,384]{1,0:T(8,128)(2,1)S(1)} %get-tuple-element.78), channel_id=1, source_target_pairs={{0,28},{4,24},{8,4},{12,0},{16,12},{20,8},{24,20},{28,16},{1,29},{... | collective-permute-start | bytes 884744 | tf_op jit(solution)/shard_map/ppermute | solution.py:386
  134.1 40.1 %collective-permute-start.14 = (bf16[384,384]{1,0:T(8,128)(2,1)S(1)}, bf16[384,384]{1,0:T(8,128)(2,1)S(1)}, u32[]{:S(2)}, u32[]{:S(2)}) collective-permute-start(bf16[384,384]{1,0:T(8,128)(2,1)S(1)} %get-tuple-element.64), channel_id=1, source_target_pairs={{0,4},{4,0},{8,12},{12,8},{16,20},{20,16},{24,28},{28,24},{1,5},{5... | collective-permute-start | bytes 884744 | tf_op jit(solution)/shard_map/ppermute | solution.py:386
  135.8 39.3 %collective-permute-start.15 = (bf16[384,384]{1,0:T(8,128)(2,1)S(1)}, bf16[384,384]{1,0:T(8,128)(2,1)S(1)}, u32[]{:S(2)}, u32[]{:S(2)}) collective-permute-start(bf16[384,384]{1,0:T(8,128)(2,1)S(1)} %get-tuple-element.65), channel_id=1, source_target_pairs={{0,8},{4,12},{8,16},{12,20},{16,24},{20,28},{24,0},{28,4},{1,9},{5... | collective-permute-start | bytes 884744 | tf_op jit(solution)/shard_map/ppermute | solution.py:386
  147.1 37.2 %collective-permute-start.16 = (bf16[384,384]{1,0:T(8,128)(2,1)S(1)}, bf16[384,384]{1,0:T(8,128)(2,1)S(1)}, u32[]{:S(2)}, u32[]{:S(2)}) collective-permute-start(bf16[384,384]{1,0:T(8,128)(2,1)S(1)} %get-tuple-element.66), channel_id=1, source_target_pairs={{0,12},{4,8},{8,20},{12,16},{16,28},{20,24},{24,4},{28,0},{1,13},{... | collective-permute-start | bytes 884744 | tf_op jit(solution)/shard_map/ppermute | solution.py:386
  161.8 31.9 %collective-permute-start.17 = (bf16[384,384]{1,0:T(8,128)(2,1)S(1)}, bf16[384,384]{1,0:T(8,128)(2,1)S(1)}, u32[]{:S(2)}, u32[]{:S(2)}) collective-permute-start(bf16[384,384]{1,0:T(8,128)(2,1)S(1)} %get-tuple-element.67), channel_id=1, source_target_pairs={{0,16},{4,20},{8,24},{12,28},{16,0},{20,4},{24,8},{28,12},{1,17},{... | collective-permute-start | bytes 884744 | tf_op jit(solution)/shard_map/ppermute | solution.py:386
  174.1 25.2 %collective-permute-start.18 = (bf16[384,384]{1,0:T(8,128)(2,1)S(1)}, bf16[384,384]{1,0:T(8,128)(2,1)S(1)}, u32[]{:S(2)}, u32[]{:S(2)}) collective-permute-start(bf16[384,384]{1,0:T(8,128)(2,1)S(1)} %get-tuple-element.68), channel_id=1, source_target_pairs={{0,20},{4,16},{8,28},{12,24},{16,4},{20,0},{24,12},{28,8},{1,21},{... | collective-permute-start | bytes 884744 | tf_op jit(solution)/shard_map/ppermute | solution.py:386
  174.1 25.2 %collective-permute-start.19 = (bf16[384,384]{1,0:T(8,128)(2,1)S(1)}, bf16[384,384]{1,0:T(8,128)(2,1)S(1)}, u32[]{:S(2)}, u32[]{:S(2)}) collective-permute-start(bf16[384,384]{1,0:T(8,128)(2,1)S(1)} %get-tuple-element.69), channel_id=1, source_target_pairs={{0,24},{4,28},{8,0},{12,4},{16,8},{20,12},{24,16},{28,20},{1,25},{... | collective-permute-start | bytes 884744 | tf_op jit(solution)/shard_map/ppermute | solution.py:386
  175.2 24.2 %collective-permute-start.20 = (bf16[384,384]{1,0:T(8,128)(2,1)S(1)}, bf16[384,384]{1,0:T(8,128)(2,1)S(1)}, u32[]{:S(2)}, u32[]{:S(2)}) collective-permute-start(bf16[384,384]{1,0:T(8,128)(2,1)S(1)} %get-tuple-element.70), channel_id=1, source_target_pairs={{0,28},{4,24},{8,4},{12,0},{16,12},{20,8},{24,20},{28,16},{1,29},{... | collective-permute-start | bytes 884744 | tf_op jit(solution)/shard_map/ppermute | solution.py:386

commit v5 on v4

--- a/solution.py
+++ b/solution.py
@@ -37,10 +37,15 @@
     return pl.multiple_of(((2 * row + col) * (HEADS // n) + place[2]) * HEAD, HEAD)
 
 
+def rows_together(m, width, most):
+    return max(count for count in range(1, m + 1) if m % count == 0 and (count == 1 or 2 * width * count <= most))
+
+
 def local_body(n, widths, swaps, place, low, keys, values, *refs):
     outs, (kbuf, vbuf, sems) = refs[:-3], refs[-3:]
     total = sum(widths)
     here = place[0], place[1], low[0]
+    together = rows_together(n // 2, total, 16)
 
     def copies(row, side):
         cols = pl.ds(column(here, row, side, n), total * HEAD)
@@ -56,15 +61,16 @@
                 copy.start()
         return carry
 
-    def work(row, carry):
-        for side in range(2):
+    def work(step, carry):
+        slots = [(step * together + index, side) for index in range(together) for side in range(2)]
+        for row, side in slots:
             for copy in copies(row, side):
                 copy.wait()
         places = [
             [(out, head) for out, width in zip(arrays, sizes) for head in range(width)]
             for arrays, sizes in ((outs[: len(widths)], widths), (outs[len(widths) :], swaps))
         ]
-        for side in range(2):
+        for row, side in slots:
             for first in range(0, total, 2):
                 size = min(2, total - first)
                 cols = slice(first * HEAD, (first + size) * HEAD)
@@ -81,7 +87,7 @@
         return carry
 
     lax.fori_loop(0, n // 2, fetch, 0)
-    lax.fori_loop(0, n // 2, work, 0)
+    lax.fori_loop(0, n // 2 // together, work, 0)
 
 
 def local_states(place, keys, values, n, low, widths, swaps):
@@ -128,6 +134,7 @@
     qbuf, kbuf, vbuf, sown, soth, gbuf, held, sems, extra = refs[-9:]
     width = sum(size for _, size in spans)
     m, wide = n // 2, width * HEAD
+    together = rows_together(m, width, 12)
     here = place[0], place[1], low[0]
     small, start = [(gain, gbuf)], 0
     for chunk, (skip, size) in enumerate(spans):
@@ -156,31 +163,41 @@
                 copy.start()
         return carry
 
-    def work(step, carry):
-        for side in range(2):
-            for copy in copies(step, side):
-                copy.wait()
-        row = lax.rem(here[0] + step, m)
-        heads = [(side, head, slice(head * HEAD, (head + 1) * HEAD)) for side in range(2) for head in range(width)]
-        scores = [masked_scores(qbuf[2 * step + side, :, cols], kbuf[2 * step + side, :, cols]) for side, _, cols in heads]
+    def work(group, carry):
+        steps = [group * together + index for index in range(together)]
+        for step in steps:
+            for side in range(2):
+                for copy in copies(step, side):
+                    copy.wait()
+        heads = [
+            (step, side, head, slice(head * HEAD, (head + 1) * HEAD))
+            for step in steps
+            for side in range(2)
+            for head in range(width)
+        ]
+        scores = [
+            masked_scores(qbuf[2 * step + side, :, cols], kbuf[2 * step + side, :, cols])
+            for step, side, _, cols in heads
+        ]
         attended = []
-        for (side, head, cols), tiles in zip(heads, scores):
+        for (step, side, head, cols), tiles in zip(heads, scores):
             slot = 2 * step + side
-            state = (sown if side == 0 else soth)[row, head]
+            state = (sown if side == 0 else soth)[lax.rem(here[0] + step, m), head]
             left = jnp.concatenate([*tiles, qbuf[slot, :, cols]], axis=1)
             right = jnp.concatenate([vbuf[slot, :, cols], state], axis=0)
             attended.append(jnp.dot(left, right, preferred_element_type=jnp.float32))
-        for (side, head, cols), value in zip(heads, attended):
+        for (step, side, head, cols), value in zip(heads, attended):
             square = jnp.mean(value * value, axis=-1, keepdims=True)
-            begin = pl.multiple_of(column(here, row, side, n) + head * HEAD, HEAD)
+            begin = pl.multiple_of(column(here, lax.rem(here[0] + step, m), side, n) + head * HEAD, HEAD)
             mixed = value * lax.rsqrt(square + 1e-05) * gbuf[:, pl.ds(begin, HEAD)]
             held[2 * step + side, :, cols] = mixed.astype(held.dtype)
-        for fixed in range(m):
-
-            @pl.when(step == fixed)
+        for fixed in range(m // together):
+
+            @pl.when(group == fixed)
             def _(fixed=fixed):
-                for copy in sends(fixed):
-                    copy.start()
+                for index in range(together):
+                    for copy in sends(fixed * together + index):
+                        copy.start()
 
         return carry
 
@@ -190,7 +207,7 @@
     lax.fori_loop(1, m, fetch, 0)
     for copy in small:
         copy.wait()
-    lax.fori_loop(0, m, work, 0)
+    lax.fori_loop(0, m // together, work, 0)
     for step in range(m):
         for copy in sends(step):
             copy.wait()

time: 203 us -> 203 us (level)
  transfers between devices with their start and end apart: 36 -> 36, of which waited for: 13 -> 14; matrix products, arithmetic and copies ran while one was open for 4% -> 4% of each run, Pallas kernels for 17% -> 18%
where the time goes in v5:
time: 203 us; the launch traced here: 202 us
  waiting for transfers between devices  102 us (50%)
  starting transfers between devices  50.6 us (25%)
  Pallas kernels  41.3 us (20%)
  other arithmetic  7.65 us (4%)
    ppermute x21, waiting for transfers between devices, sent(): lax.ppermute(self.hold(self.get('mixed', c)[k], 'sent', c, k), 'seq', pairs)  75.3 us
    ppermute x21, starting transfers between devices, sent(): lax.ppermute(self.hold(self.get('mixed', c)[k], 'sent', c, k), 'seq', pairs)  31.1 us
    pallas_call x3, Pallas kernels, attend(): pl.pallas_call(functools.partial(attend_body, n, spans), in_specs=[pl.Blo...  25.5 us
    ppermute x12, waiting for transfers between devices, prefix(): return lax.ppermute(self.get('message', c, s), 'seq', pairs)  25.1 us
    ppermute x12, starting transfers between devices, prefix(): return lax.ppermute(self.get('message', c, s), 'seq', pairs)  14.7 us
    pallas_call x2, Pallas kernels, local_states(): pl.pallas_call(functools.partial(local_body, n, widths, swaps), in_specs=...  8.47 us
    pallas_call x3, Pallas kernels, put(): pl.pallas_call(functools.partial(put_body, n), in_specs=[pl.BlockSpec(mem...  7.33 us
    convert_element_type x10, other arithmetic, message(): return self.hold(value.astype(jnp.bfloat16), 'message', c, s)  4.88 us
  transfers between devices with their start and end apart: 36, of which 14 were waited for; matrix products, arithmetic and copies ran while one was open for 4% of the time, Pallas kernels for 18%

profile of v5, /device:TPU:8, one launch (start us, length us, event | category | flops | bytes accessed | tf_op | source)
XLA Modules:
  0.0 201.7 jit_solution(13346312694118558019)
XLA Ops:
  0.1 3.4 %local.3 = (f32[4,2,128,128]{3,2,1,0:T(8,128)S(1)}, bf16[4,2,128,128]{3,2,1,0:T(8,128)(2,1)S(1)}) custom-call(s32[2]{0:T(128)S(1)} %pad_add_fusion.place, s32[1]{0:T(128)} %constant.38.clone.1.low, bf16[384,8192]{1,0:T(8,128)(2,1)} %keys.9, bf16[384,8192]{1,0:T(8,128)(2,1)} %values.9), custom_call_target="tpu_custom_call" | custom-call | flops 201326592 | bytes 3145728 | tf_op jit(solution)/shard_map/local/pallas_call | solution.py:98
  3.5 1.6 collective-permute-start.2
  5.1 5.0 %local.2 = (f32[4,3,128,128]{3,2,1,0:T(8,128)S(1)}, f32[4,3,128,128]{3,2,1,0:T(8,128)S(1)}, bf16[4,3,128,128]{3,2,1,0:T(8,128)(2,1)S(1)}, bf16[4,3,128,128]{3,2,1,0:T(8,128)(2,1)S(1)}) custom-call(s32[2]{0:T(128)S(1)} %pad_add_fusion.place, s32[1]{0:T(128)} %constant.37.clone.1.low, bf16[384,8192]{1,0:T(8,128)(2,1)} %keys.9, bf16[384,8192]{1,0:T(8,128)(2,1)} %values.9), custom_call_target="tpu_custom_call" | custom-call | flops 603979776 | bytes 9437184 | tf_op jit(solution)/shard_map/local/pallas_call | solution.py:98
  10.1 1.5 collective-permute-done.2
  11.7 1.3 collective-permute-start.3
  13.0 1.6 collective-permute-start.1
  14.6 6.2 %collective-permute-done.3 = bf16[4,2,128,128]{3,2,1,0:T(8,128)(2,1)S(1)} collective-permute-done((bf16[4,2,128,128]{3,2,1,0:T(8,128)(2,1)S(1)}, bf16[4,2,128,128]{3,2,1,0:T(8,128)(2,1)S(1)}, u32[]{:S(2)}, u32[]{:S(2)}) %collective-permute-start.3) | collective-permute-done | bytes 262176 | tf_op jit(solution)/shard_map/ppermute | solution.py:380
  21.5 2.1 %collective-permute-start.5 = (bf16[4,2,128,128]{3,2,1,0:T(8,128)(2,1)}, bf16[4,2,128,128]{3,2,1,0:T(8,128)(2,1)}, u32[]{:S(2)}, u32[]{:S(2)}) collective-permute-start(bf16[4,2,128,128]{3,2,1,0:T(8,128)(2,1)} %add_convert_fusion.5), channel_id=1, source_target_pairs={{8,16},{12,20},{9,17},{13,21},{10,18},{14,22},{11,19},{15,23}} | collective-permute-start | bytes 786440 | tf_op jit(solution)/shard_map/ppermute | solution.py:380
  23.7 0.8 fusion.7
  24.5 1.3 collective-permute-start.4
  25.8 1.6 collective-permute-start
  27.4 1.1 add_convert_fusion.4
  29.2 6.5 %collective-permute-done.4 = bf16[4,3,128,128]{3,2,1,0:T(8,128)(2,1)} collective-permute-done((bf16[4,3,128,128]{3,2,1,0:T(8,128)(2,1)}, bf16[4,3,128,128]{3,2,1,0:T(8,128)(2,1)}, u32[]{:S(2)}, u32[]{:S(2)}) %collective-permute-start.4) | collective-permute-done | bytes 393248 | tf_op jit(solution)/shard_map/ppermute | solution.py:380
  35.8 1.2 add_convert_fusion.3
  36.9 1.3 collective-permute-start.7
  38.4 1.3 collective-permute-start.6
  39.7 1.4 fusion.5
  41.0 1.6 collective-permute-start.11
  42.6 1.5 collective-permute-done.7
  45.0 3.4 %collective-permute-done.6 = bf16[4,3,128,128]{3,2,1,0:T(8,128)(2,1)S(1)} collective-permute-done((bf16[4,3,128,128]{3,2,1,0:T(8,128)(2,1)S(1)}, bf16[4,3,128,128]{3,2,1,0:T(8,128)(2,1)S(1)}, u32[]{:S(2)}, u32[]{:S(2)}) %collective-permute-start.6) | collective-permute-done | bytes 393248 | tf_op jit(solution)/shard_map/ppermute | solution.py:380
  48.5 1.6 collective-permute-start.9
  50.2 8.5 %attend.3 = (bf16[384,256]{1,0:T(8,128)(2,1)S(1)}, bf16[384,256]{1,0:T(8,128)(2,1)S(1)}, bf16[384,256]{1,0:T(8,128)(2,1)S(1)}, bf16[384,256]{1,0:T(8,128)(2,1)S(...) custom-call(s32[2]{0:T(128)S(1)} %pad_add_fusion.place, ...), custom_call_target="tpu_custom_call" | custom-call | flops 1409286144 | bytes 6291456 | tf_op jit(solution)/shard_map/attend/pallas_call | solution.py:222
  58.8 1.3 fusion.1
  61.0 1.6 collective-permute-start.29
  63.4 1.6 collective-permute-start.13
  65.0 7.9 %collective-permute-start.31 = (bf16[384,256]{1,0:T(8,128)(2,1)S(1)}, bf16[384,256]{1,0:T(8,128)(2,1)S(1)}, u32[]{:S(2)}, u32[]{:S(2)}) collective-permute-start(bf16[384,256]{1,0:T(8,128)(2,1)S(1)} %get-tuple-element.82), channel_id=1, source_target_pairs={{0,12},{4,8},{8,20},{12,16},{16,28},{20,24},{24,4},{28,0},{1,13},{... | collective-permute-start | bytes 589832 | tf_op jit(solution)/shard_map/ppermute | solution.py:403
  72.9 2.9 %collective-permute-start.32 = (bf16[384,256]{1,0:T(8,128)(2,1)S(1)}, bf16[384,256]{1,0:T(8,128)(2,1)S(1)}, u32[]{:S(2)}, u32[]{:S(2)}) collective-permute-start(bf16[384,256]{1,0:T(8,128)(2,1)S(1)} %get-tuple-element.83), channel_id=1, source_target_pairs={{0,16},{4,20},{8,24},{12,28},{16,0},{20,4},{24,8},{28,12},{1,17},{... | collective-permute-start | bytes 589832 | tf_op jit(solution)/shard_map/ppermute | solution.py:403
  75.8 1.9 collective-permute-start.33
  77.7 7.4 %collective-permute-done.21.refs_1_ = bf16[4,3,128,128]{3,2,1,0:T(8,128)(2,1)S(1)} collective-permute-done((bf16[4,3,128,128]{3,2,1,0:T(8,128)(2,1)S(1)}, bf16[4,3,128,128]{3,2,1,0:T(8,128)(2,1)S(1)}, u32[]{:S(2)}, u32[]{:S(2)}) %collective-permute-start.21) | collective-permute-done | bytes 393248 | tf_op jit(solution)/shard_map/ppermute | solution.py:380
  85.1 8.4 %attend.5 = (bf16[384,384]{1,0:T(8,128)(2,1)S(1)}, bf16[384,384]{1,0:T(8,128)(2,1)S(1)}, bf16[384,384]{1,0:T(8,128)(2,1)S(1)}, bf16[384,384]{1,0:T(8,128)(2,1)S(...) custom-call(s32[2]{0:T(128)S(1)} %pad_add_fusion.place, ...), custom_call_target="tpu_custom_call" | custom-call | flops 2113929216 | bytes 9437184 | tf_op jit(solution)/shard_map/attend/pallas_call | solution.py:222
  94.1 2.0 collective-permute-start.23
  96.1 1.1 collective-permute-start.24
  97.2 14.5 %collective-permute-done.34.refs_6_ = bf16[384,256]{1,0:T(8,128)(2,1)S(1)} collective-permute-done((bf16[384,256]{1,0:T(8,128)(2,1)S(1)}, bf16[384,256]{1,0:T(8,128)(2,1)S(1)}, u32[]{:S(2)}, u32[]{:S(2)}) %collective-permute-start.34) | collective-permute-done | bytes 196640 | tf_op jit(solution)/shard_map/ppermute | solution.py:403
  112.3 8.5 %attend.4 = (bf16[384,384]{1,0:T(8,128)(2,1)S(1)}, bf16[384,384]{1,0:T(8,128)(2,1)S(1)}, bf16[384,384]{1,0:T(8,128)(2,1)S(1)}, bf16[384,384]{1,0:T(8,128)(2,1)S(...) custom-call(s32[2]{0:T(128)S(1)} %pad_add_fusion.place, ...), custom_call_target="tpu_custom_call" | custom-call | flops 2113929216 | bytes 9437184 | tf_op jit(solution)/shard_map/attend/pallas_call | solution.py:222
  120.8 7.9 %collective-permute-done.35.refs_7_ = bf16[384,256]{1,0:T(8,128)(2,1)S(1)} collective-permute-done((bf16[384,256]{1,0:T(8,128)(2,1)S(1)}, bf16[384,256]{1,0:T(8,128)(2,1)S(1)}, u32[]{:S(2)}, u32[]{:S(2)}) %collective-permute-start.35) | collective-permute-done | bytes 196640 | tf_op jit(solution)/shard_map/ppermute | solution.py:403
  128.7 1.0 collective-permute-start.27
  129.7 4.3 %collective-permute-start.28 = (bf16[384,384]{1,0:T(8,128)(2,1)S(1)}, bf16[384,384]{1,0:T(8,128)(2,1)S(1)}, u32[]{:S(2)}, u32[]{:S(2)}) collective-permute-start(bf16[384,384]{1,0:T(8,128)(2,1)S(1)} %get-tuple-element.78), channel_id=1, source_target_pairs={{0,28},{4,24},{8,4},{12,0},{16,12},{20,8},{24,20},{28,16},{1,29},{... | collective-permute-start | bytes 884744 | tf_op jit(solution)/shard_map/ppermute | solution.py:403
  134.0 2.1 %collective-permute-start.14 = (bf16[384,384]{1,0:T(8,128)(2,1)S(1)}, bf16[384,384]{1,0:T(8,128)(2,1)S(1)}, u32[]{:S(2)}, u32[]{:S(2)}) collective-permute-start(bf16[384,384]{1,0:T(8,128)(2,1)S(1)} %get-tuple-element.64), channel_id=1, source_target_pairs={{0,4},{4,0},{8,12},{12,8},{16,20},{20,16},{24,28},{28,24},{1,5},{5... | collective-permute-start | bytes 884744 | tf_op jit(solution)/shard_map/ppermute | solution.py:403
  136.1 11.2 %collective-permute-done.26.refs_5_ = bf16[384,384]{1,0:T(8,128)(2,1)S(1)} collective-permute-done((bf16[384,384]{1,0:T(8,128)(2,1)S(1)}, bf16[384,384]{1,0:T(8,128)(2,1)S(1)}, u32[]{:S(2)}, u32[]{:S(2)}) %collective-permute-start.26) | collective-permute-done | bytes 294944 | tf_op jit(solution)/shard_map/ppermute | solution.py:403
  147.3 14.8 %collective-permute-done.27.refs_6_ = bf16[384,384]{1,0:T(8,128)(2,1)S(1)} collective-permute-done((bf16[384,384]{1,0:T(8,128)(2,1)S(1)}, bf16[384,384]{1,0:T(8,128)(2,1)S(1)}, u32[]{:S(2)}, u32[]{:S(2)}) %collective-permute-start.27) | collective-permute-done | bytes 294944 | tf_op jit(solution)/shard_map/ppermute | solution.py:403
  162.1 12.0 %collective-permute-done.28.refs_7_ = bf16[384,384]{1,0:T(8,128)(2,1)S(1)} collective-permute-done((bf16[384,384]{1,0:T(8,128)(2,1)S(1)}, bf16[384,384]{1,0:T(8,128)(2,1)S(1)}, u32[]{:S(2)}, u32[]{:S(2)}) %collective-permute-start.28) | collective-permute-done | bytes 294944 | tf_op jit(solution)/shard_map/ppermute | solution.py:403
  174.1 1.0 collective-permute-start.19
  175.1 4.3 %collective-permute-start.20 = (bf16[384,384]{1,0:T(8,128)(2,1)S(1)}, bf16[384,384]{1,0:T(8,128)(2,1)S(1)}, u32[]{:S(2)}, u32[]{:S(2)}) collective-permute-start(bf16[384,384]{1,0:T(8,128)(2,1)S(1)} %get-tuple-element.70), channel_id=1, source_target_pairs={{0,28},{4,24},{8,4},{12,0},{16,12},{20,8},{24,20},{28,16},{1,29},{... | collective-permute-start | bytes 884744 | tf_op jit(solution)/shard_map/ppermute | solution.py:403
  179.4 2.3 %put.3 = (bf16[3072,1024]{1,0:T(8,128)(2,1)}, s32[2]{0:T(128)}) custom-call(s32[2]{0:T(128)S(1)} %pad_add_fusion.place, s32[1]{0:T(128)} %constant.38.clone.1.low, bf16[384,256]{1,0:T(8,128)(2,1)S(1)} %get-tuple-element.79.refs_0_, bf16[384,256]{1,0:T(8,128)(2,1)S(1)} %collective-permute-done.29.refs_1_, ...), custom_call_target="tpu_custom_call" | custom-call | tf_op jit(solution)/shard_map/put/pallas_call | solution.py:274
  181.7 2.5 %put.4 = (bf16[3072,1024]{1,0:T(8,128)(2,1)}, s32[2]{0:T(128)}) custom-call(s32[2]{0:T(128)S(1)} %pad_add_fusion.place, s32[1]{0:T(128)} %constant.37.clone.1.low, bf16[384,384]{1,0:T(8,128)(2,1)S(1)} %get-tuple-element.71.refs_0_, bf16[384,384]{1,0:T(8,128)(2,1)S(1)} %collective-permute-done.22.refs_1_, ...), custom_call_target="tpu_custom_call", output_to_operand_aliasing={{0}: (10, {})} | custom-call | tf_op jit(solution)/shard_map/put/pallas_call | solution.py:274
  184.2 8.9 %collective-permute-done.17.refs_4_ = bf16[384,384]{1,0:T(8,128)(2,1)S(1)} collective-permute-done((bf16[384,384]{1,0:T(8,128)(2,1)S(1)}, bf16[384,384]{1,0:T(8,128)(2,1)S(1)}, u32[]{:S(2)}, u32[]{:S(2)}) %collective-permute-start.17) | collective-permute-done | bytes 294944 | tf_op jit(solution)/shard_map/ppermute | solution.py:403
  193.1 5.6 %collective-permute-done.18.refs_5_ = bf16[384,384]{1,0:T(8,128)(2,1)S(1)} collective-permute-done((bf16[384,384]{1,0:T(8,128)(2,1)S(1)}, bf16[384,384]{1,0:T(8,128)(2,1)S(1)}, u32[]{:S(2)}, u32[]{:S(2)}) %collective-permute-start.18) | collective-permute-done | bytes 294944 | tf_op jit(solution)/shard_map/ppermute | solution.py:403
  199.1 2.5 %put.5 = (bf16[3072,1024]{1,0:T(8,128)(2,1)}, s32[2]{0:T(128)}) custom-call(s32[2]{0:T(128)S(1)} %pad_add_fusion.place, s32[1]{0:T(128)} %constant.36.clone.1.low, bf16[384,384]{1,0:T(8,128)(2,1)S(1)} %get-tuple-element.63.refs_0_, bf16[384,384]{1,0:T(8,128)(2,1)S(1)} %collective-permute-done.14.refs_1_, ...), custom_call_target="tpu_custom_call", output_to_operand_aliasing={{0}: (10, {})} | custom-call | tf_op jit(solution)/shard_map/put/pallas_call | solution.py:274
  (51 shorter events, 5.8 us)
Async XLA Ops:
  3.5 8.1 %collective-permute-start.2 = (bf16[4,2,128,128]{3,2,1,0:T(8,128)(2,1)S(1)}, bf16[4,2,128,128]{3,2,1,0:T(8,128)(2,1)S(1)}, u32[]{:S(2)}, u32[]{:S(2)}) collective-permute-start(bf16[4,2,128,128]{3,2,1,0:T(8,128)(2,1)S(1)} %get-tuple-element.52), channel_id=1, source_target_pairs={{0,4},{4,0},{8,12},{12,8},{16,20},{20,16},{24,28},{28,24},{1,5},{5... | collective-permute-start | bytes 786440 | tf_op jit(solution)/shard_map/ppermute | solution.py:353
  11.6 12.9 %copy-start.1 = (bf16[4,2,128,128]{3,2,1,0:T(8,128)(2,1)}, bf16[4,2,128,128]{3,2,1,0:T(8,128)(2,1)S(1)}, u32[]{:S(2)}) copy-start(bf16[4,2,128,128]{3,2,1,0:T(8,128)(2,1)S(1)} %collective-permute-done.2) | copy-start | bytes 786436
  11.7 9.1 %collective-permute-start.3 = (bf16[4,2,128,128]{3,2,1,0:T(8,128)(2,1)S(1)}, bf16[4,2,128,128]{3,2,1,0:T(8,128)(2,1)S(1)}, u32[]{:S(2)}, u32[]{:S(2)}) collective-permute-start(bf16[4,2,128,128]{3,2,1,0:T(8,128)(2,1)S(1)} %fusion.8), channel_id=1, source_target_pairs={{0,8},{4,12},{1,9},{5,13},{2,10},{6,14},{3,11},{7,15}} | collective-permute-start | bytes 786440 | tf_op jit(solution)/shard_map/ppermute | solution.py:380
  13.0 10.7 %collective-permute-start.1 = (bf16[4,3,128,128]{3,2,1,0:T(8,128)(2,1)S(1)}, bf16[4,3,128,128]{3,2,1,0:T(8,128)(2,1)S(1)}, u32[]{:S(2)}, u32[]{:S(2)}) collective-permute-start(bf16[4,3,128,128]{3,2,1,0:T(8,128)(2,1)S(1)} %get-tuple-element.50), channel_id=1, source_target_pairs={{0,4},{4,0},{8,12},{12,8},{16,20},{20,16},{24,28},{28,24},{1,5},{5... | collective-permute-start | bytes 1179656 | tf_op jit(solution)/shard_map/ppermute | solution.py:353
  20.7 2.9 %copy-start.2 = (bf16[4,2,128,128]{3,2,1,0:T(8,128)(2,1)}, bf16[4,2,128,128]{3,2,1,0:T(8,128)(2,1)S(1)}, u32[]{:S(2)}) copy-start(bf16[4,2,128,128]{3,2,1,0:T(8,128)(2,1)S(1)} %collective-permute-done.3) | copy-start | bytes 786436
  21.5 28.7 %copy-start = (f32[8192]{0:T(1024)S(1)}, f32[8192]{0:T(1024)}, u32[]{:S(2)}) copy-start(f32[8192]{0:T(1024)} %param.7) | copy-start | bytes 98308
  21.5 5.9 %collective-permute-start.5 = (bf16[4,2,128,128]{3,2,1,0:T(8,128)(2,1)}, bf16[4,2,128,128]{3,2,1,0:T(8,128)(2,1)}, u32[]{:S(2)}, u32[]{:S(2)}) collective-permute-start(bf16[4,2,128,128]{3,2,1,0:T(8,128)(2,1)} %add_convert_fusion.5), channel_id=1, source_target_pairs={{8,16},{12,20},{9,17},{13,21},{10,18},{14,22},{11,19},{15,23}} | collective-permute-start | bytes 786440 | tf_op jit(solution)/shard_map/ppermute | solution.py:380
  24.5 11.2 %collective-permute-start.4 = (bf16[4,3,128,128]{3,2,1,0:T(8,128)(2,1)}, bf16[4,3,128,128]{3,2,1,0:T(8,128)(2,1)}, u32[]{:S(2)}, u32[]{:S(2)}) collective-permute-start(bf16[4,3,128,128]{3,2,1,0:T(8,128)(2,1)} %fusion.7), channel_id=1, source_target_pairs={{0,8},{4,12},{1,9},{5,13},{2,10},{6,14},{3,11},{7,15}} | collective-permute-start | bytes 1179656 | tf_op jit(solution)/shard_map/ppermute | solution.py:380
  25.8 12.5 %collective-permute-start = (bf16[4,3,128,128]{3,2,1,0:T(8,128)(2,1)S(1)}, bf16[4,3,128,128]{3,2,1,0:T(8,128)(2,1)S(1)}, u32[]{:S(2)}, u32[]{:S(2)}) collective-permute-start(bf16[4,3,128,128]{3,2,1,0:T(8,128)(2,1)S(1)} %get-tuple-element.48), channel_id=1, source_target_pairs={{0,4},{4,0},{8,12},{12,8},{16,20},{20,16},{24,28},{28,24},{1,5},{5... | collective-permute-start | bytes 1179656 | tf_op jit(solution)/shard_map/ppermute | solution.py:353
  28.5 11.1 %collective-permute-start.8 = (bf16[4,2,128,128]{3,2,1,0:T(8,128)(2,1)S(1)}, bf16[4,2,128,128]{3,2,1,0:T(8,128)(2,1)S(1)}, u32[]{:S(2)}, u32[]{:S(2)}) collective-permute-start(bf16[4,2,128,128]{3,2,1,0:T(8,128)(2,1)S(1)} %add_convert_fusion.4), channel_id=1, source_target_pairs={{16,24},{20,28},{17,25},{21,29},{18,26},{22,30},{19,27},{23,31}} | collective-permute-start | bytes 786440 | tf_op jit(solution)/shard_map/ppermute | solution.py:380
  36.9 7.2 %collective-permute-start.7 = (bf16[4,3,128,128]{3,2,1,0:T(8,128)(2,1)S(1)}, bf16[4,3,128,128]{3,2,1,0:T(8,128)(2,1)S(1)}, u32[]{:S(2)}, u32[]{:S(2)}) collective-permute-start(bf16[4,3,128,128]{3,2,1,0:T(8,128)(2,1)S(1)} %add_convert_fusion.3), channel_id=1, source_target_pairs={{8,16},{12,20},{9,17},{13,21},{10,18},{14,22},{11,19},{15,23}} | collective-permute-start | bytes 1179656 | tf_op jit(solution)/shard_map/ppermute | solution.py:380
  38.4 10.0 %collective-permute-start.6 = (bf16[4,3,128,128]{3,2,1,0:T(8,128)(2,1)S(1)}, bf16[4,3,128,128]{3,2,1,0:T(8,128)(2,1)S(1)}, u32[]{:S(2)}, u32[]{:S(2)}) collective-permute-start(bf16[4,3,128,128]{3,2,1,0:T(8,128)(2,1)S(1)} %fusion.6), channel_id=1, source_target_pairs={{0,8},{4,12},{1,9},{5,13},{2,10},{6,14},{3,11},{7,15}} | collective-permute-start | bytes 1179656 | tf_op jit(solution)/shard_map/ppermute | solution.py:380
  41.0 9.2 %collective-permute-start.11 = (bf16[4,2,128,128]{3,2,1,0:T(8,128)(2,1)S(1)}, bf16[4,2,128,128]{3,2,1,0:T(8,128)(2,1)S(1)}, u32[]{:S(2)}, u32[]{:S(2)}) collective-permute-start(bf16[4,2,128,128]{3,2,1,0:T(8,128)(2,1)S(1)} %get-tuple-element.94), channel_id=1, source_target_pairs={{0,4},{4,0},{8,12},{12,8},{16,20},{20,16},{24,28},{28,24},{1,5},{5... | collective-permute-start | bytes 786440 | tf_op jit(solution)/shard_map/ppermute | solution.py:380
  44.3 14.5 %collective-permute-start.10 = (bf16[4,3,128,128]{3,2,1,0:T(8,128)(2,1)S(1)}, bf16[4,3,128,128]{3,2,1,0:T(8,128)(2,1)S(1)}, u32[]{:S(2)}, u32[]{:S(2)}) collective-permute-start(bf16[4,3,128,128]{3,2,1,0:T(8,128)(2,1)S(1)} %add_convert_fusion.1), channel_id=1, source_target_pairs={{16,24},{20,28},{17,25},{21,29},{18,26},{22,30},{19,27},{23,31}} | collective-permute-start | bytes 1179656 | tf_op jit(solution)/shard_map/ppermute | solution.py:380
  48.5 11.6 %collective-permute-start.9 = (bf16[4,3,128,128]{3,2,1,0:T(8,128)(2,1)S(1)}, bf16[4,3,128,128]{3,2,1,0:T(8,128)(2,1)S(1)}, u32[]{:S(2)}, u32[]{:S(2)}) collective-permute-start(bf16[4,3,128,128]{3,2,1,0:T(8,128)(2,1)S(1)} %add_convert_fusion.2), channel_id=1, source_target_pairs={{8,16},{12,20},{9,17},{13,21},{10,18},{14,22},{11,19},{15,23}} | collective-permute-start | bytes 1179656 | tf_op jit(solution)/shard_map/ppermute | solution.py:380
  60.3 2.8 %collective-permute-start.12 = (bf16[4,3,128,128]{3,2,1,0:T(8,128)(2,1)S(1)}, bf16[4,3,128,128]{3,2,1,0:T(8,128)(2,1)S(1)}, u32[]{:S(2)}, u32[]{:S(2)}) collective-permute-start(bf16[4,3,128,128]{3,2,1,0:T(8,128)(2,1)S(1)} %add_convert_fusion), channel_id=1, source_target_pairs={{16,24},{20,28},{17,25},{21,29},{18,26},{22,30},{19,27},{23,31}} | collective-permute-start | bytes 1179656 | tf_op jit(solution)/shard_map/ppermute | solution.py:380
  61.0 11.9 %collective-permute-start.29 = (bf16[384,256]{1,0:T(8,128)(2,1)S(1)}, bf16[384,256]{1,0:T(8,128)(2,1)S(1)}, u32[]{:S(2)}, u32[]{:S(2)}) collective-permute-start(bf16[384,256]{1,0:T(8,128)(2,1)S(1)} %get-tuple-element.80), channel_id=1, source_target_pairs={{0,4},{4,0},{8,12},{12,8},{16,20},{20,16},{24,28},{28,24},{1,5},{5... | collective-permute-start | bytes 589832 | tf_op jit(solution)/shard_map/ppermute | solution.py:403
  62.6 13.2 %collective-permute-start.30 = (bf16[384,256]{1,0:T(8,128)(2,1)S(1)}, bf16[384,256]{1,0:T(8,128)(2,1)S(1)}, u32[]{:S(2)}, u32[]{:S(2)}) collective-permute-start(bf16[384,256]{1,0:T(8,128)(2,1)S(1)} %get-tuple-element.81), channel_id=1, source_target_pairs={{0,8},{4,12},{8,16},{12,20},{16,24},{20,28},{24,0},{28,4},{1,9},{5... | collective-permute-start | bytes 589832 | tf_op jit(solution)/shard_map/ppermute | solution.py:403
  62.6 22.6 %collective-permute-start.21 = (bf16[4,3,128,128]{3,2,1,0:T(8,128)(2,1)S(1)}, bf16[4,3,128,128]{3,2,1,0:T(8,128)(2,1)S(1)}, u32[]{:S(2)}, u32[]{:S(2)}) collective-permute-start(bf16[4,3,128,128]{3,2,1,0:T(8,128)(2,1)S(1)} %get-tuple-element.61), channel_id=1, source_target_pairs={{0,4},{4,0},{8,12},{12,8},{16,20},{20,16},{24,28},{28,24},{1,5},{5... | collective-permute-start | bytes 1179656 | tf_op jit(solution)/shard_map/ppermute | solution.py:380
  63.4 48.3 %collective-permute-start.13 = (bf16[4,3,128,128]{3,2,1,0:T(8,128)(2,1)S(1)}, bf16[4,3,128,128]{3,2,1,0:T(8,128)(2,1)S(1)}, u32[]{:S(2)}, u32[]{:S(2)}) collective-permute-start(bf16[4,3,128,128]{3,2,1,0:T(8,128)(2,1)S(1)} %get-tuple-element.91), channel_id=1, source_target_pairs={{0,4},{4,0},{8,12},{12,8},{16,20},{20,16},{24,28},{28,24},{1,5},{5... | collective-permute-start | bytes 1179656 | tf_op jit(solution)/shard_map/ppermute | solution.py:380
  65.0 28.6 %collective-permute-start.31 = (bf16[384,256]{1,0:T(8,128)(2,1)S(1)}, bf16[384,256]{1,0:T(8,128)(2,1)S(1)}, u32[]{:S(2)}, u32[]{:S(2)}) collective-permute-start(bf16[384,256]{1,0:T(8,128)(2,1)S(1)} %get-tuple-element.82), channel_id=1, source_target_pairs={{0,12},{4,8},{8,20},{12,16},{16,28},{20,24},{24,4},{28,0},{1,13},{... | collective-permute-start | bytes 589832 | tf_op jit(solution)/shard_map/ppermute | solution.py:403
  72.9 21.2 %collective-permute-start.32 = (bf16[384,256]{1,0:T(8,128)(2,1)S(1)}, bf16[384,256]{1,0:T(8,128)(2,1)S(1)}, u32[]{:S(2)}, u32[]{:S(2)}) collective-permute-start(bf16[384,256]{1,0:T(8,128)(2,1)S(1)} %get-tuple-element.83), channel_id=1, source_target_pairs={{0,16},{4,20},{8,24},{12,28},{16,0},{20,4},{24,8},{28,12},{1,17},{... | collective-permute-start | bytes 589832 | tf_op jit(solution)/shard_map/ppermute | solution.py:403
  75.8 20.3 %collective-permute-start.33 = (bf16[384,256]{1,0:T(8,128)(2,1)S(1)}, bf16[384,256]{1,0:T(8,128)(2,1)S(1)}, u32[]{:S(2)}, u32[]{:S(2)}) collective-permute-start(bf16[384,256]{1,0:T(8,128)(2,1)S(1)} %get-tuple-element.84), channel_id=1, source_target_pairs={{0,20},{4,16},{8,28},{12,24},{16,4},{20,0},{24,12},{28,8},{1,21},{... | collective-permute-start | bytes 589832 | tf_op jit(solution)/shard_map/ppermute | solution.py:403
  85.1 26.6 %collective-permute-start.34 = (bf16[384,256]{1,0:T(8,128)(2,1)S(1)}, bf16[384,256]{1,0:T(8,128)(2,1)S(1)}, u32[]{:S(2)}, u32[]{:S(2)}) collective-permute-start(bf16[384,256]{1,0:T(8,128)(2,1)S(1)} %get-tuple-element.85), channel_id=1, source_target_pairs={{0,24},{4,28},{8,0},{12,4},{16,8},{20,12},{24,16},{28,20},{1,25},{... | collective-permute-start | bytes 589832 | tf_op jit(solution)/shard_map/ppermute | solution.py:403
  93.6 35.2 %collective-permute-start.22 = (bf16[384,384]{1,0:T(8,128)(2,1)S(1)}, bf16[384,384]{1,0:T(8,128)(2,1)S(1)}, u32[]{:S(2)}, u32[]{:S(2)}) collective-permute-start(bf16[384,384]{1,0:T(8,128)(2,1)S(1)} %get-tuple-element.72), channel_id=1, source_target_pairs={{0,4},{4,0},{8,12},{12,8},{16,20},{20,16},{24,28},{28,24},{1,5},{5... | collective-permute-start | bytes 884744 | tf_op jit(solution)/shard_map/ppermute | solution.py:403
  94.1 35.6 %collective-permute-start.23 = (bf16[384,384]{1,0:T(8,128)(2,1)S(1)}, bf16[384,384]{1,0:T(8,128)(2,1)S(1)}, u32[]{:S(2)}, u32[]{:S(2)}) collective-permute-start(bf16[384,384]{1,0:T(8,128)(2,1)S(1)} %get-tuple-element.73), channel_id=1, source_target_pairs={{0,8},{4,12},{8,16},{12,20},{16,24},{20,28},{24,0},{28,4},{1,9},{5... | collective-permute-start | bytes 884744 | tf_op jit(solution)/shard_map/ppermute | solution.py:403
  96.1 37.9 %collective-permute-start.24 = (bf16[384,384]{1,0:T(8,128)(2,1)S(1)}, bf16[384,384]{1,0:T(8,128)(2,1)S(1)}, u32[]{:S(2)}, u32[]{:S(2)}) collective-permute-start(bf16[384,384]{1,0:T(8,128)(2,1)S(1)} %get-tuple-element.74), channel_id=1, source_target_pairs={{0,12},{4,8},{8,20},{12,16},{16,28},{20,24},{24,4},{28,0},{1,13},{... | collective-permute-start | bytes 884744 | tf_op jit(solution)/shard_map/ppermute | solution.py:403
  111.7 24.3 %collective-permute-start.25 = (bf16[384,384]{1,0:T(8,128)(2,1)S(1)}, bf16[384,384]{1,0:T(8,128)(2,1)S(1)}, u32[]{:S(2)}, u32[]{:S(2)}) collective-permute-start(bf16[384,384]{1,0:T(8,128)(2,1)S(1)} %get-tuple-element.75), channel_id=1, source_target_pairs={{0,16},{4,20},{8,24},{12,28},{16,0},{20,4},{24,8},{28,12},{1,17},{... | collective-permute-start | bytes 884744 | tf_op jit(solution)/shard_map/ppermute | solution.py:403
  111.7 17.0 %collective-permute-start.35 = (bf16[384,256]{1,0:T(8,128)(2,1)S(1)}, bf16[384,256]{1,0:T(8,128)(2,1)S(1)}, u32[]{:S(2)}, u32[]{:S(2)}) collective-permute-start(bf16[384,256]{1,0:T(8,128)(2,1)S(1)} %get-tuple-element.60), channel_id=1, source_target_pairs={{0,28},{4,24},{8,4},{12,0},{16,12},{20,8},{24,20},{28,16},{1,29},{... | collective-permute-start | bytes 589832 | tf_op jit(solution)/shard_map/ppermute | solution.py:403
  128.7 18.5 %collective-permute-start.26 = (bf16[384,384]{1,0:T(8,128)(2,1)S(1)}, bf16[384,384]{1,0:T(8,128)(2,1)S(1)}, u32[]{:S(2)}, u32[]{:S(2)}) collective-permute-start(bf16[384,384]{1,0:T(8,128)(2,1)S(1)} %get-tuple-element.76), channel_id=1, source_target_pairs={{0,20},{4,16},{8,28},{12,24},{16,4},{20,0},{24,12},{28,8},{1,21},{... | collective-permute-start | bytes 884744 | tf_op jit(solution)/shard_map/ppermute | solution.py:403
  128.7 33.3 %collective-permute-start.27 = (bf16[384,384]{1,0:T(8,128)(2,1)S(1)}, bf16[384,384]{1,0:T(8,128)(2,1)S(1)}, u32[]{:S(2)}, u32[]{:S(2)}) collective-permute-start(bf16[384,384]{1,0:T(8,128)(2,1)S(1)} %get-tuple-element.77), channel_id=1, source_target_pairs={{0,24},{4,28},{8,0},{12,4},{16,8},{20,12},{24,16},{28,20},{1,25},{... | collective-permute-start | bytes 884744 | tf_op jit(solution)/shard_map/ppermute | solution.py:403
  129.7 44.4 %collective-permute-start.28 = (bf16[384,384]{1,0:T(8,128)(2,1)S(1)}, bf16[384,384]{1,0:T(8,128)(2,1)S(1)}, u32[]{:S(2)}, u32[]{:S(2)}) collective-permute-start(bf16[384,384]{1,0:T(8,128)(2,1)S(1)} %get-tuple-element.78), channel_id=1, source_target_pairs={{0,28},{4,24},{8,4},{12,0},{16,12},{20,8},{24,20},{28,16},{1,29},{... | collective-permute-start | bytes 884744 | tf_op jit(solution)/shard_map/ppermute | solution.py:403
  134.0 40.1 %collective-permute-start.14 = (bf16[384,384]{1,0:T(8,128)(2,1)S(1)}, bf16[384,384]{1,0:T(8,128)(2,1)S(1)}, u32[]{:S(2)}, u32[]{:S(2)}) collective-permute-start(bf16[384,384]{1,0:T(8,128)(2,1)S(1)} %get-tuple-element.64), channel_id=1, source_target_pairs={{0,4},{4,0},{8,12},{12,8},{16,20},{20,16},{24,28},{28,24},{1,5},{5... | collective-permute-start | bytes 884744 | tf_op jit(solution)/shard_map/ppermute | solution.py:403
  136.1 39.0 %collective-permute-start.15 = (bf16[384,384]{1,0:T(8,128)(2,1)S(1)}, bf16[384,384]{1,0:T(8,128)(2,1)S(1)}, u32[]{:S(2)}, u32[]{:S(2)}) collective-permute-start(bf16[384,384]{1,0:T(8,128)(2,1)S(1)} %get-tuple-element.65), channel_id=1, source_target_pairs={{0,8},{4,12},{8,16},{12,20},{16,24},{20,28},{24,0},{28,4},{1,9},{5... | collective-permute-start | bytes 884744 | tf_op jit(solution)/shard_map/ppermute | solution.py:403
  147.3 37.0 %collective-permute-start.16 = (bf16[384,384]{1,0:T(8,128)(2,1)S(1)}, bf16[384,384]{1,0:T(8,128)(2,1)S(1)}, u32[]{:S(2)}, u32[]{:S(2)}) collective-permute-start(bf16[384,384]{1,0:T(8,128)(2,1)S(1)} %get-tuple-element.66), channel_id=1, source_target_pairs={{0,12},{4,8},{8,20},{12,16},{16,28},{20,24},{24,4},{28,0},{1,13},{... | collective-permute-start | bytes 884744 | tf_op jit(solution)/shard_map/ppermute | solution.py:403
  162.1 31.1 %collective-permute-start.17 = (bf16[384,384]{1,0:T(8,128)(2,1)S(1)}, bf16[384,384]{1,0:T(8,128)(2,1)S(1)}, u32[]{:S(2)}, u32[]{:S(2)}) collective-permute-start(bf16[384,384]{1,0:T(8,128)(2,1)S(1)} %get-tuple-element.67), channel_id=1, source_target_pairs={{0,16},{4,20},{8,24},{12,28},{16,0},{20,4},{24,8},{28,12},{1,17},{... | collective-permute-start | bytes 884744 | tf_op jit(solution)/shard_map/ppermute | solution.py:403
  174.1 24.7 %collective-permute-start.18 = (bf16[384,384]{1,0:T(8,128)(2,1)S(1)}, bf16[384,384]{1,0:T(8,128)(2,1)S(1)}, u32[]{:S(2)}, u32[]{:S(2)}) collective-permute-start(bf16[384,384]{1,0:T(8,128)(2,1)S(1)} %get-tuple-element.68), channel_id=1, source_target_pairs={{0,20},{4,16},{8,28},{12,24},{16,4},{20,0},{24,12},{28,8},{1,21},{... | collective-permute-start | bytes 884744 | tf_op jit(solution)/shard_map/ppermute | solution.py:403
  174.1 24.7 %collective-permute-start.19 = (bf16[384,384]{1,0:T(8,128)(2,1)S(1)}, bf16[384,384]{1,0:T(8,128)(2,1)S(1)}, u32[]{:S(2)}, u32[]{:S(2)}) collective-permute-start(bf16[384,384]{1,0:T(8,128)(2,1)S(1)} %get-tuple-element.69), channel_id=1, source_target_pairs={{0,24},{4,28},{8,0},{12,4},{16,8},{20,12},{24,16},{28,20},{1,25},{... | collective-permute-start | bytes 884744 | tf_op jit(solution)/shard_map/ppermute | solution.py:403
  175.1 23.9 %collective-permute-start.20 = (bf16[384,384]{1,0:T(8,128)(2,1)S(1)}, bf16[384,384]{1,0:T(8,128)(2,1)S(1)}, u32[]{:S(2)}, u32[]{:S(2)}) collective-permute-start(bf16[384,384]{1,0:T(8,128)(2,1)S(1)} %get-tuple-element.70), channel_id=1, source_target_pairs={{0,28},{4,24},{8,4},{12,0},{16,12},{20,8},{24,20},{28,16},{1,29},{... | collective-permute-start | bytes 884744 | tf_op jit(solution)/shard_map/ppermute | solution.py:403

commit v6 on v5

--- a/solution.py
+++ b/solution.py
@@ -19,12 +19,13 @@
     ("message", 0, 1): [("group", 1)],
     ("message", 1, 1): [("message", 0, 2)],
     ("message", 1, 2): [("message", 0, 3)],
-    ("message", 1, 3): [("message", 0, 4)],
+    ("message", 1, 3): [("message", 0, 4), ("mixed", 0)],
     ("message", 2, 1): [("message", 1, 2)],
-    ("message", 2, 2): [("message", 1, 3)],
-    ("message", 2, 3): [("message", 1, 4), ("mixed", 0)],
-    ("mixed", 0): [("message", 1, 3), ("message", 2, 2)],
-    ("message", 1, 4): [("mixed", 0)],
+    ("message", 2, 2): [("message", 1, 3), ("mixed", 0)],
+    ("message", 2, 3): [("message", 1, 4), ("sent", 0, 2)],
+    ("mixed", 0): [("message", 1, 2), ("message", 2, 1)],
+    ("message", 1, 4): [("sent", 0, 1)],
+    ("mixed", 1): [("sent", 0, 1), ("sent", 0, 2), ("sent", 0, 3), ("sent", 0, 4)],
 }
 
 
@@ -129,7 +130,7 @@
     return tiles
 
 
-def attend_body(n, spans, place, low, queries, keys, values, gain, *refs):
+def attend_body(n, spans, order, place, low, queries, keys, values, gain, *refs):
     states, outs = refs[: 2 * len(spans)], refs[2 * len(spans) :][:n]
     qbuf, kbuf, vbuf, sown, soth, gbuf, held, sems, extra = refs[-9:]
     width = sum(size for _, size in spans)
@@ -153,7 +154,7 @@
 
     def sends(step):
         return [
-            pltpu.make_async_copy(held.at[slot], outs[slot], sems.at[3, slot])
+            pltpu.make_async_copy(held.at[slot], outs[order.index(slot)], sems.at[3, slot])
             for slot in (2 * step, 2 * step + 1)
         ]
 
@@ -213,14 +214,14 @@
             copy.wait()
 
 
-def attend(place, queries, keys, values, gain, states, spans, n, low):
+def attend(place, queries, keys, values, gain, states, spans, order, n, low):
     rows, m = queries.shape[0], n // 2
     width = sum(size for _, size in spans)
     wide = width * HEAD
     tokens = pltpu.VMEM((n, rows, wide), jnp.bfloat16)
     state = pltpu.VMEM((m, width, HEAD, HEAD), jnp.bfloat16)
     return pl.pallas_call(
-        functools.partial(attend_body, n, spans),
+        functools.partial(attend_body, n, spans, order),
         in_specs=[pl.BlockSpec(memory_space=pltpu.SMEM)] * 2
         + [pl.BlockSpec(memory_space=pltpu.HBM)] * 3
         + [pl.BlockSpec(memory_space=pl.ANY)] * (1 + 2 * len(states)),
@@ -247,18 +248,18 @@
     )(place, jnp.full((1,), low, jnp.int32), queries, keys, values, gain, *(array for pair in states for array in pair))
 
 
-def put_body(n, place, low, *refs):
+def put_body(n, order, place, low, *refs):
     parts, out, again, sems = refs[:n], refs[-3], refs[-2], refs[-1]
     m = n // 2
     rows, wide = parts[0].shape
     cols = pl.ds(pl.multiple_of(low[0] * HEAD, HEAD), wide)
     copies = []
-    for shift in range(n):
+    for index, shift in enumerate(order):
         row = lax.rem(place[0] + m - shift // 2, m)
         col = place[1] if shift % 2 == 0 else 1 - place[1]
         start = pl.multiple_of((2 * row + col) * rows, rows)
         copies.append(
-            pltpu.make_async_copy(parts[shift], out.at[pl.ds(start, rows), cols], sems.at[shift])
+            pltpu.make_async_copy(parts[index], out.at[pl.ds(start, rows), cols], sems.at[index])
         )
     for copy in copies:
         copy.start()
@@ -268,11 +269,11 @@
         copy.wait()
 
 
-def put(place, parts, out, n, low):
+def put(place, parts, out, order, n, low):
     rows, first = parts[0].shape[0], out is None
     anywhere = pl.BlockSpec(memory_space=pltpu.HBM)
     return pl.pallas_call(
-        functools.partial(put_body, n),
+        functools.partial(put_body, n, order),
         in_specs=[pl.BlockSpec(memory_space=pltpu.SMEM)] * 2 + [anywhere] * (n if first else n + 1),
         out_specs=[anywhere, pl.BlockSpec(memory_space=pltpu.SMEM)],
         out_shape=[
@@ -311,6 +312,7 @@
         self.groups, self.swaps, self.parts, self.chunks = (
             split(widths, HEADS // n) for widths in (LOCAL, SWAP, PREFIX, MIXED)
         )
+        self.shifts = sorted(range(1, n), key=lambda k: (-min(k // 2, self.m - k // 2), k))
         self.made = {}
 
     def has(self, key):
@@ -394,18 +396,19 @@
             if first < last:
                 states.append(self.get("states", part))
                 spans.append((first - start, last - first))
-        return attend(place, *self.arrays, self.gain, states, tuple(spans), self.n, low)
+        return attend(place, *self.arrays, self.gain, states, tuple(spans), (0, *self.shifts), self.n, low)
 
     def sent(self, c, k):
+        shift = self.shifts[k - 1]
         pairs = [
-            (2 * z + y, 2 * ((z + k // 2) % self.m) + (y + k) % 2) for z in range(self.m) for y in range(2)
+            (2 * z + y, 2 * ((z + shift // 2) % self.m) + (y + shift) % 2) for z in range(self.m) for y in range(2)
         ]
         return lax.ppermute(self.hold(self.get("mixed", c)[k], "sent", c, k), "seq", pairs)
 
     def put(self, c):
         parts = [self.get("mixed", c)[0]] + [self.get("sent", c, k) for k in range(1, self.n)]
         out = self.get("put", c - 1)[0] if c else None
-        return put(self.place, parts, out, self.n, self.chunks[c][0])
+        return put(self.place, parts, out, (0, *self.shifts), self.n, self.chunks[c][0])
 
 
 def per_device(n, *arrays):

time: 203 us -> 224 us (1.10); the launches traced: 202 us -> 220 us
  starting transfers between devices: 50.6 us -> 96.6 us
  waiting for transfers between devices: 102 us -> 74.1 us
    ppermute x21, starting transfers between devices: 31.1 us -> 75.2 us  [sent(): lax.ppermute(self.hold(self.get('mixed', c)[k], 'sent', c, k), 'seq', pairs)]
    ppermute x21, waiting for transfers between devices: 75.3 us -> 54.5 us  [sent(): lax.ppermute(self.hold(self.get('mixed', c)[k], 'sent', c, k), 'seq', pairs)]
    ppermute x12, waiting for transfers between devices: 25.1 us -> 18.1 us  [prefix(): return lax.ppermute(self.get('message', c, s), 'seq', pairs)]
  transfers between devices with their start and end apart: 36 -> 36, of which waited for: 14 -> 15; matrix products, arithmetic and copies ran while one was open for 4% -> 3% of each run, Pallas kernels for 18% -> 16%
where the time goes in v6:
time: 224 us; the launch traced here: 220 us
  starting transfers between devices  96.6 us (43%)
  waiting for transfers between devices  74.1 us (33%)
  Pallas kernels  41.3 us (18%)
  other arithmetic  7.62 us (3%)
    ppermute x21, starting transfers between devices, sent(): lax.ppermute(self.hold(self.get('mixed', c)[k], 'sent', c, k), 'seq', pairs)  75.2 us
    ppermute x21, waiting for transfers between devices, sent(): lax.ppermute(self.hold(self.get('mixed', c)[k], 'sent', c, k), 'seq', pairs)  54.5 us
    pallas_call x3, Pallas kernels, attend(): pl.pallas_call(functools.partial(attend_body, n, spans, order), in_specs=...  25.5 us
    ppermute x12, waiting for transfers between devices, prefix(): return lax.ppermute(self.get('message', c, s), 'seq', pairs)  18.1 us
    ppermute x12, starting transfers between devices, prefix(): return lax.ppermute(self.get('message', c, s), 'seq', pairs)  16.7 us
    pallas_call x2, Pallas kernels, local_states(): pl.pallas_call(functools.partial(local_body, n, widths, swaps), in_specs=...  8.47 us
    pallas_call x3, Pallas kernels, put(): pl.pallas_call(functools.partial(put_body, n, order), in_specs=[pl.BlockS...  7.33 us
    convert_element_type x10, other arithmetic, message(): return self.hold(value.astype(jnp.bfloat16), 'message', c, s)  4.85 us
  transfers between devices with their start and end apart: 36, of which 15 were waited for; matrix products, arithmetic and copies ran while one was open for 3% of the time, Pallas kernels for 16%

profile of v6, /device:TPU:8, one launch (start us, length us, event | category | flops | bytes accessed | tf_op | source)
XLA Modules:
  0.0 220.0 jit_solution(7250729124182812214)
XLA Ops:
  0.1 3.4 %local.3 = (f32[4,2,128,128]{3,2,1,0:T(8,128)S(1)}, bf16[4,2,128,128]{3,2,1,0:T(8,128)(2,1)S(1)}) custom-call(s32[2]{0:T(128)S(1)} %pad_add_fusion.place, s32[1]{0:T(128)} %constant.38.clone.1.low, bf16[384,8192]{1,0:T(8,128)(2,1)} %keys.9, bf16[384,8192]{1,0:T(8,128)(2,1)} %values.9), custom_call_target="tpu_custom_call" | custom-call | flops 201326592 | bytes 3145728 | tf_op jit(solution)/shard_map/local/pallas_call | solution.py:99
  3.5 1.6 collective-permute-start.2
  5.1 5.0 %local.2 = (f32[4,3,128,128]{3,2,1,0:T(8,128)S(1)}, f32[4,3,128,128]{3,2,1,0:T(8,128)S(1)}, bf16[4,3,128,128]{3,2,1,0:T(8,128)(2,1)S(1)}, bf16[4,3,128,128]{3,2,1,0:T(8,128)(2,1)S(1)}) custom-call(s32[2]{0:T(128)S(1)} %pad_add_fusion.place, s32[1]{0:T(128)} %constant.37.clone.1.low, bf16[384,8192]{1,0:T(8,128)(2,1)} %keys.9, bf16[384,8192]{1,0:T(8,128)(2,1)} %values.9), custom_call_target="tpu_custom_call" | custom-call | flops 603979776 | bytes 9437184 | tf_op jit(solution)/shard_map/local/pallas_call | solution.py:99
  10.2 1.5 collective-permute-done.2
  11.7 1.3 collective-permute-start.3
  13.0 1.6 collective-permute-start.1
  14.6 6.2 %collective-permute-done.3 = bf16[4,2,128,128]{3,2,1,0:T(8,128)(2,1)S(1)} collective-permute-done((bf16[4,2,128,128]{3,2,1,0:T(8,128)(2,1)S(1)}, bf16[4,2,128,128]{3,2,1,0:T(8,128)(2,1)S(1)}, u32[]{:S(2)}, u32[]{:S(2)}) %collective-permute-start.3) | collective-permute-done | bytes 262176 | tf_op jit(solution)/shard_map/ppermute | solution.py:382
  21.5 2.0 collective-permute-start.5
  24.4 1.3 collective-permute-start.4
  25.7 1.6 collective-permute-start
  27.3 1.1 add_convert_fusion.4
  29.1 6.5 %collective-permute-done.4 = bf16[4,3,128,128]{3,2,1,0:T(8,128)(2,1)} collective-permute-done((bf16[4,3,128,128]{3,2,1,0:T(8,128)(2,1)}, bf16[4,3,128,128]{3,2,1,0:T(8,128)(2,1)}, u32[]{:S(2)}, u32[]{:S(2)}) %collective-permute-start.4) | collective-permute-done | bytes 393248 | tf_op jit(solution)/shard_map/ppermute | solution.py:382
  35.6 1.2 add_convert_fusion.3
  36.8 1.3 collective-permute-start.7
  38.1 1.4 fusion.5
  39.5 1.6 collective-permute-start.9
  41.2 1.3 collective-permute-start.6
  42.5 3.4 %collective-permute-done.9.refs_1_ = bf16[4,2,128,128]{3,2,1,0:T(8,128)(2,1)S(1)} collective-permute-done((bf16[4,2,128,128]{3,2,1,0:T(8,128)(2,1)S(1)}, bf16[4,2,128,128]{3,2,1,0:T(8,128)(2,1)S(1)}, u32[]{:S(2)}, u32[]{:S(2)}) %collective-permute-start.9) | collective-permute-done | bytes 262176 | tf_op jit(solution)/shard_map/ppermute | solution.py:382
  45.9 8.5 %attend.3 = (bf16[384,256]{1,0:T(8,128)(2,1)S(1)}, bf16[384,256]{1,0:T(8,128)(2,1)S(1)}, bf16[384,256]{1,0:T(8,128)(2,1)S(1)}, bf16[384,256]{1,0:T(8,128)(2,1)S(...) custom-call(s32[2]{0:T(128)S(1)} %pad_add_fusion.place, ...), custom_call_target="tpu_custom_call" | custom-call | flops 1409286144 | bytes 6291456 | tf_op jit(solution)/shard_map/attend/pallas_call | solution.py:223
  55.5 3.8 %collective-permute-start.10 = (bf16[4,3,128,128]{3,2,1,0:T(8,128)(2,1)S(1)}, bf16[4,3,128,128]{3,2,1,0:T(8,128)(2,1)S(1)}, u32[]{:S(2)}, u32[]{:S(2)}) collective-permute-start(bf16[4,3,128,128]{3,2,1,0:T(8,128)(2,1)S(1)} %add_convert_fusion.2), channel_id=1, source_target_pairs={{8,16},{12,20},{9,17},{13,21},{10,18},{14,22},{11,19},{15,23}} | collective-permute-start | bytes 1179656 | tf_op jit(solution)/shard_map/ppermute | solution.py:382
  59.4 3.5 %collective-permute-start.13 = (bf16[384,256]{1,0:T(8,128)(2,1)S(1)}, bf16[384,256]{1,0:T(8,128)(2,1)S(1)}, u32[]{:S(2)}, u32[]{:S(2)}) collective-permute-start(bf16[384,256]{1,0:T(8,128)(2,1)S(1)} %get-tuple-element.64), channel_id=1, source_target_pairs={{0,20},{4,16},{8,28},{12,24},{16,4},{20,0},{24,12},{28,8},{1,21},{... | collective-permute-start | bytes 589832 | tf_op jit(solution)/shard_map/ppermute | solution.py:406
  62.9 1.3 fusion.1
  64.2 13.0 %collective-permute-done.12.refs_1_ = bf16[384,256]{1,0:T(8,128)(2,1)S(1)} collective-permute-done((bf16[384,256]{1,0:T(8,128)(2,1)S(1)}, bf16[384,256]{1,0:T(8,128)(2,1)S(1)}, u32[]{:S(2)}, u32[]{:S(2)}) %collective-permute-start.12) | collective-permute-done | bytes 196640 | tf_op jit(solution)/shard_map/ppermute | solution.py:406
  77.4 2.7 %collective-permute-done.13.refs_2_ = bf16[384,256]{1,0:T(8,128)(2,1)S(1)} collective-permute-done((bf16[384,256]{1,0:T(8,128)(2,1)S(1)}, bf16[384,256]{1,0:T(8,128)(2,1)S(1)}, u32[]{:S(2)}, u32[]{:S(2)}) %collective-permute-start.13) | collective-permute-done | bytes 196640 | tf_op jit(solution)/shard_map/ppermute | solution.py:406
  80.8 5.8 %collective-permute-start.23 = (bf16[384,256]{1,0:T(8,128)(2,1)S(1)}, bf16[384,256]{1,0:T(8,128)(2,1)S(1)}, u32[]{:S(2)}, u32[]{:S(2)}) collective-permute-start(bf16[384,256]{1,0:T(8,128)(2,1)S(1)} %get-tuple-element.74), channel_id=1, source_target_pairs={{0,8},{4,12},{8,16},{12,20},{16,24},{20,28},{24,0},{28,4},{1,9},{5... | collective-permute-start | bytes 589832 | tf_op jit(solution)/shard_map/ppermute | solution.py:406
  87.0 1.1 collective-permute-start.25
  89.4 2.0 collective-permute-start.33
  91.5 9.8 %collective-permute-start.34 = (bf16[384,256]{1,0:T(8,128)(2,1)S(1)}, bf16[384,256]{1,0:T(8,128)(2,1)S(1)}, u32[]{:S(2)}, u32[]{:S(2)}) collective-permute-start(bf16[384,256]{1,0:T(8,128)(2,1)S(1)} %get-tuple-element.87), channel_id=1, source_target_pairs={{0,28},{4,24},{8,4},{12,0},{16,12},{20,8},{24,20},{28,16},{1,29},{... | collective-permute-start | bytes 589832 | tf_op jit(solution)/shard_map/ppermute | solution.py:406
  101.3 1.9 collective-permute-done.25.refs_1_
  103.3 8.4 %attend.5 = (bf16[384,384]{1,0:T(8,128)(2,1)S(1)}, bf16[384,384]{1,0:T(8,128)(2,1)S(1)}, bf16[384,384]{1,0:T(8,128)(2,1)S(1)}, bf16[384,384]{1,0:T(8,128)(2,1)S(...) custom-call(s32[2]{0:T(128)S(1)} %pad_add_fusion.place, ...), custom_call_target="tpu_custom_call" | custom-call | flops 2113929216 | bytes 9437184 | tf_op jit(solution)/shard_map/attend/pallas_call | solution.py:223
  111.7 7.8 %collective-permute-start.26 = (bf16[384,384]{1,0:T(8,128)(2,1)S(1)}, bf16[384,384]{1,0:T(8,128)(2,1)S(1)}, u32[]{:S(2)}, u32[]{:S(2)}) collective-permute-start(bf16[384,384]{1,0:T(8,128)(2,1)S(1)} %get-tuple-element.78), channel_id=1, source_target_pairs={{0,16},{4,20},{8,24},{12,28},{16,0},{20,4},{24,8},{28,12},{1,17},{... | collective-permute-start | bytes 884744 | tf_op jit(solution)/shard_map/ppermute | solution.py:406
  120.8 3.1 %collective-permute-start.29 = (bf16[384,384]{1,0:T(8,128)(2,1)S(1)}, bf16[384,384]{1,0:T(8,128)(2,1)S(1)}, u32[]{:S(2)}, u32[]{:S(2)}) collective-permute-start(bf16[384,384]{1,0:T(8,128)(2,1)S(1)} %get-tuple-element.81), channel_id=1, source_target_pairs={{0,12},{4,8},{8,20},{12,16},{16,28},{20,24},{24,4},{28,0},{1,13},{... | collective-permute-start | bytes 884744 | tf_op jit(solution)/shard_map/ppermute | solution.py:406
  123.9 1.0 collective-permute-start.35
  124.9 8.5 %attend.4 = (bf16[384,384]{1,0:T(8,128)(2,1)S(1)}, bf16[384,384]{1,0:T(8,128)(2,1)S(1)}, bf16[384,384]{1,0:T(8,128)(2,1)S(1)}, bf16[384,384]{1,0:T(8,128)(2,1)S(...) custom-call(s32[2]{0:T(128)S(1)} %pad_add_fusion.place, ...), custom_call_target="tpu_custom_call" | custom-call | flops 2113929216 | bytes 9437184 | tf_op jit(solution)/shard_map/attend/pallas_call | solution.py:223
  133.5 1.6 collective-permute-done.26.refs_1_
  135.0 16.6 %collective-permute-start.31 = (bf16[384,384]{1,0:T(8,128)(2,1)S(1)}, bf16[384,384]{1,0:T(8,128)(2,1)S(1)}, u32[]{:S(2)}, u32[]{:S(2)}) collective-permute-start(bf16[384,384]{1,0:T(8,128)(2,1)S(1)} %get-tuple-element.83), channel_id=1, source_target_pairs={{0,28},{4,24},{8,4},{12,0},{16,12},{20,8},{24,20},{28,16},{1,29},{... | collective-permute-start | bytes 884744 | tf_op jit(solution)/shard_map/ppermute | solution.py:406
  152.5 7.8 %collective-permute-done.28.refs_3_ = bf16[384,384]{1,0:T(8,128)(2,1)S(1)} collective-permute-done((bf16[384,384]{1,0:T(8,128)(2,1)S(1)}, bf16[384,384]{1,0:T(8,128)(2,1)S(1)}, u32[]{:S(2)}, u32[]{:S(2)}) %collective-permute-start.28) | collective-permute-done | bytes 294944 | tf_op jit(solution)/shard_map/ppermute | solution.py:406
  160.3 12.6 %collective-permute-done.29.refs_4_ = bf16[384,384]{1,0:T(8,128)(2,1)S(1)} collective-permute-done((bf16[384,384]{1,0:T(8,128)(2,1)S(1)}, bf16[384,384]{1,0:T(8,128)(2,1)S(1)}, u32[]{:S(2)}, u32[]{:S(2)}) %collective-permute-start.29) | collective-permute-done | bytes 294944 | tf_op jit(solution)/shard_map/ppermute | solution.py:406
  173.0 2.9 %collective-permute-start.18 = (bf16[384,384]{1,0:T(8,128)(2,1)S(1)}, bf16[384,384]{1,0:T(8,128)(2,1)S(1)}, u32[]{:S(2)}, u32[]{:S(2)}) collective-permute-start(bf16[384,384]{1,0:T(8,128)(2,1)S(1)} %get-tuple-element.69), channel_id=1, source_target_pairs={{0,8},{4,12},{8,16},{12,20},{16,24},{20,28},{24,0},{28,4},{1,9},{5... | collective-permute-start | bytes 884744 | tf_op jit(solution)/shard_map/ppermute | solution.py:406
  175.8 1.5 collective-permute-start.19
  178.4 7.3 %collective-permute-done.16.refs_1_ = bf16[384,384]{1,0:T(8,128)(2,1)S(1)} collective-permute-done((bf16[384,384]{1,0:T(8,128)(2,1)S(1)}, bf16[384,384]{1,0:T(8,128)(2,1)S(1)}, u32[]{:S(2)}, u32[]{:S(2)}) %collective-permute-start.16) | collective-permute-done | bytes 294944 | tf_op jit(solution)/shard_map/ppermute | solution.py:406
  185.6 16.4 %collective-permute-start.21 = (bf16[384,384]{1,0:T(8,128)(2,1)S(1)}, bf16[384,384]{1,0:T(8,128)(2,1)S(1)}, u32[]{:S(2)}, u32[]{:S(2)}) collective-permute-start(bf16[384,384]{1,0:T(8,128)(2,1)S(1)} %get-tuple-element.72), channel_id=1, source_target_pairs={{0,28},{4,24},{8,4},{12,0},{16,12},{20,8},{24,20},{28,16},{1,29},{... | collective-permute-start | bytes 884744 | tf_op jit(solution)/shard_map/ppermute | solution.py:406
  202.1 1.1 collective-permute-start.22
  203.1 2.3 %put.3 = (bf16[3072,1024]{1,0:T(8,128)(2,1)}, s32[2]{0:T(128)}) custom-call(s32[2]{0:T(128)S(1)} %pad_add_fusion.place, s32[1]{0:T(128)} %constant.38.clone.1.low, bf16[384,256]{1,0:T(8,128)(2,1)S(1)} %get-tuple-element.85.refs_0_, bf16[384,256]{1,0:T(8,128)(2,1)S(1)} %collective-permute-done.12.refs_1_, ...), custom_call_target="tpu_custom_call" | custom-call | tf_op jit(solution)/shard_map/put/pallas_call | solution.py:275
  205.4 2.5 %put.4 = (bf16[3072,1024]{1,0:T(8,128)(2,1)}, s32[2]{0:T(128)}) custom-call(s32[2]{0:T(128)S(1)} %pad_add_fusion.place, s32[1]{0:T(128)} %constant.37.clone.1.low, bf16[384,384]{1,0:T(8,128)(2,1)S(1)} %get-tuple-element.77.refs_0_, bf16[384,384]{1,0:T(8,128)(2,1)S(1)} %collective-permute-done.26.refs_1_, ...), custom_call_target="tpu_custom_call", output_to_operand_aliasing={{0}: (10, {})} | custom-call | tf_op jit(solution)/shard_map/put/pallas_call | solution.py:275
  208.0 3.0 %collective-permute-done.18.refs_3_ = bf16[384,384]{1,0:T(8,128)(2,1)S(1)} collective-permute-done((bf16[384,384]{1,0:T(8,128)(2,1)S(1)}, bf16[384,384]{1,0:T(8,128)(2,1)S(1)}, u32[]{:S(2)}, u32[]{:S(2)}) %collective-permute-start.18) | collective-permute-done | bytes 294944 | tf_op jit(solution)/shard_map/ppermute | solution.py:406
  211.0 6.3 %collective-permute-done.19.refs_4_ = bf16[384,384]{1,0:T(8,128)(2,1)S(1)} collective-permute-done((bf16[384,384]{1,0:T(8,128)(2,1)S(1)}, bf16[384,384]{1,0:T(8,128)(2,1)S(1)}, u32[]{:S(2)}, u32[]{:S(2)}) %collective-permute-start.19) | collective-permute-done | bytes 294944 | tf_op jit(solution)/shard_map/ppermute | solution.py:406
  217.3 2.5 %put.5 = (bf16[3072,1024]{1,0:T(8,128)(2,1)}, s32[2]{0:T(128)}) custom-call(s32[2]{0:T(128)S(1)} %pad_add_fusion.place, s32[1]{0:T(128)} %constant.36.clone.1.low, bf16[384,384]{1,0:T(8,128)(2,1)S(1)} %get-tuple-element.66.refs_0_, bf16[384,384]{1,0:T(8,128)(2,1)S(1)} %collective-permute-done.16.refs_1_, ...), custom_call_target="tpu_custom_call", output_to_operand_aliasing={{0}: (10, {})} | custom-call | tf_op jit(solution)/shard_map/put/pallas_call | solution.py:275
  (51 shorter events, 9.7 us)
Async XLA Ops:
  3.5 8.1 %collective-permute-start.2 = (bf16[4,2,128,128]{3,2,1,0:T(8,128)(2,1)S(1)}, bf16[4,2,128,128]{3,2,1,0:T(8,128)(2,1)S(1)}, u32[]{:S(2)}, u32[]{:S(2)}) collective-permute-start(bf16[4,2,128,128]{3,2,1,0:T(8,128)(2,1)S(1)} %get-tuple-element.53), channel_id=1, source_target_pairs={{0,4},{4,0},{8,12},{12,8},{16,20},{20,16},{24,28},{28,24},{1,5},{5... | collective-permute-start | bytes 786440 | tf_op jit(solution)/shard_map/ppermute | solution.py:355
  10.1 35.8 %copy-start = (f32[8192]{0:T(1024)S(1)}, f32[8192]{0:T(1024)}, u32[]{:S(2)}) copy-start(f32[8192]{0:T(1024)} %param.7) | copy-start | bytes 98308
  11.6 12.8 %copy-start.1 = (bf16[4,2,128,128]{3,2,1,0:T(8,128)(2,1)}, bf16[4,2,128,128]{3,2,1,0:T(8,128)(2,1)S(1)}, u32[]{:S(2)}) copy-start(bf16[4,2,128,128]{3,2,1,0:T(8,128)(2,1)S(1)} %collective-permute-done.2) | copy-start | bytes 786436
  11.7 9.1 %collective-permute-start.3 = (bf16[4,2,128,128]{3,2,1,0:T(8,128)(2,1)S(1)}, bf16[4,2,128,128]{3,2,1,0:T(8,128)(2,1)S(1)}, u32[]{:S(2)}, u32[]{:S(2)}) collective-permute-start(bf16[4,2,128,128]{3,2,1,0:T(8,128)(2,1)S(1)} %fusion.8), channel_id=1, source_target_pairs={{0,8},{4,12},{1,9},{5,13},{2,10},{6,14},{3,11},{7,15}} | collective-permute-start | bytes 786440 | tf_op jit(solution)/shard_map/ppermute | solution.py:382
  13.0 10.5 %collective-permute-start.1 = (bf16[4,3,128,128]{3,2,1,0:T(8,128)(2,1)S(1)}, bf16[4,3,128,128]{3,2,1,0:T(8,128)(2,1)S(1)}, u32[]{:S(2)}, u32[]{:S(2)}) collective-permute-start(bf16[4,3,128,128]{3,2,1,0:T(8,128)(2,1)S(1)} %get-tuple-element.51), channel_id=1, source_target_pairs={{0,4},{4,0},{8,12},{12,8},{16,20},{20,16},{24,28},{28,24},{1,5},{5... | collective-permute-start | bytes 1179656 | tf_op jit(solution)/shard_map/ppermute | solution.py:355
  20.7 2.8 %copy-start.2 = (bf16[4,2,128,128]{3,2,1,0:T(8,128)(2,1)}, bf16[4,2,128,128]{3,2,1,0:T(8,128)(2,1)S(1)}, u32[]{:S(2)}) copy-start(bf16[4,2,128,128]{3,2,1,0:T(8,128)(2,1)S(1)} %collective-permute-done.3) | copy-start | bytes 786436
  21.5 5.7 %collective-permute-start.5 = (bf16[4,2,128,128]{3,2,1,0:T(8,128)(2,1)}, bf16[4,2,128,128]{3,2,1,0:T(8,128)(2,1)}, u32[]{:S(2)}, u32[]{:S(2)}) collective-permute-start(bf16[4,2,128,128]{3,2,1,0:T(8,128)(2,1)} %add_convert_fusion.5), channel_id=1, source_target_pairs={{8,16},{12,20},{9,17},{13,21},{10,18},{14,22},{11,19},{15,23}} | collective-permute-start | bytes 786440 | tf_op jit(solution)/shard_map/ppermute | solution.py:382
  24.4 11.2 %collective-permute-start.4 = (bf16[4,3,128,128]{3,2,1,0:T(8,128)(2,1)}, bf16[4,3,128,128]{3,2,1,0:T(8,128)(2,1)}, u32[]{:S(2)}, u32[]{:S(2)}) collective-permute-start(bf16[4,3,128,128]{3,2,1,0:T(8,128)(2,1)} %fusion.7), channel_id=1, source_target_pairs={{0,8},{4,12},{1,9},{5,13},{2,10},{6,14},{3,11},{7,15}} | collective-permute-start | bytes 1179656 | tf_op jit(solution)/shard_map/ppermute | solution.py:382
  25.7 15.4 %collective-permute-start = (bf16[4,3,128,128]{3,2,1,0:T(8,128)(2,1)S(1)}, bf16[4,3,128,128]{3,2,1,0:T(8,128)(2,1)S(1)}, u32[]{:S(2)}, u32[]{:S(2)}) collective-permute-start(bf16[4,3,128,128]{3,2,1,0:T(8,128)(2,1)S(1)} %get-tuple-element.49), channel_id=1, source_target_pairs={{0,4},{4,0},{8,12},{12,8},{16,20},{20,16},{24,28},{28,24},{1,5},{5... | collective-permute-start | bytes 1179656 | tf_op jit(solution)/shard_map/ppermute | solution.py:355
  28.4 9.7 %collective-permute-start.8 = (bf16[4,2,128,128]{3,2,1,0:T(8,128)(2,1)S(1)}, bf16[4,2,128,128]{3,2,1,0:T(8,128)(2,1)S(1)}, u32[]{:S(2)}, u32[]{:S(2)}) collective-permute-start(bf16[4,2,128,128]{3,2,1,0:T(8,128)(2,1)S(1)} %add_convert_fusion.4), channel_id=1, source_target_pairs={{16,24},{20,28},{17,25},{21,29},{18,26},{22,30},{19,27},{23,31}} | collective-permute-start | bytes 786440 | tf_op jit(solution)/shard_map/ppermute | solution.py:382
  36.8 17.7 %collective-permute-start.7 = (bf16[4,3,128,128]{3,2,1,0:T(8,128)(2,1)S(1)}, bf16[4,3,128,128]{3,2,1,0:T(8,128)(2,1)S(1)}, u32[]{:S(2)}, u32[]{:S(2)}) collective-permute-start(bf16[4,3,128,128]{3,2,1,0:T(8,128)(2,1)S(1)} %add_convert_fusion.3), channel_id=1, source_target_pairs={{8,16},{12,20},{9,17},{13,21},{10,18},{14,22},{11,19},{15,23}} | collective-permute-start | bytes 1179656 | tf_op jit(solution)/shard_map/ppermute | solution.py:382
  39.5 6.4 %collective-permute-start.9 = (bf16[4,2,128,128]{3,2,1,0:T(8,128)(2,1)S(1)}, bf16[4,2,128,128]{3,2,1,0:T(8,128)(2,1)S(1)}, u32[]{:S(2)}, u32[]{:S(2)}) collective-permute-start(bf16[4,2,128,128]{3,2,1,0:T(8,128)(2,1)S(1)} %get-tuple-element.96), channel_id=1, source_target_pairs={{0,4},{4,0},{8,12},{12,8},{16,20},{20,16},{24,28},{28,24},{1,5},{5... | collective-permute-start | bytes 786440 | tf_op jit(solution)/shard_map/ppermute | solution.py:382
  41.2 14.1 %collective-permute-start.6 = (bf16[4,3,128,128]{3,2,1,0:T(8,128)(2,1)S(1)}, bf16[4,3,128,128]{3,2,1,0:T(8,128)(2,1)S(1)}, u32[]{:S(2)}, u32[]{:S(2)}) collective-permute-start(bf16[4,3,128,128]{3,2,1,0:T(8,128)(2,1)S(1)} %fusion.6), channel_id=1, source_target_pairs={{0,8},{4,12},{1,9},{5,13},{2,10},{6,14},{3,11},{7,15}} | collective-permute-start | bytes 1179656 | tf_op jit(solution)/shard_map/ppermute | solution.py:382
  54.6 8.2 %collective-permute-start.11 = (bf16[4,3,128,128]{3,2,1,0:T(8,128)(2,1)S(1)}, bf16[4,3,128,128]{3,2,1,0:T(8,128)(2,1)S(1)}, u32[]{:S(2)}, u32[]{:S(2)}) collective-permute-start(bf16[4,3,128,128]{3,2,1,0:T(8,128)(2,1)S(1)} %add_convert_fusion.1), channel_id=1, source_target_pairs={{16,24},{20,28},{17,25},{21,29},{18,26},{22,30},{19,27},{23,31}} | collective-permute-start | bytes 1179656 | tf_op jit(solution)/shard_map/ppermute | solution.py:382
  55.5 21.8 %collective-permute-start.10 = (bf16[4,3,128,128]{3,2,1,0:T(8,128)(2,1)S(1)}, bf16[4,3,128,128]{3,2,1,0:T(8,128)(2,1)S(1)}, u32[]{:S(2)}, u32[]{:S(2)}) collective-permute-start(bf16[4,3,128,128]{3,2,1,0:T(8,128)(2,1)S(1)} %add_convert_fusion.2), channel_id=1, source_target_pairs={{8,16},{12,20},{9,17},{13,21},{10,18},{14,22},{11,19},{15,23}} | collective-permute-start | bytes 1179656 | tf_op jit(solution)/shard_map/ppermute | solution.py:382
  59.3 18.0 %collective-permute-start.12 = (bf16[384,256]{1,0:T(8,128)(2,1)S(1)}, bf16[384,256]{1,0:T(8,128)(2,1)S(1)}, u32[]{:S(2)}, u32[]{:S(2)}) collective-permute-start(bf16[384,256]{1,0:T(8,128)(2,1)S(1)} %get-tuple-element.62), channel_id=1, source_target_pairs={{0,16},{4,20},{8,24},{12,28},{16,0},{20,4},{24,8},{28,12},{1,17},{... | collective-permute-start | bytes 589832 | tf_op jit(solution)/shard_map/ppermute | solution.py:406
  59.4 20.7 %collective-permute-start.13 = (bf16[384,256]{1,0:T(8,128)(2,1)S(1)}, bf16[384,256]{1,0:T(8,128)(2,1)S(1)}, u32[]{:S(2)}, u32[]{:S(2)}) collective-permute-start(bf16[384,256]{1,0:T(8,128)(2,1)S(1)} %get-tuple-element.64), channel_id=1, source_target_pairs={{0,20},{4,16},{8,28},{12,24},{16,4},{20,0},{24,12},{28,8},{1,21},{... | collective-permute-start | bytes 589832 | tf_op jit(solution)/shard_map/ppermute | solution.py:406
  80.1 8.0 %collective-permute-start.14 = (bf16[4,3,128,128]{3,2,1,0:T(8,128)(2,1)S(1)}, bf16[4,3,128,128]{3,2,1,0:T(8,128)(2,1)S(1)}, u32[]{:S(2)}, u32[]{:S(2)}) collective-permute-start(bf16[4,3,128,128]{3,2,1,0:T(8,128)(2,1)S(1)} %add_convert_fusion), channel_id=1, source_target_pairs={{16,24},{20,28},{17,25},{21,29},{18,26},{22,30},{19,27},{23,31}} | collective-permute-start | bytes 1179656 | tf_op jit(solution)/shard_map/ppermute | solution.py:382
  80.8 10.7 %collective-permute-start.23 = (bf16[384,256]{1,0:T(8,128)(2,1)S(1)}, bf16[384,256]{1,0:T(8,128)(2,1)S(1)}, u32[]{:S(2)}, u32[]{:S(2)}) collective-permute-start(bf16[384,256]{1,0:T(8,128)(2,1)S(1)} %get-tuple-element.74), channel_id=1, source_target_pairs={{0,8},{4,12},{8,16},{12,20},{16,24},{20,28},{24,0},{28,4},{1,9},{5... | collective-permute-start | bytes 589832 | tf_op jit(solution)/shard_map/ppermute | solution.py:406
  86.6 14.7 %collective-permute-start.24 = (bf16[384,256]{1,0:T(8,128)(2,1)S(1)}, bf16[384,256]{1,0:T(8,128)(2,1)S(1)}, u32[]{:S(2)}, u32[]{:S(2)}) collective-permute-start(bf16[384,256]{1,0:T(8,128)(2,1)S(1)} %get-tuple-element.75), channel_id=1, source_target_pairs={{0,12},{4,8},{8,20},{12,16},{16,28},{20,24},{24,4},{28,0},{1,13},{... | collective-permute-start | bytes 589832 | tf_op jit(solution)/shard_map/ppermute | solution.py:406
  87.0 16.3 %collective-permute-start.25 = (bf16[4,3,128,128]{3,2,1,0:T(8,128)(2,1)S(1)}, bf16[4,3,128,128]{3,2,1,0:T(8,128)(2,1)S(1)}, u32[]{:S(2)}, u32[]{:S(2)}) collective-permute-start(bf16[4,3,128,128]{3,2,1,0:T(8,128)(2,1)S(1)} %get-tuple-element.63), channel_id=1, source_target_pairs={{0,4},{4,0},{8,12},{12,8},{16,20},{20,16},{24,28},{28,24},{1,5},{5... | collective-permute-start | bytes 1179656 | tf_op jit(solution)/shard_map/ppermute | solution.py:382
  88.4 35.4 %collective-permute-start.15 = (bf16[4,3,128,128]{3,2,1,0:T(8,128)(2,1)S(1)}, bf16[4,3,128,128]{3,2,1,0:T(8,128)(2,1)S(1)}, u32[]{:S(2)}, u32[]{:S(2)}) collective-permute-start(bf16[4,3,128,128]{3,2,1,0:T(8,128)(2,1)S(1)} %get-tuple-element.93), channel_id=1, source_target_pairs={{0,4},{4,0},{8,12},{12,8},{16,20},{20,16},{24,28},{28,24},{1,5},{5... | collective-permute-start | bytes 1179656 | tf_op jit(solution)/shard_map/ppermute | solution.py:382
  89.4 30.6 %collective-permute-start.33 = (bf16[384,256]{1,0:T(8,128)(2,1)S(1)}, bf16[384,256]{1,0:T(8,128)(2,1)S(1)}, u32[]{:S(2)}, u32[]{:S(2)}) collective-permute-start(bf16[384,256]{1,0:T(8,128)(2,1)S(1)} %get-tuple-element.86), channel_id=1, source_target_pairs={{0,24},{4,28},{8,0},{12,4},{16,8},{20,12},{24,16},{28,20},{1,25},{... | collective-permute-start | bytes 589832 | tf_op jit(solution)/shard_map/ppermute | solution.py:406
  91.5 29.3 %collective-permute-start.34 = (bf16[384,256]{1,0:T(8,128)(2,1)S(1)}, bf16[384,256]{1,0:T(8,128)(2,1)S(1)}, u32[]{:S(2)}, u32[]{:S(2)}) collective-permute-start(bf16[384,256]{1,0:T(8,128)(2,1)S(1)} %get-tuple-element.87), channel_id=1, source_target_pairs={{0,28},{4,24},{8,4},{12,0},{16,12},{20,8},{24,20},{28,16},{1,29},{... | collective-permute-start | bytes 589832 | tf_op jit(solution)/shard_map/ppermute | solution.py:406
  111.7 23.4 %collective-permute-start.26 = (bf16[384,384]{1,0:T(8,128)(2,1)S(1)}, bf16[384,384]{1,0:T(8,128)(2,1)S(1)}, u32[]{:S(2)}, u32[]{:S(2)}) collective-permute-start(bf16[384,384]{1,0:T(8,128)(2,1)S(1)} %get-tuple-element.78), channel_id=1, source_target_pairs={{0,16},{4,20},{8,24},{12,28},{16,0},{20,4},{24,8},{28,12},{1,17},{... | collective-permute-start | bytes 884744 | tf_op jit(solution)/shard_map/ppermute | solution.py:406
  119.5 32.2 %collective-permute-start.27 = (bf16[384,384]{1,0:T(8,128)(2,1)S(1)}, bf16[384,384]{1,0:T(8,128)(2,1)S(1)}, u32[]{:S(2)}, u32[]{:S(2)}) collective-permute-start(bf16[384,384]{1,0:T(8,128)(2,1)S(1)} %get-tuple-element.79), channel_id=1, source_target_pairs={{0,20},{4,16},{8,28},{12,24},{16,4},{20,0},{24,12},{28,8},{1,21},{... | collective-permute-start | bytes 884744 | tf_op jit(solution)/shard_map/ppermute | solution.py:406
  120.0 40.3 %collective-permute-start.28 = (bf16[384,384]{1,0:T(8,128)(2,1)S(1)}, bf16[384,384]{1,0:T(8,128)(2,1)S(1)}, u32[]{:S(2)}, u32[]{:S(2)}) collective-permute-start(bf16[384,384]{1,0:T(8,128)(2,1)S(1)} %get-tuple-element.80), channel_id=1, source_target_pairs={{0,8},{4,12},{8,16},{12,20},{16,24},{20,28},{24,0},{28,4},{1,9},{5... | collective-permute-start | bytes 884744 | tf_op jit(solution)/shard_map/ppermute | solution.py:406
  120.8 52.2 %collective-permute-start.29 = (bf16[384,384]{1,0:T(8,128)(2,1)S(1)}, bf16[384,384]{1,0:T(8,128)(2,1)S(1)}, u32[]{:S(2)}, u32[]{:S(2)}) collective-permute-start(bf16[384,384]{1,0:T(8,128)(2,1)S(1)} %get-tuple-element.81), channel_id=1, source_target_pairs={{0,12},{4,8},{8,20},{12,16},{16,28},{20,24},{24,4},{28,0},{1,13},{... | collective-permute-start | bytes 884744 | tf_op jit(solution)/shard_map/ppermute | solution.py:406
  123.9 9.5 %collective-permute-start.35 = (bf16[384,256]{1,0:T(8,128)(2,1)S(1)}, bf16[384,256]{1,0:T(8,128)(2,1)S(1)}, u32[]{:S(2)}, u32[]{:S(2)}) collective-permute-start(bf16[384,256]{1,0:T(8,128)(2,1)S(1)} %get-tuple-element.59), channel_id=1, source_target_pairs={{0,4},{4,0},{8,12},{12,8},{16,20},{20,16},{24,28},{28,24},{1,5},{5... | collective-permute-start | bytes 589832 | tf_op jit(solution)/shard_map/ppermute | solution.py:406
  133.4 39.6 %collective-permute-start.30 = (bf16[384,384]{1,0:T(8,128)(2,1)S(1)}, bf16[384,384]{1,0:T(8,128)(2,1)S(1)}, u32[]{:S(2)}, u32[]{:S(2)}) collective-permute-start(bf16[384,384]{1,0:T(8,128)(2,1)S(1)} %get-tuple-element.82), channel_id=1, source_target_pairs={{0,24},{4,28},{8,0},{12,4},{16,8},{20,12},{24,16},{28,20},{1,25},{... | collective-permute-start | bytes 884744 | tf_op jit(solution)/shard_map/ppermute | solution.py:406
  135.0 40.8 %collective-permute-start.31 = (bf16[384,384]{1,0:T(8,128)(2,1)S(1)}, bf16[384,384]{1,0:T(8,128)(2,1)S(1)}, u32[]{:S(2)}, u32[]{:S(2)}) collective-permute-start(bf16[384,384]{1,0:T(8,128)(2,1)S(1)} %get-tuple-element.83), channel_id=1, source_target_pairs={{0,28},{4,24},{8,4},{12,0},{16,12},{20,8},{24,20},{28,16},{1,29},{... | collective-permute-start | bytes 884744 | tf_op jit(solution)/shard_map/ppermute | solution.py:406
  151.6 25.7 %collective-permute-start.32 = (bf16[384,384]{1,0:T(8,128)(2,1)S(1)}, bf16[384,384]{1,0:T(8,128)(2,1)S(1)}, u32[]{:S(2)}, u32[]{:S(2)}) collective-permute-start(bf16[384,384]{1,0:T(8,128)(2,1)S(1)} %get-tuple-element.84), channel_id=1, source_target_pairs={{0,4},{4,0},{8,12},{12,8},{16,20},{20,16},{24,28},{28,24},{1,5},{5... | collective-permute-start | bytes 884744 | tf_op jit(solution)/shard_map/ppermute | solution.py:406
  160.3 25.3 %collective-permute-start.16 = (bf16[384,384]{1,0:T(8,128)(2,1)S(1)}, bf16[384,384]{1,0:T(8,128)(2,1)S(1)}, u32[]{:S(2)}, u32[]{:S(2)}) collective-permute-start(bf16[384,384]{1,0:T(8,128)(2,1)S(1)} %get-tuple-element.67), channel_id=1, source_target_pairs={{0,16},{4,20},{8,24},{12,28},{16,0},{20,4},{24,8},{28,12},{1,17},{... | collective-permute-start | bytes 884744 | tf_op jit(solution)/shard_map/ppermute | solution.py:406
  173.0 29.1 %collective-permute-start.17 = (bf16[384,384]{1,0:T(8,128)(2,1)S(1)}, bf16[384,384]{1,0:T(8,128)(2,1)S(1)}, u32[]{:S(2)}, u32[]{:S(2)}) collective-permute-start(bf16[384,384]{1,0:T(8,128)(2,1)S(1)} %get-tuple-element.68), channel_id=1, source_target_pairs={{0,20},{4,16},{8,28},{12,24},{16,4},{20,0},{24,12},{28,8},{1,21},{... | collective-permute-start | bytes 884744 | tf_op jit(solution)/shard_map/ppermute | solution.py:406
  173.0 38.0 %collective-permute-start.18 = (bf16[384,384]{1,0:T(8,128)(2,1)S(1)}, bf16[384,384]{1,0:T(8,128)(2,1)S(1)}, u32[]{:S(2)}, u32[]{:S(2)}) collective-permute-start(bf16[384,384]{1,0:T(8,128)(2,1)S(1)} %get-tuple-element.69), channel_id=1, source_target_pairs={{0,8},{4,12},{8,16},{12,20},{16,24},{20,28},{24,0},{28,4},{1,9},{5... | collective-permute-start | bytes 884744 | tf_op jit(solution)/shard_map/ppermute | solution.py:406
  175.8 41.4 %collective-permute-start.19 = (bf16[384,384]{1,0:T(8,128)(2,1)S(1)}, bf16[384,384]{1,0:T(8,128)(2,1)S(1)}, u32[]{:S(2)}, u32[]{:S(2)}) collective-permute-start(bf16[384,384]{1,0:T(8,128)(2,1)S(1)} %get-tuple-element.70), channel_id=1, source_target_pairs={{0,12},{4,8},{8,20},{12,16},{16,28},{20,24},{24,4},{28,0},{1,13},{... | collective-permute-start | bytes 884744 | tf_op jit(solution)/shard_map/ppermute | solution.py:406
  177.4 39.9 %collective-permute-start.20 = (bf16[384,384]{1,0:T(8,128)(2,1)S(1)}, bf16[384,384]{1,0:T(8,128)(2,1)S(1)}, u32[]{:S(2)}, u32[]{:S(2)}) collective-permute-start(bf16[384,384]{1,0:T(8,128)(2,1)S(1)} %get-tuple-element.71), channel_id=1, source_target_pairs={{0,24},{4,28},{8,0},{12,4},{16,8},{20,12},{24,16},{28,20},{1,25},{... | collective-permute-start | bytes 884744 | tf_op jit(solution)/shard_map/ppermute | solution.py:406
  185.6 31.7 %collective-permute-start.21 = (bf16[384,384]{1,0:T(8,128)(2,1)S(1)}, bf16[384,384]{1,0:T(8,128)(2,1)S(1)}, u32[]{:S(2)}, u32[]{:S(2)}) collective-permute-start(bf16[384,384]{1,0:T(8,128)(2,1)S(1)} %get-tuple-element.72), channel_id=1, source_target_pairs={{0,28},{4,24},{8,4},{12,0},{16,12},{20,8},{24,20},{28,16},{1,29},{... | collective-permute-start | bytes 884744 | tf_op jit(solution)/shard_map/ppermute | solution.py:406
  202.1 15.3 %collective-permute-start.22 = (bf16[384,384]{1,0:T(8,128)(2,1)S(1)}, bf16[384,384]{1,0:T(8,128)(2,1)S(1)}, u32[]{:S(2)}, u32[]{:S(2)}) collective-permute-start(bf16[384,384]{1,0:T(8,128)(2,1)S(1)} %get-tuple-element.73), channel_id=1, source_target_pairs={{0,4},{4,0},{8,12},{12,8},{16,20},{20,16},{24,28},{28,24},{1,5},{5... | collective-permute-start | bytes 884744 | tf_op jit(solution)/shard_map/ppermute | solution.py:406

commit v7 on v6

--- a/solution.py
+++ b/solution.py
@@ -19,13 +19,12 @@
     ("message", 0, 1): [("group", 1)],
     ("message", 1, 1): [("message", 0, 2)],
     ("message", 1, 2): [("message", 0, 3)],
-    ("message", 1, 3): [("message", 0, 4), ("mixed", 0)],
+    ("message", 1, 3): [("message", 0, 4)],
     ("message", 2, 1): [("message", 1, 2)],
-    ("message", 2, 2): [("message", 1, 3), ("mixed", 0)],
-    ("message", 2, 3): [("message", 1, 4), ("sent", 0, 2)],
-    ("mixed", 0): [("message", 1, 2), ("message", 2, 1)],
-    ("message", 1, 4): [("sent", 0, 1)],
-    ("mixed", 1): [("sent", 0, 1), ("sent", 0, 2), ("sent", 0, 3), ("sent", 0, 4)],
+    ("message", 2, 2): [("message", 1, 3)],
+    ("message", 2, 3): [("message", 1, 4), ("mixed", 0)],
+    ("mixed", 0): [("message", 1, 3), ("message", 2, 2)],
+    ("message", 1, 4): [("mixed", 0)],
 }
 
 

time: 224 us -> 201 us (0.90)
  starting transfers between devices: 96.6 us -> 74.2 us
    ppermute x21, starting transfers between devices: 75.2 us -> 54.8 us  [sent(): lax.ppermute(self.hold(self.get('mixed', c)[k], 'sent', c, k), 'seq', pairs)]
  transfers between devices with their start and end apart: 36 -> 36, of which waited for: 15 -> 14; matrix products, arithmetic and copies ran while one was open for 3% -> 4% of each run, Pallas kernels for 16% -> 18%
where the time goes in v7:
time: 201 us; the launch traced here: 197 us
  starting transfers between devices  74.2 us (37%)
  waiting for transfers between devices  73.7 us (37%)
  Pallas kernels  41.3 us (21%)
  other arithmetic  7.65 us (4%)
    ppermute x21, starting transfers between devices, sent(): lax.ppermute(self.hold(self.get('mixed', c)[k], 'sent', c, k), 'seq', pairs)  54.8 us
    ppermute x21, waiting for transfers between devices, sent(): lax.ppermute(self.hold(self.get('mixed', c)[k], 'sent', c, k), 'seq', pairs)  54.6 us
    pallas_call x3, Pallas kernels, attend(): pl.pallas_call(functools.partial(attend_body, n, spans, order), in_specs=...  25.5 us
    ppermute x12, waiting for transfers between devices, prefix(): return lax.ppermute(self.get('message', c, s), 'seq', pairs)  17.6 us
    ppermute x12, starting transfers between devices, prefix(): return lax.ppermute(self.get('message', c, s), 'seq', pairs)  14.7 us
    pallas_call x2, Pallas kernels, local_states(): pl.pallas_call(functools.partial(local_body, n, widths, swaps), in_specs=...  8.47 us
    pallas_call x3, Pallas kernels, put(): pl.pallas_call(functools.partial(put_body, n, order), in_specs=[pl.BlockS...  7.33 us
    convert_element_type x10, other arithmetic, message(): return self.hold(value.astype(jnp.bfloat16), 'message', c, s)  4.88 us
  transfers between devices with their start and end apart: 36, of which 14 were waited for; matrix products, arithmetic and copies ran while one was open for 4% of the time, Pallas kernels for 18%

profile of v7, /device:TPU:8, one launch (start us, length us, event | category | flops | bytes accessed | tf_op | source)
XLA Modules:
  0.0 197.3 jit_solution(12256833835985032742)
XLA Ops:
  0.1 3.4 %local.3 = (f32[4,2,128,128]{3,2,1,0:T(8,128)S(1)}, bf16[4,2,128,128]{3,2,1,0:T(8,128)(2,1)S(1)}) custom-call(s32[2]{0:T(128)S(1)} %pad_add_fusion.place, s32[1]{0:T(128)} %constant.38.clone.1.low, bf16[384,8192]{1,0:T(8,128)(2,1)} %keys.9, bf16[384,8192]{1,0:T(8,128)(2,1)} %values.9), custom_call_target="tpu_custom_call" | custom-call | flops 201326592 | bytes 3145728 | tf_op jit(solution)/shard_map/local/pallas_call | solution.py:98
  3.5 1.6 collective-permute-start.2
  5.1 5.0 %local.2 = (f32[4,3,128,128]{3,2,1,0:T(8,128)S(1)}, f32[4,3,128,128]{3,2,1,0:T(8,128)S(1)}, bf16[4,3,128,128]{3,2,1,0:T(8,128)(2,1)S(1)}, bf16[4,3,128,128]{3,2,1,0:T(8,128)(2,1)S(1)}) custom-call(s32[2]{0:T(128)S(1)} %pad_add_fusion.place, s32[1]{0:T(128)} %constant.37.clone.1.low, bf16[384,8192]{1,0:T(8,128)(2,1)} %keys.9, bf16[384,8192]{1,0:T(8,128)(2,1)} %values.9), custom_call_target="tpu_custom_call" | custom-call | flops 603979776 | bytes 9437184 | tf_op jit(solution)/shard_map/local/pallas_call | solution.py:98
  10.1 1.5 collective-permute-done.2
  11.7 1.3 collective-permute-start.3
  13.0 1.6 collective-permute-start.1
  14.6 6.2 %collective-permute-done.3 = bf16[4,2,128,128]{3,2,1,0:T(8,128)(2,1)S(1)} collective-permute-done((bf16[4,2,128,128]{3,2,1,0:T(8,128)(2,1)S(1)}, bf16[4,2,128,128]{3,2,1,0:T(8,128)(2,1)S(1)}, u32[]{:S(2)}, u32[]{:S(2)}) %collective-permute-start.3) | collective-permute-done | bytes 262176 | tf_op jit(solution)/shard_map/ppermute | solution.py:381
  20.7 0.8 add_convert_fusion.5
  21.5 2.1 %collective-permute-start.5 = (bf16[4,2,128,128]{3,2,1,0:T(8,128)(2,1)}, bf16[4,2,128,128]{3,2,1,0:T(8,128)(2,1)}, u32[]{:S(2)}, u32[]{:S(2)}) collective-permute-start(bf16[4,2,128,128]{3,2,1,0:T(8,128)(2,1)} %add_convert_fusion.5), channel_id=1, source_target_pairs={{8,16},{12,20},{9,17},{13,21},{10,18},{14,22},{11,19},{15,23}} | collective-permute-start | bytes 786440 | tf_op jit(solution)/shard_map/ppermute | solution.py:381
  23.7 0.8 fusion.7
  24.5 1.3 collective-permute-start.4
  25.8 1.6 collective-permute-start
  27.4 1.1 add_convert_fusion.4
  29.2 6.5 %collective-permute-done.4 = bf16[4,3,128,128]{3,2,1,0:T(8,128)(2,1)} collective-permute-done((bf16[4,3,128,128]{3,2,1,0:T(8,128)(2,1)}, bf16[4,3,128,128]{3,2,1,0:T(8,128)(2,1)}, u32[]{:S(2)}, u32[]{:S(2)}) %collective-permute-start.4) | collective-permute-done | bytes 393248 | tf_op jit(solution)/shard_map/ppermute | solution.py:381
  35.8 1.2 add_convert_fusion.3
  36.9 1.3 collective-permute-start.7
  38.4 1.3 collective-permute-start.6
  39.7 1.4 fusion.5
  41.0 1.6 collective-permute-start.11
  42.6 1.5 collective-permute-done.7
  45.0 3.4 %collective-permute-done.6 = bf16[4,3,128,128]{3,2,1,0:T(8,128)(2,1)S(1)} collective-permute-done((bf16[4,3,128,128]{3,2,1,0:T(8,128)(2,1)S(1)}, bf16[4,3,128,128]{3,2,1,0:T(8,128)(2,1)S(1)}, u32[]{:S(2)}, u32[]{:S(2)}) %collective-permute-start.6) | collective-permute-done | bytes 393248 | tf_op jit(solution)/shard_map/ppermute | solution.py:381
  48.5 1.6 collective-permute-start.9
  50.2 8.5 %attend.3 = (bf16[384,256]{1,0:T(8,128)(2,1)S(1)}, bf16[384,256]{1,0:T(8,128)(2,1)S(1)}, bf16[384,256]{1,0:T(8,128)(2,1)S(1)}, bf16[384,256]{1,0:T(8,128)(2,1)S(...) custom-call(s32[2]{0:T(128)S(1)} %pad_add_fusion.place, ...), custom_call_target="tpu_custom_call" | custom-call | flops 1409286144 | bytes 6291456 | tf_op jit(solution)/shard_map/attend/pallas_call | solution.py:222
  58.8 1.3 fusion.1
  61.1 3.9 %collective-permute-start.30 = (bf16[384,256]{1,0:T(8,128)(2,1)S(1)}, bf16[384,256]{1,0:T(8,128)(2,1)S(1)}, u32[]{:S(2)}, u32[]{:S(2)}) collective-permute-start(bf16[384,256]{1,0:T(8,128)(2,1)S(1)} %get-tuple-element.81), channel_id=1, source_target_pairs={{0,20},{4,16},{8,28},{12,24},{16,4},{20,0},{24,12},{28,8},{1,21},{... | collective-permute-start | bytes 589832 | tf_op jit(solution)/shard_map/ppermute | solution.py:405
  65.8 1.6 collective-permute-start.13
  67.3 5.4 %collective-permute-start.31 = (bf16[384,256]{1,0:T(8,128)(2,1)S(1)}, bf16[384,256]{1,0:T(8,128)(2,1)S(1)}, u32[]{:S(2)}, u32[]{:S(2)}) collective-permute-start(bf16[384,256]{1,0:T(8,128)(2,1)S(1)} %get-tuple-element.82), channel_id=1, source_target_pairs={{0,8},{4,12},{8,16},{12,20},{16,24},{20,28},{24,0},{28,4},{1,9},{5... | collective-permute-start | bytes 589832 | tf_op jit(solution)/shard_map/ppermute | solution.py:405
  72.8 6.2 %collective-permute-start.32 = (bf16[384,256]{1,0:T(8,128)(2,1)S(1)}, bf16[384,256]{1,0:T(8,128)(2,1)S(1)}, u32[]{:S(2)}, u32[]{:S(2)}) collective-permute-start(bf16[384,256]{1,0:T(8,128)(2,1)S(1)} %get-tuple-element.83), channel_id=1, source_target_pairs={{0,12},{4,8},{8,20},{12,16},{16,28},{20,24},{24,4},{28,0},{1,13},{... | collective-permute-start | bytes 589832 | tf_op jit(solution)/shard_map/ppermute | solution.py:405
  79.0 7.3 %collective-permute-start.33 = (bf16[384,256]{1,0:T(8,128)(2,1)S(1)}, bf16[384,256]{1,0:T(8,128)(2,1)S(1)}, u32[]{:S(2)}, u32[]{:S(2)}) collective-permute-start(bf16[384,256]{1,0:T(8,128)(2,1)S(1)} %get-tuple-element.84), channel_id=1, source_target_pairs={{0,24},{4,28},{8,0},{12,4},{16,8},{20,12},{24,16},{28,20},{1,25},{... | collective-permute-start | bytes 589832 | tf_op jit(solution)/shard_map/ppermute | solution.py:405
  86.3 8.5 %attend.5 = (bf16[384,384]{1,0:T(8,128)(2,1)S(1)}, bf16[384,384]{1,0:T(8,128)(2,1)S(1)}, bf16[384,384]{1,0:T(8,128)(2,1)S(1)}, bf16[384,384]{1,0:T(8,128)(2,1)S(...) custom-call(s32[2]{0:T(128)S(1)} %pad_add_fusion.place, ...), custom_call_target="tpu_custom_call" | custom-call | flops 2113929216 | bytes 9437184 | tf_op jit(solution)/shard_map/attend/pallas_call | solution.py:222
  94.9 3.5 %collective-permute-done.32.refs_4_ = bf16[384,256]{1,0:T(8,128)(2,1)S(1)} collective-permute-done((bf16[384,256]{1,0:T(8,128)(2,1)S(1)}, bf16[384,256]{1,0:T(8,128)(2,1)S(1)}, u32[]{:S(2)}, u32[]{:S(2)}) %collective-permute-start.32) | collective-permute-done | bytes 196640 | tf_op jit(solution)/shard_map/ppermute | solution.py:405
  98.7 3.8 %collective-permute-start.24 = (bf16[384,384]{1,0:T(8,128)(2,1)S(1)}, bf16[384,384]{1,0:T(8,128)(2,1)S(1)}, u32[]{:S(2)}, u32[]{:S(2)}) collective-permute-start(bf16[384,384]{1,0:T(8,128)(2,1)S(1)} %get-tuple-element.74), channel_id=1, source_target_pairs={{0,8},{4,12},{8,16},{12,20},{16,24},{20,28},{24,0},{28,4},{1,9},{5... | collective-permute-start | bytes 884744 | tf_op jit(solution)/shard_map/ppermute | solution.py:405
  102.5 12.7 %collective-permute-done.34.refs_6_ = bf16[384,256]{1,0:T(8,128)(2,1)S(1)} collective-permute-done((bf16[384,256]{1,0:T(8,128)(2,1)S(1)}, bf16[384,256]{1,0:T(8,128)(2,1)S(1)}, u32[]{:S(2)}, u32[]{:S(2)}) %collective-permute-start.34) | collective-permute-done | bytes 196640 | tf_op jit(solution)/shard_map/ppermute | solution.py:405
  115.3 8.4 %attend.4 = (bf16[384,384]{1,0:T(8,128)(2,1)S(1)}, bf16[384,384]{1,0:T(8,128)(2,1)S(1)}, bf16[384,384]{1,0:T(8,128)(2,1)S(1)}, bf16[384,384]{1,0:T(8,128)(2,1)S(...) custom-call(s32[2]{0:T(128)S(1)} %pad_add_fusion.place, ...), custom_call_target="tpu_custom_call" | custom-call | flops 2113929216 | bytes 9437184 | tf_op jit(solution)/shard_map/attend/pallas_call | solution.py:222
  124.1 3.2 %collective-permute-start.26 = (bf16[384,384]{1,0:T(8,128)(2,1)S(1)}, bf16[384,384]{1,0:T(8,128)(2,1)S(1)}, u32[]{:S(2)}, u32[]{:S(2)}) collective-permute-start(bf16[384,384]{1,0:T(8,128)(2,1)S(1)} %get-tuple-element.76), channel_id=1, source_target_pairs={{0,24},{4,28},{8,0},{12,4},{16,8},{20,12},{24,16},{28,20},{1,25},{... | collective-permute-start | bytes 884744 | tf_op jit(solution)/shard_map/ppermute | solution.py:405
  127.3 1.0 collective-permute-start.27
  128.8 7.1 %collective-permute-done.24.refs_3_ = bf16[384,384]{1,0:T(8,128)(2,1)S(1)} collective-permute-done((bf16[384,384]{1,0:T(8,128)(2,1)S(1)}, bf16[384,384]{1,0:T(8,128)(2,1)S(1)}, u32[]{:S(2)}, u32[]{:S(2)}) %collective-permute-start.24) | collective-permute-done | bytes 294944 | tf_op jit(solution)/shard_map/ppermute | solution.py:405
  135.9 12.7 %collective-permute-done.25.refs_4_ = bf16[384,384]{1,0:T(8,128)(2,1)S(1)} collective-permute-done((bf16[384,384]{1,0:T(8,128)(2,1)S(1)}, bf16[384,384]{1,0:T(8,128)(2,1)S(1)}, u32[]{:S(2)}, u32[]{:S(2)}) %collective-permute-start.25) | collective-permute-done | bytes 294944 | tf_op jit(solution)/shard_map/ppermute | solution.py:405
  148.6 4.4 %collective-permute-start.16 = (bf16[384,384]{1,0:T(8,128)(2,1)S(1)}, bf16[384,384]{1,0:T(8,128)(2,1)S(1)}, u32[]{:S(2)}, u32[]{:S(2)}) collective-permute-start(bf16[384,384]{1,0:T(8,128)(2,1)S(1)} %get-tuple-element.66), channel_id=1, source_target_pairs={{0,8},{4,12},{8,16},{12,20},{16,24},{20,28},{24,0},{28,4},{1,9},{5... | collective-permute-start | bytes 884744 | tf_op jit(solution)/shard_map/ppermute | solution.py:405
  153.1 1.0 collective-permute-start.18
  154.0 7.3 %collective-permute-done.14.refs_1_ = bf16[384,384]{1,0:T(8,128)(2,1)S(1)} collective-permute-done((bf16[384,384]{1,0:T(8,128)(2,1)S(1)}, bf16[384,384]{1,0:T(8,128)(2,1)S(1)}, u32[]{:S(2)}, u32[]{:S(2)}) %collective-permute-start.14) | collective-permute-done | bytes 294944 | tf_op jit(solution)/shard_map/ppermute | solution.py:405
  161.3 17.6 %collective-permute-start.19 = (bf16[384,384]{1,0:T(8,128)(2,1)S(1)}, bf16[384,384]{1,0:T(8,128)(2,1)S(1)}, u32[]{:S(2)}, u32[]{:S(2)}) collective-permute-start(bf16[384,384]{1,0:T(8,128)(2,1)S(1)} %get-tuple-element.69), channel_id=1, source_target_pairs={{0,28},{4,24},{8,4},{12,0},{16,12},{20,8},{24,20},{28,16},{1,29},{... | collective-permute-start | bytes 884744 | tf_op jit(solution)/shard_map/ppermute | solution.py:405
  178.9 2.3 %put.3 = (bf16[3072,1024]{1,0:T(8,128)(2,1)}, s32[2]{0:T(128)}) custom-call(s32[2]{0:T(128)S(1)} %pad_add_fusion.place, s32[1]{0:T(128)} %constant.38.clone.1.low, bf16[384,256]{1,0:T(8,128)(2,1)S(1)} %get-tuple-element.79.refs_0_, bf16[384,256]{1,0:T(8,128)(2,1)S(1)} %collective-permute-done.29.refs_1_, ...), custom_call_target="tpu_custom_call" | custom-call | tf_op jit(solution)/shard_map/put/pallas_call | solution.py:274
  181.2 2.5 %put.4 = (bf16[3072,1024]{1,0:T(8,128)(2,1)}, s32[2]{0:T(128)}) custom-call(s32[2]{0:T(128)S(1)} %pad_add_fusion.place, s32[1]{0:T(128)} %constant.37.clone.1.low, bf16[384,384]{1,0:T(8,128)(2,1)S(1)} %get-tuple-element.71.refs_0_, bf16[384,384]{1,0:T(8,128)(2,1)S(1)} %collective-permute-done.22.refs_1_, ...), custom_call_target="tpu_custom_call", output_to_operand_aliasing={{0}: (10, {})} | custom-call | tf_op jit(solution)/shard_map/put/pallas_call | solution.py:274
  183.8 2.9 %collective-permute-done.16.refs_3_ = bf16[384,384]{1,0:T(8,128)(2,1)S(1)} collective-permute-done((bf16[384,384]{1,0:T(8,128)(2,1)S(1)}, bf16[384,384]{1,0:T(8,128)(2,1)S(1)}, u32[]{:S(2)}, u32[]{:S(2)}) %collective-permute-start.16) | collective-permute-done | bytes 294944 | tf_op jit(solution)/shard_map/ppermute | solution.py:405
  186.6 6.1 %collective-permute-done.17.refs_4_ = bf16[384,384]{1,0:T(8,128)(2,1)S(1)} collective-permute-done((bf16[384,384]{1,0:T(8,128)(2,1)S(1)}, bf16[384,384]{1,0:T(8,128)(2,1)S(1)}, u32[]{:S(2)}, u32[]{:S(2)}) %collective-permute-start.17) | collective-permute-done | bytes 294944 | tf_op jit(solution)/shard_map/ppermute | solution.py:405
  192.8 1.8 collective-permute-done.19.refs_6_
  194.6 2.5 %put.5 = (bf16[3072,1024]{1,0:T(8,128)(2,1)}, s32[2]{0:T(128)}) custom-call(s32[2]{0:T(128)S(1)} %pad_add_fusion.place, s32[1]{0:T(128)} %constant.36.clone.1.low, bf16[384,384]{1,0:T(8,128)(2,1)S(1)} %get-tuple-element.63.refs_0_, bf16[384,384]{1,0:T(8,128)(2,1)S(1)} %collective-permute-done.14.refs_1_, ...), custom_call_target="tpu_custom_call", output_to_operand_aliasing={{0}: (10, {})} | custom-call | tf_op jit(solution)/shard_map/put/pallas_call | solution.py:274
  (51 shorter events, 5.0 us)
Async XLA Ops:
  3.5 8.1 %collective-permute-start.2 = (bf16[4,2,128,128]{3,2,1,0:T(8,128)(2,1)S(1)}, bf16[4,2,128,128]{3,2,1,0:T(8,128)(2,1)S(1)}, u32[]{:S(2)}, u32[]{:S(2)}) collective-permute-start(bf16[4,2,128,128]{3,2,1,0:T(8,128)(2,1)S(1)} %get-tuple-element.52), channel_id=1, source_target_pairs={{0,4},{4,0},{8,12},{12,8},{16,20},{20,16},{24,28},{28,24},{1,5},{5... | collective-permute-start | bytes 786440 | tf_op jit(solution)/shard_map/ppermute | solution.py:354
  11.6 12.9 %copy-start.1 = (bf16[4,2,128,128]{3,2,1,0:T(8,128)(2,1)}, bf16[4,2,128,128]{3,2,1,0:T(8,128)(2,1)S(1)}, u32[]{:S(2)}) copy-start(bf16[4,2,128,128]{3,2,1,0:T(8,128)(2,1)S(1)} %collective-permute-done.2) | copy-start | bytes 786436
  11.7 9.1 %collective-permute-start.3 = (bf16[4,2,128,128]{3,2,1,0:T(8,128)(2,1)S(1)}, bf16[4,2,128,128]{3,2,1,0:T(8,128)(2,1)S(1)}, u32[]{:S(2)}, u32[]{:S(2)}) collective-permute-start(bf16[4,2,128,128]{3,2,1,0:T(8,128)(2,1)S(1)} %fusion.8), channel_id=1, source_target_pairs={{0,8},{4,12},{1,9},{5,13},{2,10},{6,14},{3,11},{7,15}} | collective-permute-start | bytes 786440 | tf_op jit(solution)/shard_map/ppermute | solution.py:381
  13.0 10.7 %collective-permute-start.1 = (bf16[4,3,128,128]{3,2,1,0:T(8,128)(2,1)S(1)}, bf16[4,3,128,128]{3,2,1,0:T(8,128)(2,1)S(1)}, u32[]{:S(2)}, u32[]{:S(2)}) collective-permute-start(bf16[4,3,128,128]{3,2,1,0:T(8,128)(2,1)S(1)} %get-tuple-element.50), channel_id=1, source_target_pairs={{0,4},{4,0},{8,12},{12,8},{16,20},{20,16},{24,28},{28,24},{1,5},{5... | collective-permute-start | bytes 1179656 | tf_op jit(solution)/shard_map/ppermute | solution.py:354
  20.7 2.9 %copy-start.2 = (bf16[4,2,128,128]{3,2,1,0:T(8,128)(2,1)}, bf16[4,2,128,128]{3,2,1,0:T(8,128)(2,1)S(1)}, u32[]{:S(2)}) copy-start(bf16[4,2,128,128]{3,2,1,0:T(8,128)(2,1)S(1)} %collective-permute-done.3) | copy-start | bytes 786436
  21.5 28.7 %copy-start = (f32[8192]{0:T(1024)S(1)}, f32[8192]{0:T(1024)}, u32[]{:S(2)}) copy-start(f32[8192]{0:T(1024)} %param.7) | copy-start | bytes 98308
  21.5 5.9 %collective-permute-start.5 = (bf16[4,2,128,128]{3,2,1,0:T(8,128)(2,1)}, bf16[4,2,128,128]{3,2,1,0:T(8,128)(2,1)}, u32[]{:S(2)}, u32[]{:S(2)}) collective-permute-start(bf16[4,2,128,128]{3,2,1,0:T(8,128)(2,1)} %add_convert_fusion.5), channel_id=1, source_target_pairs={{8,16},{12,20},{9,17},{13,21},{10,18},{14,22},{11,19},{15,23}} | collective-permute-start | bytes 786440 | tf_op jit(solution)/shard_map/ppermute | solution.py:381
  24.5 11.2 %collective-permute-start.4 = (bf16[4,3,128,128]{3,2,1,0:T(8,128)(2,1)}, bf16[4,3,128,128]{3,2,1,0:T(8,128)(2,1)}, u32[]{:S(2)}, u32[]{:S(2)}) collective-permute-start(bf16[4,3,128,128]{3,2,1,0:T(8,128)(2,1)} %fusion.7), channel_id=1, source_target_pairs={{0,8},{4,12},{1,9},{5,13},{2,10},{6,14},{3,11},{7,15}} | collective-permute-start | bytes 1179656 | tf_op jit(solution)/shard_map/ppermute | solution.py:381
  25.8 12.5 %collective-permute-start = (bf16[4,3,128,128]{3,2,1,0:T(8,128)(2,1)S(1)}, bf16[4,3,128,128]{3,2,1,0:T(8,128)(2,1)S(1)}, u32[]{:S(2)}, u32[]{:S(2)}) collective-permute-start(bf16[4,3,128,128]{3,2,1,0:T(8,128)(2,1)S(1)} %get-tuple-element.48), channel_id=1, source_target_pairs={{0,4},{4,0},{8,12},{12,8},{16,20},{20,16},{24,28},{28,24},{1,5},{5... | collective-permute-start | bytes 1179656 | tf_op jit(solution)/shard_map/ppermute | solution.py:354
  28.5 11.1 %collective-permute-start.8 = (bf16[4,2,128,128]{3,2,1,0:T(8,128)(2,1)S(1)}, bf16[4,2,128,128]{3,2,1,0:T(8,128)(2,1)S(1)}, u32[]{:S(2)}, u32[]{:S(2)}) collective-permute-start(bf16[4,2,128,128]{3,2,1,0:T(8,128)(2,1)S(1)} %add_convert_fusion.4), channel_id=1, source_target_pairs={{16,24},{20,28},{17,25},{21,29},{18,26},{22,30},{19,27},{23,31}} | collective-permute-start | bytes 786440 | tf_op jit(solution)/shard_map/ppermute | solution.py:381
  36.9 7.2 %collective-permute-start.7 = (bf16[4,3,128,128]{3,2,1,0:T(8,128)(2,1)S(1)}, bf16[4,3,128,128]{3,2,1,0:T(8,128)(2,1)S(1)}, u32[]{:S(2)}, u32[]{:S(2)}) collective-permute-start(bf16[4,3,128,128]{3,2,1,0:T(8,128)(2,1)S(1)} %add_convert_fusion.3), channel_id=1, source_target_pairs={{8,16},{12,20},{9,17},{13,21},{10,18},{14,22},{11,19},{15,23}} | collective-permute-start | bytes 1179656 | tf_op jit(solution)/shard_map/ppermute | solution.py:381
  38.4 10.0 %collective-permute-start.6 = (bf16[4,3,128,128]{3,2,1,0:T(8,128)(2,1)S(1)}, bf16[4,3,128,128]{3,2,1,0:T(8,128)(2,1)S(1)}, u32[]{:S(2)}, u32[]{:S(2)}) collective-permute-start(bf16[4,3,128,128]{3,2,1,0:T(8,128)(2,1)S(1)} %fusion.6), channel_id=1, source_target_pairs={{0,8},{4,12},{1,9},{5,13},{2,10},{6,14},{3,11},{7,15}} | collective-permute-start | bytes 1179656 | tf_op jit(solution)/shard_map/ppermute | solution.py:381
  41.0 9.2 %collective-permute-start.11 = (bf16[4,2,128,128]{3,2,1,0:T(8,128)(2,1)S(1)}, bf16[4,2,128,128]{3,2,1,0:T(8,128)(2,1)S(1)}, u32[]{:S(2)}, u32[]{:S(2)}) collective-permute-start(bf16[4,2,128,128]{3,2,1,0:T(8,128)(2,1)S(1)} %get-tuple-element.94), channel_id=1, source_target_pairs={{0,4},{4,0},{8,12},{12,8},{16,20},{20,16},{24,28},{28,24},{1,5},{5... | collective-permute-start | bytes 786440 | tf_op jit(solution)/shard_map/ppermute | solution.py:381
  44.3 14.5 %collective-permute-start.10 = (bf16[4,3,128,128]{3,2,1,0:T(8,128)(2,1)S(1)}, bf16[4,3,128,128]{3,2,1,0:T(8,128)(2,1)S(1)}, u32[]{:S(2)}, u32[]{:S(2)}) collective-permute-start(bf16[4,3,128,128]{3,2,1,0:T(8,128)(2,1)S(1)} %add_convert_fusion.1), channel_id=1, source_target_pairs={{16,24},{20,28},{17,25},{21,29},{18,26},{22,30},{19,27},{23,31}} | collective-permute-start | bytes 1179656 | tf_op jit(solution)/shard_map/ppermute | solution.py:381
  48.5 11.6 %collective-permute-start.9 = (bf16[4,3,128,128]{3,2,1,0:T(8,128)(2,1)S(1)}, bf16[4,3,128,128]{3,2,1,0:T(8,128)(2,1)S(1)}, u32[]{:S(2)}, u32[]{:S(2)}) collective-permute-start(bf16[4,3,128,128]{3,2,1,0:T(8,128)(2,1)S(1)} %add_convert_fusion.2), channel_id=1, source_target_pairs={{8,16},{12,20},{9,17},{13,21},{10,18},{14,22},{11,19},{15,23}} | collective-permute-start | bytes 1179656 | tf_op jit(solution)/shard_map/ppermute | solution.py:381
  60.3 5.2 %collective-permute-start.12 = (bf16[4,3,128,128]{3,2,1,0:T(8,128)(2,1)S(1)}, bf16[4,3,128,128]{3,2,1,0:T(8,128)(2,1)S(1)}, u32[]{:S(2)}, u32[]{:S(2)}) collective-permute-start(bf16[4,3,128,128]{3,2,1,0:T(8,128)(2,1)S(1)} %add_convert_fusion), channel_id=1, source_target_pairs={{16,24},{20,28},{17,25},{21,29},{18,26},{22,30},{19,27},{23,31}} | collective-permute-start | bytes 1179656 | tf_op jit(solution)/shard_map/ppermute | solution.py:381
  61.0 11.8 %collective-permute-start.29 = (bf16[384,256]{1,0:T(8,128)(2,1)S(1)}, bf16[384,256]{1,0:T(8,128)(2,1)S(1)}, u32[]{:S(2)}, u32[]{:S(2)}) collective-permute-start(bf16[384,256]{1,0:T(8,128)(2,1)S(1)} %get-tuple-element.80), channel_id=1, source_target_pairs={{0,16},{4,20},{8,24},{12,28},{16,0},{20,4},{24,8},{28,12},{1,17},{... | collective-permute-start | bytes 589832 | tf_op jit(solution)/shard_map/ppermute | solution.py:405
  61.1 17.9 %collective-permute-start.30 = (bf16[384,256]{1,0:T(8,128)(2,1)S(1)}, bf16[384,256]{1,0:T(8,128)(2,1)S(1)}, u32[]{:S(2)}, u32[]{:S(2)}) collective-permute-start(bf16[384,256]{1,0:T(8,128)(2,1)S(1)} %get-tuple-element.81), channel_id=1, source_target_pairs={{0,20},{4,16},{8,28},{12,24},{16,4},{20,0},{24,12},{28,8},{1,21},{... | collective-permute-start | bytes 589832 | tf_op jit(solution)/shard_map/ppermute | solution.py:405
  64.9 21.4 %collective-permute-start.21 = (bf16[4,3,128,128]{3,2,1,0:T(8,128)(2,1)S(1)}, bf16[4,3,128,128]{3,2,1,0:T(8,128)(2,1)S(1)}, u32[]{:S(2)}, u32[]{:S(2)}) collective-permute-start(bf16[4,3,128,128]{3,2,1,0:T(8,128)(2,1)S(1)} %get-tuple-element.61), channel_id=1, source_target_pairs={{0,4},{4,0},{8,12},{12,8},{16,20},{20,16},{24,28},{28,24},{1,5},{5... | collective-permute-start | bytes 1179656 | tf_op jit(solution)/shard_map/ppermute | solution.py:381
  65.8 49.5 %collective-permute-start.13 = (bf16[4,3,128,128]{3,2,1,0:T(8,128)(2,1)S(1)}, bf16[4,3,128,128]{3,2,1,0:T(8,128)(2,1)S(1)}, u32[]{:S(2)}, u32[]{:S(2)}) collective-permute-start(bf16[4,3,128,128]{3,2,1,0:T(8,128)(2,1)S(1)} %get-tuple-element.91), channel_id=1, source_target_pairs={{0,4},{4,0},{8,12},{12,8},{16,20},{20,16},{24,28},{28,24},{1,5},{5... | collective-permute-start | bytes 1179656 | tf_op jit(solution)/shard_map/ppermute | solution.py:381
  67.3 27.4 %collective-permute-start.31 = (bf16[384,256]{1,0:T(8,128)(2,1)S(1)}, bf16[384,256]{1,0:T(8,128)(2,1)S(1)}, u32[]{:S(2)}, u32[]{:S(2)}) collective-permute-start(bf16[384,256]{1,0:T(8,128)(2,1)S(1)} %get-tuple-element.82), channel_id=1, source_target_pairs={{0,8},{4,12},{8,16},{12,20},{16,24},{20,28},{24,0},{28,4},{1,9},{5... | collective-permute-start | bytes 589832 | tf_op jit(solution)/shard_map/ppermute | solution.py:405
  72.8 25.6 %collective-permute-start.32 = (bf16[384,256]{1,0:T(8,128)(2,1)S(1)}, bf16[384,256]{1,0:T(8,128)(2,1)S(1)}, u32[]{:S(2)}, u32[]{:S(2)}) collective-permute-start(bf16[384,256]{1,0:T(8,128)(2,1)S(1)} %get-tuple-element.83), channel_id=1, source_target_pairs={{0,12},{4,8},{8,20},{12,16},{16,28},{20,24},{24,4},{28,0},{1,13},{... | collective-permute-start | bytes 589832 | tf_op jit(solution)/shard_map/ppermute | solution.py:405
  79.0 19.7 %collective-permute-start.33 = (bf16[384,256]{1,0:T(8,128)(2,1)S(1)}, bf16[384,256]{1,0:T(8,128)(2,1)S(1)}, u32[]{:S(2)}, u32[]{:S(2)}) collective-permute-start(bf16[384,256]{1,0:T(8,128)(2,1)S(1)} %get-tuple-element.84), channel_id=1, source_target_pairs={{0,24},{4,28},{8,0},{12,4},{16,8},{20,12},{24,16},{28,20},{1,25},{... | collective-permute-start | bytes 589832 | tf_op jit(solution)/shard_map/ppermute | solution.py:405
  86.3 29.0 %collective-permute-start.34 = (bf16[384,256]{1,0:T(8,128)(2,1)S(1)}, bf16[384,256]{1,0:T(8,128)(2,1)S(1)}, u32[]{:S(2)}, u32[]{:S(2)}) collective-permute-start(bf16[384,256]{1,0:T(8,128)(2,1)S(1)} %get-tuple-element.85), channel_id=1, source_target_pairs={{0,28},{4,24},{8,4},{12,0},{16,12},{20,8},{24,20},{28,16},{1,29},{... | collective-permute-start | bytes 589832 | tf_op jit(solution)/shard_map/ppermute | solution.py:405
  94.8 32.5 %collective-permute-start.22 = (bf16[384,384]{1,0:T(8,128)(2,1)S(1)}, bf16[384,384]{1,0:T(8,128)(2,1)S(1)}, u32[]{:S(2)}, u32[]{:S(2)}) collective-permute-start(bf16[384,384]{1,0:T(8,128)(2,1)S(1)} %get-tuple-element.72), channel_id=1, source_target_pairs={{0,16},{4,20},{8,24},{12,28},{16,0},{20,4},{24,8},{28,12},{1,17},{... | collective-permute-start | bytes 884744 | tf_op jit(solution)/shard_map/ppermute | solution.py:405
  98.4 29.8 %collective-permute-start.23 = (bf16[384,384]{1,0:T(8,128)(2,1)S(1)}, bf16[384,384]{1,0:T(8,128)(2,1)S(1)}, u32[]{:S(2)}, u32[]{:S(2)}) collective-permute-start(bf16[384,384]{1,0:T(8,128)(2,1)S(1)} %get-tuple-element.73), channel_id=1, source_target_pairs={{0,20},{4,16},{8,28},{12,24},{16,4},{20,0},{24,12},{28,8},{1,21},{... | collective-permute-start | bytes 884744 | tf_op jit(solution)/shard_map/ppermute | solution.py:405
  98.7 37.2 %collective-permute-start.24 = (bf16[384,384]{1,0:T(8,128)(2,1)S(1)}, bf16[384,384]{1,0:T(8,128)(2,1)S(1)}, u32[]{:S(2)}, u32[]{:S(2)}) collective-permute-start(bf16[384,384]{1,0:T(8,128)(2,1)S(1)} %get-tuple-element.74), channel_id=1, source_target_pairs={{0,8},{4,12},{8,16},{12,20},{16,24},{20,28},{24,0},{28,4},{1,9},{5... | collective-permute-start | bytes 884744 | tf_op jit(solution)/shard_map/ppermute | solution.py:405
  115.3 33.4 %collective-permute-start.25 = (bf16[384,384]{1,0:T(8,128)(2,1)S(1)}, bf16[384,384]{1,0:T(8,128)(2,1)S(1)}, u32[]{:S(2)}, u32[]{:S(2)}) collective-permute-start(bf16[384,384]{1,0:T(8,128)(2,1)S(1)} %get-tuple-element.75), channel_id=1, source_target_pairs={{0,12},{4,8},{8,20},{12,16},{16,28},{20,24},{24,4},{28,0},{1,13},{... | collective-permute-start | bytes 884744 | tf_op jit(solution)/shard_map/ppermute | solution.py:405
  115.3 8.8 %collective-permute-start.35 = (bf16[384,256]{1,0:T(8,128)(2,1)S(1)}, bf16[384,256]{1,0:T(8,128)(2,1)S(1)}, u32[]{:S(2)}, u32[]{:S(2)}) collective-permute-start(bf16[384,256]{1,0:T(8,128)(2,1)S(1)} %get-tuple-element.60), channel_id=1, source_target_pairs={{0,4},{4,0},{8,12},{12,8},{16,20},{20,16},{24,28},{28,24},{1,5},{5... | collective-permute-start | bytes 589832 | tf_op jit(solution)/shard_map/ppermute | solution.py:405
  124.1 24.5 %collective-permute-start.26 = (bf16[384,384]{1,0:T(8,128)(2,1)S(1)}, bf16[384,384]{1,0:T(8,128)(2,1)S(1)}, u32[]{:S(2)}, u32[]{:S(2)}) collective-permute-start(bf16[384,384]{1,0:T(8,128)(2,1)S(1)} %get-tuple-element.76), channel_id=1, source_target_pairs={{0,24},{4,28},{8,0},{12,4},{16,8},{20,12},{24,16},{28,20},{1,25},{... | collective-permute-start | bytes 884744 | tf_op jit(solution)/shard_map/ppermute | solution.py:405
  127.3 25.8 %collective-permute-start.27 = (bf16[384,384]{1,0:T(8,128)(2,1)S(1)}, bf16[384,384]{1,0:T(8,128)(2,1)S(1)}, u32[]{:S(2)}, u32[]{:S(2)}) collective-permute-start(bf16[384,384]{1,0:T(8,128)(2,1)S(1)} %get-tuple-element.77), channel_id=1, source_target_pairs={{0,28},{4,24},{8,4},{12,0},{16,12},{20,8},{24,20},{28,16},{1,29},{... | collective-permute-start | bytes 884744 | tf_op jit(solution)/shard_map/ppermute | solution.py:405
  128.3 24.8 %collective-permute-start.28 = (bf16[384,384]{1,0:T(8,128)(2,1)S(1)}, bf16[384,384]{1,0:T(8,128)(2,1)S(1)}, u32[]{:S(2)}, u32[]{:S(2)}) collective-permute-start(bf16[384,384]{1,0:T(8,128)(2,1)S(1)} %get-tuple-element.78), channel_id=1, source_target_pairs={{0,4},{4,0},{8,12},{12,8},{16,20},{20,16},{24,28},{28,24},{1,5},{5... | collective-permute-start | bytes 884744 | tf_op jit(solution)/shard_map/ppermute | solution.py:405
  135.9 25.4 %collective-permute-start.14 = (bf16[384,384]{1,0:T(8,128)(2,1)S(1)}, bf16[384,384]{1,0:T(8,128)(2,1)S(1)}, u32[]{:S(2)}, u32[]{:S(2)}) collective-permute-start(bf16[384,384]{1,0:T(8,128)(2,1)S(1)} %get-tuple-element.64), channel_id=1, source_target_pairs={{0,16},{4,20},{8,24},{12,28},{16,0},{20,4},{24,8},{28,12},{1,17},{... | collective-permute-start | bytes 884744 | tf_op jit(solution)/shard_map/ppermute | solution.py:405
  148.6 30.3 %collective-permute-start.15 = (bf16[384,384]{1,0:T(8,128)(2,1)S(1)}, bf16[384,384]{1,0:T(8,128)(2,1)S(1)}, u32[]{:S(2)}, u32[]{:S(2)}) collective-permute-start(bf16[384,384]{1,0:T(8,128)(2,1)S(1)} %get-tuple-element.65), channel_id=1, source_target_pairs={{0,20},{4,16},{8,28},{12,24},{16,4},{20,0},{24,12},{28,8},{1,21},{... | collective-permute-start | bytes 884744 | tf_op jit(solution)/shard_map/ppermute | solution.py:405
  148.6 38.0 %collective-permute-start.16 = (bf16[384,384]{1,0:T(8,128)(2,1)S(1)}, bf16[384,384]{1,0:T(8,128)(2,1)S(1)}, u32[]{:S(2)}, u32[]{:S(2)}) collective-permute-start(bf16[384,384]{1,0:T(8,128)(2,1)S(1)} %get-tuple-element.66), channel_id=1, source_target_pairs={{0,8},{4,12},{8,16},{12,20},{16,24},{20,28},{24,0},{28,4},{1,9},{5... | collective-permute-start | bytes 884744 | tf_op jit(solution)/shard_map/ppermute | solution.py:405
  153.1 39.7 %collective-permute-start.17 = (bf16[384,384]{1,0:T(8,128)(2,1)S(1)}, bf16[384,384]{1,0:T(8,128)(2,1)S(1)}, u32[]{:S(2)}, u32[]{:S(2)}) collective-permute-start(bf16[384,384]{1,0:T(8,128)(2,1)S(1)} %get-tuple-element.67), channel_id=1, source_target_pairs={{0,12},{4,8},{8,20},{12,16},{16,28},{20,24},{24,4},{28,0},{1,13},{... | collective-permute-start | bytes 884744 | tf_op jit(solution)/shard_map/ppermute | solution.py:405
  153.1 39.7 %collective-permute-start.18 = (bf16[384,384]{1,0:T(8,128)(2,1)S(1)}, bf16[384,384]{1,0:T(8,128)(2,1)S(1)}, u32[]{:S(2)}, u32[]{:S(2)}) collective-permute-start(bf16[384,384]{1,0:T(8,128)(2,1)S(1)} %get-tuple-element.68), channel_id=1, source_target_pairs={{0,24},{4,28},{8,0},{12,4},{16,8},{20,12},{24,16},{28,20},{1,25},{... | collective-permute-start | bytes 884744 | tf_op jit(solution)/shard_map/ppermute | solution.py:405
  161.3 33.3 %collective-permute-start.19 = (bf16[384,384]{1,0:T(8,128)(2,1)S(1)}, bf16[384,384]{1,0:T(8,128)(2,1)S(1)}, u32[]{:S(2)}, u32[]{:S(2)}) collective-permute-start(bf16[384,384]{1,0:T(8,128)(2,1)S(1)} %get-tuple-element.69), channel_id=1, source_target_pairs={{0,28},{4,24},{8,4},{12,0},{16,12},{20,8},{24,20},{28,16},{1,29},{... | collective-permute-start | bytes 884744 | tf_op jit(solution)/shard_map/ppermute | solution.py:405
  178.9 15.7 %collective-permute-start.20 = (bf16[384,384]{1,0:T(8,128)(2,1)S(1)}, bf16[384,384]{1,0:T(8,128)(2,1)S(1)}, u32[]{:S(2)}, u32[]{:S(2)}) collective-permute-start(bf16[384,384]{1,0:T(8,128)(2,1)S(1)} %get-tuple-element.70), channel_id=1, source_target_pairs={{0,4},{4,0},{8,12},{12,8},{16,20},{20,16},{24,28},{28,24},{1,5},{5... | collective-permute-start | bytes 884744 | tf_op jit(solution)/shard_map/ppermute | solution.py:405

commit v8 on v7

--- a/solution.py
+++ b/solution.py
@@ -9,10 +9,10 @@
 
 HEADS = 64
 HEAD = 128
-LOCAL = (2, 6)
-SWAP = (2, 3, 3)
-PREFIX = (2, 3, 3)
-MIXED = (2, 3, 3)
+LOCAL = (1, 7)
+SWAP = (1, 2, 2, 3)
+PREFIX = (1, 2, 2, 3)
+MIXED = (1, 2, 2, 3)
 TILE = 256
 SPARE = 8 * 1024 * 1024
 ORDER = {
@@ -22,9 +22,12 @@
     ("message", 1, 3): [("message", 0, 4)],
     ("message", 2, 1): [("message", 1, 2)],
     ("message", 2, 2): [("message", 1, 3)],
-    ("message", 2, 3): [("message", 1, 4), ("mixed", 0)],
-    ("mixed", 0): [("message", 1, 3), ("message", 2, 2)],
-    ("message", 1, 4): [("mixed", 0)],
+    ("message", 2, 3): [("message", 1, 4)],
+    ("message", 3, 1): [("message", 2, 2)],
+    ("message", 3, 2): [("message", 2, 3)],
+    ("message", 3, 3): [("message", 2, 4), ("mixed", 0)],
+    ("mixed", 0): [("message", 1, 4), ("message", 2, 3), ("message", 3, 2)],
+    ("message", 2, 4): [("mixed", 0)],
 }
 
 

time: 201 us -> 212 us (1.055); the launches traced: 197 us -> 211 us
  waiting for transfers between devices: 73.7 us -> 90.9 us
  starting transfers between devices: 74.2 us -> 63 us
  Pallas kernels: 41.3 us -> 48.5 us
    ppermute x21 -> x28, starting transfers between devices: 54.8 us -> 42.2 us  [sent(): lax.ppermute(self.hold(self.get('mixed', c)[k], 'sent', c, k), 'seq', pairs)]
    ppermute x21 -> x28, waiting for transfers between devices: 54.6 us -> 64.7 us  [sent(): lax.ppermute(self.hold(self.get('mixed', c)[k], 'sent', c, k), 'seq', pairs)]
    pallas_call x3 -> x4, Pallas kernels: 25.5 us -> 31.2 us  [attend(): pl.pallas_call(functools.partial(attend_body, n, spans, order), in_specs=...]
    ppermute x3 -> x4, waiting for transfers between devices: 1.48 us -> 5.14 us  [swap(): return lax.ppermute(other, 'seq', [(d, d ^ 1) for d in range(self.n)])]
    ppermute x12 -> x16, waiting for transfers between devices: 17.6 us -> 21.1 us  [prefix(): return lax.ppermute(self.get('message', c, s), 'seq', pairs)]
    ppermute x12 -> x16, starting transfers between devices: 14.7 us -> 16.5 us  [prefix(): return lax.ppermute(self.get('message', c, s), 'seq', pairs)]
    pallas_call x3 -> x4, Pallas kernels: 7.33 us -> 9.14 us  [put(): pl.pallas_call(functools.partial(put_body, n, order), in_specs=[pl.BlockS...]
    convert_element_type x10 -> x13, other arithmetic: 4.88 us -> 5.68 us  [message(): return self.hold(value.astype(jnp.bfloat16), 'message', c, s)]
  transfers between devices with their start and end apart: 36 -> 48, of which waited for: 14 -> 16; matrix products, arithmetic and copies ran while one was open for 4% -> 4% of each run, Pallas kernels for 18% -> 21%
where the time goes in v8:
time: 212 us; the launch traced here: 211 us
  waiting for transfers between devices  90.9 us (43%)
  starting transfers between devices  63 us (30%)
  Pallas kernels  48.5 us (23%)
  other arithmetic  8.26 us (4%)
    ppermute x28, waiting for transfers between devices, sent(): lax.ppermute(self.hold(self.get('mixed', c)[k], 'sent', c, k), 'seq', pairs)  64.7 us
    ppermute x28, starting transfers between devices, sent(): lax.ppermute(self.hold(self.get('mixed', c)[k], 'sent', c, k), 'seq', pairs)  42.2 us
    pallas_call x4, Pallas kernels, attend(): pl.pallas_call(functools.partial(attend_body, n, spans, order), in_specs=...  31.2 us
    ppermute x16, waiting for transfers between devices, prefix(): return lax.ppermute(self.get('message', c, s), 'seq', pairs)  21.1 us
    ppermute x16, starting transfers between devices, prefix(): return lax.ppermute(self.get('message', c, s), 'seq', pairs)  16.5 us
    pallas_call x4, Pallas kernels, put(): pl.pallas_call(functools.partial(put_body, n, order), in_specs=[pl.BlockS...  9.14 us
    pallas_call x2, Pallas kernels, local_states(): pl.pallas_call(functools.partial(local_body, n, widths, swaps), in_specs=...  8.15 us
    convert_element_type x13, other arithmetic, message(): return self.hold(value.astype(jnp.bfloat16), 'message', c, s)  5.68 us
  transfers between devices with their start and end apart: 48, of which 16 were waited for; matrix products, arithmetic and copies ran while one was open for 4% of the time, Pallas kernels for 21%

profile of v8, /device:TPU:8, one launch (start us, length us, event | category | flops | bytes accessed | tf_op | source)
XLA Modules:
  0.0 211.3 jit_solution(2700717553745927285)
XLA Ops:
  0.1 2.6 %local.3 = (f32[4,1,128,128]{3,2,1,0:T(8,128)S(1)}, bf16[4,1,128,128]{3,2,1,0:T(8,128)(2,1)S(1)}) custom-call(s32[2]{0:T(128)S(1)} %pad_add_fusion.place, s32[1]{0:T(128)} %constant.38.clone.1.low, bf16[384,8192]{1,0:T(8,128)(2,1)} %keys.11, bf16[384,8192]{1,0:T(8,128)(2,1)} %values.11), custom_call_target="tpu_custom_call" | custom-call | flops 100663296 | bytes 1572864 | tf_op jit(solution)/shard_map/local/pallas_call | solution.py:101
  2.7 1.6 collective-permute-start.1
  4.3 5.5 %local.2 = (f32[4,2,128,128]{3,2,1,0:T(8,128)S(1)}, f32[4,2,128,128]{3,2,1,0:T(8,128)S(1)}, f32[4,3,128,128]{3,2,1,0:T(8,128)S(1)}, bf16[4,2,128,128]{3,2,1,0:T(...) custom-call(s32[2]{0:T(128)S(1)} %pad_add_fusion.place, ...), custom_call_target="tpu_custom_call" | custom-call | flops 704643072 | bytes 11010048 | tf_op jit(solution)/shard_map/local/pallas_call | solution.py:101
  9.9 1.3 collective-permute-start.2
  11.7 5.0 %collective-permute-done.2 = bf16[4,1,128,128]{3,2,1,0:T(8,128)(2,1)S(1)} collective-permute-done((bf16[4,1,128,128]{3,2,1,0:T(8,128)(2,1)S(1)}, bf16[4,1,128,128]{3,2,1,0:T(8,128)(2,1)S(1)}, u32[]{:S(2)}, u32[]{:S(2)}) %collective-permute-start.2) | collective-permute-done | bytes 131104 | tf_op jit(solution)/shard_map/ppermute | solution.py:384
  17.4 1.9 collective-permute-start.4
  20.2 1.3 collective-permute-start.3
  22.1 1.5 collective-permute-start.8
  25.3 4.0 %collective-permute-done.3 = bf16[4,2,128,128]{3,2,1,0:T(8,128)(2,1)} collective-permute-done((bf16[4,2,128,128]{3,2,1,0:T(8,128)(2,1)}, bf16[4,2,128,128]{3,2,1,0:T(8,128)(2,1)}, u32[]{:S(2)}, u32[]{:S(2)}) %collective-permute-start.3) | collective-permute-done | bytes 262176 | tf_op jit(solution)/shard_map/ppermute | solution.py:384
  30.5 1.3 collective-permute-start.5
  31.8 5.1 %collective-permute-done.8 = bf16[4,2,128,128]{3,2,1,0:T(8,128)(2,1)S(1)} collective-permute-done((bf16[4,2,128,128]{3,2,1,0:T(8,128)(2,1)S(1)}, bf16[4,2,128,128]{3,2,1,0:T(8,128)(2,1)S(1)}, u32[]{:S(2)}, u32[]{:S(2)}) %collective-permute-start.8) | collective-permute-done | bytes 262176 | tf_op jit(solution)/shard_map/ppermute | solution.py:357
  37.0 1.3 collective-permute-start.9
  41.1 4.5 %collective-permute-done.9 = bf16[4,2,128,128]{3,2,1,0:T(8,128)(2,1)S(1)} collective-permute-done((bf16[4,2,128,128]{3,2,1,0:T(8,128)(2,1)S(1)}, bf16[4,2,128,128]{3,2,1,0:T(8,128)(2,1)S(1)}, u32[]{:S(2)}, u32[]{:S(2)}) %collective-permute-start.9) | collective-permute-done | bytes 262176 | tf_op jit(solution)/shard_map/ppermute | solution.py:384
  45.7 1.3 collective-permute-start.10
  47.7 1.3 collective-permute-start.12
  49.0 1.9 collective-permute-done.10
  52.9 4.5 %collective-permute-done.12 = bf16[4,3,128,128]{3,2,1,0:T(8,128)(2,1)S(1)} collective-permute-done((bf16[4,3,128,128]{3,2,1,0:T(8,128)(2,1)S(1)}, bf16[4,3,128,128]{3,2,1,0:T(8,128)(2,1)S(1)}, u32[]{:S(2)}, u32[]{:S(2)}) %collective-permute-start.12) | collective-permute-done | bytes 393248 | tf_op jit(solution)/shard_map/ppermute | solution.py:384
  57.5 1.3 collective-permute-start.21
  58.8 1.6 collective-permute-start.40
  60.4 5.7 %attend.4 = (bf16[384,128]{1,0:T(8,128)(2,1)S(1)}, bf16[384,128]{1,0:T(8,128)(2,1)S(1)}, bf16[384,128]{1,0:T(8,128)(2,1)S(1)}, bf16[384,128]{1,0:T(8,128)(2,1)S(...) custom-call(s32[2]{0:T(128)S(1)} %pad_add_fusion.place, ...), custom_call_target="tpu_custom_call" | custom-call | flops 704643072 | bytes 3145728 | tf_op jit(solution)/shard_map/attend/pallas_call | solution.py:225
  68.5 4.8 %collective-permute-start.15 = (bf16[384,128]{1,0:T(8,128)(2,1)S(1)}, bf16[384,128]{1,0:T(8,128)(2,1)S(1)}, u32[]{:S(2)}, u32[]{:S(2)}) collective-permute-start(bf16[384,128]{1,0:T(8,128)(2,1)S(1)} %get-tuple-element.82), channel_id=1, source_target_pairs={{0,20},{4,16},{8,28},{12,24},{16,4},{20,0},{24,12},{28,8},{1,21},{... | collective-permute-start | bytes 294920 | tf_op jit(solution)/shard_map/ppermute | solution.py:408
  73.2 3.1 %collective-permute-start.16 = (bf16[384,128]{1,0:T(8,128)(2,1)S(1)}, bf16[384,128]{1,0:T(8,128)(2,1)S(1)}, u32[]{:S(2)}, u32[]{:S(2)}) collective-permute-start(bf16[384,128]{1,0:T(8,128)(2,1)S(1)} %get-tuple-element.83), channel_id=1, source_target_pairs={{0,8},{4,12},{8,16},{12,20},{16,24},{20,28},{24,0},{28,4},{1,9},{5... | collective-permute-start | bytes 294920 | tf_op jit(solution)/shard_map/ppermute | solution.py:408
  76.4 8.5 %attend.7 = (bf16[384,256]{1,0:T(8,128)(2,1)S(1)}, bf16[384,256]{1,0:T(8,128)(2,1)S(1)}, bf16[384,256]{1,0:T(8,128)(2,1)S(1)}, bf16[384,256]{1,0:T(8,128)(2,1)S(...) custom-call(s32[2]{0:T(128)S(1)} %pad_add_fusion.place, ...), custom_call_target="tpu_custom_call" | custom-call | flops 1409286144 | bytes 6291456 | tf_op jit(solution)/shard_map/attend/pallas_call | solution.py:225
  86.1 2.5 %collective-permute-start.19 = (bf16[384,128]{1,0:T(8,128)(2,1)S(1)}, bf16[384,128]{1,0:T(8,128)(2,1)S(1)}, u32[]{:S(2)}, u32[]{:S(2)}) collective-permute-start(bf16[384,128]{1,0:T(8,128)(2,1)S(1)} %get-tuple-element.86), channel_id=1, source_target_pairs={{0,28},{4,24},{8,4},{12,0},{16,12},{20,8},{24,20},{28,16},{1,29},{... | collective-permute-start | bytes 294920 | tf_op jit(solution)/shard_map/ppermute | solution.py:408
  89.9 3.0 %collective-permute-start.42 = (bf16[384,256]{1,0:T(8,128)(2,1)S(1)}, bf16[384,256]{1,0:T(8,128)(2,1)S(1)}, u32[]{:S(2)}, u32[]{:S(2)}) collective-permute-start(bf16[384,256]{1,0:T(8,128)(2,1)S(1)} %get-tuple-element.109), channel_id=1, source_target_pairs={{0,20},{4,16},{8,28},{12,24},{16,4},{20,0},{24,12},{28,8},{1,21},{... | collective-permute-start | bytes 589832 | tf_op jit(solution)/shard_map/ppermute | solution.py:408
  93.7 1.7 collective-permute-start.20
  95.4 11.2 %collective-permute-done.20.refs_7_ = bf16[384,128]{1,0:T(8,128)(2,1)S(1)} collective-permute-done((bf16[384,128]{1,0:T(8,128)(2,1)S(1)}, bf16[384,128]{1,0:T(8,128)(2,1)S(1)}, u32[]{:S(2)}, u32[]{:S(2)}) %collective-permute-start.20) | collective-permute-done | bytes 98336 | tf_op jit(solution)/shard_map/ppermute | solution.py:408
  106.7 1.2 collective-permute-start.44
  108.0 6.6 %collective-permute-start.45 = (bf16[384,256]{1,0:T(8,128)(2,1)S(1)}, bf16[384,256]{1,0:T(8,128)(2,1)S(1)}, u32[]{:S(2)}, u32[]{:S(2)}) collective-permute-start(bf16[384,256]{1,0:T(8,128)(2,1)S(1)} %get-tuple-element.112), channel_id=1, source_target_pairs={{0,24},{4,28},{8,0},{12,4},{16,8},{20,12},{24,16},{28,20},{1,25},{... | collective-permute-start | bytes 589832 | tf_op jit(solution)/shard_map/ppermute | solution.py:408
  114.6 2.1 put.4
  116.7 8.5 %attend.6 = (bf16[384,256]{1,0:T(8,128)(2,1)S(1)}, bf16[384,256]{1,0:T(8,128)(2,1)S(1)}, bf16[384,256]{1,0:T(8,128)(2,1)S(1)}, bf16[384,256]{1,0:T(8,128)(2,1)S(...) custom-call(s32[2]{0:T(128)S(1)} %pad_add_fusion.place, ...), custom_call_target="tpu_custom_call" | custom-call | flops 1409286144 | bytes 6291456 | tf_op jit(solution)/shard_map/attend/pallas_call | solution.py:225
  125.2 1.6 collective-permute-start.47
  126.8 2.9 %collective-permute-start.34 = (bf16[384,256]{1,0:T(8,128)(2,1)S(1)}, bf16[384,256]{1,0:T(8,128)(2,1)S(1)}, u32[]{:S(2)}, u32[]{:S(2)}) collective-permute-start(bf16[384,256]{1,0:T(8,128)(2,1)S(1)} %get-tuple-element.101), channel_id=1, source_target_pairs={{0,20},{4,16},{8,28},{12,24},{16,4},{20,0},{24,12},{28,8},{1,21},{... | collective-permute-start | bytes 589832 | tf_op jit(solution)/shard_map/ppermute | solution.py:408
  129.7 15.3 %collective-permute-done.46.refs_6_ = bf16[384,256]{1,0:T(8,128)(2,1)S(1)} collective-permute-done((bf16[384,256]{1,0:T(8,128)(2,1)S(1)}, bf16[384,256]{1,0:T(8,128)(2,1)S(1)}, u32[]{:S(2)}, u32[]{:S(2)}) %collective-permute-start.46) | collective-permute-done | bytes 196640 | tf_op jit(solution)/shard_map/ppermute | solution.py:408
  145.0 8.4 %attend.5 = (bf16[384,384]{1,0:T(8,128)(2,1)S(1)}, bf16[384,384]{1,0:T(8,128)(2,1)S(1)}, bf16[384,384]{1,0:T(8,128)(2,1)S(1)}, bf16[384,384]{1,0:T(8,128)(2,1)S(...) custom-call(s32[2]{0:T(128)S(1)} %get-tuple-element.88.place, ...), custom_call_target="tpu_custom_call" | custom-call | flops 2113929216 | bytes 9437184 | tf_op jit(solution)/shard_map/attend/pallas_call | solution.py:225
  153.4 3.2 %collective-permute-start.25 = (bf16[384,384]{1,0:T(8,128)(2,1)S(1)}, bf16[384,384]{1,0:T(8,128)(2,1)S(1)}, u32[]{:S(2)}, u32[]{:S(2)}) collective-permute-start(bf16[384,384]{1,0:T(8,128)(2,1)S(1)} %get-tuple-element.92), channel_id=1, source_target_pairs={{0,16},{4,20},{8,24},{12,28},{16,0},{20,4},{24,8},{28,12},{1,17},{... | collective-permute-start | bytes 884744 | tf_op jit(solution)/shard_map/ppermute | solution.py:408
  156.6 2.2 %collective-permute-start.26 = (bf16[384,384]{1,0:T(8,128)(2,1)S(1)}, bf16[384,384]{1,0:T(8,128)(2,1)S(1)}, u32[]{:S(2)}, u32[]{:S(2)}) collective-permute-start(bf16[384,384]{1,0:T(8,128)(2,1)S(1)} %get-tuple-element.93), channel_id=1, source_target_pairs={{0,20},{4,16},{8,28},{12,24},{16,4},{20,0},{24,12},{28,8},{1,21},{... | collective-permute-start | bytes 884744 | tf_op jit(solution)/shard_map/ppermute | solution.py:408
  159.4 2.5 %collective-permute-start.38 = (bf16[384,256]{1,0:T(8,128)(2,1)S(1)}, bf16[384,256]{1,0:T(8,128)(2,1)S(1)}, u32[]{:S(2)}, u32[]{:S(2)}) collective-permute-start(bf16[384,256]{1,0:T(8,128)(2,1)S(1)} %get-tuple-element.105), channel_id=1, source_target_pairs={{0,28},{4,24},{8,4},{12,0},{16,12},{20,8},{24,20},{28,16},{1,29},{... | collective-permute-start | bytes 589832 | tf_op jit(solution)/shard_map/ppermute | solution.py:408
  161.9 5.7 %collective-permute-done.36.refs_4_ = bf16[384,256]{1,0:T(8,128)(2,1)S(1)} collective-permute-done((bf16[384,256]{1,0:T(8,128)(2,1)S(1)}, bf16[384,256]{1,0:T(8,128)(2,1)S(1)}, u32[]{:S(2)}, u32[]{:S(2)}) %collective-permute-start.36) | collective-permute-done | bytes 196640 | tf_op jit(solution)/shard_map/ppermute | solution.py:408
  167.7 21.7 %collective-permute-done.37.refs_5_ = bf16[384,256]{1,0:T(8,128)(2,1)S(1)} collective-permute-done((bf16[384,256]{1,0:T(8,128)(2,1)S(1)}, bf16[384,256]{1,0:T(8,128)(2,1)S(1)}, u32[]{:S(2)}, u32[]{:S(2)}) %collective-permute-start.37) | collective-permute-done | bytes 196640 | tf_op jit(solution)/shard_map/ppermute | solution.py:408
  189.3 5.3 %collective-permute-done.38.refs_6_ = bf16[384,256]{1,0:T(8,128)(2,1)S(1)} collective-permute-done((bf16[384,256]{1,0:T(8,128)(2,1)S(1)}, bf16[384,256]{1,0:T(8,128)(2,1)S(1)}, u32[]{:S(2)}, u32[]{:S(2)}) %collective-permute-start.38) | collective-permute-done | bytes 196640 | tf_op jit(solution)/shard_map/ppermute | solution.py:408
  194.6 1.8 collective-permute-start.29
  196.4 1.2 collective-permute-start.30
  198.7 2.3 %put.5 = (bf16[3072,1024]{1,0:T(8,128)(2,1)}, s32[2]{0:T(128)}) custom-call(s32[2]{0:T(128)S(1)} %pad_add_fusion.place, s32[1]{0:T(128)} %constant.39.clone.1.low, bf16[384,256]{1,0:T(8,128)(2,1)S(1)} %get-tuple-element.107.refs_0_, bf16[384,256]{1,0:T(8,128)(2,1)S(1)} %collective-permute-done.41.refs_1_, ...), custom_call_target="tpu_custom_call", output_to_operand_aliasing={{0}: (10, {})} | custom-call | tf_op jit(solution)/shard_map/put/pallas_call | solution.py:277
  201.0 2.3 %put.6 = (bf16[3072,1024]{1,0:T(8,128)(2,1)}, s32[2]{0:T(128)}) custom-call(s32[2]{0:T(128)S(1)} %pad_add_fusion.place, s32[1]{0:T(128)} %constant.41.clone.1.low, bf16[384,256]{1,0:T(8,128)(2,1)S(1)} %get-tuple-element.99.refs_0_, bf16[384,256]{1,0:T(8,128)(2,1)S(1)} %collective-permute-done.33.refs_1_, ...), custom_call_target="tpu_custom_call", output_to_operand_aliasing={{0}: (10, {})} | custom-call | tf_op jit(solution)/shard_map/put/pallas_call | solution.py:277
  203.6 2.2 %collective-permute-done.30.refs_6_ = bf16[384,384]{1,0:T(8,128)(2,1)S(1)} collective-permute-done((bf16[384,384]{1,0:T(8,128)(2,1)S(1)}, bf16[384,384]{1,0:T(8,128)(2,1)S(1)}, u32[]{:S(2)}, u32[]{:S(2)}) %collective-permute-start.30) | collective-permute-done | bytes 294944 | tf_op jit(solution)/shard_map/ppermute | solution.py:408
  205.8 2.8 %collective-permute-done.31.refs_7_ = bf16[384,384]{1,0:T(8,128)(2,1)S(1)} collective-permute-done((bf16[384,384]{1,0:T(8,128)(2,1)S(1)}, bf16[384,384]{1,0:T(8,128)(2,1)S(1)}, u32[]{:S(2)}, u32[]{:S(2)}) %collective-permute-start.31) | collective-permute-done | bytes 294944 | tf_op jit(solution)/shard_map/ppermute | solution.py:408
  208.6 2.5 %put.7 = (bf16[3072,1024]{1,0:T(8,128)(2,1)}, s32[2]{0:T(128)}) custom-call(s32[2]{0:T(128)S(1)} %pad_add_fusion.place, s32[1]{0:T(128)} %constant.37.clone.1.low, bf16[384,384]{1,0:T(8,128)(2,1)S(1)} %get-tuple-element.91.refs_0_, bf16[384,384]{1,0:T(8,128)(2,1)S(1)} %collective-permute-done.25.refs_1_, ...), custom_call_target="tpu_custom_call", output_to_operand_aliasing={{0}: (10, {})} | custom-call | tf_op jit(solution)/shard_map/put/pallas_call | solution.py:277
  (83 shorter events, 19.0 us)
Async XLA Ops:
  2.7 7.1 %collective-permute-start.1 = (bf16[4,1,128,128]{3,2,1,0:T(8,128)(2,1)S(1)}, bf16[4,1,128,128]{3,2,1,0:T(8,128)(2,1)S(1)}, u32[]{:S(2)}, u32[]{:S(2)}) collective-permute-start(bf16[4,1,128,128]{3,2,1,0:T(8,128)(2,1)S(1)} %get-tuple-element.65), channel_id=1, source_target_pairs={{0,4},{4,0},{8,12},{12,8},{16,20},{20,16},{24,28},{28,24},{1,5},{5... | collective-permute-start | bytes 393224 | tf_op jit(solution)/shard_map/ppermute | solution.py:357
  9.9 6.9 %collective-permute-start.2 = (bf16[4,1,128,128]{3,2,1,0:T(8,128)(2,1)S(1)}, bf16[4,1,128,128]{3,2,1,0:T(8,128)(2,1)S(1)}, u32[]{:S(2)}, u32[]{:S(2)}) collective-permute-start(bf16[4,1,128,128]{3,2,1,0:T(8,128)(2,1)S(1)} %fusion.11), channel_id=1, source_target_pairs={{0,8},{4,12},{1,9},{5,13},{2,10},{6,14},{3,11},{7,15}} | collective-permute-start | bytes 393224 | tf_op jit(solution)/shard_map/ppermute | solution.py:384
  11.2 8.2 %collective-permute-start = (bf16[4,2,128,128]{3,2,1,0:T(8,128)(2,1)S(1)}, bf16[4,2,128,128]{3,2,1,0:T(8,128)(2,1)S(1)}, u32[]{:S(2)}, u32[]{:S(2)}) collective-permute-start(bf16[4,2,128,128]{3,2,1,0:T(8,128)(2,1)S(1)} %get-tuple-element.63), channel_id=1, source_target_pairs={{0,4},{4,0},{8,12},{12,8},{16,20},{20,16},{24,28},{28,24},{1,5},{5... | collective-permute-start | bytes 786440 | tf_op jit(solution)/shard_map/ppermute | solution.py:357
  17.4 6.1 %collective-permute-start.4 = (bf16[4,1,128,128]{3,2,1,0:T(8,128)(2,1)}, bf16[4,1,128,128]{3,2,1,0:T(8,128)(2,1)}, u32[]{:S(2)}, u32[]{:S(2)}) collective-permute-start(bf16[4,1,128,128]{3,2,1,0:T(8,128)(2,1)} %add_convert_fusion.7), channel_id=1, source_target_pairs={{8,16},{12,20},{9,17},{13,21},{10,18},{14,22},{11,19},{15,23}} | collective-permute-start | bytes 393224 | tf_op jit(solution)/shard_map/ppermute | solution.py:384
  20.2 9.1 %collective-permute-start.3 = (bf16[4,2,128,128]{3,2,1,0:T(8,128)(2,1)}, bf16[4,2,128,128]{3,2,1,0:T(8,128)(2,1)}, u32[]{:S(2)}, u32[]{:S(2)}) collective-permute-start(bf16[4,2,128,128]{3,2,1,0:T(8,128)(2,1)} %fusion.9), channel_id=1, source_target_pairs={{0,8},{4,12},{1,9},{5,13},{2,10},{6,14},{3,11},{7,15}} | collective-permute-start | bytes 786440 | tf_op jit(solution)/shard_map/ppermute | solution.py:384
  21.5 25.5 %collective-permute-start.11 = (bf16[4,3,128,128]{3,2,1,0:T(8,128)(2,1)S(1)}, bf16[4,3,128,128]{3,2,1,0:T(8,128)(2,1)S(1)}, u32[]{:S(2)}, u32[]{:S(2)}) collective-permute-start(bf16[4,3,128,128]{3,2,1,0:T(8,128)(2,1)S(1)} %get-tuple-element.66), channel_id=1, source_target_pairs={{0,4},{4,0},{8,12},{12,8},{16,20},{20,16},{24,28},{28,24},{1,5},{5... | collective-permute-start | bytes 1179656 | tf_op jit(solution)/shard_map/ppermute | solution.py:357
  22.1 14.8 %collective-permute-start.8 = (bf16[4,2,128,128]{3,2,1,0:T(8,128)(2,1)S(1)}, bf16[4,2,128,128]{3,2,1,0:T(8,128)(2,1)S(1)}, u32[]{:S(2)}, u32[]{:S(2)}) collective-permute-start(bf16[4,2,128,128]{3,2,1,0:T(8,128)(2,1)S(1)} %get-tuple-element.72), channel_id=1, source_target_pairs={{0,4},{4,0},{8,12},{12,8},{16,20},{20,16},{24,28},{28,24},{1,5},{5... | collective-permute-start | bytes 786440 | tf_op jit(solution)/shard_map/ppermute | solution.py:357
  24.6 13.7 %collective-permute-start.6 = (bf16[4,1,128,128]{3,2,1,0:T(8,128)(2,1)S(1)}, bf16[4,1,128,128]{3,2,1,0:T(8,128)(2,1)S(1)}, u32[]{:S(2)}, u32[]{:S(2)}) collective-permute-start(bf16[4,1,128,128]{3,2,1,0:T(8,128)(2,1)S(1)} %add_convert_fusion.6), channel_id=1, source_target_pairs={{16,24},{20,28},{17,25},{21,29},{18,26},{22,30},{19,27},{23,31}} | collective-permute-start | bytes 393224 | tf_op jit(solution)/shard_map/ppermute | solution.py:384
  30.5 8.9 %collective-permute-start.5 = (bf16[4,2,128,128]{3,2,1,0:T(8,128)(2,1)S(1)}, bf16[4,2,128,128]{3,2,1,0:T(8,128)(2,1)S(1)}, u32[]{:S(2)}, u32[]{:S(2)}) collective-permute-start(bf16[4,2,128,128]{3,2,1,0:T(8,128)(2,1)S(1)} %add_convert_fusion.5), channel_id=1, source_target_pairs={{8,16},{12,20},{9,17},{13,21},{10,18},{14,22},{11,19},{15,23}} | collective-permute-start | bytes 786440 | tf_op jit(solution)/shard_map/ppermute | solution.py:384
  37.0 8.6 %collective-permute-start.9 = (bf16[4,2,128,128]{3,2,1,0:T(8,128)(2,1)S(1)}, bf16[4,2,128,128]{3,2,1,0:T(8,128)(2,1)S(1)}, u32[]{:S(2)}, u32[]{:S(2)}) collective-permute-start(bf16[4,2,128,128]{3,2,1,0:T(8,128)(2,1)S(1)} %fusion.10), channel_id=1, source_target_pairs={{0,8},{4,12},{1,9},{5,13},{2,10},{6,14},{3,11},{7,15}} | collective-permute-start | bytes 786440 | tf_op jit(solution)/shard_map/ppermute | solution.py:384
  40.4 10.5 %collective-permute-start.7 = (bf16[4,2,128,128]{3,2,1,0:T(8,128)(2,1)S(1)}, bf16[4,2,128,128]{3,2,1,0:T(8,128)(2,1)S(1)}, u32[]{:S(2)}, u32[]{:S(2)}) collective-permute-start(bf16[4,2,128,128]{3,2,1,0:T(8,128)(2,1)S(1)} %add_convert_fusion.4), channel_id=1, source_target_pairs={{16,24},{20,28},{17,25},{21,29},{18,26},{22,30},{19,27},{23,31}} | collective-permute-start | bytes 786440 | tf_op jit(solution)/shard_map/ppermute | solution.py:384
  45.7 5.2 %collective-permute-start.10 = (bf16[4,2,128,128]{3,2,1,0:T(8,128)(2,1)S(1)}, bf16[4,2,128,128]{3,2,1,0:T(8,128)(2,1)S(1)}, u32[]{:S(2)}, u32[]{:S(2)}) collective-permute-start(bf16[4,2,128,128]{3,2,1,0:T(8,128)(2,1)S(1)} %add_convert_fusion.3), channel_id=1, source_target_pairs={{8,16},{12,20},{9,17},{13,21},{10,18},{14,22},{11,19},{15,23}} | collective-permute-start | bytes 786440 | tf_op jit(solution)/shard_map/ppermute | solution.py:384
  47.1 13.3 %collective-permute-start.13 = (bf16[4,1,128,128]{3,2,1,0:T(8,128)(2,1)S(1)}, bf16[4,1,128,128]{3,2,1,0:T(8,128)(2,1)S(1)}, u32[]{:S(2)}, u32[]{:S(2)}) collective-permute-start(bf16[4,1,128,128]{3,2,1,0:T(8,128)(2,1)S(1)} %get-tuple-element.126), channel_id=1, source_target_pairs={{0,4},{4,0},{8,12},{12,8},{16,20},{20,16},{24,28},{28,24},{1,5},{5... | collective-permute-start | bytes 393224 | tf_op jit(solution)/shard_map/ppermute | solution.py:384
  47.7 9.7 %collective-permute-start.12 = (bf16[4,3,128,128]{3,2,1,0:T(8,128)(2,1)S(1)}, bf16[4,3,128,128]{3,2,1,0:T(8,128)(2,1)S(1)}, u32[]{:S(2)}, u32[]{:S(2)}) collective-permute-start(bf16[4,3,128,128]{3,2,1,0:T(8,128)(2,1)S(1)} %fusion.6), channel_id=1, source_target_pairs={{0,8},{4,12},{1,9},{5,13},{2,10},{6,14},{3,11},{7,15}} | collective-permute-start | bytes 1179656 | tf_op jit(solution)/shard_map/ppermute | solution.py:384
  52.2 13.9 %collective-permute-start.22 = (bf16[4,2,128,128]{3,2,1,0:T(8,128)(2,1)S(1)}, bf16[4,2,128,128]{3,2,1,0:T(8,128)(2,1)S(1)}, u32[]{:S(2)}, u32[]{:S(2)}) collective-permute-start(bf16[4,2,128,128]{3,2,1,0:T(8,128)(2,1)S(1)} %add_convert_fusion.2), channel_id=1, source_target_pairs={{16,24},{20,28},{17,25},{21,29},{18,26},{22,30},{19,27},{23,31}} | collective-permute-start | bytes 786440 | tf_op jit(solution)/shard_map/ppermute | solution.py:384
  57.5 10.1 %collective-permute-start.21 = (bf16[4,3,128,128]{3,2,1,0:T(8,128)(2,1)S(1)}, bf16[4,3,128,128]{3,2,1,0:T(8,128)(2,1)S(1)}, u32[]{:S(2)}, u32[]{:S(2)}) collective-permute-start(bf16[4,3,128,128]{3,2,1,0:T(8,128)(2,1)S(1)} %add_convert_fusion.1), channel_id=1, source_target_pairs={{8,16},{12,20},{9,17},{13,21},{10,18},{14,22},{11,19},{15,23}} | collective-permute-start | bytes 1179656 | tf_op jit(solution)/shard_map/ppermute | solution.py:384
  58.8 17.6 %collective-permute-start.40 = (bf16[4,2,128,128]{3,2,1,0:T(8,128)(2,1)S(1)}, bf16[4,2,128,128]{3,2,1,0:T(8,128)(2,1)S(1)}, u32[]{:S(2)}, u32[]{:S(2)}) collective-permute-start(bf16[4,2,128,128]{3,2,1,0:T(8,128)(2,1)S(1)} %get-tuple-element.122), channel_id=1, source_target_pairs={{0,4},{4,0},{8,12},{12,8},{16,20},{20,16},{24,28},{28,24},{1,5},{5... | collective-permute-start | bytes 786440 | tf_op jit(solution)/shard_map/ppermute | solution.py:384
  67.7 22.2 %collective-permute-start.23 = (bf16[4,3,128,128]{3,2,1,0:T(8,128)(2,1)S(1)}, bf16[4,3,128,128]{3,2,1,0:T(8,128)(2,1)S(1)}, u32[]{:S(2)}, u32[]{:S(2)}) collective-permute-start(bf16[4,3,128,128]{3,2,1,0:T(8,128)(2,1)S(1)} %add_convert_fusion), channel_id=1, source_target_pairs={{16,24},{20,28},{17,25},{21,29},{18,26},{22,30},{19,27},{23,31}} | collective-permute-start | bytes 1179656 | tf_op jit(solution)/shard_map/ppermute | solution.py:384
  68.4 16.5 %collective-permute-start.14 = (bf16[384,128]{1,0:T(8,128)(2,1)S(1)}, bf16[384,128]{1,0:T(8,128)(2,1)S(1)}, u32[]{:S(2)}, u32[]{:S(2)}) collective-permute-start(bf16[384,128]{1,0:T(8,128)(2,1)S(1)} %get-tuple-element.81), channel_id=1, source_target_pairs={{0,16},{4,20},{8,24},{12,28},{16,0},{20,4},{24,8},{28,12},{1,17},{... | collective-permute-start | bytes 294920 | tf_op jit(solution)/shard_map/ppermute | solution.py:408
  68.5 17.6 %collective-permute-start.15 = (bf16[384,128]{1,0:T(8,128)(2,1)S(1)}, bf16[384,128]{1,0:T(8,128)(2,1)S(1)}, u32[]{:S(2)}, u32[]{:S(2)}) collective-permute-start(bf16[384,128]{1,0:T(8,128)(2,1)S(1)} %get-tuple-element.82), channel_id=1, source_target_pairs={{0,20},{4,16},{8,28},{12,24},{16,4},{20,0},{24,12},{28,8},{1,21},{... | collective-permute-start | bytes 294920 | tf_op jit(solution)/shard_map/ppermute | solution.py:408
  73.2 15.3 %collective-permute-start.16 = (bf16[384,128]{1,0:T(8,128)(2,1)S(1)}, bf16[384,128]{1,0:T(8,128)(2,1)S(1)}, u32[]{:S(2)}, u32[]{:S(2)}) collective-permute-start(bf16[384,128]{1,0:T(8,128)(2,1)S(1)} %get-tuple-element.83), channel_id=1, source_target_pairs={{0,8},{4,12},{8,16},{12,20},{16,24},{20,28},{24,0},{28,4},{1,9},{5... | collective-permute-start | bytes 294920 | tf_op jit(solution)/shard_map/ppermute | solution.py:408
  76.4 12.5 %collective-permute-start.17 = (bf16[384,128]{1,0:T(8,128)(2,1)S(1)}, bf16[384,128]{1,0:T(8,128)(2,1)S(1)}, u32[]{:S(2)}, u32[]{:S(2)}) collective-permute-start(bf16[384,128]{1,0:T(8,128)(2,1)S(1)} %get-tuple-element.84), channel_id=1, source_target_pairs={{0,12},{4,8},{8,20},{12,16},{16,28},{20,24},{24,4},{28,0},{1,13},{... | collective-permute-start | bytes 294920 | tf_op jit(solution)/shard_map/ppermute | solution.py:408
  84.9 8.4 %collective-permute-start.18 = (bf16[384,128]{1,0:T(8,128)(2,1)S(1)}, bf16[384,128]{1,0:T(8,128)(2,1)S(1)}, u32[]{:S(2)}, u32[]{:S(2)}) collective-permute-start(bf16[384,128]{1,0:T(8,128)(2,1)S(1)} %get-tuple-element.85), channel_id=1, source_target_pairs={{0,24},{4,28},{8,0},{12,4},{16,8},{20,12},{24,16},{28,20},{1,25},{... | collective-permute-start | bytes 294920 | tf_op jit(solution)/shard_map/ppermute | solution.py:408
  86.1 7.7 %collective-permute-start.19 = (bf16[384,128]{1,0:T(8,128)(2,1)S(1)}, bf16[384,128]{1,0:T(8,128)(2,1)S(1)}, u32[]{:S(2)}, u32[]{:S(2)}) collective-permute-start(bf16[384,128]{1,0:T(8,128)(2,1)S(1)} %get-tuple-element.86), channel_id=1, source_target_pairs={{0,28},{4,24},{8,4},{12,0},{16,12},{20,8},{24,20},{28,16},{1,29},{... | collective-permute-start | bytes 294920 | tf_op jit(solution)/shard_map/ppermute | solution.py:408
  88.6 26.0 %collective-permute-start.32 = (bf16[4,2,128,128]{3,2,1,0:T(8,128)(2,1)S(1)}, bf16[4,2,128,128]{3,2,1,0:T(8,128)(2,1)S(1)}, u32[]{:S(2)}, u32[]{:S(2)}) collective-permute-start(bf16[4,2,128,128]{3,2,1,0:T(8,128)(2,1)S(1)} %get-tuple-element.89), channel_id=1, source_target_pairs={{0,4},{4,0},{8,12},{12,8},{16,20},{20,16},{24,28},{28,24},{1,5},{5... | collective-permute-start | bytes 786440 | tf_op jit(solution)/shard_map/ppermute | solution.py:384
  88.9 17.8 %collective-permute-start.41 = (bf16[384,256]{1,0:T(8,128)(2,1)S(1)}, bf16[384,256]{1,0:T(8,128)(2,1)S(1)}, u32[]{:S(2)}, u32[]{:S(2)}) collective-permute-start(bf16[384,256]{1,0:T(8,128)(2,1)S(1)} %get-tuple-element.108), channel_id=1, source_target_pairs={{0,16},{4,20},{8,24},{12,28},{16,0},{20,4},{24,8},{28,12},{1,17},{... | collective-permute-start | bytes 589832 | tf_op jit(solution)/shard_map/ppermute | solution.py:408
  89.9 18.1 %collective-permute-start.42 = (bf16[384,256]{1,0:T(8,128)(2,1)S(1)}, bf16[384,256]{1,0:T(8,128)(2,1)S(1)}, u32[]{:S(2)}, u32[]{:S(2)}) collective-permute-start(bf16[384,256]{1,0:T(8,128)(2,1)S(1)} %get-tuple-element.109), channel_id=1, source_target_pairs={{0,20},{4,16},{8,28},{12,24},{16,4},{20,0},{24,12},{28,8},{1,21},{... | collective-permute-start | bytes 589832 | tf_op jit(solution)/shard_map/ppermute | solution.py:408
  93.3 51.6 %collective-permute-start.24 = (bf16[4,3,128,128]{3,2,1,0:T(8,128)(2,1)S(1)}, bf16[4,3,128,128]{3,2,1,0:T(8,128)(2,1)S(1)}, u32[]{:S(2)}, u32[]{:S(2)}) collective-permute-start(bf16[4,3,128,128]{3,2,1,0:T(8,128)(2,1)S(1)} %get-tuple-element.119), channel_id=1, source_target_pairs={{0,4},{4,0},{8,12},{12,8},{16,20},{20,16},{24,28},{28,24},{1,5},{5... | collective-permute-start | bytes 1179656 | tf_op jit(solution)/shard_map/ppermute | solution.py:384
  93.7 12.9 %collective-permute-start.20 = (bf16[384,128]{1,0:T(8,128)(2,1)S(1)}, bf16[384,128]{1,0:T(8,128)(2,1)S(1)}, u32[]{:S(2)}, u32[]{:S(2)}) collective-permute-start(bf16[384,128]{1,0:T(8,128)(2,1)S(1)} %get-tuple-element.87), channel_id=1, source_target_pairs={{0,4},{4,0},{8,12},{12,8},{16,20},{20,16},{24,28},{28,24},{1,5},{5... | collective-permute-start | bytes 294920 | tf_op jit(solution)/shard_map/ppermute | solution.py:408
  106.7 18.6 %collective-permute-start.43 = (bf16[384,256]{1,0:T(8,128)(2,1)S(1)}, bf16[384,256]{1,0:T(8,128)(2,1)S(1)}, u32[]{:S(2)}, u32[]{:S(2)}) collective-permute-start(bf16[384,256]{1,0:T(8,128)(2,1)S(1)} %get-tuple-element.110), channel_id=1, source_target_pairs={{0,8},{4,12},{8,16},{12,20},{16,24},{20,28},{24,0},{28,4},{1,9},{5... | collective-permute-start | bytes 589832 | tf_op jit(solution)/shard_map/ppermute | solution.py:408
  106.7 20.2 %collective-permute-start.44 = (bf16[384,256]{1,0:T(8,128)(2,1)S(1)}, bf16[384,256]{1,0:T(8,128)(2,1)S(1)}, u32[]{:S(2)}, u32[]{:S(2)}) collective-permute-start(bf16[384,256]{1,0:T(8,128)(2,1)S(1)} %get-tuple-element.111), channel_id=1, source_target_pairs={{0,12},{4,8},{8,20},{12,16},{16,28},{20,24},{24,4},{28,0},{1,13},{... | collective-permute-start | bytes 589832 | tf_op jit(solution)/shard_map/ppermute | solution.py:408
  108.0 18.8 %collective-permute-start.45 = (bf16[384,256]{1,0:T(8,128)(2,1)S(1)}, bf16[384,256]{1,0:T(8,128)(2,1)S(1)}, u32[]{:S(2)}, u32[]{:S(2)}) collective-permute-start(bf16[384,256]{1,0:T(8,128)(2,1)S(1)} %get-tuple-element.112), channel_id=1, source_target_pairs={{0,24},{4,28},{8,0},{12,4},{16,8},{20,12},{24,16},{28,20},{1,25},{... | collective-permute-start | bytes 589832 | tf_op jit(solution)/shard_map/ppermute | solution.py:408
  114.6 30.3 %collective-permute-start.46 = (bf16[384,256]{1,0:T(8,128)(2,1)S(1)}, bf16[384,256]{1,0:T(8,128)(2,1)S(1)}, u32[]{:S(2)}, u32[]{:S(2)}) collective-permute-start(bf16[384,256]{1,0:T(8,128)(2,1)S(1)} %get-tuple-element.113), channel_id=1, source_target_pairs={{0,28},{4,24},{8,4},{12,0},{16,12},{20,8},{24,20},{28,16},{1,29},{... | collective-permute-start | bytes 589832 | tf_op jit(solution)/shard_map/ppermute | solution.py:408
  125.2 28.2 %collective-permute-start.47 = (bf16[384,256]{1,0:T(8,128)(2,1)S(1)}, bf16[384,256]{1,0:T(8,128)(2,1)S(1)}, u32[]{:S(2)}, u32[]{:S(2)}) collective-permute-start(bf16[384,256]{1,0:T(8,128)(2,1)S(1)} %get-tuple-element.114), channel_id=1, source_target_pairs={{0,4},{4,0},{8,12},{12,8},{16,20},{20,16},{24,28},{28,24},{1,5},{5... | collective-permute-start | bytes 589832 | tf_op jit(solution)/shard_map/ppermute | solution.py:408
  126.8 29.8 %collective-permute-start.33 = (bf16[384,256]{1,0:T(8,128)(2,1)S(1)}, bf16[384,256]{1,0:T(8,128)(2,1)S(1)}, u32[]{:S(2)}, u32[]{:S(2)}) collective-permute-start(bf16[384,256]{1,0:T(8,128)(2,1)S(1)} %get-tuple-element.100), channel_id=1, source_target_pairs={{0,16},{4,20},{8,24},{12,28},{16,0},{20,4},{24,8},{28,12},{1,17},{... | collective-permute-start | bytes 589832 | tf_op jit(solution)/shard_map/ppermute | solution.py:408
  126.8 32.1 %collective-permute-start.34 = (bf16[384,256]{1,0:T(8,128)(2,1)S(1)}, bf16[384,256]{1,0:T(8,128)(2,1)S(1)}, u32[]{:S(2)}, u32[]{:S(2)}) collective-permute-start(bf16[384,256]{1,0:T(8,128)(2,1)S(1)} %get-tuple-element.101), channel_id=1, source_target_pairs={{0,20},{4,16},{8,28},{12,24},{16,4},{20,0},{24,12},{28,8},{1,21},{... | collective-permute-start | bytes 589832 | tf_op jit(solution)/shard_map/ppermute | solution.py:408
  144.9 14.4 %collective-permute-start.35 = (bf16[384,256]{1,0:T(8,128)(2,1)S(1)}, bf16[384,256]{1,0:T(8,128)(2,1)S(1)}, u32[]{:S(2)}, u32[]{:S(2)}) collective-permute-start(bf16[384,256]{1,0:T(8,128)(2,1)S(1)} %get-tuple-element.102), channel_id=1, source_target_pairs={{0,8},{4,12},{8,16},{12,20},{16,24},{20,28},{24,0},{28,4},{1,9},{5... | collective-permute-start | bytes 589832 | tf_op jit(solution)/shard_map/ppermute | solution.py:408
  144.9 22.7 %collective-permute-start.36 = (bf16[384,256]{1,0:T(8,128)(2,1)S(1)}, bf16[384,256]{1,0:T(8,128)(2,1)S(1)}, u32[]{:S(2)}, u32[]{:S(2)}) collective-permute-start(bf16[384,256]{1,0:T(8,128)(2,1)S(1)} %get-tuple-element.103), channel_id=1, source_target_pairs={{0,12},{4,8},{8,20},{12,16},{16,28},{20,24},{24,4},{28,0},{1,13},{... | collective-permute-start | bytes 589832 | tf_op jit(solution)/shard_map/ppermute | solution.py:408
  153.4 43.0 %collective-permute-start.25 = (bf16[384,384]{1,0:T(8,128)(2,1)S(1)}, bf16[384,384]{1,0:T(8,128)(2,1)S(1)}, u32[]{:S(2)}, u32[]{:S(2)}) collective-permute-start(bf16[384,384]{1,0:T(8,128)(2,1)S(1)} %get-tuple-element.92), channel_id=1, source_target_pairs={{0,16},{4,20},{8,24},{12,28},{16,0},{20,4},{24,8},{28,12},{1,17},{... | collective-permute-start | bytes 884744 | tf_op jit(solution)/shard_map/ppermute | solution.py:408
  156.6 41.0 %collective-permute-start.26 = (bf16[384,384]{1,0:T(8,128)(2,1)S(1)}, bf16[384,384]{1,0:T(8,128)(2,1)S(1)}, u32[]{:S(2)}, u32[]{:S(2)}) collective-permute-start(bf16[384,384]{1,0:T(8,128)(2,1)S(1)} %get-tuple-element.93), channel_id=1, source_target_pairs={{0,20},{4,16},{8,28},{12,24},{16,4},{20,0},{24,12},{28,8},{1,21},{... | collective-permute-start | bytes 884744 | tf_op jit(solution)/shard_map/ppermute | solution.py:408
  158.9 30.5 %collective-permute-start.37 = (bf16[384,256]{1,0:T(8,128)(2,1)S(1)}, bf16[384,256]{1,0:T(8,128)(2,1)S(1)}, u32[]{:S(2)}, u32[]{:S(2)}) collective-permute-start(bf16[384,256]{1,0:T(8,128)(2,1)S(1)} %get-tuple-element.104), channel_id=1, source_target_pairs={{0,24},{4,28},{8,0},{12,4},{16,8},{20,12},{24,16},{28,20},{1,25},{... | collective-permute-start | bytes 589832 | tf_op jit(solution)/shard_map/ppermute | solution.py:408
  159.4 35.2 %collective-permute-start.38 = (bf16[384,256]{1,0:T(8,128)(2,1)S(1)}, bf16[384,256]{1,0:T(8,128)(2,1)S(1)}, u32[]{:S(2)}, u32[]{:S(2)}) collective-permute-start(bf16[384,256]{1,0:T(8,128)(2,1)S(1)} %get-tuple-element.105), channel_id=1, source_target_pairs={{0,28},{4,24},{8,4},{12,0},{16,12},{20,8},{24,20},{28,16},{1,29},{... | collective-permute-start | bytes 589832 | tf_op jit(solution)/shard_map/ppermute | solution.py:408
  167.6 27.0 %collective-permute-start.39 = (bf16[384,256]{1,0:T(8,128)(2,1)S(1)}, bf16[384,256]{1,0:T(8,128)(2,1)S(1)}, u32[]{:S(2)}, u32[]{:S(2)}) collective-permute-start(bf16[384,256]{1,0:T(8,128)(2,1)S(1)} %get-tuple-element.106), channel_id=1, source_target_pairs={{0,4},{4,0},{8,12},{12,8},{16,20},{20,16},{24,28},{28,24},{1,5},{5... | collective-permute-start | bytes 589832 | tf_op jit(solution)/shard_map/ppermute | solution.py:408
  189.3 13.9 %collective-permute-start.27 = (bf16[384,384]{1,0:T(8,128)(2,1)S(1)}, bf16[384,384]{1,0:T(8,128)(2,1)S(1)}, u32[]{:S(2)}, u32[]{:S(2)}) collective-permute-start(bf16[384,384]{1,0:T(8,128)(2,1)S(1)} %get-tuple-element.94), channel_id=1, source_target_pairs={{0,8},{4,12},{8,16},{12,20},{16,24},{20,28},{24,0},{28,4},{1,9},{5... | collective-permute-start | bytes 884744 | tf_op jit(solution)/shard_map/ppermute | solution.py:408
  194.6 8.6 %collective-permute-start.28 = (bf16[384,384]{1,0:T(8,128)(2,1)S(1)}, bf16[384,384]{1,0:T(8,128)(2,1)S(1)}, u32[]{:S(2)}, u32[]{:S(2)}) collective-permute-start(bf16[384,384]{1,0:T(8,128)(2,1)S(1)} %get-tuple-element.95), channel_id=1, source_target_pairs={{0,12},{4,8},{8,20},{12,16},{16,28},{20,24},{24,4},{28,0},{1,13},{... | collective-permute-start | bytes 884744 | tf_op jit(solution)/shard_map/ppermute | solution.py:408
  194.6 9.0 %collective-permute-start.29 = (bf16[384,384]{1,0:T(8,128)(2,1)S(1)}, bf16[384,384]{1,0:T(8,128)(2,1)S(1)}, u32[]{:S(2)}, u32[]{:S(2)}) collective-permute-start(bf16[384,384]{1,0:T(8,128)(2,1)S(1)} %get-tuple-element.96), channel_id=1, source_target_pairs={{0,24},{4,28},{8,0},{12,4},{16,8},{20,12},{24,16},{28,20},{1,25},{... | collective-permute-start | bytes 884744 | tf_op jit(solution)/shard_map/ppermute | solution.py:408
  196.4 9.4 %collective-permute-start.30 = (bf16[384,384]{1,0:T(8,128)(2,1)S(1)}, bf16[384,384]{1,0:T(8,128)(2,1)S(1)}, u32[]{:S(2)}, u32[]{:S(2)}) collective-permute-start(bf16[384,384]{1,0:T(8,128)(2,1)S(1)} %get-tuple-element.97), channel_id=1, source_target_pairs={{0,28},{4,24},{8,4},{12,0},{16,12},{20,8},{24,20},{28,16},{1,29},{... | collective-permute-start | bytes 884744 | tf_op jit(solution)/shard_map/ppermute | solution.py:408
  197.6 10.9 %collective-permute-start.31 = (bf16[384,384]{1,0:T(8,128)(2,1)S(1)}, bf16[384,384]{1,0:T(8,128)(2,1)S(1)}, u32[]{:S(2)}, u32[]{:S(2)}) collective-permute-start(bf16[384,384]{1,0:T(8,128)(2,1)S(1)} %get-tuple-element.98), channel_id=1, source_target_pairs={{0,4},{4,0},{8,12},{12,8},{16,20},{20,16},{24,28},{28,24},{1,5},{5... | collective-permute-start | bytes 884744 | tf_op jit(solution)/shard_map/ppermute | solution.py:408
  (4 other events, 67.5 us)

commit v9 on v7

--- a/solution.py
+++ b/solution.py
@@ -147,13 +147,13 @@
         cols = pl.ds(column(here, lax.rem(here[0] + step, m), side, n), wide)
         slot = 2 * step + side
         return [
-            pltpu.make_async_copy(source.at[:, cols], buf.at[slot], sems.at[which, slot])
+            pltpu.make_async_copy(source.at[:, cols], buf.at[slot, :, :wide], sems.at[which, slot])
             for which, (source, buf) in enumerate(((queries, qbuf), (keys, kbuf), (values, vbuf)))
         ]
 
     def sends(step):
         return [
-            pltpu.make_async_copy(held.at[slot], outs[order.index(slot)], sems.at[3, slot])
+            pltpu.make_async_copy(held.at[slot, :, :wide], outs[order.index(slot)], sems.at[3, slot])
             for slot in (2 * step, 2 * step + 1)
         ]
 
@@ -217,7 +217,7 @@
     rows, m = queries.shape[0], n // 2
     width = sum(size for _, size in spans)
     wide = width * HEAD
-    tokens = pltpu.VMEM((n, rows, wide), jnp.bfloat16)
+    tokens = pltpu.VMEM((n, rows, (width + 1 - width % 2) * HEAD), jnp.bfloat16)
     state = pltpu.VMEM((m, width, HEAD, HEAD), jnp.bfloat16)
     return pl.pallas_call(
         functools.partial(attend_body, n, spans, order),
@@ -237,7 +237,7 @@
             pltpu.SemaphoreType.DMA((4, n)),
             pltpu.SemaphoreType.DMA((1 + 2 * len(states),)),
         ],
-        compiler_params=params(8 * n * rows * wide + 2 * n * width * HEAD * HEAD + 4 * HEADS * HEAD),
+        compiler_params=params(8 * n * rows * (wide + HEAD) + 2 * n * width * HEAD * HEAD + 4 * HEADS * HEAD),
         cost_estimate=pl.CostEstimate(
             flops=2 * n * width * rows * HEAD * (2 * rows + HEAD),
             bytes_accessed=8 * rows * n * wide,

time: 201 us -> 199 us (0.990)
  starting transfers between devices: 74.2 us -> 76.6 us
  Pallas kernels: 41.3 us -> 39 us
  waiting for transfers between devices: 73.7 us -> 71.6 us
    ppermute x21, starting transfers between devices: 54.8 us -> 57.2 us  [sent(): lax.ppermute(self.hold(self.get('mixed', c)[k], 'sent', c, k), 'seq', pairs)]
    pallas_call x3, Pallas kernels: 25.5 us -> 23.2 us  [attend(): pl.pallas_call(functools.partial(attend_body, n, spans, order), in_specs=...]
    ppermute x21, waiting for transfers between devices: 54.6 us -> 52.5 us  [sent(): lax.ppermute(self.hold(self.get('mixed', c)[k], 'sent', c, k), 'seq', pairs)]
  transfers between devices with their start and end apart: 36 -> 36, of which waited for: 14 -> 14; matrix products, arithmetic and copies ran while one was open for 4% -> 4% of each run, Pallas kernels for 18% -> 17%
where the time goes in v9:
time: 199 us; the launch traced here: 195 us
  starting transfers between devices  76.6 us (38%)
  waiting for transfers between devices  71.6 us (36%)
  Pallas kernels  39 us (20%)
  other arithmetic  7.61 us (4%)
    ppermute x21, starting transfers between devices, sent(): lax.ppermute(self.hold(self.get('mixed', c)[k], 'sent', c, k), 'seq', pairs)  57.2 us
    ppermute x21, waiting for transfers between devices, sent(): lax.ppermute(self.hold(self.get('mixed', c)[k], 'sent', c, k), 'seq', pairs)  52.5 us
    pallas_call x3, Pallas kernels, attend(): pl.pallas_call(functools.partial(attend_body, n, spans, order), in_specs=...  23.2 us
    ppermute x12, waiting for transfers between devices, prefix(): return lax.ppermute(self.get('message', c, s), 'seq', pairs)  17.7 us
    ppermute x12, starting transfers between devices, prefix(): return lax.ppermute(self.get('message', c, s), 'seq', pairs)  14.7 us
    pallas_call x2, Pallas kernels, local_states(): pl.pallas_call(functools.partial(local_body, n, widths, swaps), in_specs=...  8.47 us
    pallas_call x3, Pallas kernels, put(): pl.pallas_call(functools.partial(put_body, n, order), in_specs=[pl.BlockS...  7.33 us
    convert_element_type x10, other arithmetic, message(): return self.hold(value.astype(jnp.bfloat16), 'message', c, s)  4.84 us
  transfers between devices with their start and end apart: 36, of which 14 were waited for; matrix products, arithmetic and copies ran while one was open for 4% of the time, Pallas kernels for 17%

profile of v9, /device:TPU:8, one launch (start us, length us, event | category | flops | bytes accessed | tf_op | source)
XLA Modules:
  0.0 195.3 jit_solution(10116778891138731798)
XLA Ops:
  0.1 3.4 %local.3 = (f32[4,2,128,128]{3,2,1,0:T(8,128)S(1)}, bf16[4,2,128,128]{3,2,1,0:T(8,128)(2,1)S(1)}) custom-call(s32[2]{0:T(128)S(1)} %pad_add_fusion.place, s32[1]{0:T(128)} %constant.38.clone.1.low, bf16[384,8192]{1,0:T(8,128)(2,1)} %keys.9, bf16[384,8192]{1,0:T(8,128)(2,1)} %values.9), custom_call_target="tpu_custom_call" | custom-call | flops 201326592 | bytes 3145728 | tf_op jit(solution)/shard_map/local/pallas_call | solution.py:98
  3.5 1.6 collective-permute-start.2
  5.1 5.0 %local.2 = (f32[4,3,128,128]{3,2,1,0:T(8,128)S(1)}, f32[4,3,128,128]{3,2,1,0:T(8,128)S(1)}, bf16[4,3,128,128]{3,2,1,0:T(8,128)(2,1)S(1)}, bf16[4,3,128,128]{3,2,1,0:T(8,128)(2,1)S(1)}) custom-call(s32[2]{0:T(128)S(1)} %pad_add_fusion.place, s32[1]{0:T(128)} %constant.37.clone.1.low, bf16[384,8192]{1,0:T(8,128)(2,1)} %keys.9, bf16[384,8192]{1,0:T(8,128)(2,1)} %values.9), custom_call_target="tpu_custom_call" | custom-call | flops 603979776 | bytes 9437184 | tf_op jit(solution)/shard_map/local/pallas_call | solution.py:98
  10.1 1.5 collective-permute-done.2
  11.7 1.3 collective-permute-start.3
  13.0 1.6 collective-permute-start.1
  14.6 6.2 %collective-permute-done.3 = bf16[4,2,128,128]{3,2,1,0:T(8,128)(2,1)S(1)} collective-permute-done((bf16[4,2,128,128]{3,2,1,0:T(8,128)(2,1)S(1)}, bf16[4,2,128,128]{3,2,1,0:T(8,128)(2,1)S(1)}, u32[]{:S(2)}, u32[]{:S(2)}) %collective-permute-start.3) | collective-permute-done | bytes 262176 | tf_op jit(solution)/shard_map/ppermute | solution.py:381
  20.7 0.8 add_convert_fusion.5
  21.5 2.1 %collective-permute-start.5 = (bf16[4,2,128,128]{3,2,1,0:T(8,128)(2,1)}, bf16[4,2,128,128]{3,2,1,0:T(8,128)(2,1)}, u32[]{:S(2)}, u32[]{:S(2)}) collective-permute-start(bf16[4,2,128,128]{3,2,1,0:T(8,128)(2,1)} %add_convert_fusion.5), channel_id=1, source_target_pairs={{8,16},{12,20},{9,17},{13,21},{10,18},{14,22},{11,19},{15,23}} | collective-permute-start | bytes 786440 | tf_op jit(solution)/shard_map/ppermute | solution.py:381
  23.7 0.8 fusion.7
  24.5 1.3 collective-permute-start.4
  25.8 1.6 collective-permute-start
  27.4 1.1 add_convert_fusion.4
  29.2 6.5 %collective-permute-done.4 = bf16[4,3,128,128]{3,2,1,0:T(8,128)(2,1)} collective-permute-done((bf16[4,3,128,128]{3,2,1,0:T(8,128)(2,1)}, bf16[4,3,128,128]{3,2,1,0:T(8,128)(2,1)}, u32[]{:S(2)}, u32[]{:S(2)}) %collective-permute-start.4) | collective-permute-done | bytes 393248 | tf_op jit(solution)/shard_map/ppermute | solution.py:381
  35.8 1.2 add_convert_fusion.3
  36.9 1.3 collective-permute-start.7
  38.4 1.3 collective-permute-start.6
  39.7 1.4 fusion.5
  41.0 1.6 collective-permute-start.11
  42.6 1.5 collective-permute-done.7
  45.0 3.4 %collective-permute-done.6 = bf16[4,3,128,128]{3,2,1,0:T(8,128)(2,1)S(1)} collective-permute-done((bf16[4,3,128,128]{3,2,1,0:T(8,128)(2,1)S(1)}, bf16[4,3,128,128]{3,2,1,0:T(8,128)(2,1)S(1)}, u32[]{:S(2)}, u32[]{:S(2)}) %collective-permute-start.6) | collective-permute-done | bytes 393248 | tf_op jit(solution)/shard_map/ppermute | solution.py:381
  48.5 1.6 collective-permute-start.9
  50.2 6.2 %attend.3 = (bf16[384,256]{1,0:T(8,128)(2,1)S(1)}, bf16[384,256]{1,0:T(8,128)(2,1)S(1)}, bf16[384,256]{1,0:T(8,128)(2,1)S(1)}, bf16[384,256]{1,0:T(8,128)(2,1)S(...) custom-call(s32[2]{0:T(128)S(1)} %pad_add_fusion.place, ...), custom_call_target="tpu_custom_call" | custom-call | flops 1409286144 | bytes 6291456 | tf_op jit(solution)/shard_map/attend/pallas_call | solution.py:222
  56.4 1.4 fusion.1
  58.7 3.9 %collective-permute-start.30 = (bf16[384,256]{1,0:T(8,128)(2,1)S(1)}, bf16[384,256]{1,0:T(8,128)(2,1)S(1)}, u32[]{:S(2)}, u32[]{:S(2)}) collective-permute-start(bf16[384,256]{1,0:T(8,128)(2,1)S(1)} %get-tuple-element.81), channel_id=1, source_target_pairs={{0,20},{4,16},{8,28},{12,24},{16,4},{20,0},{24,12},{28,8},{1,21},{... | collective-permute-start | bytes 589832 | tf_op jit(solution)/shard_map/ppermute | solution.py:405
  63.4 1.6 collective-permute-start.13
  65.0 10.7 %collective-permute-start.31 = (bf16[384,256]{1,0:T(8,128)(2,1)S(1)}, bf16[384,256]{1,0:T(8,128)(2,1)S(1)}, u32[]{:S(2)}, u32[]{:S(2)}) collective-permute-start(bf16[384,256]{1,0:T(8,128)(2,1)S(1)} %get-tuple-element.82), channel_id=1, source_target_pairs={{0,8},{4,12},{8,16},{12,20},{16,24},{20,28},{24,0},{28,4},{1,9},{5... | collective-permute-start | bytes 589832 | tf_op jit(solution)/shard_map/ppermute | solution.py:405
  75.7 2.5 %collective-permute-start.32 = (bf16[384,256]{1,0:T(8,128)(2,1)S(1)}, bf16[384,256]{1,0:T(8,128)(2,1)S(1)}, u32[]{:S(2)}, u32[]{:S(2)}) collective-permute-start(bf16[384,256]{1,0:T(8,128)(2,1)S(1)} %get-tuple-element.83), channel_id=1, source_target_pairs={{0,12},{4,8},{8,20},{12,16},{16,28},{20,24},{24,4},{28,0},{1,13},{... | collective-permute-start | bytes 589832 | tf_op jit(solution)/shard_map/ppermute | solution.py:405
  78.2 4.2 %collective-permute-start.33 = (bf16[384,256]{1,0:T(8,128)(2,1)S(1)}, bf16[384,256]{1,0:T(8,128)(2,1)S(1)}, u32[]{:S(2)}, u32[]{:S(2)}) collective-permute-start(bf16[384,256]{1,0:T(8,128)(2,1)S(1)} %get-tuple-element.84), channel_id=1, source_target_pairs={{0,24},{4,28},{8,0},{12,4},{16,8},{20,12},{24,16},{28,20},{1,25},{... | collective-permute-start | bytes 589832 | tf_op jit(solution)/shard_map/ppermute | solution.py:405
  82.4 8.5 %attend.5 = (bf16[384,384]{1,0:T(8,128)(2,1)S(1)}, bf16[384,384]{1,0:T(8,128)(2,1)S(1)}, bf16[384,384]{1,0:T(8,128)(2,1)S(1)}, bf16[384,384]{1,0:T(8,128)(2,1)S(...) custom-call(s32[2]{0:T(128)S(1)} %pad_add_fusion.place, ...), custom_call_target="tpu_custom_call" | custom-call | flops 2113929216 | bytes 9437184 | tf_op jit(solution)/shard_map/attend/pallas_call | solution.py:222
  90.9 0.8 collective-permute-start.22
  91.8 8.2 %collective-permute-done.32.refs_4_ = bf16[384,256]{1,0:T(8,128)(2,1)S(1)} collective-permute-done((bf16[384,256]{1,0:T(8,128)(2,1)S(1)}, bf16[384,256]{1,0:T(8,128)(2,1)S(1)}, u32[]{:S(2)}, u32[]{:S(2)}) %collective-permute-start.32) | collective-permute-done | bytes 196640 | tf_op jit(solution)/shard_map/ppermute | solution.py:405
  100.0 4.3 %collective-permute-start.24 = (bf16[384,384]{1,0:T(8,128)(2,1)S(1)}, bf16[384,384]{1,0:T(8,128)(2,1)S(1)}, u32[]{:S(2)}, u32[]{:S(2)}) collective-permute-start(bf16[384,384]{1,0:T(8,128)(2,1)S(1)} %get-tuple-element.74), channel_id=1, source_target_pairs={{0,8},{4,12},{8,16},{12,20},{16,24},{20,28},{24,0},{28,4},{1,9},{5... | collective-permute-start | bytes 884744 | tf_op jit(solution)/shard_map/ppermute | solution.py:405
  104.2 7.7 %collective-permute-done.34.refs_6_ = bf16[384,256]{1,0:T(8,128)(2,1)S(1)} collective-permute-done((bf16[384,256]{1,0:T(8,128)(2,1)S(1)}, bf16[384,256]{1,0:T(8,128)(2,1)S(1)}, u32[]{:S(2)}, u32[]{:S(2)}) %collective-permute-start.34) | collective-permute-done | bytes 196640 | tf_op jit(solution)/shard_map/ppermute | solution.py:405
  112.0 8.4 %attend.4 = (bf16[384,384]{1,0:T(8,128)(2,1)S(1)}, bf16[384,384]{1,0:T(8,128)(2,1)S(1)}, bf16[384,384]{1,0:T(8,128)(2,1)S(1)}, bf16[384,384]{1,0:T(8,128)(2,1)S(...) custom-call(s32[2]{0:T(128)S(1)} %pad_add_fusion.place, ...), custom_call_target="tpu_custom_call" | custom-call | flops 2113929216 | bytes 9437184 | tf_op jit(solution)/shard_map/attend/pallas_call | solution.py:222
  120.8 3.2 %collective-permute-start.26 = (bf16[384,384]{1,0:T(8,128)(2,1)S(1)}, bf16[384,384]{1,0:T(8,128)(2,1)S(1)}, u32[]{:S(2)}, u32[]{:S(2)}) collective-permute-start(bf16[384,384]{1,0:T(8,128)(2,1)S(1)} %get-tuple-element.76), channel_id=1, source_target_pairs={{0,24},{4,28},{8,0},{12,4},{16,8},{20,12},{24,16},{28,20},{1,25},{... | collective-permute-start | bytes 884744 | tf_op jit(solution)/shard_map/ppermute | solution.py:405
  124.0 2.0 %collective-permute-start.27 = (bf16[384,384]{1,0:T(8,128)(2,1)S(1)}, bf16[384,384]{1,0:T(8,128)(2,1)S(1)}, u32[]{:S(2)}, u32[]{:S(2)}) collective-permute-start(bf16[384,384]{1,0:T(8,128)(2,1)S(1)} %get-tuple-element.77), channel_id=1, source_target_pairs={{0,28},{4,24},{8,4},{12,0},{16,12},{20,8},{24,20},{28,16},{1,29},{... | collective-permute-start | bytes 884744 | tf_op jit(solution)/shard_map/ppermute | solution.py:405
  126.2 9.0 %collective-permute-done.24.refs_3_ = bf16[384,384]{1,0:T(8,128)(2,1)S(1)} collective-permute-done((bf16[384,384]{1,0:T(8,128)(2,1)S(1)}, bf16[384,384]{1,0:T(8,128)(2,1)S(1)}, u32[]{:S(2)}, u32[]{:S(2)}) %collective-permute-start.24) | collective-permute-done | bytes 294944 | tf_op jit(solution)/shard_map/ppermute | solution.py:405
  135.3 12.6 %collective-permute-done.25.refs_4_ = bf16[384,384]{1,0:T(8,128)(2,1)S(1)} collective-permute-done((bf16[384,384]{1,0:T(8,128)(2,1)S(1)}, bf16[384,384]{1,0:T(8,128)(2,1)S(1)}, u32[]{:S(2)}, u32[]{:S(2)}) %collective-permute-start.25) | collective-permute-done | bytes 294944 | tf_op jit(solution)/shard_map/ppermute | solution.py:405
  147.9 7.3 %collective-permute-start.16 = (bf16[384,384]{1,0:T(8,128)(2,1)S(1)}, bf16[384,384]{1,0:T(8,128)(2,1)S(1)}, u32[]{:S(2)}, u32[]{:S(2)}) collective-permute-start(bf16[384,384]{1,0:T(8,128)(2,1)S(1)} %get-tuple-element.66), channel_id=1, source_target_pairs={{0,8},{4,12},{8,16},{12,20},{16,24},{20,28},{24,0},{28,4},{1,9},{5... | collective-permute-start | bytes 884744 | tf_op jit(solution)/shard_map/ppermute | solution.py:405
  155.2 8.3 %collective-permute-done.27.refs_6_ = bf16[384,384]{1,0:T(8,128)(2,1)S(1)} collective-permute-done((bf16[384,384]{1,0:T(8,128)(2,1)S(1)}, bf16[384,384]{1,0:T(8,128)(2,1)S(1)}, u32[]{:S(2)}, u32[]{:S(2)}) %collective-permute-start.27) | collective-permute-done | bytes 294944 | tf_op jit(solution)/shard_map/ppermute | solution.py:405
  163.4 13.2 %collective-permute-start.19 = (bf16[384,384]{1,0:T(8,128)(2,1)S(1)}, bf16[384,384]{1,0:T(8,128)(2,1)S(1)}, u32[]{:S(2)}, u32[]{:S(2)}) collective-permute-start(bf16[384,384]{1,0:T(8,128)(2,1)S(1)} %get-tuple-element.69), channel_id=1, source_target_pairs={{0,28},{4,24},{8,4},{12,0},{16,12},{20,8},{24,20},{28,16},{1,29},{... | collective-permute-start | bytes 884744 | tf_op jit(solution)/shard_map/ppermute | solution.py:405
  176.6 5.0 %collective-permute-start.20 = (bf16[384,384]{1,0:T(8,128)(2,1)S(1)}, bf16[384,384]{1,0:T(8,128)(2,1)S(1)}, u32[]{:S(2)}, u32[]{:S(2)}) collective-permute-start(bf16[384,384]{1,0:T(8,128)(2,1)S(1)} %get-tuple-element.70), channel_id=1, source_target_pairs={{0,4},{4,0},{8,12},{12,8},{16,20},{20,16},{24,28},{28,24},{1,5},{5... | collective-permute-start | bytes 884744 | tf_op jit(solution)/shard_map/ppermute | solution.py:405
  181.6 2.3 %put.3 = (bf16[3072,1024]{1,0:T(8,128)(2,1)}, s32[2]{0:T(128)}) custom-call(s32[2]{0:T(128)S(1)} %pad_add_fusion.place, s32[1]{0:T(128)} %constant.38.clone.1.low, bf16[384,256]{1,0:T(8,128)(2,1)S(1)} %get-tuple-element.79.refs_0_, bf16[384,256]{1,0:T(8,128)(2,1)S(1)} %collective-permute-done.29.refs_1_, ...), custom_call_target="tpu_custom_call" | custom-call | tf_op jit(solution)/shard_map/put/pallas_call | solution.py:274
  183.8 2.5 %put.4 = (bf16[3072,1024]{1,0:T(8,128)(2,1)}, s32[2]{0:T(128)}) custom-call(s32[2]{0:T(128)S(1)} %pad_add_fusion.place, s32[1]{0:T(128)} %constant.37.clone.1.low, bf16[384,384]{1,0:T(8,128)(2,1)S(1)} %get-tuple-element.71.refs_0_, bf16[384,384]{1,0:T(8,128)(2,1)S(1)} %collective-permute-done.22.refs_1_, ...), custom_call_target="tpu_custom_call", output_to_operand_aliasing={{0}: (10, {})} | custom-call | tf_op jit(solution)/shard_map/put/pallas_call | solution.py:274
  186.4 4.4 %collective-permute-done.17.refs_4_ = bf16[384,384]{1,0:T(8,128)(2,1)S(1)} collective-permute-done((bf16[384,384]{1,0:T(8,128)(2,1)S(1)}, bf16[384,384]{1,0:T(8,128)(2,1)S(1)}, u32[]{:S(2)}, u32[]{:S(2)}) %collective-permute-start.17) | collective-permute-done | bytes 294944 | tf_op jit(solution)/shard_map/ppermute | solution.py:405
  190.8 1.6 collective-permute-done.19.refs_6_
  192.6 2.5 %put.5 = (bf16[3072,1024]{1,0:T(8,128)(2,1)}, s32[2]{0:T(128)}) custom-call(s32[2]{0:T(128)S(1)} %pad_add_fusion.place, s32[1]{0:T(128)} %constant.36.clone.1.low, bf16[384,384]{1,0:T(8,128)(2,1)S(1)} %get-tuple-element.63.refs_0_, bf16[384,384]{1,0:T(8,128)(2,1)S(1)} %collective-permute-done.14.refs_1_, ...), custom_call_target="tpu_custom_call", output_to_operand_aliasing={{0}: (10, {})} | custom-call | tf_op jit(solution)/shard_map/put/pallas_call | solution.py:274
  (51 shorter events, 4.4 us)
Async XLA Ops:
  3.5 8.1 %collective-permute-start.2 = (bf16[4,2,128,128]{3,2,1,0:T(8,128)(2,1)S(1)}, bf16[4,2,128,128]{3,2,1,0:T(8,128)(2,1)S(1)}, u32[]{:S(2)}, u32[]{:S(2)}) collective-permute-start(bf16[4,2,128,128]{3,2,1,0:T(8,128)(2,1)S(1)} %get-tuple-element.52), channel_id=1, source_target_pairs={{0,4},{4,0},{8,12},{12,8},{16,20},{20,16},{24,28},{28,24},{1,5},{5... | collective-permute-start | bytes 786440 | tf_op jit(solution)/shard_map/ppermute | solution.py:354
  11.6 12.9 %copy-start.1 = (bf16[4,2,128,128]{3,2,1,0:T(8,128)(2,1)}, bf16[4,2,128,128]{3,2,1,0:T(8,128)(2,1)S(1)}, u32[]{:S(2)}) copy-start(bf16[4,2,128,128]{3,2,1,0:T(8,128)(2,1)S(1)} %collective-permute-done.2) | copy-start | bytes 786436
  11.7 9.1 %collective-permute-start.3 = (bf16[4,2,128,128]{3,2,1,0:T(8,128)(2,1)S(1)}, bf16[4,2,128,128]{3,2,1,0:T(8,128)(2,1)S(1)}, u32[]{:S(2)}, u32[]{:S(2)}) collective-permute-start(bf16[4,2,128,128]{3,2,1,0:T(8,128)(2,1)S(1)} %fusion.8), channel_id=1, source_target_pairs={{0,8},{4,12},{1,9},{5,13},{2,10},{6,14},{3,11},{7,15}} | collective-permute-start | bytes 786440 | tf_op jit(solution)/shard_map/ppermute | solution.py:381
  13.0 10.7 %collective-permute-start.1 = (bf16[4,3,128,128]{3,2,1,0:T(8,128)(2,1)S(1)}, bf16[4,3,128,128]{3,2,1,0:T(8,128)(2,1)S(1)}, u32[]{:S(2)}, u32[]{:S(2)}) collective-permute-start(bf16[4,3,128,128]{3,2,1,0:T(8,128)(2,1)S(1)} %get-tuple-element.50), channel_id=1, source_target_pairs={{0,4},{4,0},{8,12},{12,8},{16,20},{20,16},{24,28},{28,24},{1,5},{5... | collective-permute-start | bytes 1179656 | tf_op jit(solution)/shard_map/ppermute | solution.py:354
  20.7 2.9 %copy-start.2 = (bf16[4,2,128,128]{3,2,1,0:T(8,128)(2,1)}, bf16[4,2,128,128]{3,2,1,0:T(8,128)(2,1)S(1)}, u32[]{:S(2)}) copy-start(bf16[4,2,128,128]{3,2,1,0:T(8,128)(2,1)S(1)} %collective-permute-done.3) | copy-start | bytes 786436
  21.5 28.6 %copy-start = (f32[8192]{0:T(1024)S(1)}, f32[8192]{0:T(1024)}, u32[]{:S(2)}) copy-start(f32[8192]{0:T(1024)} %param.7) | copy-start | bytes 98308
  21.5 5.9 %collective-permute-start.5 = (bf16[4,2,128,128]{3,2,1,0:T(8,128)(2,1)}, bf16[4,2,128,128]{3,2,1,0:T(8,128)(2,1)}, u32[]{:S(2)}, u32[]{:S(2)}) collective-permute-start(bf16[4,2,128,128]{3,2,1,0:T(8,128)(2,1)} %add_convert_fusion.5), channel_id=1, source_target_pairs={{8,16},{12,20},{9,17},{13,21},{10,18},{14,22},{11,19},{15,23}} | collective-permute-start | bytes 786440 | tf_op jit(solution)/shard_map/ppermute | solution.py:381
  24.5 11.2 %collective-permute-start.4 = (bf16[4,3,128,128]{3,2,1,0:T(8,128)(2,1)}, bf16[4,3,128,128]{3,2,1,0:T(8,128)(2,1)}, u32[]{:S(2)}, u32[]{:S(2)}) collective-permute-start(bf16[4,3,128,128]{3,2,1,0:T(8,128)(2,1)} %fusion.7), channel_id=1, source_target_pairs={{0,8},{4,12},{1,9},{5,13},{2,10},{6,14},{3,11},{7,15}} | collective-permute-start | bytes 1179656 | tf_op jit(solution)/shard_map/ppermute | solution.py:381
  25.8 12.5 %collective-permute-start = (bf16[4,3,128,128]{3,2,1,0:T(8,128)(2,1)S(1)}, bf16[4,3,128,128]{3,2,1,0:T(8,128)(2,1)S(1)}, u32[]{:S(2)}, u32[]{:S(2)}) collective-permute-start(bf16[4,3,128,128]{3,2,1,0:T(8,128)(2,1)S(1)} %get-tuple-element.48), channel_id=1, source_target_pairs={{0,4},{4,0},{8,12},{12,8},{16,20},{20,16},{24,28},{28,24},{1,5},{5... | collective-permute-start | bytes 1179656 | tf_op jit(solution)/shard_map/ppermute | solution.py:354
  28.5 11.1 %collective-permute-start.8 = (bf16[4,2,128,128]{3,2,1,0:T(8,128)(2,1)S(1)}, bf16[4,2,128,128]{3,2,1,0:T(8,128)(2,1)S(1)}, u32[]{:S(2)}, u32[]{:S(2)}) collective-permute-start(bf16[4,2,128,128]{3,2,1,0:T(8,128)(2,1)S(1)} %add_convert_fusion.4), channel_id=1, source_target_pairs={{16,24},{20,28},{17,25},{21,29},{18,26},{22,30},{19,27},{23,31}} | collective-permute-start | bytes 786440 | tf_op jit(solution)/shard_map/ppermute | solution.py:381
  36.9 7.2 %collective-permute-start.7 = (bf16[4,3,128,128]{3,2,1,0:T(8,128)(2,1)S(1)}, bf16[4,3,128,128]{3,2,1,0:T(8,128)(2,1)S(1)}, u32[]{:S(2)}, u32[]{:S(2)}) collective-permute-start(bf16[4,3,128,128]{3,2,1,0:T(8,128)(2,1)S(1)} %add_convert_fusion.3), channel_id=1, source_target_pairs={{8,16},{12,20},{9,17},{13,21},{10,18},{14,22},{11,19},{15,23}} | collective-permute-start | bytes 1179656 | tf_op jit(solution)/shard_map/ppermute | solution.py:381
  38.4 10.0 %collective-permute-start.6 = (bf16[4,3,128,128]{3,2,1,0:T(8,128)(2,1)S(1)}, bf16[4,3,128,128]{3,2,1,0:T(8,128)(2,1)S(1)}, u32[]{:S(2)}, u32[]{:S(2)}) collective-permute-start(bf16[4,3,128,128]{3,2,1,0:T(8,128)(2,1)S(1)} %fusion.6), channel_id=1, source_target_pairs={{0,8},{4,12},{1,9},{5,13},{2,10},{6,14},{3,11},{7,15}} | collective-permute-start | bytes 1179656 | tf_op jit(solution)/shard_map/ppermute | solution.py:381
  41.0 9.1 %collective-permute-start.11 = (bf16[4,2,128,128]{3,2,1,0:T(8,128)(2,1)S(1)}, bf16[4,2,128,128]{3,2,1,0:T(8,128)(2,1)S(1)}, u32[]{:S(2)}, u32[]{:S(2)}) collective-permute-start(bf16[4,2,128,128]{3,2,1,0:T(8,128)(2,1)S(1)} %get-tuple-element.94), channel_id=1, source_target_pairs={{0,4},{4,0},{8,12},{12,8},{16,20},{20,16},{24,28},{28,24},{1,5},{5... | collective-permute-start | bytes 786440 | tf_op jit(solution)/shard_map/ppermute | solution.py:381
  44.3 12.2 %collective-permute-start.10 = (bf16[4,3,128,128]{3,2,1,0:T(8,128)(2,1)S(1)}, bf16[4,3,128,128]{3,2,1,0:T(8,128)(2,1)S(1)}, u32[]{:S(2)}, u32[]{:S(2)}) collective-permute-start(bf16[4,3,128,128]{3,2,1,0:T(8,128)(2,1)S(1)} %add_convert_fusion.1), channel_id=1, source_target_pairs={{16,24},{20,28},{17,25},{21,29},{18,26},{22,30},{19,27},{23,31}} | collective-permute-start | bytes 1179656 | tf_op jit(solution)/shard_map/ppermute | solution.py:381
  48.5 9.3 %collective-permute-start.9 = (bf16[4,3,128,128]{3,2,1,0:T(8,128)(2,1)S(1)}, bf16[4,3,128,128]{3,2,1,0:T(8,128)(2,1)S(1)}, u32[]{:S(2)}, u32[]{:S(2)}) collective-permute-start(bf16[4,3,128,128]{3,2,1,0:T(8,128)(2,1)S(1)} %add_convert_fusion.2), channel_id=1, source_target_pairs={{8,16},{12,20},{9,17},{13,21},{10,18},{14,22},{11,19},{15,23}} | collective-permute-start | bytes 1179656 | tf_op jit(solution)/shard_map/ppermute | solution.py:381
  58.0 5.2 %collective-permute-start.12 = (bf16[4,3,128,128]{3,2,1,0:T(8,128)(2,1)S(1)}, bf16[4,3,128,128]{3,2,1,0:T(8,128)(2,1)S(1)}, u32[]{:S(2)}, u32[]{:S(2)}) collective-permute-start(bf16[4,3,128,128]{3,2,1,0:T(8,128)(2,1)S(1)} %add_convert_fusion), channel_id=1, source_target_pairs={{16,24},{20,28},{17,25},{21,29},{18,26},{22,30},{19,27},{23,31}} | collective-permute-start | bytes 1179656 | tf_op jit(solution)/shard_map/ppermute | solution.py:381
  58.7 17.1 %collective-permute-start.29 = (bf16[384,256]{1,0:T(8,128)(2,1)S(1)}, bf16[384,256]{1,0:T(8,128)(2,1)S(1)}, u32[]{:S(2)}, u32[]{:S(2)}) collective-permute-start(bf16[384,256]{1,0:T(8,128)(2,1)S(1)} %get-tuple-element.80), channel_id=1, source_target_pairs={{0,16},{4,20},{8,24},{12,28},{16,0},{20,4},{24,8},{28,12},{1,17},{... | collective-permute-start | bytes 589832 | tf_op jit(solution)/shard_map/ppermute | solution.py:405
  58.7 19.5 %collective-permute-start.30 = (bf16[384,256]{1,0:T(8,128)(2,1)S(1)}, bf16[384,256]{1,0:T(8,128)(2,1)S(1)}, u32[]{:S(2)}, u32[]{:S(2)}) collective-permute-start(bf16[384,256]{1,0:T(8,128)(2,1)S(1)} %get-tuple-element.81), channel_id=1, source_target_pairs={{0,20},{4,16},{8,28},{12,24},{16,4},{20,0},{24,12},{28,8},{1,21},{... | collective-permute-start | bytes 589832 | tf_op jit(solution)/shard_map/ppermute | solution.py:405
  62.6 19.8 %collective-permute-start.21 = (bf16[4,3,128,128]{3,2,1,0:T(8,128)(2,1)S(1)}, bf16[4,3,128,128]{3,2,1,0:T(8,128)(2,1)S(1)}, u32[]{:S(2)}, u32[]{:S(2)}) collective-permute-start(bf16[4,3,128,128]{3,2,1,0:T(8,128)(2,1)S(1)} %get-tuple-element.61), channel_id=1, source_target_pairs={{0,4},{4,0},{8,12},{12,8},{16,20},{20,16},{24,28},{28,24},{1,5},{5... | collective-permute-start | bytes 1179656 | tf_op jit(solution)/shard_map/ppermute | solution.py:381
  63.4 48.6 %collective-permute-start.13 = (bf16[4,3,128,128]{3,2,1,0:T(8,128)(2,1)S(1)}, bf16[4,3,128,128]{3,2,1,0:T(8,128)(2,1)S(1)}, u32[]{:S(2)}, u32[]{:S(2)}) collective-permute-start(bf16[4,3,128,128]{3,2,1,0:T(8,128)(2,1)S(1)} %get-tuple-element.91), channel_id=1, source_target_pairs={{0,4},{4,0},{8,12},{12,8},{16,20},{20,16},{24,28},{28,24},{1,5},{5... | collective-permute-start | bytes 1179656 | tf_op jit(solution)/shard_map/ppermute | solution.py:381
  65.0 25.9 %collective-permute-start.31 = (bf16[384,256]{1,0:T(8,128)(2,1)S(1)}, bf16[384,256]{1,0:T(8,128)(2,1)S(1)}, u32[]{:S(2)}, u32[]{:S(2)}) collective-permute-start(bf16[384,256]{1,0:T(8,128)(2,1)S(1)} %get-tuple-element.82), channel_id=1, source_target_pairs={{0,8},{4,12},{8,16},{12,20},{16,24},{20,28},{24,0},{28,4},{1,9},{5... | collective-permute-start | bytes 589832 | tf_op jit(solution)/shard_map/ppermute | solution.py:405
  75.7 24.3 %collective-permute-start.32 = (bf16[384,256]{1,0:T(8,128)(2,1)S(1)}, bf16[384,256]{1,0:T(8,128)(2,1)S(1)}, u32[]{:S(2)}, u32[]{:S(2)}) collective-permute-start(bf16[384,256]{1,0:T(8,128)(2,1)S(1)} %get-tuple-element.83), channel_id=1, source_target_pairs={{0,12},{4,8},{8,20},{12,16},{16,28},{20,24},{24,4},{28,0},{1,13},{... | collective-permute-start | bytes 589832 | tf_op jit(solution)/shard_map/ppermute | solution.py:405
  78.2 21.8 %collective-permute-start.33 = (bf16[384,256]{1,0:T(8,128)(2,1)S(1)}, bf16[384,256]{1,0:T(8,128)(2,1)S(1)}, u32[]{:S(2)}, u32[]{:S(2)}) collective-permute-start(bf16[384,256]{1,0:T(8,128)(2,1)S(1)} %get-tuple-element.84), channel_id=1, source_target_pairs={{0,24},{4,28},{8,0},{12,4},{16,8},{20,12},{24,16},{28,20},{1,25},{... | collective-permute-start | bytes 589832 | tf_op jit(solution)/shard_map/ppermute | solution.py:405
  82.4 29.6 %collective-permute-start.34 = (bf16[384,256]{1,0:T(8,128)(2,1)S(1)}, bf16[384,256]{1,0:T(8,128)(2,1)S(1)}, u32[]{:S(2)}, u32[]{:S(2)}) collective-permute-start(bf16[384,256]{1,0:T(8,128)(2,1)S(1)} %get-tuple-element.85), channel_id=1, source_target_pairs={{0,28},{4,24},{8,4},{12,0},{16,12},{20,8},{24,20},{28,16},{1,29},{... | collective-permute-start | bytes 589832 | tf_op jit(solution)/shard_map/ppermute | solution.py:405
  90.9 33.1 %collective-permute-start.22 = (bf16[384,384]{1,0:T(8,128)(2,1)S(1)}, bf16[384,384]{1,0:T(8,128)(2,1)S(1)}, u32[]{:S(2)}, u32[]{:S(2)}) collective-permute-start(bf16[384,384]{1,0:T(8,128)(2,1)S(1)} %get-tuple-element.72), channel_id=1, source_target_pairs={{0,16},{4,20},{8,24},{12,28},{16,0},{20,4},{24,8},{28,12},{1,17},{... | collective-permute-start | bytes 884744 | tf_op jit(solution)/shard_map/ppermute | solution.py:405
  100.0 26.1 %collective-permute-start.23 = (bf16[384,384]{1,0:T(8,128)(2,1)S(1)}, bf16[384,384]{1,0:T(8,128)(2,1)S(1)}, u32[]{:S(2)}, u32[]{:S(2)}) collective-permute-start(bf16[384,384]{1,0:T(8,128)(2,1)S(1)} %get-tuple-element.73), channel_id=1, source_target_pairs={{0,20},{4,16},{8,28},{12,24},{16,4},{20,0},{24,12},{28,8},{1,21},{... | collective-permute-start | bytes 884744 | tf_op jit(solution)/shard_map/ppermute | solution.py:405
  100.0 35.3 %collective-permute-start.24 = (bf16[384,384]{1,0:T(8,128)(2,1)S(1)}, bf16[384,384]{1,0:T(8,128)(2,1)S(1)}, u32[]{:S(2)}, u32[]{:S(2)}) collective-permute-start(bf16[384,384]{1,0:T(8,128)(2,1)S(1)} %get-tuple-element.74), channel_id=1, source_target_pairs={{0,8},{4,12},{8,16},{12,20},{16,24},{20,28},{24,0},{28,4},{1,9},{5... | collective-permute-start | bytes 884744 | tf_op jit(solution)/shard_map/ppermute | solution.py:405
  112.0 35.9 %collective-permute-start.25 = (bf16[384,384]{1,0:T(8,128)(2,1)S(1)}, bf16[384,384]{1,0:T(8,128)(2,1)S(1)}, u32[]{:S(2)}, u32[]{:S(2)}) collective-permute-start(bf16[384,384]{1,0:T(8,128)(2,1)S(1)} %get-tuple-element.75), channel_id=1, source_target_pairs={{0,12},{4,8},{8,20},{12,16},{16,28},{20,24},{24,4},{28,0},{1,13},{... | collective-permute-start | bytes 884744 | tf_op jit(solution)/shard_map/ppermute | solution.py:405
  112.0 8.8 %collective-permute-start.35 = (bf16[384,256]{1,0:T(8,128)(2,1)S(1)}, bf16[384,256]{1,0:T(8,128)(2,1)S(1)}, u32[]{:S(2)}, u32[]{:S(2)}) collective-permute-start(bf16[384,256]{1,0:T(8,128)(2,1)S(1)} %get-tuple-element.60), channel_id=1, source_target_pairs={{0,4},{4,0},{8,12},{12,8},{16,20},{20,16},{24,28},{28,24},{1,5},{5... | collective-permute-start | bytes 589832 | tf_op jit(solution)/shard_map/ppermute | solution.py:405
  120.8 27.1 %collective-permute-start.26 = (bf16[384,384]{1,0:T(8,128)(2,1)S(1)}, bf16[384,384]{1,0:T(8,128)(2,1)S(1)}, u32[]{:S(2)}, u32[]{:S(2)}) collective-permute-start(bf16[384,384]{1,0:T(8,128)(2,1)S(1)} %get-tuple-element.76), channel_id=1, source_target_pairs={{0,24},{4,28},{8,0},{12,4},{16,8},{20,12},{24,16},{28,20},{1,25},{... | collective-permute-start | bytes 884744 | tf_op jit(solution)/shard_map/ppermute | solution.py:405
  124.0 39.4 %collective-permute-start.27 = (bf16[384,384]{1,0:T(8,128)(2,1)S(1)}, bf16[384,384]{1,0:T(8,128)(2,1)S(1)}, u32[]{:S(2)}, u32[]{:S(2)}) collective-permute-start(bf16[384,384]{1,0:T(8,128)(2,1)S(1)} %get-tuple-element.77), channel_id=1, source_target_pairs={{0,28},{4,24},{8,4},{12,0},{16,12},{20,8},{24,20},{28,16},{1,29},{... | collective-permute-start | bytes 884744 | tf_op jit(solution)/shard_map/ppermute | solution.py:405
  126.0 37.4 %collective-permute-start.28 = (bf16[384,384]{1,0:T(8,128)(2,1)S(1)}, bf16[384,384]{1,0:T(8,128)(2,1)S(1)}, u32[]{:S(2)}, u32[]{:S(2)}) collective-permute-start(bf16[384,384]{1,0:T(8,128)(2,1)S(1)} %get-tuple-element.78), channel_id=1, source_target_pairs={{0,4},{4,0},{8,12},{12,8},{16,20},{20,16},{24,28},{28,24},{1,5},{5... | collective-permute-start | bytes 884744 | tf_op jit(solution)/shard_map/ppermute | solution.py:405
  135.3 28.2 %collective-permute-start.14 = (bf16[384,384]{1,0:T(8,128)(2,1)S(1)}, bf16[384,384]{1,0:T(8,128)(2,1)S(1)}, u32[]{:S(2)}, u32[]{:S(2)}) collective-permute-start(bf16[384,384]{1,0:T(8,128)(2,1)S(1)} %get-tuple-element.64), channel_id=1, source_target_pairs={{0,16},{4,20},{8,24},{12,28},{16,0},{20,4},{24,8},{28,12},{1,17},{... | collective-permute-start | bytes 884744 | tf_op jit(solution)/shard_map/ppermute | solution.py:405
  147.9 28.7 %collective-permute-start.15 = (bf16[384,384]{1,0:T(8,128)(2,1)S(1)}, bf16[384,384]{1,0:T(8,128)(2,1)S(1)}, u32[]{:S(2)}, u32[]{:S(2)}) collective-permute-start(bf16[384,384]{1,0:T(8,128)(2,1)S(1)} %get-tuple-element.65), channel_id=1, source_target_pairs={{0,20},{4,16},{8,28},{12,24},{16,4},{20,0},{24,12},{28,8},{1,21},{... | collective-permute-start | bytes 884744 | tf_op jit(solution)/shard_map/ppermute | solution.py:405
  147.9 38.5 %collective-permute-start.16 = (bf16[384,384]{1,0:T(8,128)(2,1)S(1)}, bf16[384,384]{1,0:T(8,128)(2,1)S(1)}, u32[]{:S(2)}, u32[]{:S(2)}) collective-permute-start(bf16[384,384]{1,0:T(8,128)(2,1)S(1)} %get-tuple-element.66), channel_id=1, source_target_pairs={{0,8},{4,12},{8,16},{12,20},{16,24},{20,28},{24,0},{28,4},{1,9},{5... | collective-permute-start | bytes 884744 | tf_op jit(solution)/shard_map/ppermute | solution.py:405
  163.4 27.3 %collective-permute-start.17 = (bf16[384,384]{1,0:T(8,128)(2,1)S(1)}, bf16[384,384]{1,0:T(8,128)(2,1)S(1)}, u32[]{:S(2)}, u32[]{:S(2)}) collective-permute-start(bf16[384,384]{1,0:T(8,128)(2,1)S(1)} %get-tuple-element.67), channel_id=1, source_target_pairs={{0,12},{4,8},{8,20},{12,16},{16,28},{20,24},{24,4},{28,0},{1,13},{... | collective-permute-start | bytes 884744 | tf_op jit(solution)/shard_map/ppermute | solution.py:405
  163.4 27.3 %collective-permute-start.18 = (bf16[384,384]{1,0:T(8,128)(2,1)S(1)}, bf16[384,384]{1,0:T(8,128)(2,1)S(1)}, u32[]{:S(2)}, u32[]{:S(2)}) collective-permute-start(bf16[384,384]{1,0:T(8,128)(2,1)S(1)} %get-tuple-element.68), channel_id=1, source_target_pairs={{0,24},{4,28},{8,0},{12,4},{16,8},{20,12},{24,16},{28,20},{1,25},{... | collective-permute-start | bytes 884744 | tf_op jit(solution)/shard_map/ppermute | solution.py:405
  163.4 28.9 %collective-permute-start.19 = (bf16[384,384]{1,0:T(8,128)(2,1)S(1)}, bf16[384,384]{1,0:T(8,128)(2,1)S(1)}, u32[]{:S(2)}, u32[]{:S(2)}) collective-permute-start(bf16[384,384]{1,0:T(8,128)(2,1)S(1)} %get-tuple-element.69), channel_id=1, source_target_pairs={{0,28},{4,24},{8,4},{12,0},{16,12},{20,8},{24,20},{28,16},{1,29},{... | collective-permute-start | bytes 884744 | tf_op jit(solution)/shard_map/ppermute | solution.py:405
  176.6 16.0 %collective-permute-start.20 = (bf16[384,384]{1,0:T(8,128)(2,1)S(1)}, bf16[384,384]{1,0:T(8,128)(2,1)S(1)}, u32[]{:S(2)}, u32[]{:S(2)}) collective-permute-start(bf16[384,384]{1,0:T(8,128)(2,1)S(1)} %get-tuple-element.70), channel_id=1, source_target_pairs={{0,4},{4,0},{8,12},{12,8},{16,20},{20,16},{24,28},{28,24},{1,5},{5... | collective-permute-start | bytes 884744 | tf_op jit(solution)/shard_map/ppermute | solution.py:405

commit v10 on v9

--- a/solution.py
+++ b/solution.py
@@ -37,6 +37,10 @@
     return pl.multiple_of(((2 * row + col) * (HEADS // n) + place[2]) * HEAD, HEAD)
 
 
+def odd(tiles):
+    return tiles + 1 - tiles % 2
+
+
 def rows_together(m, width, most):
     return max(count for count in range(1, m + 1) if m % count == 0 and (count == 1 or 2 * width * count <= most))
 
@@ -51,7 +55,7 @@
         cols = pl.ds(column(here, row, side, n), total * HEAD)
         slot = 2 * row + side
         return [
-            pltpu.make_async_copy(source.at[:, cols], buf.at[slot], sems.at[which, slot])
+            pltpu.make_async_copy(source.at[:, cols], buf.at[slot, :, : total * HEAD], sems.at[which, slot])
             for which, (source, buf) in enumerate(((keys, kbuf), (values, vbuf)))
         ]
 
@@ -92,7 +96,7 @@
 
 def local_states(place, keys, values, n, low, widths, swaps):
     rows, m, total = keys.shape[0], n // 2, sum(widths)
-    buf = pltpu.VMEM((n, rows, total * HEAD), keys.dtype)
+    buf = pltpu.VMEM((n, rows, odd(total) * HEAD), keys.dtype)
     shapes = [jax.ShapeDtypeStruct((m, width, HEAD, HEAD), jnp.float32) for width in widths]
     shapes += [jax.ShapeDtypeStruct((m, width, HEAD, HEAD), jnp.bfloat16) for width in swaps]
     return pl.pallas_call(
@@ -101,7 +105,7 @@
         out_specs=[pl.BlockSpec(memory_space=pltpu.VMEM)] * len(shapes),
         out_shape=shapes,
         scratch_shapes=[buf, buf, pltpu.SemaphoreType.DMA((2, n))],
-        compiler_params=params(4 * n * rows * total * HEAD + 3 * n * total * HEAD * HEAD),
+        compiler_params=params(4 * n * rows * odd(total) * HEAD + 3 * n * total * HEAD * HEAD),
         cost_estimate=pl.CostEstimate(
             flops=2 * n * total * rows * HEAD * HEAD, bytes_accessed=4 * rows * n * total * HEAD, transcendentals=0
         ),
@@ -217,7 +221,7 @@
     rows, m = queries.shape[0], n // 2
     width = sum(size for _, size in spans)
     wide = width * HEAD
-    tokens = pltpu.VMEM((n, rows, (width + 1 - width % 2) * HEAD), jnp.bfloat16)
+    tokens = pltpu.VMEM((n, rows, odd(width) * HEAD), jnp.bfloat16)
     state = pltpu.VMEM((m, width, HEAD, HEAD), jnp.bfloat16)
     return pl.pallas_call(
         functools.partial(attend_body, n, spans, order),
@@ -237,7 +241,7 @@
             pltpu.SemaphoreType.DMA((4, n)),
             pltpu.SemaphoreType.DMA((1 + 2 * len(states),)),
         ],
-        compiler_params=params(8 * n * rows * (wide + HEAD) + 2 * n * width * HEAD * HEAD + 4 * HEADS * HEAD),
+        compiler_params=params(8 * n * rows * odd(width) * HEAD + 2 * n * width * HEAD * HEAD + 4 * HEADS * HEAD),
         cost_estimate=pl.CostEstimate(
             flops=2 * n * width * rows * HEAD * (2 * rows + HEAD),
             bytes_accessed=8 * rows * n * wide,
@@ -248,7 +252,7 @@
 
 
 def put_body(n, order, place, low, *refs):
-    parts, out, again, sems = refs[:n], refs[-3], refs[-2], refs[-1]
+    parts, out, again, sems = refs[: len(order)], refs[-3], refs[-2], refs[-1]
     m = n // 2
     rows, wide = parts[0].shape
     cols = pl.ds(pl.multiple_of(low[0] * HEAD, HEAD), wide)
@@ -273,14 +277,14 @@
     anywhere = pl.BlockSpec(memory_space=pltpu.HBM)
     return pl.pallas_call(
         functools.partial(put_body, n, order),
-        in_specs=[pl.BlockSpec(memory_space=pltpu.SMEM)] * 2 + [anywhere] * (n if first else n + 1),
+        in_specs=[pl.BlockSpec(memory_space=pltpu.SMEM)] * 2 + [anywhere] * (len(parts) + (not first)),
         out_specs=[anywhere, pl.BlockSpec(memory_space=pltpu.SMEM)],
         out_shape=[
             jax.ShapeDtypeStruct((n * rows, HEADS // n * HEAD), jnp.bfloat16),
             jax.ShapeDtypeStruct((2,), jnp.int32),
         ],
-        scratch_shapes=[pltpu.SemaphoreType.DMA((n,))],
-        input_output_aliases={} if first else {n + 2: 0},
+        scratch_shapes=[pltpu.SemaphoreType.DMA((len(parts),))],
+        input_output_aliases={} if first else {len(parts) + 2: 0},
         compiler_params=params(),
         name="put",
     )(place, jnp.full((1,), low, jnp.int32), *parts, *(() if first else (out,)))
@@ -406,8 +410,12 @@
 
     def put(self, c):
         parts = [self.get("mixed", c)[0]] + [self.get("sent", c, k) for k in range(1, self.n)]
-        out = self.get("put", c - 1)[0] if c else None
-        return put(self.place, parts, out, (0, *self.shifts), self.n, self.chunks[c][0])
+        out, order, low = self.get("put", c - 1)[0] if c else None, (0, *self.shifts), self.chunks[c][0]
+        if c == len(self.chunks) - 1:
+            late = self.n // 2 + 1
+            out, _ = put(self.place, parts[:late], out, order[:late], self.n, low)
+            parts, order = parts[late:], order[late:]
+        return put(self.place, parts, out, order, self.n, low)
 
 
 def per_device(n, *arrays):

time: 199 us -> 198 us (level)
  starting transfers between devices: 76.6 us -> 71.3 us
  waiting for transfers between devices: 71.6 us -> 75.4 us
    ppermute x21, starting transfers between devices: 57.2 us -> 51.9 us  [sent(): lax.ppermute(self.hold(self.get('mixed', c)[k], 'sent', c, k), 'seq', pairs)]
    ppermute x21, waiting for transfers between devices: 52.5 us -> 56.2 us  [sent(): lax.ppermute(self.hold(self.get('mixed', c)[k], 'sent', c, k), 'seq', pairs)]
    pallas_call x3 -> x4, Pallas kernels: 7.33 us -> 9.02 us  [put(): pl.pallas_call(functools.partial(put_body, n, order), in_specs=[pl.BlockS...]
  transfers between devices with their start and end apart: 36 -> 36, of which waited for: 14 -> 14; matrix products, arithmetic and copies ran while one was open for 4% -> 4% of each run, Pallas kernels for 17% -> 18%
where the time goes in v10:
time: 198 us; the launch traced here: 195 us
  waiting for transfers between devices  75.4 us (38%)
  starting transfers between devices  71.3 us (36%)
  Pallas kernels  40.7 us (21%)
  other arithmetic  7.63 us (4%)
    ppermute x21, waiting for transfers between devices, sent(): lax.ppermute(self.hold(self.get('mixed', c)[k], 'sent', c, k), 'seq', pairs)  56.2 us
    ppermute x21, starting transfers between devices, sent(): lax.ppermute(self.hold(self.get('mixed', c)[k], 'sent', c, k), 'seq', pairs)  51.9 us
    pallas_call x3, Pallas kernels, attend(): pl.pallas_call(functools.partial(attend_body, n, spans, order), in_specs=...  23.2 us
    ppermute x12, waiting for transfers between devices, prefix(): return lax.ppermute(self.get('message', c, s), 'seq', pairs)  17.7 us
    ppermute x12, starting transfers between devices, prefix(): return lax.ppermute(self.get('message', c, s), 'seq', pairs)  14.7 us
    pallas_call x4, Pallas kernels, put(): pl.pallas_call(functools.partial(put_body, n, order), in_specs=[pl.BlockS...  9.02 us
    pallas_call x2, Pallas kernels, local_states(): pl.pallas_call(functools.partial(local_body, n, widths, swaps), in_specs=...  8.47 us
    convert_element_type x10, other arithmetic, message(): return self.hold(value.astype(jnp.bfloat16), 'message', c, s)  4.85 us
  transfers between devices with their start and end apart: 36, of which 14 were waited for; matrix products, arithmetic and copies ran while one was open for 4% of the time, Pallas kernels for 18%

profile of v10, /device:TPU:8, one launch (start us, length us, event | category | flops | bytes accessed | tf_op | source)
XLA Modules:
  0.0 195.5 jit_solution(4128804324129835599)
XLA Ops:
  0.1 3.4 %local.3 = (f32[4,2,128,128]{3,2,1,0:T(8,128)S(1)}, bf16[4,2,128,128]{3,2,1,0:T(8,128)(2,1)S(1)}) custom-call(s32[2]{0:T(128)S(1)} %pad_add_fusion.place, s32[1]{0:T(128)} %constant.38.clone.1.low, bf16[384,8192]{1,0:T(8,128)(2,1)} %keys.9, bf16[384,8192]{1,0:T(8,128)(2,1)} %values.9), custom_call_target="tpu_custom_call" | custom-call | flops 201326592 | bytes 3145728 | tf_op jit(solution)/shard_map/local/pallas_call | solution.py:102
  3.5 1.6 collective-permute-start.2
  5.1 5.0 %local.2 = (f32[4,3,128,128]{3,2,1,0:T(8,128)S(1)}, f32[4,3,128,128]{3,2,1,0:T(8,128)S(1)}, bf16[4,3,128,128]{3,2,1,0:T(8,128)(2,1)S(1)}, bf16[4,3,128,128]{3,2,1,0:T(8,128)(2,1)S(1)}) custom-call(s32[2]{0:T(128)S(1)} %pad_add_fusion.place, s32[1]{0:T(128)} %constant.37.clone.1.low, bf16[384,8192]{1,0:T(8,128)(2,1)} %keys.9, bf16[384,8192]{1,0:T(8,128)(2,1)} %values.9), custom_call_target="tpu_custom_call" | custom-call | flops 603979776 | bytes 9437184 | tf_op jit(solution)/shard_map/local/pallas_call | solution.py:102
  10.1 1.5 collective-permute-done.2
  11.7 1.3 collective-permute-start.3
  13.0 1.6 collective-permute-start.1
  14.6 6.2 %collective-permute-done.3 = bf16[4,2,128,128]{3,2,1,0:T(8,128)(2,1)S(1)} collective-permute-done((bf16[4,2,128,128]{3,2,1,0:T(8,128)(2,1)S(1)}, bf16[4,2,128,128]{3,2,1,0:T(8,128)(2,1)S(1)}, u32[]{:S(2)}, u32[]{:S(2)}) %collective-permute-start.3) | collective-permute-done | bytes 262176 | tf_op jit(solution)/shard_map/ppermute | solution.py:385
  21.6 2.1 %collective-permute-start.5 = (bf16[4,2,128,128]{3,2,1,0:T(8,128)(2,1)}, bf16[4,2,128,128]{3,2,1,0:T(8,128)(2,1)}, u32[]{:S(2)}, u32[]{:S(2)}) collective-permute-start(bf16[4,2,128,128]{3,2,1,0:T(8,128)(2,1)} %add_convert_fusion.5), channel_id=1, source_target_pairs={{8,16},{12,20},{9,17},{13,21},{10,18},{14,22},{11,19},{15,23}} | collective-permute-start | bytes 786440 | tf_op jit(solution)/shard_map/ppermute | solution.py:385
  24.5 1.3 collective-permute-start.4
  25.8 1.6 collective-permute-start
  27.4 1.1 add_convert_fusion.4
  29.3 6.5 %collective-permute-done.4 = bf16[4,3,128,128]{3,2,1,0:T(8,128)(2,1)} collective-permute-done((bf16[4,3,128,128]{3,2,1,0:T(8,128)(2,1)}, bf16[4,3,128,128]{3,2,1,0:T(8,128)(2,1)}, u32[]{:S(2)}, u32[]{:S(2)}) %collective-permute-start.4) | collective-permute-done | bytes 393248 | tf_op jit(solution)/shard_map/ppermute | solution.py:385
  35.8 1.2 add_convert_fusion.3
  37.0 1.3 collective-permute-start.7
  38.4 1.3 collective-permute-start.6
  39.7 1.4 fusion.5
  41.1 1.6 collective-permute-start.11
  42.7 1.5 collective-permute-done.7
  45.0 3.4 %collective-permute-done.6 = bf16[4,3,128,128]{3,2,1,0:T(8,128)(2,1)S(1)} collective-permute-done((bf16[4,3,128,128]{3,2,1,0:T(8,128)(2,1)S(1)}, bf16[4,3,128,128]{3,2,1,0:T(8,128)(2,1)S(1)}, u32[]{:S(2)}, u32[]{:S(2)}) %collective-permute-start.6) | collective-permute-done | bytes 393248 | tf_op jit(solution)/shard_map/ppermute | solution.py:385
  48.6 1.6 collective-permute-start.9
  50.2 6.2 %attend.3 = (bf16[384,256]{1,0:T(8,128)(2,1)S(1)}, bf16[384,256]{1,0:T(8,128)(2,1)S(1)}, bf16[384,256]{1,0:T(8,128)(2,1)S(1)}, bf16[384,256]{1,0:T(8,128)(2,1)S(...) custom-call(s32[2]{0:T(128)S(1)} %pad_add_fusion.place, ...), custom_call_target="tpu_custom_call" | custom-call | flops 1409286144 | bytes 6291456 | tf_op jit(solution)/shard_map/attend/pallas_call | solution.py:226
  56.5 1.4 fusion.1
  58.8 3.9 %collective-permute-start.30 = (bf16[384,256]{1,0:T(8,128)(2,1)S(1)}, bf16[384,256]{1,0:T(8,128)(2,1)S(1)}, u32[]{:S(2)}, u32[]{:S(2)}) collective-permute-start(bf16[384,256]{1,0:T(8,128)(2,1)S(1)} %get-tuple-element.82), channel_id=1, source_target_pairs={{0,20},{4,16},{8,28},{12,24},{16,4},{20,0},{24,12},{28,8},{1,21},{... | collective-permute-start | bytes 589832 | tf_op jit(solution)/shard_map/ppermute | solution.py:409
  63.5 1.6 collective-permute-start.13
  65.1 11.0 %collective-permute-start.31 = (bf16[384,256]{1,0:T(8,128)(2,1)S(1)}, bf16[384,256]{1,0:T(8,128)(2,1)S(1)}, u32[]{:S(2)}, u32[]{:S(2)}) collective-permute-start(bf16[384,256]{1,0:T(8,128)(2,1)S(1)} %get-tuple-element.83), channel_id=1, source_target_pairs={{0,8},{4,12},{8,16},{12,20},{16,24},{20,28},{24,0},{28,4},{1,9},{5... | collective-permute-start | bytes 589832 | tf_op jit(solution)/shard_map/ppermute | solution.py:409
  76.1 2.5 %collective-permute-start.32 = (bf16[384,256]{1,0:T(8,128)(2,1)S(1)}, bf16[384,256]{1,0:T(8,128)(2,1)S(1)}, u32[]{:S(2)}, u32[]{:S(2)}) collective-permute-start(bf16[384,256]{1,0:T(8,128)(2,1)S(1)} %get-tuple-element.84), channel_id=1, source_target_pairs={{0,12},{4,8},{8,20},{12,16},{16,28},{20,24},{24,4},{28,0},{1,13},{... | collective-permute-start | bytes 589832 | tf_op jit(solution)/shard_map/ppermute | solution.py:409
  78.5 3.6 %collective-permute-start.33 = (bf16[384,256]{1,0:T(8,128)(2,1)S(1)}, bf16[384,256]{1,0:T(8,128)(2,1)S(1)}, u32[]{:S(2)}, u32[]{:S(2)}) collective-permute-start(bf16[384,256]{1,0:T(8,128)(2,1)S(1)} %get-tuple-element.85), channel_id=1, source_target_pairs={{0,24},{4,28},{8,0},{12,4},{16,8},{20,12},{24,16},{28,20},{1,25},{... | collective-permute-start | bytes 589832 | tf_op jit(solution)/shard_map/ppermute | solution.py:409
  82.1 8.5 %attend.5 = (bf16[384,384]{1,0:T(8,128)(2,1)S(1)}, bf16[384,384]{1,0:T(8,128)(2,1)S(1)}, bf16[384,384]{1,0:T(8,128)(2,1)S(1)}, bf16[384,384]{1,0:T(8,128)(2,1)S(...) custom-call(s32[2]{0:T(128)S(1)} %pad_add_fusion.place, ...), custom_call_target="tpu_custom_call" | custom-call | flops 2113929216 | bytes 9437184 | tf_op jit(solution)/shard_map/attend/pallas_call | solution.py:226
  90.6 1.4 collective-permute-start.22
  92.0 8.9 %collective-permute-done.32.refs_4_ = bf16[384,256]{1,0:T(8,128)(2,1)S(1)} collective-permute-done((bf16[384,256]{1,0:T(8,128)(2,1)S(1)}, bf16[384,256]{1,0:T(8,128)(2,1)S(1)}, u32[]{:S(2)}, u32[]{:S(2)}) %collective-permute-start.32) | collective-permute-done | bytes 196640 | tf_op jit(solution)/shard_map/ppermute | solution.py:409
  100.9 3.5 %collective-permute-start.24 = (bf16[384,384]{1,0:T(8,128)(2,1)S(1)}, bf16[384,384]{1,0:T(8,128)(2,1)S(1)}, u32[]{:S(2)}, u32[]{:S(2)}) collective-permute-start(bf16[384,384]{1,0:T(8,128)(2,1)S(1)} %get-tuple-element.75), channel_id=1, source_target_pairs={{0,8},{4,12},{8,16},{12,20},{16,24},{20,28},{24,0},{28,4},{1,9},{5... | collective-permute-start | bytes 884744 | tf_op jit(solution)/shard_map/ppermute | solution.py:409
  104.4 6.7 %collective-permute-done.34.refs_6_ = bf16[384,256]{1,0:T(8,128)(2,1)S(1)} collective-permute-done((bf16[384,256]{1,0:T(8,128)(2,1)S(1)}, bf16[384,256]{1,0:T(8,128)(2,1)S(1)}, u32[]{:S(2)}, u32[]{:S(2)}) %collective-permute-start.34) | collective-permute-done | bytes 196640 | tf_op jit(solution)/shard_map/ppermute | solution.py:409
  111.2 8.5 %attend.4 = (bf16[384,384]{1,0:T(8,128)(2,1)S(1)}, bf16[384,384]{1,0:T(8,128)(2,1)S(1)}, bf16[384,384]{1,0:T(8,128)(2,1)S(1)}, bf16[384,384]{1,0:T(8,128)(2,1)S(...) custom-call(s32[2]{0:T(128)S(1)} %pad_add_fusion.place, ...), custom_call_target="tpu_custom_call" | custom-call | flops 2113929216 | bytes 9437184 | tf_op jit(solution)/shard_map/attend/pallas_call | solution.py:226
  120.0 3.2 %collective-permute-start.26 = (bf16[384,384]{1,0:T(8,128)(2,1)S(1)}, bf16[384,384]{1,0:T(8,128)(2,1)S(1)}, u32[]{:S(2)}, u32[]{:S(2)}) collective-permute-start(bf16[384,384]{1,0:T(8,128)(2,1)S(1)} %get-tuple-element.77), channel_id=1, source_target_pairs={{0,24},{4,28},{8,0},{12,4},{16,8},{20,12},{24,16},{28,20},{1,25},{... | collective-permute-start | bytes 884744 | tf_op jit(solution)/shard_map/ppermute | solution.py:409
  123.2 2.9 %collective-permute-start.27 = (bf16[384,384]{1,0:T(8,128)(2,1)S(1)}, bf16[384,384]{1,0:T(8,128)(2,1)S(1)}, u32[]{:S(2)}, u32[]{:S(2)}) collective-permute-start(bf16[384,384]{1,0:T(8,128)(2,1)S(1)} %get-tuple-element.78), channel_id=1, source_target_pairs={{0,28},{4,24},{8,4},{12,0},{16,12},{20,8},{24,20},{28,16},{1,29},{... | collective-permute-start | bytes 884744 | tf_op jit(solution)/shard_map/ppermute | solution.py:409
  126.4 9.5 %collective-permute-done.24.refs_3_ = bf16[384,384]{1,0:T(8,128)(2,1)S(1)} collective-permute-done((bf16[384,384]{1,0:T(8,128)(2,1)S(1)}, bf16[384,384]{1,0:T(8,128)(2,1)S(1)}, u32[]{:S(2)}, u32[]{:S(2)}) %collective-permute-start.24) | collective-permute-done | bytes 294944 | tf_op jit(solution)/shard_map/ppermute | solution.py:409
  135.9 12.6 %collective-permute-done.25.refs_4_ = bf16[384,384]{1,0:T(8,128)(2,1)S(1)} collective-permute-done((bf16[384,384]{1,0:T(8,128)(2,1)S(1)}, bf16[384,384]{1,0:T(8,128)(2,1)S(1)}, u32[]{:S(2)}, u32[]{:S(2)}) %collective-permute-start.25) | collective-permute-done | bytes 294944 | tf_op jit(solution)/shard_map/ppermute | solution.py:409
  148.6 4.8 %collective-permute-start.14 = (bf16[384,384]{1,0:T(8,128)(2,1)S(1)}, bf16[384,384]{1,0:T(8,128)(2,1)S(1)}, u32[]{:S(2)}, u32[]{:S(2)}) collective-permute-start(bf16[384,384]{1,0:T(8,128)(2,1)S(1)} %get-tuple-element.64), channel_id=1, source_target_pairs={{0,24},{4,28},{8,0},{12,4},{16,8},{20,12},{24,16},{28,20},{1,25},{... | collective-permute-start | bytes 884744 | tf_op jit(solution)/shard_map/ppermute | solution.py:409
  153.4 5.0 %collective-permute-start.19 = (bf16[384,384]{1,0:T(8,128)(2,1)S(1)}, bf16[384,384]{1,0:T(8,128)(2,1)S(1)}, u32[]{:S(2)}, u32[]{:S(2)}) collective-permute-start(bf16[384,384]{1,0:T(8,128)(2,1)S(1)} %get-tuple-element.70), channel_id=1, source_target_pairs={{0,8},{4,12},{8,16},{12,20},{16,24},{20,28},{24,0},{28,4},{1,9},{5... | collective-permute-start | bytes 884744 | tf_op jit(solution)/shard_map/ppermute | solution.py:409
  158.4 9.0 %collective-permute-done.17.refs_1_ = bf16[384,384]{1,0:T(8,128)(2,1)S(1)} collective-permute-done((bf16[384,384]{1,0:T(8,128)(2,1)S(1)}, bf16[384,384]{1,0:T(8,128)(2,1)S(1)}, u32[]{:S(2)}, u32[]{:S(2)}) %collective-permute-start.17) | collective-permute-done | bytes 294944 | tf_op jit(solution)/shard_map/ppermute | solution.py:409
  167.4 5.1 %collective-permute-start.15 = (bf16[384,384]{1,0:T(8,128)(2,1)S(1)}, bf16[384,384]{1,0:T(8,128)(2,1)S(1)}, u32[]{:S(2)}, u32[]{:S(2)}) collective-permute-start(bf16[384,384]{1,0:T(8,128)(2,1)S(1)} %get-tuple-element.65), channel_id=1, source_target_pairs={{0,28},{4,24},{8,4},{12,0},{16,12},{20,8},{24,20},{28,16},{1,29},{... | collective-permute-start | bytes 884744 | tf_op jit(solution)/shard_map/ppermute | solution.py:409
  172.5 4.4 %collective-permute-done.18.refs_2_ = bf16[384,384]{1,0:T(8,128)(2,1)S(1)} collective-permute-done((bf16[384,384]{1,0:T(8,128)(2,1)S(1)}, bf16[384,384]{1,0:T(8,128)(2,1)S(1)}, u32[]{:S(2)}, u32[]{:S(2)}) %collective-permute-start.18) | collective-permute-done | bytes 294944 | tf_op jit(solution)/shard_map/ppermute | solution.py:409
  176.9 4.7 %collective-permute-start.16 = (bf16[384,384]{1,0:T(8,128)(2,1)S(1)}, bf16[384,384]{1,0:T(8,128)(2,1)S(1)}, u32[]{:S(2)}, u32[]{:S(2)}) collective-permute-start(bf16[384,384]{1,0:T(8,128)(2,1)S(1)} %get-tuple-element.66), channel_id=1, source_target_pairs={{0,4},{4,0},{8,12},{12,8},{16,20},{20,16},{24,28},{28,24},{1,5},{5... | collective-permute-start | bytes 884744 | tf_op jit(solution)/shard_map/ppermute | solution.py:409
  181.5 2.3 %put.4 = (bf16[3072,1024]{1,0:T(8,128)(2,1)}, s32[2]{0:T(128)}) custom-call(s32[2]{0:T(128)S(1)} %pad_add_fusion.place, s32[1]{0:T(128)} %constant.38.clone.1.low, bf16[384,256]{1,0:T(8,128)(2,1)S(1)} %get-tuple-element.80.refs_0_, bf16[384,256]{1,0:T(8,128)(2,1)S(1)} %collective-permute-done.29.refs_1_, ...), custom_call_target="tpu_custom_call" | custom-call | tf_op jit(solution)/shard_map/put/pallas_call | solution.py:278
  183.8 2.5 %put.5 = (bf16[3072,1024]{1,0:T(8,128)(2,1)}, s32[2]{0:T(128)}) custom-call(s32[2]{0:T(128)S(1)} %pad_add_fusion.place, s32[1]{0:T(128)} %constant.37.clone.1.low, bf16[384,384]{1,0:T(8,128)(2,1)S(1)} %get-tuple-element.72.refs_0_, bf16[384,384]{1,0:T(8,128)(2,1)S(1)} %collective-permute-done.22.refs_1_, ...), custom_call_target="tpu_custom_call", output_to_operand_aliasing={{0}: (10, {})} | custom-call | tf_op jit(solution)/shard_map/put/pallas_call | solution.py:278
  186.5 4.6 %collective-permute-done.20.refs_4_ = bf16[384,384]{1,0:T(8,128)(2,1)S(1)} collective-permute-done((bf16[384,384]{1,0:T(8,128)(2,1)S(1)}, bf16[384,384]{1,0:T(8,128)(2,1)S(1)}, u32[]{:S(2)}, u32[]{:S(2)}) %collective-permute-start.20) | collective-permute-done | bytes 294944 | tf_op jit(solution)/shard_map/ppermute | solution.py:409
  191.1 2.2 %put.6 = (bf16[3072,1024]{1,0:T(8,128)(2,1)}, s32[2]{0:T(128)}) custom-call(s32[2]{0:T(128)S(1)} %pad_add_fusion.place, s32[1]{0:T(128)} %constant.36.clone.1.low, bf16[384,384]{1,0:T(8,128)(2,1)S(1)} %get-tuple-element.67.refs_0_, bf16[384,384]{1,0:T(8,128)(2,1)S(1)} %collective-permute-done.17.refs_1_, ...), custom_call_target="tpu_custom_call", output_to_operand_aliasing={{0}: (7, {})} | custom-call | tf_op jit(solution)/shard_map/put/pallas_call | solution.py:278
  193.3 2.0 %put.7 = (bf16[3072,1024]{1,0:T(8,128)(2,1)}, s32[2]{0:T(128)}) custom-call(s32[2]{0:T(128)S(1)} %pad_add_fusion.place, s32[1]{0:T(128)} %constant.36.clone.1.low, bf16[384,384]{1,0:T(8,128)(2,1)S(1)} %collective-permute-done.14.refs_0_, bf16[384,384]{1,0:T(8,128)(2,1)S(1)} %collective-permute-done.15.refs_1_, ...), custom_call_target="tpu_custom_call", output_to_operand_aliasing={{0}: (5, {})} | custom-call | tf_op jit(solution)/shard_map/put/pallas_call | solution.py:278
  (52 shorter events, 6.1 us)
Async XLA Ops:
  3.5 8.1 %collective-permute-start.2 = (bf16[4,2,128,128]{3,2,1,0:T(8,128)(2,1)S(1)}, bf16[4,2,128,128]{3,2,1,0:T(8,128)(2,1)S(1)}, u32[]{:S(2)}, u32[]{:S(2)}) collective-permute-start(bf16[4,2,128,128]{3,2,1,0:T(8,128)(2,1)S(1)} %get-tuple-element.53), channel_id=1, source_target_pairs={{0,4},{4,0},{8,12},{12,8},{16,20},{20,16},{24,28},{28,24},{1,5},{5... | collective-permute-start | bytes 786440 | tf_op jit(solution)/shard_map/ppermute | solution.py:358
  11.6 12.9 %copy-start.1 = (bf16[4,2,128,128]{3,2,1,0:T(8,128)(2,1)}, bf16[4,2,128,128]{3,2,1,0:T(8,128)(2,1)S(1)}, u32[]{:S(2)}) copy-start(bf16[4,2,128,128]{3,2,1,0:T(8,128)(2,1)S(1)} %collective-permute-done.2) | copy-start | bytes 786436
  11.7 9.1 %collective-permute-start.3 = (bf16[4,2,128,128]{3,2,1,0:T(8,128)(2,1)S(1)}, bf16[4,2,128,128]{3,2,1,0:T(8,128)(2,1)S(1)}, u32[]{:S(2)}, u32[]{:S(2)}) collective-permute-start(bf16[4,2,128,128]{3,2,1,0:T(8,128)(2,1)S(1)} %fusion.8), channel_id=1, source_target_pairs={{0,8},{4,12},{1,9},{5,13},{2,10},{6,14},{3,11},{7,15}} | collective-permute-start | bytes 786440 | tf_op jit(solution)/shard_map/ppermute | solution.py:385
  13.0 10.7 %collective-permute-start.1 = (bf16[4,3,128,128]{3,2,1,0:T(8,128)(2,1)S(1)}, bf16[4,3,128,128]{3,2,1,0:T(8,128)(2,1)S(1)}, u32[]{:S(2)}, u32[]{:S(2)}) collective-permute-start(bf16[4,3,128,128]{3,2,1,0:T(8,128)(2,1)S(1)} %get-tuple-element.51), channel_id=1, source_target_pairs={{0,4},{4,0},{8,12},{12,8},{16,20},{20,16},{24,28},{28,24},{1,5},{5... | collective-permute-start | bytes 1179656 | tf_op jit(solution)/shard_map/ppermute | solution.py:358
  20.7 3.0 %copy-start.2 = (bf16[4,2,128,128]{3,2,1,0:T(8,128)(2,1)}, bf16[4,2,128,128]{3,2,1,0:T(8,128)(2,1)S(1)}, u32[]{:S(2)}) copy-start(bf16[4,2,128,128]{3,2,1,0:T(8,128)(2,1)S(1)} %collective-permute-done.3) | copy-start | bytes 786436
  21.6 28.7 %copy-start = (f32[8192]{0:T(1024)S(1)}, f32[8192]{0:T(1024)}, u32[]{:S(2)}) copy-start(f32[8192]{0:T(1024)} %param.7) | copy-start | bytes 98308
  21.6 5.9 %collective-permute-start.5 = (bf16[4,2,128,128]{3,2,1,0:T(8,128)(2,1)}, bf16[4,2,128,128]{3,2,1,0:T(8,128)(2,1)}, u32[]{:S(2)}, u32[]{:S(2)}) collective-permute-start(bf16[4,2,128,128]{3,2,1,0:T(8,128)(2,1)} %add_convert_fusion.5), channel_id=1, source_target_pairs={{8,16},{12,20},{9,17},{13,21},{10,18},{14,22},{11,19},{15,23}} | collective-permute-start | bytes 786440 | tf_op jit(solution)/shard_map/ppermute | solution.py:385
  24.5 11.2 %collective-permute-start.4 = (bf16[4,3,128,128]{3,2,1,0:T(8,128)(2,1)}, bf16[4,3,128,128]{3,2,1,0:T(8,128)(2,1)}, u32[]{:S(2)}, u32[]{:S(2)}) collective-permute-start(bf16[4,3,128,128]{3,2,1,0:T(8,128)(2,1)} %fusion.7), channel_id=1, source_target_pairs={{0,8},{4,12},{1,9},{5,13},{2,10},{6,14},{3,11},{7,15}} | collective-permute-start | bytes 1179656 | tf_op jit(solution)/shard_map/ppermute | solution.py:385
  25.8 12.5 %collective-permute-start = (bf16[4,3,128,128]{3,2,1,0:T(8,128)(2,1)S(1)}, bf16[4,3,128,128]{3,2,1,0:T(8,128)(2,1)S(1)}, u32[]{:S(2)}, u32[]{:S(2)}) collective-permute-start(bf16[4,3,128,128]{3,2,1,0:T(8,128)(2,1)S(1)} %get-tuple-element.49), channel_id=1, source_target_pairs={{0,4},{4,0},{8,12},{12,8},{16,20},{20,16},{24,28},{28,24},{1,5},{5... | collective-permute-start | bytes 1179656 | tf_op jit(solution)/shard_map/ppermute | solution.py:358
  28.6 11.1 %collective-permute-start.8 = (bf16[4,2,128,128]{3,2,1,0:T(8,128)(2,1)S(1)}, bf16[4,2,128,128]{3,2,1,0:T(8,128)(2,1)S(1)}, u32[]{:S(2)}, u32[]{:S(2)}) collective-permute-start(bf16[4,2,128,128]{3,2,1,0:T(8,128)(2,1)S(1)} %add_convert_fusion.4), channel_id=1, source_target_pairs={{16,24},{20,28},{17,25},{21,29},{18,26},{22,30},{19,27},{23,31}} | collective-permute-start | bytes 786440 | tf_op jit(solution)/shard_map/ppermute | solution.py:385
  37.0 7.2 %collective-permute-start.7 = (bf16[4,3,128,128]{3,2,1,0:T(8,128)(2,1)S(1)}, bf16[4,3,128,128]{3,2,1,0:T(8,128)(2,1)S(1)}, u32[]{:S(2)}, u32[]{:S(2)}) collective-permute-start(bf16[4,3,128,128]{3,2,1,0:T(8,128)(2,1)S(1)} %add_convert_fusion.3), channel_id=1, source_target_pairs={{8,16},{12,20},{9,17},{13,21},{10,18},{14,22},{11,19},{15,23}} | collective-permute-start | bytes 1179656 | tf_op jit(solution)/shard_map/ppermute | solution.py:385
  38.4 10.0 %collective-permute-start.6 = (bf16[4,3,128,128]{3,2,1,0:T(8,128)(2,1)S(1)}, bf16[4,3,128,128]{3,2,1,0:T(8,128)(2,1)S(1)}, u32[]{:S(2)}, u32[]{:S(2)}) collective-permute-start(bf16[4,3,128,128]{3,2,1,0:T(8,128)(2,1)S(1)} %fusion.6), channel_id=1, source_target_pairs={{0,8},{4,12},{1,9},{5,13},{2,10},{6,14},{3,11},{7,15}} | collective-permute-start | bytes 1179656 | tf_op jit(solution)/shard_map/ppermute | solution.py:385
  41.1 9.1 %collective-permute-start.11 = (bf16[4,2,128,128]{3,2,1,0:T(8,128)(2,1)S(1)}, bf16[4,2,128,128]{3,2,1,0:T(8,128)(2,1)S(1)}, u32[]{:S(2)}, u32[]{:S(2)}) collective-permute-start(bf16[4,2,128,128]{3,2,1,0:T(8,128)(2,1)S(1)} %get-tuple-element.96), channel_id=1, source_target_pairs={{0,4},{4,0},{8,12},{12,8},{16,20},{20,16},{24,28},{28,24},{1,5},{5... | collective-permute-start | bytes 786440 | tf_op jit(solution)/shard_map/ppermute | solution.py:385
  44.3 12.2 %collective-permute-start.10 = (bf16[4,3,128,128]{3,2,1,0:T(8,128)(2,1)S(1)}, bf16[4,3,128,128]{3,2,1,0:T(8,128)(2,1)S(1)}, u32[]{:S(2)}, u32[]{:S(2)}) collective-permute-start(bf16[4,3,128,128]{3,2,1,0:T(8,128)(2,1)S(1)} %add_convert_fusion.1), channel_id=1, source_target_pairs={{16,24},{20,28},{17,25},{21,29},{18,26},{22,30},{19,27},{23,31}} | collective-permute-start | bytes 1179656 | tf_op jit(solution)/shard_map/ppermute | solution.py:385
  48.6 9.3 %collective-permute-start.9 = (bf16[4,3,128,128]{3,2,1,0:T(8,128)(2,1)S(1)}, bf16[4,3,128,128]{3,2,1,0:T(8,128)(2,1)S(1)}, u32[]{:S(2)}, u32[]{:S(2)}) collective-permute-start(bf16[4,3,128,128]{3,2,1,0:T(8,128)(2,1)S(1)} %add_convert_fusion.2), channel_id=1, source_target_pairs={{8,16},{12,20},{9,17},{13,21},{10,18},{14,22},{11,19},{15,23}} | collective-permute-start | bytes 1179656 | tf_op jit(solution)/shard_map/ppermute | solution.py:385
  58.0 5.2 %collective-permute-start.12 = (bf16[4,3,128,128]{3,2,1,0:T(8,128)(2,1)S(1)}, bf16[4,3,128,128]{3,2,1,0:T(8,128)(2,1)S(1)}, u32[]{:S(2)}, u32[]{:S(2)}) collective-permute-start(bf16[4,3,128,128]{3,2,1,0:T(8,128)(2,1)S(1)} %add_convert_fusion), channel_id=1, source_target_pairs={{16,24},{20,28},{17,25},{21,29},{18,26},{22,30},{19,27},{23,31}} | collective-permute-start | bytes 1179656 | tf_op jit(solution)/shard_map/ppermute | solution.py:385
  58.7 17.4 %collective-permute-start.29 = (bf16[384,256]{1,0:T(8,128)(2,1)S(1)}, bf16[384,256]{1,0:T(8,128)(2,1)S(1)}, u32[]{:S(2)}, u32[]{:S(2)}) collective-permute-start(bf16[384,256]{1,0:T(8,128)(2,1)S(1)} %get-tuple-element.81), channel_id=1, source_target_pairs={{0,16},{4,20},{8,24},{12,28},{16,0},{20,4},{24,8},{28,12},{1,17},{... | collective-permute-start | bytes 589832 | tf_op jit(solution)/shard_map/ppermute | solution.py:409
  58.8 19.8 %collective-permute-start.30 = (bf16[384,256]{1,0:T(8,128)(2,1)S(1)}, bf16[384,256]{1,0:T(8,128)(2,1)S(1)}, u32[]{:S(2)}, u32[]{:S(2)}) collective-permute-start(bf16[384,256]{1,0:T(8,128)(2,1)S(1)} %get-tuple-element.82), channel_id=1, source_target_pairs={{0,20},{4,16},{8,28},{12,24},{16,4},{20,0},{24,12},{28,8},{1,21},{... | collective-permute-start | bytes 589832 | tf_op jit(solution)/shard_map/ppermute | solution.py:409
  62.6 19.5 %collective-permute-start.21 = (bf16[4,3,128,128]{3,2,1,0:T(8,128)(2,1)S(1)}, bf16[4,3,128,128]{3,2,1,0:T(8,128)(2,1)S(1)}, u32[]{:S(2)}, u32[]{:S(2)}) collective-permute-start(bf16[4,3,128,128]{3,2,1,0:T(8,128)(2,1)S(1)} %get-tuple-element.62), channel_id=1, source_target_pairs={{0,4},{4,0},{8,12},{12,8},{16,20},{20,16},{24,28},{28,24},{1,5},{5... | collective-permute-start | bytes 1179656 | tf_op jit(solution)/shard_map/ppermute | solution.py:385
  63.5 47.7 %collective-permute-start.13 = (bf16[4,3,128,128]{3,2,1,0:T(8,128)(2,1)S(1)}, bf16[4,3,128,128]{3,2,1,0:T(8,128)(2,1)S(1)}, u32[]{:S(2)}, u32[]{:S(2)}) collective-permute-start(bf16[4,3,128,128]{3,2,1,0:T(8,128)(2,1)S(1)} %get-tuple-element.93), channel_id=1, source_target_pairs={{0,4},{4,0},{8,12},{12,8},{16,20},{20,16},{24,28},{28,24},{1,5},{5... | collective-permute-start | bytes 1179656 | tf_op jit(solution)/shard_map/ppermute | solution.py:385
  65.1 25.6 %collective-permute-start.31 = (bf16[384,256]{1,0:T(8,128)(2,1)S(1)}, bf16[384,256]{1,0:T(8,128)(2,1)S(1)}, u32[]{:S(2)}, u32[]{:S(2)}) collective-permute-start(bf16[384,256]{1,0:T(8,128)(2,1)S(1)} %get-tuple-element.83), channel_id=1, source_target_pairs={{0,8},{4,12},{8,16},{12,20},{16,24},{20,28},{24,0},{28,4},{1,9},{5... | collective-permute-start | bytes 589832 | tf_op jit(solution)/shard_map/ppermute | solution.py:409
  76.1 24.9 %collective-permute-start.32 = (bf16[384,256]{1,0:T(8,128)(2,1)S(1)}, bf16[384,256]{1,0:T(8,128)(2,1)S(1)}, u32[]{:S(2)}, u32[]{:S(2)}) collective-permute-start(bf16[384,256]{1,0:T(8,128)(2,1)S(1)} %get-tuple-element.84), channel_id=1, source_target_pairs={{0,12},{4,8},{8,20},{12,16},{16,28},{20,24},{24,4},{28,0},{1,13},{... | collective-permute-start | bytes 589832 | tf_op jit(solution)/shard_map/ppermute | solution.py:409
  78.5 22.4 %collective-permute-start.33 = (bf16[384,256]{1,0:T(8,128)(2,1)S(1)}, bf16[384,256]{1,0:T(8,128)(2,1)S(1)}, u32[]{:S(2)}, u32[]{:S(2)}) collective-permute-start(bf16[384,256]{1,0:T(8,128)(2,1)S(1)} %get-tuple-element.85), channel_id=1, source_target_pairs={{0,24},{4,28},{8,0},{12,4},{16,8},{20,12},{24,16},{28,20},{1,25},{... | collective-permute-start | bytes 589832 | tf_op jit(solution)/shard_map/ppermute | solution.py:409
  82.1 29.0 %collective-permute-start.34 = (bf16[384,256]{1,0:T(8,128)(2,1)S(1)}, bf16[384,256]{1,0:T(8,128)(2,1)S(1)}, u32[]{:S(2)}, u32[]{:S(2)}) collective-permute-start(bf16[384,256]{1,0:T(8,128)(2,1)S(1)} %get-tuple-element.86), channel_id=1, source_target_pairs={{0,28},{4,24},{8,4},{12,0},{16,12},{20,8},{24,20},{28,16},{1,29},{... | collective-permute-start | bytes 589832 | tf_op jit(solution)/shard_map/ppermute | solution.py:409
  90.6 32.5 %collective-permute-start.22 = (bf16[384,384]{1,0:T(8,128)(2,1)S(1)}, bf16[384,384]{1,0:T(8,128)(2,1)S(1)}, u32[]{:S(2)}, u32[]{:S(2)}) collective-permute-start(bf16[384,384]{1,0:T(8,128)(2,1)S(1)} %get-tuple-element.73), channel_id=1, source_target_pairs={{0,16},{4,20},{8,24},{12,28},{16,0},{20,4},{24,8},{28,12},{1,17},{... | collective-permute-start | bytes 884744 | tf_op jit(solution)/shard_map/ppermute | solution.py:409
  100.9 25.1 %collective-permute-start.23 = (bf16[384,384]{1,0:T(8,128)(2,1)S(1)}, bf16[384,384]{1,0:T(8,128)(2,1)S(1)}, u32[]{:S(2)}, u32[]{:S(2)}) collective-permute-start(bf16[384,384]{1,0:T(8,128)(2,1)S(1)} %get-tuple-element.74), channel_id=1, source_target_pairs={{0,20},{4,16},{8,28},{12,24},{16,4},{20,0},{24,12},{28,8},{1,21},{... | collective-permute-start | bytes 884744 | tf_op jit(solution)/shard_map/ppermute | solution.py:409
  100.9 35.0 %collective-permute-start.24 = (bf16[384,384]{1,0:T(8,128)(2,1)S(1)}, bf16[384,384]{1,0:T(8,128)(2,1)S(1)}, u32[]{:S(2)}, u32[]{:S(2)}) collective-permute-start(bf16[384,384]{1,0:T(8,128)(2,1)S(1)} %get-tuple-element.75), channel_id=1, source_target_pairs={{0,8},{4,12},{8,16},{12,20},{16,24},{20,28},{24,0},{28,4},{1,9},{5... | collective-permute-start | bytes 884744 | tf_op jit(solution)/shard_map/ppermute | solution.py:409
  111.2 37.4 %collective-permute-start.25 = (bf16[384,384]{1,0:T(8,128)(2,1)S(1)}, bf16[384,384]{1,0:T(8,128)(2,1)S(1)}, u32[]{:S(2)}, u32[]{:S(2)}) collective-permute-start(bf16[384,384]{1,0:T(8,128)(2,1)S(1)} %get-tuple-element.76), channel_id=1, source_target_pairs={{0,12},{4,8},{8,20},{12,16},{16,28},{20,24},{24,4},{28,0},{1,13},{... | collective-permute-start | bytes 884744 | tf_op jit(solution)/shard_map/ppermute | solution.py:409
  111.2 8.8 %collective-permute-start.35 = (bf16[384,256]{1,0:T(8,128)(2,1)S(1)}, bf16[384,256]{1,0:T(8,128)(2,1)S(1)}, u32[]{:S(2)}, u32[]{:S(2)}) collective-permute-start(bf16[384,256]{1,0:T(8,128)(2,1)S(1)} %get-tuple-element.61), channel_id=1, source_target_pairs={{0,4},{4,0},{8,12},{12,8},{16,20},{20,16},{24,28},{28,24},{1,5},{5... | collective-permute-start | bytes 589832 | tf_op jit(solution)/shard_map/ppermute | solution.py:409
  120.0 28.6 %collective-permute-start.26 = (bf16[384,384]{1,0:T(8,128)(2,1)S(1)}, bf16[384,384]{1,0:T(8,128)(2,1)S(1)}, u32[]{:S(2)}, u32[]{:S(2)}) collective-permute-start(bf16[384,384]{1,0:T(8,128)(2,1)S(1)} %get-tuple-element.77), channel_id=1, source_target_pairs={{0,24},{4,28},{8,0},{12,4},{16,8},{20,12},{24,16},{28,20},{1,25},{... | collective-permute-start | bytes 884744 | tf_op jit(solution)/shard_map/ppermute | solution.py:409
  123.2 30.2 %collective-permute-start.27 = (bf16[384,384]{1,0:T(8,128)(2,1)S(1)}, bf16[384,384]{1,0:T(8,128)(2,1)S(1)}, u32[]{:S(2)}, u32[]{:S(2)}) collective-permute-start(bf16[384,384]{1,0:T(8,128)(2,1)S(1)} %get-tuple-element.78), channel_id=1, source_target_pairs={{0,28},{4,24},{8,4},{12,0},{16,12},{20,8},{24,20},{28,16},{1,29},{... | collective-permute-start | bytes 884744 | tf_op jit(solution)/shard_map/ppermute | solution.py:409
  126.1 32.3 %collective-permute-start.28 = (bf16[384,384]{1,0:T(8,128)(2,1)S(1)}, bf16[384,384]{1,0:T(8,128)(2,1)S(1)}, u32[]{:S(2)}, u32[]{:S(2)}) collective-permute-start(bf16[384,384]{1,0:T(8,128)(2,1)S(1)} %get-tuple-element.79), channel_id=1, source_target_pairs={{0,4},{4,0},{8,12},{12,8},{16,20},{20,16},{24,28},{28,24},{1,5},{5... | collective-permute-start | bytes 884744 | tf_op jit(solution)/shard_map/ppermute | solution.py:409
  135.9 31.5 %collective-permute-start.17 = (bf16[384,384]{1,0:T(8,128)(2,1)S(1)}, bf16[384,384]{1,0:T(8,128)(2,1)S(1)}, u32[]{:S(2)}, u32[]{:S(2)}) collective-permute-start(bf16[384,384]{1,0:T(8,128)(2,1)S(1)} %get-tuple-element.68), channel_id=1, source_target_pairs={{0,16},{4,20},{8,24},{12,28},{16,0},{20,4},{24,8},{28,12},{1,17},{... | collective-permute-start | bytes 884744 | tf_op jit(solution)/shard_map/ppermute | solution.py:409
  148.5 28.3 %collective-permute-start.18 = (bf16[384,384]{1,0:T(8,128)(2,1)S(1)}, bf16[384,384]{1,0:T(8,128)(2,1)S(1)}, u32[]{:S(2)}, u32[]{:S(2)}) collective-permute-start(bf16[384,384]{1,0:T(8,128)(2,1)S(1)} %get-tuple-element.69), channel_id=1, source_target_pairs={{0,20},{4,16},{8,28},{12,24},{16,4},{20,0},{24,12},{28,8},{1,21},{... | collective-permute-start | bytes 884744 | tf_op jit(solution)/shard_map/ppermute | solution.py:409
  148.6 44.7 %collective-permute-start.14 = (bf16[384,384]{1,0:T(8,128)(2,1)S(1)}, bf16[384,384]{1,0:T(8,128)(2,1)S(1)}, u32[]{:S(2)}, u32[]{:S(2)}) collective-permute-start(bf16[384,384]{1,0:T(8,128)(2,1)S(1)} %get-tuple-element.64), channel_id=1, source_target_pairs={{0,24},{4,28},{8,0},{12,4},{16,8},{20,12},{24,16},{28,20},{1,25},{... | collective-permute-start | bytes 884744 | tf_op jit(solution)/shard_map/ppermute | solution.py:409
  153.4 33.1 %collective-permute-start.19 = (bf16[384,384]{1,0:T(8,128)(2,1)S(1)}, bf16[384,384]{1,0:T(8,128)(2,1)S(1)}, u32[]{:S(2)}, u32[]{:S(2)}) collective-permute-start(bf16[384,384]{1,0:T(8,128)(2,1)S(1)} %get-tuple-element.70), channel_id=1, source_target_pairs={{0,8},{4,12},{8,16},{12,20},{16,24},{20,28},{24,0},{28,4},{1,9},{5... | collective-permute-start | bytes 884744 | tf_op jit(solution)/shard_map/ppermute | solution.py:409
  158.4 32.7 %collective-permute-start.20 = (bf16[384,384]{1,0:T(8,128)(2,1)S(1)}, bf16[384,384]{1,0:T(8,128)(2,1)S(1)}, u32[]{:S(2)}, u32[]{:S(2)}) collective-permute-start(bf16[384,384]{1,0:T(8,128)(2,1)S(1)} %get-tuple-element.71), channel_id=1, source_target_pairs={{0,12},{4,8},{8,20},{12,16},{16,28},{20,24},{24,4},{28,0},{1,13},{... | collective-permute-start | bytes 884744 | tf_op jit(solution)/shard_map/ppermute | solution.py:409
  167.4 25.9 %collective-permute-start.15 = (bf16[384,384]{1,0:T(8,128)(2,1)S(1)}, bf16[384,384]{1,0:T(8,128)(2,1)S(1)}, u32[]{:S(2)}, u32[]{:S(2)}) collective-permute-start(bf16[384,384]{1,0:T(8,128)(2,1)S(1)} %get-tuple-element.65), channel_id=1, source_target_pairs={{0,28},{4,24},{8,4},{12,0},{16,12},{20,8},{24,20},{28,16},{1,29},{... | collective-permute-start | bytes 884744 | tf_op jit(solution)/shard_map/ppermute | solution.py:409
  176.9 16.4 %collective-permute-start.16 = (bf16[384,384]{1,0:T(8,128)(2,1)S(1)}, bf16[384,384]{1,0:T(8,128)(2,1)S(1)}, u32[]{:S(2)}, u32[]{:S(2)}) collective-permute-start(bf16[384,384]{1,0:T(8,128)(2,1)S(1)} %get-tuple-element.66), channel_id=1, source_target_pairs={{0,4},{4,0},{8,12},{12,8},{16,20},{20,16},{24,28},{28,24},{1,5},{5... | collective-permute-start | bytes 884744 | tf_op jit(solution)/shard_map/ppermute | solution.py:409

commit v11 on v10

--- a/solution.py
+++ b/solution.py
@@ -45,11 +45,11 @@
     return max(count for count in range(1, m + 1) if m % count == 0 and (count == 1 or 2 * width * count <= most))
 
 
-def local_body(n, widths, swaps, place, low, keys, values, *refs):
-    outs, (kbuf, vbuf, sems) = refs[:-3], refs[-3:]
+def local_body(n, widths, swaps, ahead, place, low, keys, values, queries, *refs):
+    outs, (kbuf, vbuf, sems, early) = refs[:-4], refs[-4:]
     total = sum(widths)
     here = place[0], place[1], low[0]
-    together = rows_together(n // 2, total, 16)
+    together = rows_together(n // 2, total, 8)
 
     def copies(row, side):
         cols = pl.ds(column(here, row, side, n), total * HEAD)
@@ -59,10 +59,31 @@
             for which, (source, buf) in enumerate(((keys, kbuf), (values, vbuf)))
         ]
 
+    def copies_ahead(row, side):
+        wide = ahead[1] * HEAD
+        cols = pl.ds(column((place[0], place[1], ahead[0]), row, side, n), wide)
+        slot = 2 * row + side
+        return [
+            pltpu.make_async_copy(source.at[:, cols], out.at[slot, :, :wide], early.at[which, slot])
+            for which, (source, out) in enumerate(zip((queries, keys, values), outs[-3:]))
+        ]
+
     def fetch(row, carry):
         for side in range(2):
             for copy in copies(row, side):
                 copy.start()
+        return carry
+
+    def start_ahead(row, carry):
+        for side in range(2):
+            for copy in copies_ahead(row, side):
+                copy.start()
+        return carry
+
+    def wait_ahead(row, carry):
+        for side in range(2):
+            for copy in copies_ahead(row, side):
+                copy.wait()
         return carry
 
     def work(step, carry):
@@ -72,7 +93,7 @@
                 copy.wait()
         places = [
             [(out, head) for out, width in zip(arrays, sizes) for head in range(width)]
-            for arrays, sizes in ((outs[: len(widths)], widths), (outs[len(widths) :], swaps))
+            for arrays, sizes in ((outs[: len(widths)], widths), (outs[len(widths) :][: len(swaps)], swaps))
         ]
         for row, side in slots:
             for first in range(0, total, 2):
@@ -91,26 +112,34 @@
         return carry
 
     lax.fori_loop(0, n // 2, fetch, 0)
+    if ahead:
+        lax.fori_loop(0, n // 2, start_ahead, 0)
     lax.fori_loop(0, n // 2 // together, work, 0)
-
-
-def local_states(place, keys, values, n, low, widths, swaps):
+    if ahead:
+        lax.fori_loop(0, n // 2, wait_ahead, 0)
+
+
+def local_states(place, queries, keys, values, n, low, widths, swaps, ahead):
     rows, m, total = keys.shape[0], n // 2, sum(widths)
     buf = pltpu.VMEM((n, rows, odd(total) * HEAD), keys.dtype)
     shapes = [jax.ShapeDtypeStruct((m, width, HEAD, HEAD), jnp.float32) for width in widths]
     shapes += [jax.ShapeDtypeStruct((m, width, HEAD, HEAD), jnp.bfloat16) for width in swaps]
+    spare = 0
+    if ahead:
+        shapes += [jax.ShapeDtypeStruct((n, rows, odd(ahead[1]) * HEAD), jnp.bfloat16)] * 3
+        spare = 6 * n * rows * odd(ahead[1]) * HEAD
     return pl.pallas_call(
-        functools.partial(local_body, n, widths, swaps),
-        in_specs=[pl.BlockSpec(memory_space=pltpu.SMEM)] * 2 + [pl.BlockSpec(memory_space=pltpu.HBM)] * 2,
+        functools.partial(local_body, n, widths, swaps, ahead),
+        in_specs=[pl.BlockSpec(memory_space=pltpu.SMEM)] * 2 + [pl.BlockSpec(memory_space=pltpu.HBM)] * 3,
         out_specs=[pl.BlockSpec(memory_space=pltpu.VMEM)] * len(shapes),
         out_shape=shapes,
-        scratch_shapes=[buf, buf, pltpu.SemaphoreType.DMA((2, n))],
-        compiler_params=params(4 * n * rows * odd(total) * HEAD + 3 * n * total * HEAD * HEAD),
+        scratch_shapes=[buf, buf, pltpu.SemaphoreType.DMA((2, n)), pltpu.SemaphoreType.DMA((3, n))],
+        compiler_params=params(4 * n * rows * odd(total) * HEAD + 3 * n * total * HEAD * HEAD + spare),
         cost_estimate=pl.CostEstimate(
             flops=2 * n * total * rows * HEAD * HEAD, bytes_accessed=4 * rows * n * total * HEAD, transcendentals=0
         ),
         name="local",
-    )(place, jnp.full((1,), low, jnp.int32), keys, values)
+    )(place, jnp.full((1,), low, jnp.int32), keys, values, queries)
 
 
 def masked_scores(query, key):
@@ -133,12 +162,13 @@
     return tiles
 
 
-def attend_body(n, spans, order, place, low, queries, keys, values, gain, *refs):
+def attend_body(n, spans, order, early, place, low, queries, keys, values, gain, *refs):
     states, outs = refs[: 2 * len(spans)], refs[2 * len(spans) :][:n]
-    qbuf, kbuf, vbuf, sown, soth, gbuf, held, sems, extra = refs[-9:]
+    sown, soth, gbuf, held, sems, extra = refs[-6:]
+    qbuf, kbuf, vbuf = (queries, keys, values) if early else refs[-9:-6]
     width = sum(size for _, size in spans)
     m, wide = n // 2, width * HEAD
-    together = rows_together(m, width, 12)
+    together = rows_together(m, width, 8 if early else 6)
     here = place[0], place[1], low[0]
     small, start = [(gain, gbuf)], 0
     for chunk, (skip, size) in enumerate(spans):
@@ -155,6 +185,9 @@
             for which, (source, buf) in enumerate(((queries, qbuf), (keys, kbuf), (values, vbuf)))
         ]
 
+    def source_slot(step, side):
+        return 2 * (lax.rem(here[0] + step, m) if early else step) + side
+
     def sends(step):
         return [
             pltpu.make_async_copy(held.at[slot, :, :wide], outs[order.index(slot)], sems.at[3, slot])
@@ -170,7 +203,7 @@
     def work(group, carry):
         steps = [group * together + index for index in range(together)]
         for step in steps:
-            for side in range(2):
+            for side in range(0 if early else 2):
                 for copy in copies(step, side):
                     copy.wait()
         heads = [
@@ -180,12 +213,12 @@
             for head in range(width)
         ]
         scores = [
-            masked_scores(qbuf[2 * step + side, :, cols], kbuf[2 * step + side, :, cols])
+            masked_scores(qbuf[source_slot(step, side), :, cols], kbuf[source_slot(step, side), :, cols])
             for step, side, _, cols in heads
         ]
         attended = []
         for (step, side, head, cols), tiles in zip(heads, scores):
-            slot = 2 * step + side
+            slot = source_slot(step, side)
             state = (sown if side == 0 else soth)[lax.rem(here[0] + step, m), head]
             left = jnp.concatenate([*tiles, qbuf[slot, :, cols]], axis=1)
             right = jnp.concatenate([vbuf[slot, :, cols], state], axis=0)
@@ -205,10 +238,12 @@
 
         return carry
 
-    lax.fori_loop(0, 1, fetch, 0)
+    if not early:
+        lax.fori_loop(0, 1, fetch, 0)
     for copy in small:
         copy.start()
-    lax.fori_loop(1, m, fetch, 0)
+    if not early:
+        lax.fori_loop(1, m, fetch, 0)
     for copy in small:
         copy.wait()
     lax.fori_loop(0, m // together, work, 0)
@@ -217,23 +252,21 @@
             copy.wait()
 
 
-def attend(place, queries, keys, values, gain, states, spans, order, n, low):
-    rows, m = queries.shape[0], n // 2
+def attend(place, queries, keys, values, gain, states, spans, order, n, low, early):
+    rows, m = queries.shape[1 if early else 0], n // 2
     width = sum(size for _, size in spans)
     wide = width * HEAD
     tokens = pltpu.VMEM((n, rows, odd(width) * HEAD), jnp.bfloat16)
     state = pltpu.VMEM((m, width, HEAD, HEAD), jnp.bfloat16)
     return pl.pallas_call(
-        functools.partial(attend_body, n, spans, order),
+        functools.partial(attend_body, n, spans, order, early),
         in_specs=[pl.BlockSpec(memory_space=pltpu.SMEM)] * 2
-        + [pl.BlockSpec(memory_space=pltpu.HBM)] * 3
+        + [pl.BlockSpec(memory_space=pltpu.VMEM if early else pltpu.HBM)] * 3
         + [pl.BlockSpec(memory_space=pl.ANY)] * (1 + 2 * len(states)),
         out_specs=[pl.BlockSpec(memory_space=pltpu.HBM)] * n,
         out_shape=[jax.ShapeDtypeStruct((rows, wide), jnp.bfloat16)] * n,
-        scratch_shapes=[
-            tokens,
-            tokens,
-            tokens,
+        scratch_shapes=[tokens] * (0 if early else 3)
+        + [
             state,
             state,
             pltpu.VMEM((1, HEADS * HEAD), jnp.float32),
@@ -343,10 +376,11 @@
         low, width = self.groups[g]
         widths = tuple(self.parts[c][1] for c in inside(self.parts, low, width))
         swaps = tuple(self.swaps[c][1] for c in inside(self.swaps, low, width))
-        _, keys, values = self.arrays
         place = self.hold(self.place, "group", g)
-        arrays = local_states(place, keys, values, self.n, low, widths, swaps)
-        return arrays[: len(widths)], arrays[len(widths) :]
+        ahead = self.chunks[0] if g == 1 else None
+        arrays = local_states(place, *self.arrays, self.n, low, widths, swaps, ahead)
+        both = len(widths) + len(swaps)
+        return arrays[: len(widths)], arrays[len(widths) : both], *((arrays[both:],) if ahead else ())
 
     def around(self, chunks, low):
         return next(c for c, (start, width) in enumerate(chunks) if start <= low < start + width)
@@ -399,7 +433,9 @@
             if first < last:
                 states.append(self.get("states", part))
                 spans.append((first - start, last - first))
-        return attend(place, *self.arrays, self.gain, states, tuple(spans), (0, *self.shifts), self.n, low)
+        early = c == 0 and len(self.groups) > 1
+        arrays = self.get("group", 1)[2] if early else self.arrays
+        return attend(place, *arrays, self.gain, states, tuple(spans), (0, *self.shifts), self.n, low, early)
 
     def sent(self, c, k):
         shift = self.shifts[k - 1]

time: 198 us -> 204 us (1.030)
  waiting for transfers between devices: 75.4 us -> 91.4 us
  starting transfers between devices: 71.3 us -> 57.1 us
  local copies, waits for them, and re-layouts: 0.01 us -> 4.32 us
    ppermute x21, waiting for transfers between devices: 56.2 us -> 69.4 us  [sent(): lax.ppermute(self.hold(self.get('mixed', c)[k], 'sent', c, k), 'seq', pairs)]
    ppermute x21, starting transfers between devices: 51.9 us -> 40.7 us  [sent(): lax.ppermute(self.hold(self.get('mixed', c)[k], 'sent', c, k), 'seq', pairs)]
    ppermute x12, waiting for transfers between devices: 17.7 us -> 22 us  [prefix(): return lax.ppermute(self.get('message', c, s), 'seq', pairs)]
    unnamed x6 -> x18, local copies, waits for them, and re-layouts: 0.01 us -> 4.32 us
  transfers between devices with their start and end apart: 36 -> 36, of which waited for: 14 -> 14; matrix products, arithmetic and copies ran while one was open for 4% -> 4% of each run, Pallas kernels for 18% -> 17%
where the time goes in v11:
time: 204 us; the launch traced here: 201 us
  waiting for transfers between devices  91.4 us (45%)
  starting transfers between devices  57.1 us (28%)
  Pallas kernels  39.5 us (19%)
  other arithmetic  8.26 us (4%)
  local copies, waits for them, and re-layouts  4.32 us (2%)
    ppermute x21, waiting for transfers between devices, sent(): lax.ppermute(self.hold(self.get('mixed', c)[k], 'sent', c, k), 'seq', pairs)  69.4 us
    ppermute x21, starting transfers between devices, sent(): lax.ppermute(self.hold(self.get('mixed', c)[k], 'sent', c, k), 'seq', pairs)  40.7 us
    ppermute x12, waiting for transfers between devices, prefix(): return lax.ppermute(self.get('message', c, s), 'seq', pairs)  22 us
    pallas_call x3, Pallas kernels, attend(): pl.pallas_call(functools.partial(attend_body, n, spans, order, early), in...  21.1 us
    ppermute x12, starting transfers between devices, prefix(): return lax.ppermute(self.get('message', c, s), 'seq', pairs)  13.7 us
    pallas_call x2, Pallas kernels, local_states(): pl.pallas_call(functools.partial(local_body, n, widths, swaps, ahead), in...  9.41 us
    pallas_call x4, Pallas kernels, put(): pl.pallas_call(functools.partial(put_body, n, order), in_specs=[pl.BlockS...  9.01 us
    convert_element_type x10, other arithmetic, message(): return self.hold(value.astype(jnp.bfloat16), 'message', c, s)  5.53 us
  transfers between devices with their start and end apart: 36, of which 14 were waited for; matrix products, arithmetic and copies ran while one was open for 4% of the time, Pallas kernels for 17%

profile of v11, /device:TPU:8, one launch (start us, length us, event | category | flops | bytes accessed | tf_op | source)
XLA Modules:
  0.0 200.9 jit_solution(10313830990281287931)
XLA Ops:
  0.1 3.4 %local.3 = (f32[4,2,128,128]{3,2,1,0:T(8,128)S(1)}, bf16[4,2,128,128]{3,2,1,0:T(8,128)(2,1)S(1)}) custom-call(s32[2]{0:T(128)S(1)} %pad_add_fusion.place, s32[1]{0:T(128)} %constant.38.clone.1.low, bf16[384,8192]{1,0:T(8,128)(2,1)} %keys.7, bf16[384,8192]{1,0:T(8,128)(2,1)} %values.7, bf16[384,8192]{1,0:T(8,128)(2,1)} %queries.7), custom_call_target="tpu_custom_call" | custom-call | flops 201326592 | bytes 3145728 | tf_op jit(solution)/shard_map/local/pallas_call | solution.py:131
  3.5 1.6 collective-permute-start.2
  5.0 6.0 %local.2 = (f32[4,3,128,128]{3,2,1,0:T(8,128)S(1)}, f32[4,3,128,128]{3,2,1,0:T(8,128)S(1)}, bf16[4,3,128,128]{3,2,1,0:T(8,128)(2,1)S(1)}, bf16[4,3,128,128]{3,2,...) custom-call(s32[2]{0:T(128)S(1)} %pad_add_fusion.place, ...), custom_call_target="tpu_custom_call" | custom-call | flops 603979776 | bytes 9437184 | tf_op jit(solution)/shard_map/local/pallas_call | solution.py:131
  11.1 1.4 copy-done
  12.5 1.4 copy-done.2
  13.9 1.5 copy-done.4
  15.5 1.3 collective-permute-start.3
  17.3 7.8 %collective-permute-done.3 = bf16[4,2,128,128]{3,2,1,0:T(8,128)(2,1)S(1)} collective-permute-done((bf16[4,2,128,128]{3,2,1,0:T(8,128)(2,1)S(1)}, bf16[4,2,128,128]{3,2,1,0:T(8,128)(2,1)S(1)}, u32[]{:S(2)}, u32[]{:S(2)}) %collective-permute-start.3) | collective-permute-done | bytes 262176 | tf_op jit(solution)/shard_map/ppermute | solution.py:419
  26.0 2.1 %collective-permute-start.5 = (bf16[4,2,128,128]{3,2,1,0:T(8,128)(2,1)}, bf16[4,2,128,128]{3,2,1,0:T(8,128)(2,1)}, u32[]{:S(2)}, u32[]{:S(2)}) collective-permute-start(bf16[4,2,128,128]{3,2,1,0:T(8,128)(2,1)} %add_convert_fusion.5), channel_id=1, source_target_pairs={{8,16},{12,20},{9,17},{13,21},{10,18},{14,22},{11,19},{15,23}} | collective-permute-start | bytes 786440 | tf_op jit(solution)/shard_map/ppermute | solution.py:419
  29.0 1.3 collective-permute-start.4
  30.8 1.5 collective-permute-done.5
  32.3 1.7 add_convert_fusion.4
  34.7 6.1 %collective-permute-done.4 = bf16[4,3,128,128]{3,2,1,0:T(8,128)(2,1)} collective-permute-done((bf16[4,3,128,128]{3,2,1,0:T(8,128)(2,1)}, bf16[4,3,128,128]{3,2,1,0:T(8,128)(2,1)}, u32[]{:S(2)}, u32[]{:S(2)}) %collective-permute-start.4) | collective-permute-done | bytes 393248 | tf_op jit(solution)/shard_map/ppermute | solution.py:419
  40.8 1.1 add_convert_fusion.3
  42.0 1.3 collective-permute-start.7
  43.4 1.3 collective-permute-start.6
  44.7 1.3 fusion.5
  46.6 3.2 %collective-permute-done.7 = bf16[4,3,128,128]{3,2,1,0:T(8,128)(2,1)S(1)} collective-permute-done((bf16[4,3,128,128]{3,2,1,0:T(8,128)(2,1)S(1)}, bf16[4,3,128,128]{3,2,1,0:T(8,128)(2,1)S(1)}, u32[]{:S(2)}, u32[]{:S(2)}) %collective-permute-start.7) | collective-permute-done | bytes 393248 | tf_op jit(solution)/shard_map/ppermute | solution.py:419
  50.6 3.4 %collective-permute-done.6 = bf16[4,3,128,128]{3,2,1,0:T(8,128)(2,1)S(1)} collective-permute-done((bf16[4,3,128,128]{3,2,1,0:T(8,128)(2,1)S(1)}, bf16[4,3,128,128]{3,2,1,0:T(8,128)(2,1)S(1)}, u32[]{:S(2)}, u32[]{:S(2)}) %collective-permute-start.6) | collective-permute-done | bytes 393248 | tf_op jit(solution)/shard_map/ppermute | solution.py:419
  54.2 1.6 collective-permute-start.9
  55.9 4.5 %attend.3 = (bf16[384,256]{1,0:T(8,128)(2,1)S(1)}, bf16[384,256]{1,0:T(8,128)(2,1)S(1)}, bf16[384,256]{1,0:T(8,128)(2,1)S(1)}, bf16[384,256]{1,0:T(8,128)(2,1)S(...) custom-call(s32[2]{0:T(128)S(1)} %pad_add_fusion.place, ...), custom_call_target="tpu_custom_call" | custom-call | flops 1409286144 | bytes 6291456 | tf_op jit(solution)/shard_map/attend/pallas_call | solution.py:261
  60.5 1.3 fusion.1
  62.7 1.7 collective-permute-start.29
  64.4 1.3 collective-permute-start.30
  65.7 1.5 collective-permute-start.21
  68.1 12.5 %collective-permute-start.31 = (bf16[384,256]{1,0:T(8,128)(2,1)S(1)}, bf16[384,256]{1,0:T(8,128)(2,1)S(1)}, u32[]{:S(2)}, u32[]{:S(2)}) collective-permute-start(bf16[384,256]{1,0:T(8,128)(2,1)S(1)} %get-tuple-element.89), channel_id=1, source_target_pairs={{0,8},{4,12},{8,16},{12,20},{16,24},{20,28},{24,0},{28,4},{1,9},{5... | collective-permute-start | bytes 589832 | tf_op jit(solution)/shard_map/ppermute | solution.py:445
  80.6 4.4 %collective-permute-start.32 = (bf16[384,256]{1,0:T(8,128)(2,1)S(1)}, bf16[384,256]{1,0:T(8,128)(2,1)S(1)}, u32[]{:S(2)}, u32[]{:S(2)}) collective-permute-start(bf16[384,256]{1,0:T(8,128)(2,1)S(1)} %get-tuple-element.90), channel_id=1, source_target_pairs={{0,12},{4,8},{8,20},{12,16},{16,28},{20,24},{24,4},{28,0},{1,13},{... | collective-permute-start | bytes 589832 | tf_op jit(solution)/shard_map/ppermute | solution.py:445
  85.0 1.2 collective-permute-start.34
  86.2 8.3 %attend.5 = (bf16[384,384]{1,0:T(8,128)(2,1)S(1)}, bf16[384,384]{1,0:T(8,128)(2,1)S(1)}, bf16[384,384]{1,0:T(8,128)(2,1)S(1)}, bf16[384,384]{1,0:T(8,128)(2,1)S(...) custom-call(s32[2]{0:T(128)S(1)} %pad_add_fusion.place, ...), custom_call_target="tpu_custom_call" | custom-call | flops 2113929216 | bytes 9437184 | tf_op jit(solution)/shard_map/attend/pallas_call | solution.py:261
  94.5 1.8 collective-permute-start.22
  96.3 10.6 %collective-permute-done.32.refs_4_ = bf16[384,256]{1,0:T(8,128)(2,1)S(1)} collective-permute-done((bf16[384,256]{1,0:T(8,128)(2,1)S(1)}, bf16[384,256]{1,0:T(8,128)(2,1)S(1)}, u32[]{:S(2)}, u32[]{:S(2)}) %collective-permute-start.32) | collective-permute-done | bytes 196640 | tf_op jit(solution)/shard_map/ppermute | solution.py:445
  107.0 2.6 %collective-permute-start.24 = (bf16[384,384]{1,0:T(8,128)(2,1)S(1)}, bf16[384,384]{1,0:T(8,128)(2,1)S(1)}, u32[]{:S(2)}, u32[]{:S(2)}) collective-permute-start(bf16[384,384]{1,0:T(8,128)(2,1)S(1)} %get-tuple-element.81), channel_id=1, source_target_pairs={{0,8},{4,12},{8,16},{12,20},{16,24},{20,28},{24,0},{28,4},{1,9},{5... | collective-permute-start | bytes 884744 | tf_op jit(solution)/shard_map/ppermute | solution.py:445
  109.6 6.1 %collective-permute-done.34.refs_6_ = bf16[384,256]{1,0:T(8,128)(2,1)S(1)} collective-permute-done((bf16[384,256]{1,0:T(8,128)(2,1)S(1)}, bf16[384,256]{1,0:T(8,128)(2,1)S(1)}, u32[]{:S(2)}, u32[]{:S(2)}) %collective-permute-start.34) | collective-permute-done | bytes 196640 | tf_op jit(solution)/shard_map/ppermute | solution.py:445
  115.7 2.9 %collective-permute-start.35 = (bf16[384,256]{1,0:T(8,128)(2,1)S(1)}, bf16[384,256]{1,0:T(8,128)(2,1)S(1)}, u32[]{:S(2)}, u32[]{:S(2)}) collective-permute-start(bf16[384,256]{1,0:T(8,128)(2,1)S(1)} %get-tuple-element.67), channel_id=1, source_target_pairs={{0,4},{4,0},{8,12},{12,8},{16,20},{20,16},{24,28},{28,24},{1,5},{5... | collective-permute-start | bytes 589832 | tf_op jit(solution)/shard_map/ppermute | solution.py:445
  118.6 8.3 %attend.4 = (bf16[384,384]{1,0:T(8,128)(2,1)S(1)}, bf16[384,384]{1,0:T(8,128)(2,1)S(1)}, bf16[384,384]{1,0:T(8,128)(2,1)S(1)}, bf16[384,384]{1,0:T(8,128)(2,1)S(...) custom-call(s32[2]{0:T(128)S(1)} %pad_add_fusion.place, ...), custom_call_target="tpu_custom_call" | custom-call | flops 2113929216 | bytes 9437184 | tf_op jit(solution)/shard_map/attend/pallas_call | solution.py:261
  126.9 3.3 %collective-permute-start.26 = (bf16[384,384]{1,0:T(8,128)(2,1)S(1)}, bf16[384,384]{1,0:T(8,128)(2,1)S(1)}, u32[]{:S(2)}, u32[]{:S(2)}) collective-permute-start(bf16[384,384]{1,0:T(8,128)(2,1)S(1)} %get-tuple-element.83), channel_id=1, source_target_pairs={{0,24},{4,28},{8,0},{12,4},{16,8},{20,12},{24,16},{28,20},{1,25},{... | collective-permute-start | bytes 884744 | tf_op jit(solution)/shard_map/ppermute | solution.py:445
  131.3 1.8 collective-permute-start.28
  133.1 11.7 %collective-permute-done.24.refs_3_ = bf16[384,384]{1,0:T(8,128)(2,1)S(1)} collective-permute-done((bf16[384,384]{1,0:T(8,128)(2,1)S(1)}, bf16[384,384]{1,0:T(8,128)(2,1)S(1)}, u32[]{:S(2)}, u32[]{:S(2)}) %collective-permute-start.24) | collective-permute-done | bytes 294944 | tf_op jit(solution)/shard_map/ppermute | solution.py:445
  144.8 16.0 %collective-permute-done.25.refs_4_ = bf16[384,384]{1,0:T(8,128)(2,1)S(1)} collective-permute-done((bf16[384,384]{1,0:T(8,128)(2,1)S(1)}, bf16[384,384]{1,0:T(8,128)(2,1)S(1)}, u32[]{:S(2)}, u32[]{:S(2)}) %collective-permute-start.25) | collective-permute-done | bytes 294944 | tf_op jit(solution)/shard_map/ppermute | solution.py:445
  160.8 4.8 %collective-permute-start.14 = (bf16[384,384]{1,0:T(8,128)(2,1)S(1)}, bf16[384,384]{1,0:T(8,128)(2,1)S(1)}, u32[]{:S(2)}, u32[]{:S(2)}) collective-permute-start(bf16[384,384]{1,0:T(8,128)(2,1)S(1)} %get-tuple-element.70), channel_id=1, source_target_pairs={{0,24},{4,28},{8,0},{12,4},{16,8},{20,12},{24,16},{28,20},{1,25},{... | collective-permute-start | bytes 884744 | tf_op jit(solution)/shard_map/ppermute | solution.py:445
  166.2 9.0 %collective-permute-done.17.refs_1_ = bf16[384,384]{1,0:T(8,128)(2,1)S(1)} collective-permute-done((bf16[384,384]{1,0:T(8,128)(2,1)S(1)}, bf16[384,384]{1,0:T(8,128)(2,1)S(1)}, u32[]{:S(2)}, u32[]{:S(2)}) %collective-permute-start.17) | collective-permute-done | bytes 294944 | tf_op jit(solution)/shard_map/ppermute | solution.py:445
  175.9 10.1 %collective-permute-done.18.refs_2_ = bf16[384,384]{1,0:T(8,128)(2,1)S(1)} collective-permute-done((bf16[384,384]{1,0:T(8,128)(2,1)S(1)}, bf16[384,384]{1,0:T(8,128)(2,1)S(1)}, u32[]{:S(2)}, u32[]{:S(2)}) %collective-permute-start.18) | collective-permute-done | bytes 294944 | tf_op jit(solution)/shard_map/ppermute | solution.py:445
  186.0 2.3 %put.4 = (bf16[3072,1024]{1,0:T(8,128)(2,1)}, s32[2]{0:T(128)}) custom-call(s32[2]{0:T(128)S(1)} %pad_add_fusion.place, s32[1]{0:T(128)} %constant.38.clone.1.low, bf16[384,256]{1,0:T(8,128)(2,1)S(1)} %get-tuple-element.86.refs_0_, bf16[384,256]{1,0:T(8,128)(2,1)S(1)} %collective-permute-done.29.refs_1_, ...), custom_call_target="tpu_custom_call" | custom-call | tf_op jit(solution)/shard_map/put/pallas_call | solution.py:311
  188.3 2.5 %put.5 = (bf16[3072,1024]{1,0:T(8,128)(2,1)}, s32[2]{0:T(128)}) custom-call(s32[2]{0:T(128)S(1)} %pad_add_fusion.place, s32[1]{0:T(128)} %constant.37.clone.1.low, bf16[384,384]{1,0:T(8,128)(2,1)S(1)} %get-tuple-element.78.refs_0_, bf16[384,384]{1,0:T(8,128)(2,1)S(1)} %collective-permute-done.22.refs_1_, ...), custom_call_target="tpu_custom_call", output_to_operand_aliasing={{0}: (10, {})} | custom-call | tf_op jit(solution)/shard_map/put/pallas_call | solution.py:311
  190.8 1.6 collective-permute-done.19.refs_3_
  192.5 4.2 %collective-permute-done.20.refs_4_ = bf16[384,384]{1,0:T(8,128)(2,1)S(1)} collective-permute-done((bf16[384,384]{1,0:T(8,128)(2,1)S(1)}, bf16[384,384]{1,0:T(8,128)(2,1)S(1)}, u32[]{:S(2)}, u32[]{:S(2)}) %collective-permute-start.20) | collective-permute-done | bytes 294944 | tf_op jit(solution)/shard_map/ppermute | solution.py:445
  196.6 2.2 %put.6 = (bf16[3072,1024]{1,0:T(8,128)(2,1)}, s32[2]{0:T(128)}) custom-call(s32[2]{0:T(128)S(1)} %pad_add_fusion.place, s32[1]{0:T(128)} %constant.36.clone.1.low, bf16[384,384]{1,0:T(8,128)(2,1)S(1)} %get-tuple-element.73.refs_0_, bf16[384,384]{1,0:T(8,128)(2,1)S(1)} %collective-permute-done.17.refs_1_, ...), custom_call_target="tpu_custom_call", output_to_operand_aliasing={{0}: (7, {})} | custom-call | tf_op jit(solution)/shard_map/put/pallas_call | solution.py:311
  198.9 2.0 put.7
  (64 shorter events, 9.6 us)
Async XLA Ops:
  3.5 11.9 %collective-permute-start.2 = (bf16[4,2,128,128]{3,2,1,0:T(8,128)(2,1)S(1)}, bf16[4,2,128,128]{3,2,1,0:T(8,128)(2,1)S(1)}, u32[]{:S(2)}, u32[]{:S(2)}) collective-permute-start(bf16[4,2,128,128]{3,2,1,0:T(8,128)(2,1)S(1)} %get-tuple-element.56), channel_id=1, source_target_pairs={{0,4},{4,0},{8,12},{12,8},{16,20},{20,16},{24,28},{28,24},{1,5},{5... | collective-permute-start | bytes 786440 | tf_op jit(solution)/shard_map/ppermute | solution.py:392
  11.1 1.4 copy-start
  12.5 1.4 copy-start.2
  13.9 1.5 copy-start.4
  15.4 14.9 %copy-start.7 = (bf16[4,2,128,128]{3,2,1,0:T(8,128)(2,1)}, bf16[4,2,128,128]{3,2,1,0:T(8,128)(2,1)S(1)}, u32[]{:S(2)}) copy-start(bf16[4,2,128,128]{3,2,1,0:T(8,128)(2,1)S(1)} %collective-permute-done.2) | copy-start | bytes 786436
  15.5 9.7 %collective-permute-start.3 = (bf16[4,2,128,128]{3,2,1,0:T(8,128)(2,1)S(1)}, bf16[4,2,128,128]{3,2,1,0:T(8,128)(2,1)S(1)}, u32[]{:S(2)}, u32[]{:S(2)}) collective-permute-start(bf16[4,2,128,128]{3,2,1,0:T(8,128)(2,1)S(1)} %fusion.8), channel_id=1, source_target_pairs={{0,8},{4,12},{1,9},{5,13},{2,10},{6,14},{3,11},{7,15}} | collective-permute-start | bytes 786440 | tf_op jit(solution)/shard_map/ppermute | solution.py:419
  16.8 11.3 %collective-permute-start.1 = (bf16[4,3,128,128]{3,2,1,0:T(8,128)(2,1)S(1)}, bf16[4,3,128,128]{3,2,1,0:T(8,128)(2,1)S(1)}, u32[]{:S(2)}, u32[]{:S(2)}) collective-permute-start(bf16[4,3,128,128]{3,2,1,0:T(8,128)(2,1)S(1)} %get-tuple-element.54), channel_id=1, source_target_pairs={{0,4},{4,0},{8,12},{12,8},{16,20},{20,16},{24,28},{28,24},{1,5},{5... | collective-permute-start | bytes 1179656 | tf_op jit(solution)/shard_map/ppermute | solution.py:392
  25.1 3.0 %copy-start.8 = (bf16[4,2,128,128]{3,2,1,0:T(8,128)(2,1)}, bf16[4,2,128,128]{3,2,1,0:T(8,128)(2,1)S(1)}, u32[]{:S(2)}) copy-start(bf16[4,2,128,128]{3,2,1,0:T(8,128)(2,1)S(1)} %collective-permute-done.3) | copy-start | bytes 786436
  26.0 29.9 %copy-start.6 = (f32[8192]{0:T(1024)S(1)}, f32[8192]{0:T(1024)}, u32[]{:S(2)}) copy-start(f32[8192]{0:T(1024)} %param.7) | copy-start | bytes 98308
  26.0 6.4 %collective-permute-start.5 = (bf16[4,2,128,128]{3,2,1,0:T(8,128)(2,1)}, bf16[4,2,128,128]{3,2,1,0:T(8,128)(2,1)}, u32[]{:S(2)}, u32[]{:S(2)}) collective-permute-start(bf16[4,2,128,128]{3,2,1,0:T(8,128)(2,1)} %add_convert_fusion.5), channel_id=1, source_target_pairs={{8,16},{12,20},{9,17},{13,21},{10,18},{14,22},{11,19},{15,23}} | collective-permute-start | bytes 786440 | tf_op jit(solution)/shard_map/ppermute | solution.py:419
  29.0 11.9 %collective-permute-start.4 = (bf16[4,3,128,128]{3,2,1,0:T(8,128)(2,1)}, bf16[4,3,128,128]{3,2,1,0:T(8,128)(2,1)}, u32[]{:S(2)}, u32[]{:S(2)}) collective-permute-start(bf16[4,3,128,128]{3,2,1,0:T(8,128)(2,1)} %fusion.7), channel_id=1, source_target_pairs={{0,8},{4,12},{1,9},{5,13},{2,10},{6,14},{3,11},{7,15}} | collective-permute-start | bytes 1179656 | tf_op jit(solution)/shard_map/ppermute | solution.py:419
  30.3 13.0 %collective-permute-start = (bf16[4,3,128,128]{3,2,1,0:T(8,128)(2,1)S(1)}, bf16[4,3,128,128]{3,2,1,0:T(8,128)(2,1)S(1)}, u32[]{:S(2)}, u32[]{:S(2)}) collective-permute-start(bf16[4,3,128,128]{3,2,1,0:T(8,128)(2,1)S(1)} %get-tuple-element.52), channel_id=1, source_target_pairs={{0,4},{4,0},{8,12},{12,8},{16,20},{20,16},{24,28},{28,24},{1,5},{5... | collective-permute-start | bytes 1179656 | tf_op jit(solution)/shard_map/ppermute | solution.py:392
  30.8 25.1 %copy-start.1 = (bf16[8,384,384]{2,1,0:T(8,128)(2,1)S(1)}, bf16[8,384,384]{2,1,0:T(8,128)(2,1)}, u32[]{:S(2)}) copy-start(bf16[8,384,384]{2,1,0:T(8,128)(2,1)} %copy-done) | copy-start | bytes 7077892
  30.8 25.1 %copy-start.3 = (bf16[8,384,384]{2,1,0:T(8,128)(2,1)S(1)}, bf16[8,384,384]{2,1,0:T(8,128)(2,1)}, u32[]{:S(2)}) copy-start(bf16[8,384,384]{2,1,0:T(8,128)(2,1)} %copy-done.2) | copy-start | bytes 7077892
  30.8 25.1 %copy-start.5 = (bf16[8,384,384]{2,1,0:T(8,128)(2,1)S(1)}, bf16[8,384,384]{2,1,0:T(8,128)(2,1)}, u32[]{:S(2)}) copy-start(bf16[8,384,384]{2,1,0:T(8,128)(2,1)} %copy-done.4) | copy-start | bytes 7077892
  34.0 10.7 %collective-permute-start.8 = (bf16[4,2,128,128]{3,2,1,0:T(8,128)(2,1)S(1)}, bf16[4,2,128,128]{3,2,1,0:T(8,128)(2,1)S(1)}, u32[]{:S(2)}, u32[]{:S(2)}) collective-permute-start(bf16[4,2,128,128]{3,2,1,0:T(8,128)(2,1)S(1)} %add_convert_fusion.4), channel_id=1, source_target_pairs={{16,24},{20,28},{17,25},{21,29},{18,26},{22,30},{19,27},{23,31}} | collective-permute-start | bytes 786440 | tf_op jit(solution)/shard_map/ppermute | solution.py:419
  42.0 7.8 %collective-permute-start.7 = (bf16[4,3,128,128]{3,2,1,0:T(8,128)(2,1)S(1)}, bf16[4,3,128,128]{3,2,1,0:T(8,128)(2,1)S(1)}, u32[]{:S(2)}, u32[]{:S(2)}) collective-permute-start(bf16[4,3,128,128]{3,2,1,0:T(8,128)(2,1)S(1)} %add_convert_fusion.3), channel_id=1, source_target_pairs={{8,16},{12,20},{9,17},{13,21},{10,18},{14,22},{11,19},{15,23}} | collective-permute-start | bytes 1179656 | tf_op jit(solution)/shard_map/ppermute | solution.py:419
  43.4 10.6 %collective-permute-start.6 = (bf16[4,3,128,128]{3,2,1,0:T(8,128)(2,1)S(1)}, bf16[4,3,128,128]{3,2,1,0:T(8,128)(2,1)S(1)}, u32[]{:S(2)}, u32[]{:S(2)}) collective-permute-start(bf16[4,3,128,128]{3,2,1,0:T(8,128)(2,1)S(1)} %fusion.6), channel_id=1, source_target_pairs={{0,8},{4,12},{1,9},{5,13},{2,10},{6,14},{3,11},{7,15}} | collective-permute-start | bytes 1179656 | tf_op jit(solution)/shard_map/ppermute | solution.py:419
  46.1 9.8 %collective-permute-start.11 = (bf16[4,2,128,128]{3,2,1,0:T(8,128)(2,1)S(1)}, bf16[4,2,128,128]{3,2,1,0:T(8,128)(2,1)S(1)}, u32[]{:S(2)}, u32[]{:S(2)}) collective-permute-start(bf16[4,2,128,128]{3,2,1,0:T(8,128)(2,1)S(1)} %get-tuple-element.102), channel_id=1, source_target_pairs={{0,4},{4,0},{8,12},{12,8},{16,20},{20,16},{24,28},{28,24},{1,5},{5... | collective-permute-start | bytes 786440 | tf_op jit(solution)/shard_map/ppermute | solution.py:419
  50.0 10.5 %collective-permute-start.10 = (bf16[4,3,128,128]{3,2,1,0:T(8,128)(2,1)S(1)}, bf16[4,3,128,128]{3,2,1,0:T(8,128)(2,1)S(1)}, u32[]{:S(2)}, u32[]{:S(2)}) collective-permute-start(bf16[4,3,128,128]{3,2,1,0:T(8,128)(2,1)S(1)} %add_convert_fusion.1), channel_id=1, source_target_pairs={{16,24},{20,28},{17,25},{21,29},{18,26},{22,30},{19,27},{23,31}} | collective-permute-start | bytes 1179656 | tf_op jit(solution)/shard_map/ppermute | solution.py:419
  54.2 7.7 %collective-permute-start.9 = (bf16[4,3,128,128]{3,2,1,0:T(8,128)(2,1)S(1)}, bf16[4,3,128,128]{3,2,1,0:T(8,128)(2,1)S(1)}, u32[]{:S(2)}, u32[]{:S(2)}) collective-permute-start(bf16[4,3,128,128]{3,2,1,0:T(8,128)(2,1)S(1)} %add_convert_fusion.2), channel_id=1, source_target_pairs={{8,16},{12,20},{9,17},{13,21},{10,18},{14,22},{11,19},{15,23}} | collective-permute-start | bytes 1179656 | tf_op jit(solution)/shard_map/ppermute | solution.py:419
  62.0 5.2 %collective-permute-start.12 = (bf16[4,3,128,128]{3,2,1,0:T(8,128)(2,1)S(1)}, bf16[4,3,128,128]{3,2,1,0:T(8,128)(2,1)S(1)}, u32[]{:S(2)}, u32[]{:S(2)}) collective-permute-start(bf16[4,3,128,128]{3,2,1,0:T(8,128)(2,1)S(1)} %add_convert_fusion), channel_id=1, source_target_pairs={{16,24},{20,28},{17,25},{21,29},{18,26},{22,30},{19,27},{23,31}} | collective-permute-start | bytes 1179656 | tf_op jit(solution)/shard_map/ppermute | solution.py:419
  62.7 17.9 %collective-permute-start.29 = (bf16[384,256]{1,0:T(8,128)(2,1)S(1)}, bf16[384,256]{1,0:T(8,128)(2,1)S(1)}, u32[]{:S(2)}, u32[]{:S(2)}) collective-permute-start(bf16[384,256]{1,0:T(8,128)(2,1)S(1)} %get-tuple-element.87), channel_id=1, source_target_pairs={{0,16},{4,20},{8,24},{12,28},{16,0},{20,4},{24,8},{28,12},{1,17},{... | collective-permute-start | bytes 589832 | tf_op jit(solution)/shard_map/ppermute | solution.py:445
  64.4 20.6 %collective-permute-start.30 = (bf16[384,256]{1,0:T(8,128)(2,1)S(1)}, bf16[384,256]{1,0:T(8,128)(2,1)S(1)}, u32[]{:S(2)}, u32[]{:S(2)}) collective-permute-start(bf16[384,256]{1,0:T(8,128)(2,1)S(1)} %get-tuple-element.88), channel_id=1, source_target_pairs={{0,20},{4,16},{8,28},{12,24},{16,4},{20,0},{24,12},{28,8},{1,21},{... | collective-permute-start | bytes 589832 | tf_op jit(solution)/shard_map/ppermute | solution.py:445
  65.7 19.4 %collective-permute-start.21 = (bf16[4,3,128,128]{3,2,1,0:T(8,128)(2,1)S(1)}, bf16[4,3,128,128]{3,2,1,0:T(8,128)(2,1)S(1)}, u32[]{:S(2)}, u32[]{:S(2)}) collective-permute-start(bf16[4,3,128,128]{3,2,1,0:T(8,128)(2,1)S(1)} %get-tuple-element.68), channel_id=1, source_target_pairs={{0,4},{4,0},{8,12},{12,8},{16,20},{20,16},{24,28},{28,24},{1,5},{5... | collective-permute-start | bytes 1179656 | tf_op jit(solution)/shard_map/ppermute | solution.py:419
  67.5 48.2 %collective-permute-start.13 = (bf16[4,3,128,128]{3,2,1,0:T(8,128)(2,1)S(1)}, bf16[4,3,128,128]{3,2,1,0:T(8,128)(2,1)S(1)}, u32[]{:S(2)}, u32[]{:S(2)}) collective-permute-start(bf16[4,3,128,128]{3,2,1,0:T(8,128)(2,1)S(1)} %get-tuple-element.99), channel_id=1, source_target_pairs={{0,4},{4,0},{8,12},{12,8},{16,20},{20,16},{24,28},{28,24},{1,5},{5... | collective-permute-start | bytes 1179656 | tf_op jit(solution)/shard_map/ppermute | solution.py:419
  68.1 26.4 %collective-permute-start.31 = (bf16[384,256]{1,0:T(8,128)(2,1)S(1)}, bf16[384,256]{1,0:T(8,128)(2,1)S(1)}, u32[]{:S(2)}, u32[]{:S(2)}) collective-permute-start(bf16[384,256]{1,0:T(8,128)(2,1)S(1)} %get-tuple-element.89), channel_id=1, source_target_pairs={{0,8},{4,12},{8,16},{12,20},{16,24},{20,28},{24,0},{28,4},{1,9},{5... | collective-permute-start | bytes 589832 | tf_op jit(solution)/shard_map/ppermute | solution.py:445
  80.6 26.3 %collective-permute-start.32 = (bf16[384,256]{1,0:T(8,128)(2,1)S(1)}, bf16[384,256]{1,0:T(8,128)(2,1)S(1)}, u32[]{:S(2)}, u32[]{:S(2)}) collective-permute-start(bf16[384,256]{1,0:T(8,128)(2,1)S(1)} %get-tuple-element.90), channel_id=1, source_target_pairs={{0,12},{4,8},{8,20},{12,16},{16,28},{20,24},{24,4},{28,0},{1,13},{... | collective-permute-start | bytes 589832 | tf_op jit(solution)/shard_map/ppermute | solution.py:445
  85.0 22.0 %collective-permute-start.33 = (bf16[384,256]{1,0:T(8,128)(2,1)S(1)}, bf16[384,256]{1,0:T(8,128)(2,1)S(1)}, u32[]{:S(2)}, u32[]{:S(2)}) collective-permute-start(bf16[384,256]{1,0:T(8,128)(2,1)S(1)} %get-tuple-element.91), channel_id=1, source_target_pairs={{0,24},{4,28},{8,0},{12,4},{16,8},{20,12},{24,16},{28,20},{1,25},{... | collective-permute-start | bytes 589832 | tf_op jit(solution)/shard_map/ppermute | solution.py:445
  85.0 30.6 %collective-permute-start.34 = (bf16[384,256]{1,0:T(8,128)(2,1)S(1)}, bf16[384,256]{1,0:T(8,128)(2,1)S(1)}, u32[]{:S(2)}, u32[]{:S(2)}) collective-permute-start(bf16[384,256]{1,0:T(8,128)(2,1)S(1)} %get-tuple-element.92), channel_id=1, source_target_pairs={{0,28},{4,24},{8,4},{12,0},{16,12},{20,8},{24,20},{28,16},{1,29},{... | collective-permute-start | bytes 589832 | tf_op jit(solution)/shard_map/ppermute | solution.py:445
  94.5 35.7 %collective-permute-start.22 = (bf16[384,384]{1,0:T(8,128)(2,1)S(1)}, bf16[384,384]{1,0:T(8,128)(2,1)S(1)}, u32[]{:S(2)}, u32[]{:S(2)}) collective-permute-start(bf16[384,384]{1,0:T(8,128)(2,1)S(1)} %get-tuple-element.79), channel_id=1, source_target_pairs={{0,16},{4,20},{8,24},{12,28},{16,0},{20,4},{24,8},{28,12},{1,17},{... | collective-permute-start | bytes 884744 | tf_op jit(solution)/shard_map/ppermute | solution.py:445
  107.0 24.4 %collective-permute-start.23 = (bf16[384,384]{1,0:T(8,128)(2,1)S(1)}, bf16[384,384]{1,0:T(8,128)(2,1)S(1)}, u32[]{:S(2)}, u32[]{:S(2)}) collective-permute-start(bf16[384,384]{1,0:T(8,128)(2,1)S(1)} %get-tuple-element.80), channel_id=1, source_target_pairs={{0,20},{4,16},{8,28},{12,24},{16,4},{20,0},{24,12},{28,8},{1,21},{... | collective-permute-start | bytes 884744 | tf_op jit(solution)/shard_map/ppermute | solution.py:445
  107.0 37.9 %collective-permute-start.24 = (bf16[384,384]{1,0:T(8,128)(2,1)S(1)}, bf16[384,384]{1,0:T(8,128)(2,1)S(1)}, u32[]{:S(2)}, u32[]{:S(2)}) collective-permute-start(bf16[384,384]{1,0:T(8,128)(2,1)S(1)} %get-tuple-element.81), channel_id=1, source_target_pairs={{0,8},{4,12},{8,16},{12,20},{16,24},{20,28},{24,0},{28,4},{1,9},{5... | collective-permute-start | bytes 884744 | tf_op jit(solution)/shard_map/ppermute | solution.py:445
  115.7 45.1 %collective-permute-start.25 = (bf16[384,384]{1,0:T(8,128)(2,1)S(1)}, bf16[384,384]{1,0:T(8,128)(2,1)S(1)}, u32[]{:S(2)}, u32[]{:S(2)}) collective-permute-start(bf16[384,384]{1,0:T(8,128)(2,1)S(1)} %get-tuple-element.82), channel_id=1, source_target_pairs={{0,12},{4,8},{8,20},{12,16},{16,28},{20,24},{24,4},{28,0},{1,13},{... | collective-permute-start | bytes 884744 | tf_op jit(solution)/shard_map/ppermute | solution.py:445
  115.7 11.2 %collective-permute-start.35 = (bf16[384,256]{1,0:T(8,128)(2,1)S(1)}, bf16[384,256]{1,0:T(8,128)(2,1)S(1)}, u32[]{:S(2)}, u32[]{:S(2)}) collective-permute-start(bf16[384,256]{1,0:T(8,128)(2,1)S(1)} %get-tuple-element.67), channel_id=1, source_target_pairs={{0,4},{4,0},{8,12},{12,8},{16,20},{20,16},{24,28},{28,24},{1,5},{5... | collective-permute-start | bytes 589832 | tf_op jit(solution)/shard_map/ppermute | solution.py:445
  126.9 33.9 %collective-permute-start.26 = (bf16[384,384]{1,0:T(8,128)(2,1)S(1)}, bf16[384,384]{1,0:T(8,128)(2,1)S(1)}, u32[]{:S(2)}, u32[]{:S(2)}) collective-permute-start(bf16[384,384]{1,0:T(8,128)(2,1)S(1)} %get-tuple-element.83), channel_id=1, source_target_pairs={{0,24},{4,28},{8,0},{12,4},{16,8},{20,12},{24,16},{28,20},{1,25},{... | collective-permute-start | bytes 884744 | tf_op jit(solution)/shard_map/ppermute | solution.py:445
  130.2 35.4 %collective-permute-start.27 = (bf16[384,384]{1,0:T(8,128)(2,1)S(1)}, bf16[384,384]{1,0:T(8,128)(2,1)S(1)}, u32[]{:S(2)}, u32[]{:S(2)}) collective-permute-start(bf16[384,384]{1,0:T(8,128)(2,1)S(1)} %get-tuple-element.84), channel_id=1, source_target_pairs={{0,28},{4,24},{8,4},{12,0},{16,12},{20,8},{24,20},{28,16},{1,29},{... | collective-permute-start | bytes 884744 | tf_op jit(solution)/shard_map/ppermute | solution.py:445
  131.3 34.3 %collective-permute-start.28 = (bf16[384,384]{1,0:T(8,128)(2,1)S(1)}, bf16[384,384]{1,0:T(8,128)(2,1)S(1)}, u32[]{:S(2)}, u32[]{:S(2)}) collective-permute-start(bf16[384,384]{1,0:T(8,128)(2,1)S(1)} %get-tuple-element.85), channel_id=1, source_target_pairs={{0,4},{4,0},{8,12},{12,8},{16,20},{20,16},{24,28},{28,24},{1,5},{5... | collective-permute-start | bytes 884744 | tf_op jit(solution)/shard_map/ppermute | solution.py:445
  144.8 30.4 %collective-permute-start.17 = (bf16[384,384]{1,0:T(8,128)(2,1)S(1)}, bf16[384,384]{1,0:T(8,128)(2,1)S(1)}, u32[]{:S(2)}, u32[]{:S(2)}) collective-permute-start(bf16[384,384]{1,0:T(8,128)(2,1)S(1)} %get-tuple-element.74), channel_id=1, source_target_pairs={{0,16},{4,20},{8,24},{12,28},{16,0},{20,4},{24,8},{28,12},{1,17},{... | collective-permute-start | bytes 884744 | tf_op jit(solution)/shard_map/ppermute | solution.py:445
  160.8 25.2 %collective-permute-start.18 = (bf16[384,384]{1,0:T(8,128)(2,1)S(1)}, bf16[384,384]{1,0:T(8,128)(2,1)S(1)}, u32[]{:S(2)}, u32[]{:S(2)}) collective-permute-start(bf16[384,384]{1,0:T(8,128)(2,1)S(1)} %get-tuple-element.75), channel_id=1, source_target_pairs={{0,20},{4,16},{8,28},{12,24},{16,4},{20,0},{24,12},{28,8},{1,21},{... | collective-permute-start | bytes 884744 | tf_op jit(solution)/shard_map/ppermute | solution.py:445
  160.8 38.0 %collective-permute-start.14 = (bf16[384,384]{1,0:T(8,128)(2,1)S(1)}, bf16[384,384]{1,0:T(8,128)(2,1)S(1)}, u32[]{:S(2)}, u32[]{:S(2)}) collective-permute-start(bf16[384,384]{1,0:T(8,128)(2,1)S(1)} %get-tuple-element.70), channel_id=1, source_target_pairs={{0,24},{4,28},{8,0},{12,4},{16,8},{20,12},{24,16},{28,20},{1,25},{... | collective-permute-start | bytes 884744 | tf_op jit(solution)/shard_map/ppermute | solution.py:445
  165.7 26.8 %collective-permute-start.19 = (bf16[384,384]{1,0:T(8,128)(2,1)S(1)}, bf16[384,384]{1,0:T(8,128)(2,1)S(1)}, u32[]{:S(2)}, u32[]{:S(2)}) collective-permute-start(bf16[384,384]{1,0:T(8,128)(2,1)S(1)} %get-tuple-element.76), channel_id=1, source_target_pairs={{0,8},{4,12},{8,16},{12,20},{16,24},{20,28},{24,0},{28,4},{1,9},{5... | collective-permute-start | bytes 884744 | tf_op jit(solution)/shard_map/ppermute | solution.py:445
  165.7 31.0 %collective-permute-start.20 = (bf16[384,384]{1,0:T(8,128)(2,1)S(1)}, bf16[384,384]{1,0:T(8,128)(2,1)S(1)}, u32[]{:S(2)}, u32[]{:S(2)}) collective-permute-start(bf16[384,384]{1,0:T(8,128)(2,1)S(1)} %get-tuple-element.77), channel_id=1, source_target_pairs={{0,12},{4,8},{8,20},{12,16},{16,28},{20,24},{24,4},{28,0},{1,13},{... | collective-permute-start | bytes 884744 | tf_op jit(solution)/shard_map/ppermute | solution.py:445
  175.2 23.7 %collective-permute-start.15 = (bf16[384,384]{1,0:T(8,128)(2,1)S(1)}, bf16[384,384]{1,0:T(8,128)(2,1)S(1)}, u32[]{:S(2)}, u32[]{:S(2)}) collective-permute-start(bf16[384,384]{1,0:T(8,128)(2,1)S(1)} %get-tuple-element.71), channel_id=1, source_target_pairs={{0,28},{4,24},{8,4},{12,0},{16,12},{20,8},{24,20},{28,16},{1,29},{... | collective-permute-start | bytes 884744 | tf_op jit(solution)/shard_map/ppermute | solution.py:445
  186.0 12.9 %collective-permute-start.16 = (bf16[384,384]{1,0:T(8,128)(2,1)S(1)}, bf16[384,384]{1,0:T(8,128)(2,1)S(1)}, u32[]{:S(2)}, u32[]{:S(2)}) collective-permute-start(bf16[384,384]{1,0:T(8,128)(2,1)S(1)} %get-tuple-element.72), channel_id=1, source_target_pairs={{0,4},{4,0},{8,12},{12,8},{16,20},{20,16},{24,28},{28,24},{1,5},{5... | collective-permute-start | bytes 884744 | tf_op jit(solution)/shard_map/ppermute | solution.py:445

commit v12 on v11

--- a/solution.py
+++ b/solution.py
@@ -434,7 +434,9 @@
                 states.append(self.get("states", part))
                 spans.append((first - start, last - first))
         early = c == 0 and len(self.groups) > 1
-        arrays = self.get("group", 1)[2] if early else self.arrays
+        arrays = self.arrays
+        if early:
+            arrays = [pltpu.with_memory_space_constraint(x, pltpu.VMEM) for x in self.get("group", 1)[2]]
         return attend(place, *arrays, self.gain, states, tuple(spans), (0, *self.shifts), self.n, low, early)
 
     def sent(self, c, k):

time: 204 us -> 204 us (level)
  no operation moved by 1% of the time
where the time goes in v12:
time: 204 us; the launch traced here: 201 us
  waiting for transfers between devices  91.4 us (45%)
  starting transfers between devices  57.1 us (28%)
  Pallas kernels  39.5 us (19%)
  other arithmetic  8.26 us (4%)
  local copies, waits for them, and re-layouts  4.32 us (2%)
    ppermute x21, waiting for transfers between devices, sent(): lax.ppermute(self.hold(self.get('mixed', c)[k], 'sent', c, k), 'seq', pairs)  69.4 us
    ppermute x21, starting transfers between devices, sent(): lax.ppermute(self.hold(self.get('mixed', c)[k], 'sent', c, k), 'seq', pairs)  40.7 us
    ppermute x12, waiting for transfers between devices, prefix(): return lax.ppermute(self.get('message', c, s), 'seq', pairs)  22 us
    pallas_call x3, Pallas kernels, attend(): pl.pallas_call(functools.partial(attend_body, n, spans, order, early), in...  21.1 us
    ppermute x12, starting transfers between devices, prefix(): return lax.ppermute(self.get('message', c, s), 'seq', pairs)  13.7 us
    pallas_call x2, Pallas kernels, local_states(): pl.pallas_call(functools.partial(local_body, n, widths, swaps, ahead), in...  9.41 us
    pallas_call x4, Pallas kernels, put(): pl.pallas_call(functools.partial(put_body, n, order), in_specs=[pl.BlockS...  9.01 us
    convert_element_type x10, other arithmetic, message(): return self.hold(value.astype(jnp.bfloat16), 'message', c, s)  5.53 us
  transfers between devices with their start and end apart: 36, of which 14 were waited for; matrix products, arithmetic and copies ran while one was open for 4% of the time, Pallas kernels for 17%

profile of v12, /device:TPU:8, one launch (start us, length us, event | category | flops | bytes accessed | tf_op | source)
XLA Modules:
  0.0 200.9 jit_solution(10313830990281287931)
XLA Ops:
  0.1 3.4 %local.3 = (f32[4,2,128,128]{3,2,1,0:T(8,128)S(1)}, bf16[4,2,128,128]{3,2,1,0:T(8,128)(2,1)S(1)}) custom-call(s32[2]{0:T(128)S(1)} %pad_add_fusion.place, s32[1]{0:T(128)} %constant.38.clone.1.low, bf16[384,8192]{1,0:T(8,128)(2,1)} %keys.7, bf16[384,8192]{1,0:T(8,128)(2,1)} %values.7, bf16[384,8192]{1,0:T(8,128)(2,1)} %queries.7), custom_call_target="tpu_custom_call" | custom-call | flops 201326592 | bytes 3145728 | tf_op jit(solution)/shard_map/local/pallas_call | solution.py:131
  3.5 1.6 collective-permute-start.2
  5.0 6.0 %local.2 = (f32[4,3,128,128]{3,2,1,0:T(8,128)S(1)}, f32[4,3,128,128]{3,2,1,0:T(8,128)S(1)}, bf16[4,3,128,128]{3,2,1,0:T(8,128)(2,1)S(1)}, bf16[4,3,128,128]{3,2,...) custom-call(s32[2]{0:T(128)S(1)} %pad_add_fusion.place, ...), custom_call_target="tpu_custom_call" | custom-call | flops 603979776 | bytes 9437184 | tf_op jit(solution)/shard_map/local/pallas_call | solution.py:131
  11.1 1.4 copy-done
  12.5 1.4 copy-done.2
  13.9 1.5 copy-done.4
  15.5 1.3 collective-permute-start.3
  17.3 7.8 %collective-permute-done.3 = bf16[4,2,128,128]{3,2,1,0:T(8,128)(2,1)S(1)} collective-permute-done((bf16[4,2,128,128]{3,2,1,0:T(8,128)(2,1)S(1)}, bf16[4,2,128,128]{3,2,1,0:T(8,128)(2,1)S(1)}, u32[]{:S(2)}, u32[]{:S(2)}) %collective-permute-start.3) | collective-permute-done | bytes 262176 | tf_op jit(solution)/shard_map/ppermute | solution.py:419
  26.0 2.1 %collective-permute-start.5 = (bf16[4,2,128,128]{3,2,1,0:T(8,128)(2,1)}, bf16[4,2,128,128]{3,2,1,0:T(8,128)(2,1)}, u32[]{:S(2)}, u32[]{:S(2)}) collective-permute-start(bf16[4,2,128,128]{3,2,1,0:T(8,128)(2,1)} %add_convert_fusion.5), channel_id=1, source_target_pairs={{8,16},{12,20},{9,17},{13,21},{10,18},{14,22},{11,19},{15,23}} | collective-permute-start | bytes 786440 | tf_op jit(solution)/shard_map/ppermute | solution.py:419
  29.0 1.3 collective-permute-start.4
  30.8 1.5 collective-permute-done.5
  32.3 1.7 add_convert_fusion.4
  34.7 6.1 %collective-permute-done.4 = bf16[4,3,128,128]{3,2,1,0:T(8,128)(2,1)} collective-permute-done((bf16[4,3,128,128]{3,2,1,0:T(8,128)(2,1)}, bf16[4,3,128,128]{3,2,1,0:T(8,128)(2,1)}, u32[]{:S(2)}, u32[]{:S(2)}) %collective-permute-start.4) | collective-permute-done | bytes 393248 | tf_op jit(solution)/shard_map/ppermute | solution.py:419
  40.8 1.1 add_convert_fusion.3
  42.0 1.3 collective-permute-start.7
  43.4 1.3 collective-permute-start.6
  44.7 1.3 fusion.5
  46.6 3.2 %collective-permute-done.7 = bf16[4,3,128,128]{3,2,1,0:T(8,128)(2,1)S(1)} collective-permute-done((bf16[4,3,128,128]{3,2,1,0:T(8,128)(2,1)S(1)}, bf16[4,3,128,128]{3,2,1,0:T(8,128)(2,1)S(1)}, u32[]{:S(2)}, u32[]{:S(2)}) %collective-permute-start.7) | collective-permute-done | bytes 393248 | tf_op jit(solution)/shard_map/ppermute | solution.py:419
  50.6 3.4 %collective-permute-done.6 = bf16[4,3,128,128]{3,2,1,0:T(8,128)(2,1)S(1)} collective-permute-done((bf16[4,3,128,128]{3,2,1,0:T(8,128)(2,1)S(1)}, bf16[4,3,128,128]{3,2,1,0:T(8,128)(2,1)S(1)}, u32[]{:S(2)}, u32[]{:S(2)}) %collective-permute-start.6) | collective-permute-done | bytes 393248 | tf_op jit(solution)/shard_map/ppermute | solution.py:419
  54.2 1.6 collective-permute-start.9
  55.9 4.5 %attend.3 = (bf16[384,256]{1,0:T(8,128)(2,1)S(1)}, bf16[384,256]{1,0:T(8,128)(2,1)S(1)}, bf16[384,256]{1,0:T(8,128)(2,1)S(1)}, bf16[384,256]{1,0:T(8,128)(2,1)S(...) custom-call(s32[2]{0:T(128)S(1)} %pad_add_fusion.place, ...), custom_call_target="tpu_custom_call" | custom-call | flops 1409286144 | bytes 6291456 | tf_op jit(solution)/shard_map/attend/pallas_call | solution.py:261
  60.5 1.3 fusion.1
  62.7 1.7 collective-permute-start.29
  64.4 1.3 collective-permute-start.30
  65.7 1.5 collective-permute-start.21
  68.1 12.5 %collective-permute-start.31 = (bf16[384,256]{1,0:T(8,128)(2,1)S(1)}, bf16[384,256]{1,0:T(8,128)(2,1)S(1)}, u32[]{:S(2)}, u32[]{:S(2)}) collective-permute-start(bf16[384,256]{1,0:T(8,128)(2,1)S(1)} %get-tuple-element.89), channel_id=1, source_target_pairs={{0,8},{4,12},{8,16},{12,20},{16,24},{20,28},{24,0},{28,4},{1,9},{5... | collective-permute-start | bytes 589832 | tf_op jit(solution)/shard_map/ppermute | solution.py:447
  80.6 4.4 %collective-permute-start.32 = (bf16[384,256]{1,0:T(8,128)(2,1)S(1)}, bf16[384,256]{1,0:T(8,128)(2,1)S(1)}, u32[]{:S(2)}, u32[]{:S(2)}) collective-permute-start(bf16[384,256]{1,0:T(8,128)(2,1)S(1)} %get-tuple-element.90), channel_id=1, source_target_pairs={{0,12},{4,8},{8,20},{12,16},{16,28},{20,24},{24,4},{28,0},{1,13},{... | collective-permute-start | bytes 589832 | tf_op jit(solution)/shard_map/ppermute | solution.py:447
  85.0 1.2 collective-permute-start.34
  86.2 8.3 %attend.5 = (bf16[384,384]{1,0:T(8,128)(2,1)S(1)}, bf16[384,384]{1,0:T(8,128)(2,1)S(1)}, bf16[384,384]{1,0:T(8,128)(2,1)S(1)}, bf16[384,384]{1,0:T(8,128)(2,1)S(...) custom-call(s32[2]{0:T(128)S(1)} %pad_add_fusion.place, ...), custom_call_target="tpu_custom_call" | custom-call | flops 2113929216 | bytes 9437184 | tf_op jit(solution)/shard_map/attend/pallas_call | solution.py:261
  94.5 1.8 collective-permute-start.22
  96.3 10.6 %collective-permute-done.32.refs_4_ = bf16[384,256]{1,0:T(8,128)(2,1)S(1)} collective-permute-done((bf16[384,256]{1,0:T(8,128)(2,1)S(1)}, bf16[384,256]{1,0:T(8,128)(2,1)S(1)}, u32[]{:S(2)}, u32[]{:S(2)}) %collective-permute-start.32) | collective-permute-done | bytes 196640 | tf_op jit(solution)/shard_map/ppermute | solution.py:447
  107.0 2.6 %collective-permute-start.24 = (bf16[384,384]{1,0:T(8,128)(2,1)S(1)}, bf16[384,384]{1,0:T(8,128)(2,1)S(1)}, u32[]{:S(2)}, u32[]{:S(2)}) collective-permute-start(bf16[384,384]{1,0:T(8,128)(2,1)S(1)} %get-tuple-element.81), channel_id=1, source_target_pairs={{0,8},{4,12},{8,16},{12,20},{16,24},{20,28},{24,0},{28,4},{1,9},{5... | collective-permute-start | bytes 884744 | tf_op jit(solution)/shard_map/ppermute | solution.py:447
  109.6 6.1 %collective-permute-done.34.refs_6_ = bf16[384,256]{1,0:T(8,128)(2,1)S(1)} collective-permute-done((bf16[384,256]{1,0:T(8,128)(2,1)S(1)}, bf16[384,256]{1,0:T(8,128)(2,1)S(1)}, u32[]{:S(2)}, u32[]{:S(2)}) %collective-permute-start.34) | collective-permute-done | bytes 196640 | tf_op jit(solution)/shard_map/ppermute | solution.py:447
  115.7 2.9 %collective-permute-start.35 = (bf16[384,256]{1,0:T(8,128)(2,1)S(1)}, bf16[384,256]{1,0:T(8,128)(2,1)S(1)}, u32[]{:S(2)}, u32[]{:S(2)}) collective-permute-start(bf16[384,256]{1,0:T(8,128)(2,1)S(1)} %get-tuple-element.67), channel_id=1, source_target_pairs={{0,4},{4,0},{8,12},{12,8},{16,20},{20,16},{24,28},{28,24},{1,5},{5... | collective-permute-start | bytes 589832 | tf_op jit(solution)/shard_map/ppermute | solution.py:447
  118.6 8.3 %attend.4 = (bf16[384,384]{1,0:T(8,128)(2,1)S(1)}, bf16[384,384]{1,0:T(8,128)(2,1)S(1)}, bf16[384,384]{1,0:T(8,128)(2,1)S(1)}, bf16[384,384]{1,0:T(8,128)(2,1)S(...) custom-call(s32[2]{0:T(128)S(1)} %pad_add_fusion.place, ...), custom_call_target="tpu_custom_call" | custom-call | flops 2113929216 | bytes 9437184 | tf_op jit(solution)/shard_map/attend/pallas_call | solution.py:261
  126.9 3.3 %collective-permute-start.26 = (bf16[384,384]{1,0:T(8,128)(2,1)S(1)}, bf16[384,384]{1,0:T(8,128)(2,1)S(1)}, u32[]{:S(2)}, u32[]{:S(2)}) collective-permute-start(bf16[384,384]{1,0:T(8,128)(2,1)S(1)} %get-tuple-element.83), channel_id=1, source_target_pairs={{0,24},{4,28},{8,0},{12,4},{16,8},{20,12},{24,16},{28,20},{1,25},{... | collective-permute-start | bytes 884744 | tf_op jit(solution)/shard_map/ppermute | solution.py:447
  131.3 1.8 collective-permute-start.28
  133.1 11.7 %collective-permute-done.24.refs_3_ = bf16[384,384]{1,0:T(8,128)(2,1)S(1)} collective-permute-done((bf16[384,384]{1,0:T(8,128)(2,1)S(1)}, bf16[384,384]{1,0:T(8,128)(2,1)S(1)}, u32[]{:S(2)}, u32[]{:S(2)}) %collective-permute-start.24) | collective-permute-done | bytes 294944 | tf_op jit(solution)/shard_map/ppermute | solution.py:447
  144.8 16.0 %collective-permute-done.25.refs_4_ = bf16[384,384]{1,0:T(8,128)(2,1)S(1)} collective-permute-done((bf16[384,384]{1,0:T(8,128)(2,1)S(1)}, bf16[384,384]{1,0:T(8,128)(2,1)S(1)}, u32[]{:S(2)}, u32[]{:S(2)}) %collective-permute-start.25) | collective-permute-done | bytes 294944 | tf_op jit(solution)/shard_map/ppermute | solution.py:447
  160.8 4.8 %collective-permute-start.14 = (bf16[384,384]{1,0:T(8,128)(2,1)S(1)}, bf16[384,384]{1,0:T(8,128)(2,1)S(1)}, u32[]{:S(2)}, u32[]{:S(2)}) collective-permute-start(bf16[384,384]{1,0:T(8,128)(2,1)S(1)} %get-tuple-element.70), channel_id=1, source_target_pairs={{0,24},{4,28},{8,0},{12,4},{16,8},{20,12},{24,16},{28,20},{1,25},{... | collective-permute-start | bytes 884744 | tf_op jit(solution)/shard_map/ppermute | solution.py:447
  166.2 9.0 %collective-permute-done.17.refs_1_ = bf16[384,384]{1,0:T(8,128)(2,1)S(1)} collective-permute-done((bf16[384,384]{1,0:T(8,128)(2,1)S(1)}, bf16[384,384]{1,0:T(8,128)(2,1)S(1)}, u32[]{:S(2)}, u32[]{:S(2)}) %collective-permute-start.17) | collective-permute-done | bytes 294944 | tf_op jit(solution)/shard_map/ppermute | solution.py:447
  175.9 10.1 %collective-permute-done.18.refs_2_ = bf16[384,384]{1,0:T(8,128)(2,1)S(1)} collective-permute-done((bf16[384,384]{1,0:T(8,128)(2,1)S(1)}, bf16[384,384]{1,0:T(8,128)(2,1)S(1)}, u32[]{:S(2)}, u32[]{:S(2)}) %collective-permute-start.18) | collective-permute-done | bytes 294944 | tf_op jit(solution)/shard_map/ppermute | solution.py:447
  186.0 2.3 %put.4 = (bf16[3072,1024]{1,0:T(8,128)(2,1)}, s32[2]{0:T(128)}) custom-call(s32[2]{0:T(128)S(1)} %pad_add_fusion.place, s32[1]{0:T(128)} %constant.38.clone.1.low, bf16[384,256]{1,0:T(8,128)(2,1)S(1)} %get-tuple-element.86.refs_0_, bf16[384,256]{1,0:T(8,128)(2,1)S(1)} %collective-permute-done.29.refs_1_, ...), custom_call_target="tpu_custom_call" | custom-call | tf_op jit(solution)/shard_map/put/pallas_call | solution.py:311
  188.3 2.5 %put.5 = (bf16[3072,1024]{1,0:T(8,128)(2,1)}, s32[2]{0:T(128)}) custom-call(s32[2]{0:T(128)S(1)} %pad_add_fusion.place, s32[1]{0:T(128)} %constant.37.clone.1.low, bf16[384,384]{1,0:T(8,128)(2,1)S(1)} %get-tuple-element.78.refs_0_, bf16[384,384]{1,0:T(8,128)(2,1)S(1)} %collective-permute-done.22.refs_1_, ...), custom_call_target="tpu_custom_call", output_to_operand_aliasing={{0}: (10, {})} | custom-call | tf_op jit(solution)/shard_map/put/pallas_call | solution.py:311
  190.8 1.6 collective-permute-done.19.refs_3_
  192.5 4.2 %collective-permute-done.20.refs_4_ = bf16[384,384]{1,0:T(8,128)(2,1)S(1)} collective-permute-done((bf16[384,384]{1,0:T(8,128)(2,1)S(1)}, bf16[384,384]{1,0:T(8,128)(2,1)S(1)}, u32[]{:S(2)}, u32[]{:S(2)}) %collective-permute-start.20) | collective-permute-done | bytes 294944 | tf_op jit(solution)/shard_map/ppermute | solution.py:447
  196.6 2.2 %put.6 = (bf16[3072,1024]{1,0:T(8,128)(2,1)}, s32[2]{0:T(128)}) custom-call(s32[2]{0:T(128)S(1)} %pad_add_fusion.place, s32[1]{0:T(128)} %constant.36.clone.1.low, bf16[384,384]{1,0:T(8,128)(2,1)S(1)} %get-tuple-element.73.refs_0_, bf16[384,384]{1,0:T(8,128)(2,1)S(1)} %collective-permute-done.17.refs_1_, ...), custom_call_target="tpu_custom_call", output_to_operand_aliasing={{0}: (7, {})} | custom-call | tf_op jit(solution)/shard_map/put/pallas_call | solution.py:311
  198.9 2.0 put.7
  (64 shorter events, 9.6 us)
Async XLA Ops:
  3.5 11.9 %collective-permute-start.2 = (bf16[4,2,128,128]{3,2,1,0:T(8,128)(2,1)S(1)}, bf16[4,2,128,128]{3,2,1,0:T(8,128)(2,1)S(1)}, u32[]{:S(2)}, u32[]{:S(2)}) collective-permute-start(bf16[4,2,128,128]{3,2,1,0:T(8,128)(2,1)S(1)} %get-tuple-element.56), channel_id=1, source_target_pairs={{0,4},{4,0},{8,12},{12,8},{16,20},{20,16},{24,28},{28,24},{1,5},{5... | collective-permute-start | bytes 786440 | tf_op jit(solution)/shard_map/ppermute | solution.py:392
  11.1 1.4 copy-start
  12.5 1.4 copy-start.2
  13.9 1.5 copy-start.4
  15.4 14.9 %copy-start.7 = (bf16[4,2,128,128]{3,2,1,0:T(8,128)(2,1)}, bf16[4,2,128,128]{3,2,1,0:T(8,128)(2,1)S(1)}, u32[]{:S(2)}) copy-start(bf16[4,2,128,128]{3,2,1,0:T(8,128)(2,1)S(1)} %collective-permute-done.2) | copy-start | bytes 786436
  15.5 9.7 %collective-permute-start.3 = (bf16[4,2,128,128]{3,2,1,0:T(8,128)(2,1)S(1)}, bf16[4,2,128,128]{3,2,1,0:T(8,128)(2,1)S(1)}, u32[]{:S(2)}, u32[]{:S(2)}) collective-permute-start(bf16[4,2,128,128]{3,2,1,0:T(8,128)(2,1)S(1)} %fusion.8), channel_id=1, source_target_pairs={{0,8},{4,12},{1,9},{5,13},{2,10},{6,14},{3,11},{7,15}} | collective-permute-start | bytes 786440 | tf_op jit(solution)/shard_map/ppermute | solution.py:419
  16.8 11.3 %collective-permute-start.1 = (bf16[4,3,128,128]{3,2,1,0:T(8,128)(2,1)S(1)}, bf16[4,3,128,128]{3,2,1,0:T(8,128)(2,1)S(1)}, u32[]{:S(2)}, u32[]{:S(2)}) collective-permute-start(bf16[4,3,128,128]{3,2,1,0:T(8,128)(2,1)S(1)} %get-tuple-element.54), channel_id=1, source_target_pairs={{0,4},{4,0},{8,12},{12,8},{16,20},{20,16},{24,28},{28,24},{1,5},{5... | collective-permute-start | bytes 1179656 | tf_op jit(solution)/shard_map/ppermute | solution.py:392
  25.1 3.0 %copy-start.8 = (bf16[4,2,128,128]{3,2,1,0:T(8,128)(2,1)}, bf16[4,2,128,128]{3,2,1,0:T(8,128)(2,1)S(1)}, u32[]{:S(2)}) copy-start(bf16[4,2,128,128]{3,2,1,0:T(8,128)(2,1)S(1)} %collective-permute-done.3) | copy-start | bytes 786436
  26.0 29.9 %copy-start.6 = (f32[8192]{0:T(1024)S(1)}, f32[8192]{0:T(1024)}, u32[]{:S(2)}) copy-start(f32[8192]{0:T(1024)} %param.7) | copy-start | bytes 98308
  26.0 6.4 %collective-permute-start.5 = (bf16[4,2,128,128]{3,2,1,0:T(8,128)(2,1)}, bf16[4,2,128,128]{3,2,1,0:T(8,128)(2,1)}, u32[]{:S(2)}, u32[]{:S(2)}) collective-permute-start(bf16[4,2,128,128]{3,2,1,0:T(8,128)(2,1)} %add_convert_fusion.5), channel_id=1, source_target_pairs={{8,16},{12,20},{9,17},{13,21},{10,18},{14,22},{11,19},{15,23}} | collective-permute-start | bytes 786440 | tf_op jit(solution)/shard_map/ppermute | solution.py:419
  29.0 11.9 %collective-permute-start.4 = (bf16[4,3,128,128]{3,2,1,0:T(8,128)(2,1)}, bf16[4,3,128,128]{3,2,1,0:T(8,128)(2,1)}, u32[]{:S(2)}, u32[]{:S(2)}) collective-permute-start(bf16[4,3,128,128]{3,2,1,0:T(8,128)(2,1)} %fusion.7), channel_id=1, source_target_pairs={{0,8},{4,12},{1,9},{5,13},{2,10},{6,14},{3,11},{7,15}} | collective-permute-start | bytes 1179656 | tf_op jit(solution)/shard_map/ppermute | solution.py:419
  30.3 13.0 %collective-permute-start = (bf16[4,3,128,128]{3,2,1,0:T(8,128)(2,1)S(1)}, bf16[4,3,128,128]{3,2,1,0:T(8,128)(2,1)S(1)}, u32[]{:S(2)}, u32[]{:S(2)}) collective-permute-start(bf16[4,3,128,128]{3,2,1,0:T(8,128)(2,1)S(1)} %get-tuple-element.52), channel_id=1, source_target_pairs={{0,4},{4,0},{8,12},{12,8},{16,20},{20,16},{24,28},{28,24},{1,5},{5... | collective-permute-start | bytes 1179656 | tf_op jit(solution)/shard_map/ppermute | solution.py:392
  30.8 25.1 %copy-start.1 = (bf16[8,384,384]{2,1,0:T(8,128)(2,1)S(1)}, bf16[8,384,384]{2,1,0:T(8,128)(2,1)}, u32[]{:S(2)}) copy-start(bf16[8,384,384]{2,1,0:T(8,128)(2,1)} %copy-done) | copy-start | bytes 7077892
  30.8 25.1 %copy-start.3 = (bf16[8,384,384]{2,1,0:T(8,128)(2,1)S(1)}, bf16[8,384,384]{2,1,0:T(8,128)(2,1)}, u32[]{:S(2)}) copy-start(bf16[8,384,384]{2,1,0:T(8,128)(2,1)} %copy-done.2) | copy-start | bytes 7077892
  30.8 25.1 %copy-start.5 = (bf16[8,384,384]{2,1,0:T(8,128)(2,1)S(1)}, bf16[8,384,384]{2,1,0:T(8,128)(2,1)}, u32[]{:S(2)}) copy-start(bf16[8,384,384]{2,1,0:T(8,128)(2,1)} %copy-done.4) | copy-start | bytes 7077892
  34.0 10.7 %collective-permute-start.8 = (bf16[4,2,128,128]{3,2,1,0:T(8,128)(2,1)S(1)}, bf16[4,2,128,128]{3,2,1,0:T(8,128)(2,1)S(1)}, u32[]{:S(2)}, u32[]{:S(2)}) collective-permute-start(bf16[4,2,128,128]{3,2,1,0:T(8,128)(2,1)S(1)} %add_convert_fusion.4), channel_id=1, source_target_pairs={{16,24},{20,28},{17,25},{21,29},{18,26},{22,30},{19,27},{23,31}} | collective-permute-start | bytes 786440 | tf_op jit(solution)/shard_map/ppermute | solution.py:419
  42.0 7.8 %collective-permute-start.7 = (bf16[4,3,128,128]{3,2,1,0:T(8,128)(2,1)S(1)}, bf16[4,3,128,128]{3,2,1,0:T(8,128)(2,1)S(1)}, u32[]{:S(2)}, u32[]{:S(2)}) collective-permute-start(bf16[4,3,128,128]{3,2,1,0:T(8,128)(2,1)S(1)} %add_convert_fusion.3), channel_id=1, source_target_pairs={{8,16},{12,20},{9,17},{13,21},{10,18},{14,22},{11,19},{15,23}} | collective-permute-start | bytes 1179656 | tf_op jit(solution)/shard_map/ppermute | solution.py:419
  43.4 10.6 %collective-permute-start.6 = (bf16[4,3,128,128]{3,2,1,0:T(8,128)(2,1)S(1)}, bf16[4,3,128,128]{3,2,1,0:T(8,128)(2,1)S(1)}, u32[]{:S(2)}, u32[]{:S(2)}) collective-permute-start(bf16[4,3,128,128]{3,2,1,0:T(8,128)(2,1)S(1)} %fusion.6), channel_id=1, source_target_pairs={{0,8},{4,12},{1,9},{5,13},{2,10},{6,14},{3,11},{7,15}} | collective-permute-start | bytes 1179656 | tf_op jit(solution)/shard_map/ppermute | solution.py:419
  46.1 9.8 %collective-permute-start.11 = (bf16[4,2,128,128]{3,2,1,0:T(8,128)(2,1)S(1)}, bf16[4,2,128,128]{3,2,1,0:T(8,128)(2,1)S(1)}, u32[]{:S(2)}, u32[]{:S(2)}) collective-permute-start(bf16[4,2,128,128]{3,2,1,0:T(8,128)(2,1)S(1)} %get-tuple-element.102), channel_id=1, source_target_pairs={{0,4},{4,0},{8,12},{12,8},{16,20},{20,16},{24,28},{28,24},{1,5},{5... | collective-permute-start | bytes 786440 | tf_op jit(solution)/shard_map/ppermute | solution.py:419
  50.0 10.5 %collective-permute-start.10 = (bf16[4,3,128,128]{3,2,1,0:T(8,128)(2,1)S(1)}, bf16[4,3,128,128]{3,2,1,0:T(8,128)(2,1)S(1)}, u32[]{:S(2)}, u32[]{:S(2)}) collective-permute-start(bf16[4,3,128,128]{3,2,1,0:T(8,128)(2,1)S(1)} %add_convert_fusion.1), channel_id=1, source_target_pairs={{16,24},{20,28},{17,25},{21,29},{18,26},{22,30},{19,27},{23,31}} | collective-permute-start | bytes 1179656 | tf_op jit(solution)/shard_map/ppermute | solution.py:419
  54.2 7.7 %collective-permute-start.9 = (bf16[4,3,128,128]{3,2,1,0:T(8,128)(2,1)S(1)}, bf16[4,3,128,128]{3,2,1,0:T(8,128)(2,1)S(1)}, u32[]{:S(2)}, u32[]{:S(2)}) collective-permute-start(bf16[4,3,128,128]{3,2,1,0:T(8,128)(2,1)S(1)} %add_convert_fusion.2), channel_id=1, source_target_pairs={{8,16},{12,20},{9,17},{13,21},{10,18},{14,22},{11,19},{15,23}} | collective-permute-start | bytes 1179656 | tf_op jit(solution)/shard_map/ppermute | solution.py:419
  62.0 5.2 %collective-permute-start.12 = (bf16[4,3,128,128]{3,2,1,0:T(8,128)(2,1)S(1)}, bf16[4,3,128,128]{3,2,1,0:T(8,128)(2,1)S(1)}, u32[]{:S(2)}, u32[]{:S(2)}) collective-permute-start(bf16[4,3,128,128]{3,2,1,0:T(8,128)(2,1)S(1)} %add_convert_fusion), channel_id=1, source_target_pairs={{16,24},{20,28},{17,25},{21,29},{18,26},{22,30},{19,27},{23,31}} | collective-permute-start | bytes 1179656 | tf_op jit(solution)/shard_map/ppermute | solution.py:419
  62.7 17.9 %collective-permute-start.29 = (bf16[384,256]{1,0:T(8,128)(2,1)S(1)}, bf16[384,256]{1,0:T(8,128)(2,1)S(1)}, u32[]{:S(2)}, u32[]{:S(2)}) collective-permute-start(bf16[384,256]{1,0:T(8,128)(2,1)S(1)} %get-tuple-element.87), channel_id=1, source_target_pairs={{0,16},{4,20},{8,24},{12,28},{16,0},{20,4},{24,8},{28,12},{1,17},{... | collective-permute-start | bytes 589832 | tf_op jit(solution)/shard_map/ppermute | solution.py:447
  64.4 20.6 %collective-permute-start.30 = (bf16[384,256]{1,0:T(8,128)(2,1)S(1)}, bf16[384,256]{1,0:T(8,128)(2,1)S(1)}, u32[]{:S(2)}, u32[]{:S(2)}) collective-permute-start(bf16[384,256]{1,0:T(8,128)(2,1)S(1)} %get-tuple-element.88), channel_id=1, source_target_pairs={{0,20},{4,16},{8,28},{12,24},{16,4},{20,0},{24,12},{28,8},{1,21},{... | collective-permute-start | bytes 589832 | tf_op jit(solution)/shard_map/ppermute | solution.py:447
  65.7 19.4 %collective-permute-start.21 = (bf16[4,3,128,128]{3,2,1,0:T(8,128)(2,1)S(1)}, bf16[4,3,128,128]{3,2,1,0:T(8,128)(2,1)S(1)}, u32[]{:S(2)}, u32[]{:S(2)}) collective-permute-start(bf16[4,3,128,128]{3,2,1,0:T(8,128)(2,1)S(1)} %get-tuple-element.68), channel_id=1, source_target_pairs={{0,4},{4,0},{8,12},{12,8},{16,20},{20,16},{24,28},{28,24},{1,5},{5... | collective-permute-start | bytes 1179656 | tf_op jit(solution)/shard_map/ppermute | solution.py:419
  67.5 48.2 %collective-permute-start.13 = (bf16[4,3,128,128]{3,2,1,0:T(8,128)(2,1)S(1)}, bf16[4,3,128,128]{3,2,1,0:T(8,128)(2,1)S(1)}, u32[]{:S(2)}, u32[]{:S(2)}) collective-permute-start(bf16[4,3,128,128]{3,2,1,0:T(8,128)(2,1)S(1)} %get-tuple-element.99), channel_id=1, source_target_pairs={{0,4},{4,0},{8,12},{12,8},{16,20},{20,16},{24,28},{28,24},{1,5},{5... | collective-permute-start | bytes 1179656 | tf_op jit(solution)/shard_map/ppermute | solution.py:419
  68.1 26.4 %collective-permute-start.31 = (bf16[384,256]{1,0:T(8,128)(2,1)S(1)}, bf16[384,256]{1,0:T(8,128)(2,1)S(1)}, u32[]{:S(2)}, u32[]{:S(2)}) collective-permute-start(bf16[384,256]{1,0:T(8,128)(2,1)S(1)} %get-tuple-element.89), channel_id=1, source_target_pairs={{0,8},{4,12},{8,16},{12,20},{16,24},{20,28},{24,0},{28,4},{1,9},{5... | collective-permute-start | bytes 589832 | tf_op jit(solution)/shard_map/ppermute | solution.py:447
  80.6 26.3 %collective-permute-start.32 = (bf16[384,256]{1,0:T(8,128)(2,1)S(1)}, bf16[384,256]{1,0:T(8,128)(2,1)S(1)}, u32[]{:S(2)}, u32[]{:S(2)}) collective-permute-start(bf16[384,256]{1,0:T(8,128)(2,1)S(1)} %get-tuple-element.90), channel_id=1, source_target_pairs={{0,12},{4,8},{8,20},{12,16},{16,28},{20,24},{24,4},{28,0},{1,13},{... | collective-permute-start | bytes 589832 | tf_op jit(solution)/shard_map/ppermute | solution.py:447
  85.0 22.0 %collective-permute-start.33 = (bf16[384,256]{1,0:T(8,128)(2,1)S(1)}, bf16[384,256]{1,0:T(8,128)(2,1)S(1)}, u32[]{:S(2)}, u32[]{:S(2)}) collective-permute-start(bf16[384,256]{1,0:T(8,128)(2,1)S(1)} %get-tuple-element.91), channel_id=1, source_target_pairs={{0,24},{4,28},{8,0},{12,4},{16,8},{20,12},{24,16},{28,20},{1,25},{... | collective-permute-start | bytes 589832 | tf_op jit(solution)/shard_map/ppermute | solution.py:447
  85.0 30.6 %collective-permute-start.34 = (bf16[384,256]{1,0:T(8,128)(2,1)S(1)}, bf16[384,256]{1,0:T(8,128)(2,1)S(1)}, u32[]{:S(2)}, u32[]{:S(2)}) collective-permute-start(bf16[384,256]{1,0:T(8,128)(2,1)S(1)} %get-tuple-element.92), channel_id=1, source_target_pairs={{0,28},{4,24},{8,4},{12,0},{16,12},{20,8},{24,20},{28,16},{1,29},{... | collective-permute-start | bytes 589832 | tf_op jit(solution)/shard_map/ppermute | solution.py:447
  94.5 35.7 %collective-permute-start.22 = (bf16[384,384]{1,0:T(8,128)(2,1)S(1)}, bf16[384,384]{1,0:T(8,128)(2,1)S(1)}, u32[]{:S(2)}, u32[]{:S(2)}) collective-permute-start(bf16[384,384]{1,0:T(8,128)(2,1)S(1)} %get-tuple-element.79), channel_id=1, source_target_pairs={{0,16},{4,20},{8,24},{12,28},{16,0},{20,4},{24,8},{28,12},{1,17},{... | collective-permute-start | bytes 884744 | tf_op jit(solution)/shard_map/ppermute | solution.py:447
  107.0 24.4 %collective-permute-start.23 = (bf16[384,384]{1,0:T(8,128)(2,1)S(1)}, bf16[384,384]{1,0:T(8,128)(2,1)S(1)}, u32[]{:S(2)}, u32[]{:S(2)}) collective-permute-start(bf16[384,384]{1,0:T(8,128)(2,1)S(1)} %get-tuple-element.80), channel_id=1, source_target_pairs={{0,20},{4,16},{8,28},{12,24},{16,4},{20,0},{24,12},{28,8},{1,21},{... | collective-permute-start | bytes 884744 | tf_op jit(solution)/shard_map/ppermute | solution.py:447
  107.0 37.9 %collective-permute-start.24 = (bf16[384,384]{1,0:T(8,128)(2,1)S(1)}, bf16[384,384]{1,0:T(8,128)(2,1)S(1)}, u32[]{:S(2)}, u32[]{:S(2)}) collective-permute-start(bf16[384,384]{1,0:T(8,128)(2,1)S(1)} %get-tuple-element.81), channel_id=1, source_target_pairs={{0,8},{4,12},{8,16},{12,20},{16,24},{20,28},{24,0},{28,4},{1,9},{5... | collective-permute-start | bytes 884744 | tf_op jit(solution)/shard_map/ppermute | solution.py:447
  115.7 45.1 %collective-permute-start.25 = (bf16[384,384]{1,0:T(8,128)(2,1)S(1)}, bf16[384,384]{1,0:T(8,128)(2,1)S(1)}, u32[]{:S(2)}, u32[]{:S(2)}) collective-permute-start(bf16[384,384]{1,0:T(8,128)(2,1)S(1)} %get-tuple-element.82), channel_id=1, source_target_pairs={{0,12},{4,8},{8,20},{12,16},{16,28},{20,24},{24,4},{28,0},{1,13},{... | collective-permute-start | bytes 884744 | tf_op jit(solution)/shard_map/ppermute | solution.py:447
  115.7 11.2 %collective-permute-start.35 = (bf16[384,256]{1,0:T(8,128)(2,1)S(1)}, bf16[384,256]{1,0:T(8,128)(2,1)S(1)}, u32[]{:S(2)}, u32[]{:S(2)}) collective-permute-start(bf16[384,256]{1,0:T(8,128)(2,1)S(1)} %get-tuple-element.67), channel_id=1, source_target_pairs={{0,4},{4,0},{8,12},{12,8},{16,20},{20,16},{24,28},{28,24},{1,5},{5... | collective-permute-start | bytes 589832 | tf_op jit(solution)/shard_map/ppermute | solution.py:447
  126.9 33.9 %collective-permute-start.26 = (bf16[384,384]{1,0:T(8,128)(2,1)S(1)}, bf16[384,384]{1,0:T(8,128)(2,1)S(1)}, u32[]{:S(2)}, u32[]{:S(2)}) collective-permute-start(bf16[384,384]{1,0:T(8,128)(2,1)S(1)} %get-tuple-element.83), channel_id=1, source_target_pairs={{0,24},{4,28},{8,0},{12,4},{16,8},{20,12},{24,16},{28,20},{1,25},{... | collective-permute-start | bytes 884744 | tf_op jit(solution)/shard_map/ppermute | solution.py:447
  130.2 35.4 %collective-permute-start.27 = (bf16[384,384]{1,0:T(8,128)(2,1)S(1)}, bf16[384,384]{1,0:T(8,128)(2,1)S(1)}, u32[]{:S(2)}, u32[]{:S(2)}) collective-permute-start(bf16[384,384]{1,0:T(8,128)(2,1)S(1)} %get-tuple-element.84), channel_id=1, source_target_pairs={{0,28},{4,24},{8,4},{12,0},{16,12},{20,8},{24,20},{28,16},{1,29},{... | collective-permute-start | bytes 884744 | tf_op jit(solution)/shard_map/ppermute | solution.py:447
  131.3 34.3 %collective-permute-start.28 = (bf16[384,384]{1,0:T(8,128)(2,1)S(1)}, bf16[384,384]{1,0:T(8,128)(2,1)S(1)}, u32[]{:S(2)}, u32[]{:S(2)}) collective-permute-start(bf16[384,384]{1,0:T(8,128)(2,1)S(1)} %get-tuple-element.85), channel_id=1, source_target_pairs={{0,4},{4,0},{8,12},{12,8},{16,20},{20,16},{24,28},{28,24},{1,5},{5... | collective-permute-start | bytes 884744 | tf_op jit(solution)/shard_map/ppermute | solution.py:447
  144.8 30.4 %collective-permute-start.17 = (bf16[384,384]{1,0:T(8,128)(2,1)S(1)}, bf16[384,384]{1,0:T(8,128)(2,1)S(1)}, u32[]{:S(2)}, u32[]{:S(2)}) collective-permute-start(bf16[384,384]{1,0:T(8,128)(2,1)S(1)} %get-tuple-element.74), channel_id=1, source_target_pairs={{0,16},{4,20},{8,24},{12,28},{16,0},{20,4},{24,8},{28,12},{1,17},{... | collective-permute-start | bytes 884744 | tf_op jit(solution)/shard_map/ppermute | solution.py:447
  160.8 25.2 %collective-permute-start.18 = (bf16[384,384]{1,0:T(8,128)(2,1)S(1)}, bf16[384,384]{1,0:T(8,128)(2,1)S(1)}, u32[]{:S(2)}, u32[]{:S(2)}) collective-permute-start(bf16[384,384]{1,0:T(8,128)(2,1)S(1)} %get-tuple-element.75), channel_id=1, source_target_pairs={{0,20},{4,16},{8,28},{12,24},{16,4},{20,0},{24,12},{28,8},{1,21},{... | collective-permute-start | bytes 884744 | tf_op jit(solution)/shard_map/ppermute | solution.py:447
  160.8 38.0 %collective-permute-start.14 = (bf16[384,384]{1,0:T(8,128)(2,1)S(1)}, bf16[384,384]{1,0:T(8,128)(2,1)S(1)}, u32[]{:S(2)}, u32[]{:S(2)}) collective-permute-start(bf16[384,384]{1,0:T(8,128)(2,1)S(1)} %get-tuple-element.70), channel_id=1, source_target_pairs={{0,24},{4,28},{8,0},{12,4},{16,8},{20,12},{24,16},{28,20},{1,25},{... | collective-permute-start | bytes 884744 | tf_op jit(solution)/shard_map/ppermute | solution.py:447
  165.7 26.8 %collective-permute-start.19 = (bf16[384,384]{1,0:T(8,128)(2,1)S(1)}, bf16[384,384]{1,0:T(8,128)(2,1)S(1)}, u32[]{:S(2)}, u32[]{:S(2)}) collective-permute-start(bf16[384,384]{1,0:T(8,128)(2,1)S(1)} %get-tuple-element.76), channel_id=1, source_target_pairs={{0,8},{4,12},{8,16},{12,20},{16,24},{20,28},{24,0},{28,4},{1,9},{5... | collective-permute-start | bytes 884744 | tf_op jit(solution)/shard_map/ppermute | solution.py:447
  165.7 31.0 %collective-permute-start.20 = (bf16[384,384]{1,0:T(8,128)(2,1)S(1)}, bf16[384,384]{1,0:T(8,128)(2,1)S(1)}, u32[]{:S(2)}, u32[]{:S(2)}) collective-permute-start(bf16[384,384]{1,0:T(8,128)(2,1)S(1)} %get-tuple-element.77), channel_id=1, source_target_pairs={{0,12},{4,8},{8,20},{12,16},{16,28},{20,24},{24,4},{28,0},{1,13},{... | collective-permute-start | bytes 884744 | tf_op jit(solution)/shard_map/ppermute | solution.py:447
  175.2 23.7 %collective-permute-start.15 = (bf16[384,384]{1,0:T(8,128)(2,1)S(1)}, bf16[384,384]{1,0:T(8,128)(2,1)S(1)}, u32[]{:S(2)}, u32[]{:S(2)}) collective-permute-start(bf16[384,384]{1,0:T(8,128)(2,1)S(1)} %get-tuple-element.71), channel_id=1, source_target_pairs={{0,28},{4,24},{8,4},{12,0},{16,12},{20,8},{24,20},{28,16},{1,29},{... | collective-permute-start | bytes 884744 | tf_op jit(solution)/shard_map/ppermute | solution.py:447
  186.0 12.9 %collective-permute-start.16 = (bf16[384,384]{1,0:T(8,128)(2,1)S(1)}, bf16[384,384]{1,0:T(8,128)(2,1)S(1)}, u32[]{:S(2)}, u32[]{:S(2)}) collective-permute-start(bf16[384,384]{1,0:T(8,128)(2,1)S(1)} %get-tuple-element.72), channel_id=1, source_target_pairs={{0,4},{4,0},{8,12},{12,8},{16,20},{20,16},{24,28},{28,24},{1,5},{5... | collective-permute-start | bytes 884744 | tf_op jit(solution)/shard_map/ppermute | solution.py:447

commit v13 on v10

--- a/solution.py
+++ b/solution.py
@@ -138,7 +138,7 @@
     qbuf, kbuf, vbuf, sown, soth, gbuf, held, sems, extra = refs[-9:]
     width = sum(size for _, size in spans)
     m, wide = n // 2, width * HEAD
-    together = rows_together(m, width, 12)
+    together = rows_together(m, width, 6)
     here = place[0], place[1], low[0]
     small, start = [(gain, gbuf)], 0
     for chunk, (skip, size) in enumerate(spans):

time: 198 us -> 198 us (level)
  starting transfers between devices: 71.3 us -> 68.6 us
  waiting for transfers between devices: 75.4 us -> 77.7 us
    ppermute x21, starting transfers between devices: 51.9 us -> 49.2 us  [sent(): lax.ppermute(self.hold(self.get('mixed', c)[k], 'sent', c, k), 'seq', pairs)]
    ppermute x21, waiting for transfers between devices: 56.2 us -> 58.5 us  [sent(): lax.ppermute(self.hold(self.get('mixed', c)[k], 'sent', c, k), 'seq', pairs)]
  transfers between devices with their start and end apart: 36 -> 36, of which waited for: 14 -> 13; matrix products, arithmetic and copies ran while one was open for 4% -> 4% of each run, Pallas kernels for 18% -> 18%
where the time goes in v13:
time: 198 us; the launch traced here: 195 us
  waiting for transfers between devices  77.7 us (39%)
  starting transfers between devices  68.6 us (35%)
  Pallas kernels  40.5 us (20%)
  other arithmetic  7.63 us (4%)
    ppermute x21, waiting for transfers between devices, sent(): lax.ppermute(self.hold(self.get('mixed', c)[k], 'sent', c, k), 'seq', pairs)  58.5 us
    ppermute x21, starting transfers between devices, sent(): lax.ppermute(self.hold(self.get('mixed', c)[k], 'sent', c, k), 'seq', pairs)  49.2 us
    pallas_call x3, Pallas kernels, attend(): pl.pallas_call(functools.partial(attend_body, n, spans, order), in_specs=...  23 us
    ppermute x12, waiting for transfers between devices, prefix(): return lax.ppermute(self.get('message', c, s), 'seq', pairs)  17.7 us
    ppermute x12, starting transfers between devices, prefix(): return lax.ppermute(self.get('message', c, s), 'seq', pairs)  14.7 us
    pallas_call x4, Pallas kernels, put(): pl.pallas_call(functools.partial(put_body, n, order), in_specs=[pl.BlockS...  9.02 us
    pallas_call x2, Pallas kernels, local_states(): pl.pallas_call(functools.partial(local_body, n, widths, swaps), in_specs=...  8.46 us
    convert_element_type x10, other arithmetic, message(): return self.hold(value.astype(jnp.bfloat16), 'message', c, s)  4.85 us
  transfers between devices with their start and end apart: 36, of which 13 were waited for; matrix products, arithmetic and copies ran while one was open for 4% of the time, Pallas kernels for 18%

profile of v13, /device:TPU:8, one launch (start us, length us, event | category | flops | bytes accessed | tf_op | source)
XLA Modules:
  0.0 194.8 jit_solution(6771887905668696390)
XLA Ops:
  0.1 3.4 %local.3 = (f32[4,2,128,128]{3,2,1,0:T(8,128)S(1)}, bf16[4,2,128,128]{3,2,1,0:T(8,128)(2,1)S(1)}) custom-call(s32[2]{0:T(128)S(1)} %pad_add_fusion.place, s32[1]{0:T(128)} %constant.38.clone.1.low, bf16[384,8192]{1,0:T(8,128)(2,1)} %keys.9, bf16[384,8192]{1,0:T(8,128)(2,1)} %values.9), custom_call_target="tpu_custom_call" | custom-call | flops 201326592 | bytes 3145728 | tf_op jit(solution)/shard_map/local/pallas_call | solution.py:102
  3.5 1.6 collective-permute-start.2
  5.1 5.0 %local.2 = (f32[4,3,128,128]{3,2,1,0:T(8,128)S(1)}, f32[4,3,128,128]{3,2,1,0:T(8,128)S(1)}, bf16[4,3,128,128]{3,2,1,0:T(8,128)(2,1)S(1)}, bf16[4,3,128,128]{3,2,1,0:T(8,128)(2,1)S(1)}) custom-call(s32[2]{0:T(128)S(1)} %pad_add_fusion.place, s32[1]{0:T(128)} %constant.37.clone.1.low, bf16[384,8192]{1,0:T(8,128)(2,1)} %keys.9, bf16[384,8192]{1,0:T(8,128)(2,1)} %values.9), custom_call_target="tpu_custom_call" | custom-call | flops 603979776 | bytes 9437184 | tf_op jit(solution)/shard_map/local/pallas_call | solution.py:102
  10.1 1.5 collective-permute-done.2
  11.7 1.3 collective-permute-start.3
  13.0 1.6 collective-permute-start.1
  14.6 6.2 %collective-permute-done.3 = bf16[4,2,128,128]{3,2,1,0:T(8,128)(2,1)S(1)} collective-permute-done((bf16[4,2,128,128]{3,2,1,0:T(8,128)(2,1)S(1)}, bf16[4,2,128,128]{3,2,1,0:T(8,128)(2,1)S(1)}, u32[]{:S(2)}, u32[]{:S(2)}) %collective-permute-start.3) | collective-permute-done | bytes 262176 | tf_op jit(solution)/shard_map/ppermute | solution.py:385
  20.8 0.8 add_convert_fusion.5
  21.6 2.1 %collective-permute-start.5 = (bf16[4,2,128,128]{3,2,1,0:T(8,128)(2,1)}, bf16[4,2,128,128]{3,2,1,0:T(8,128)(2,1)}, u32[]{:S(2)}, u32[]{:S(2)}) collective-permute-start(bf16[4,2,128,128]{3,2,1,0:T(8,128)(2,1)} %add_convert_fusion.5), channel_id=1, source_target_pairs={{8,16},{12,20},{9,17},{13,21},{10,18},{14,22},{11,19},{15,23}} | collective-permute-start | bytes 786440 | tf_op jit(solution)/shard_map/ppermute | solution.py:385
  23.7 0.8 fusion.7
  24.6 1.3 collective-permute-start.4
  25.8 1.6 collective-permute-start
  27.4 1.1 add_convert_fusion.4
  29.3 6.6 %collective-permute-done.4 = bf16[4,3,128,128]{3,2,1,0:T(8,128)(2,1)} collective-permute-done((bf16[4,3,128,128]{3,2,1,0:T(8,128)(2,1)}, bf16[4,3,128,128]{3,2,1,0:T(8,128)(2,1)}, u32[]{:S(2)}, u32[]{:S(2)}) %collective-permute-start.4) | collective-permute-done | bytes 393248 | tf_op jit(solution)/shard_map/ppermute | solution.py:385
  35.8 1.2 add_convert_fusion.3
  37.0 1.3 collective-permute-start.7
  38.4 1.3 collective-permute-start.6
  39.7 1.4 fusion.5
  41.1 1.6 collective-permute-start.11
  42.7 1.5 collective-permute-done.7
  45.0 3.4 %collective-permute-done.6 = bf16[4,3,128,128]{3,2,1,0:T(8,128)(2,1)S(1)} collective-permute-done((bf16[4,3,128,128]{3,2,1,0:T(8,128)(2,1)S(1)}, bf16[4,3,128,128]{3,2,1,0:T(8,128)(2,1)S(1)}, u32[]{:S(2)}, u32[]{:S(2)}) %collective-permute-start.6) | collective-permute-done | bytes 393248 | tf_op jit(solution)/shard_map/ppermute | solution.py:385
  48.6 1.6 collective-permute-start.9
  50.3 6.4 %attend.3 = (bf16[384,256]{1,0:T(8,128)(2,1)S(1)}, bf16[384,256]{1,0:T(8,128)(2,1)S(1)}, bf16[384,256]{1,0:T(8,128)(2,1)S(1)}, bf16[384,256]{1,0:T(8,128)(2,1)S(...) custom-call(s32[2]{0:T(128)S(1)} %pad_add_fusion.place, ...), custom_call_target="tpu_custom_call" | custom-call | flops 1409286144 | bytes 6291456 | tf_op jit(solution)/shard_map/attend/pallas_call | solution.py:226
  56.6 1.4 fusion.1
  58.9 3.8 %collective-permute-start.30 = (bf16[384,256]{1,0:T(8,128)(2,1)S(1)}, bf16[384,256]{1,0:T(8,128)(2,1)S(1)}, u32[]{:S(2)}, u32[]{:S(2)}) collective-permute-start(bf16[384,256]{1,0:T(8,128)(2,1)S(1)} %get-tuple-element.82), channel_id=1, source_target_pairs={{0,20},{4,16},{8,28},{12,24},{16,4},{20,0},{24,12},{28,8},{1,21},{... | collective-permute-start | bytes 589832 | tf_op jit(solution)/shard_map/ppermute | solution.py:409
  63.6 1.5 collective-permute-start.13
  65.2 10.3 %collective-permute-start.31 = (bf16[384,256]{1,0:T(8,128)(2,1)S(1)}, bf16[384,256]{1,0:T(8,128)(2,1)S(1)}, u32[]{:S(2)}, u32[]{:S(2)}) collective-permute-start(bf16[384,256]{1,0:T(8,128)(2,1)S(1)} %get-tuple-element.83), channel_id=1, source_target_pairs={{0,8},{4,12},{8,16},{12,20},{16,24},{20,28},{24,0},{28,4},{1,9},{5... | collective-permute-start | bytes 589832 | tf_op jit(solution)/shard_map/ppermute | solution.py:409
  75.5 2.5 %collective-permute-start.32 = (bf16[384,256]{1,0:T(8,128)(2,1)S(1)}, bf16[384,256]{1,0:T(8,128)(2,1)S(1)}, u32[]{:S(2)}, u32[]{:S(2)}) collective-permute-start(bf16[384,256]{1,0:T(8,128)(2,1)S(1)} %get-tuple-element.84), channel_id=1, source_target_pairs={{0,12},{4,8},{8,20},{12,16},{16,28},{20,24},{24,4},{28,0},{1,13},{... | collective-permute-start | bytes 589832 | tf_op jit(solution)/shard_map/ppermute | solution.py:409
  78.0 5.0 %collective-permute-start.33 = (bf16[384,256]{1,0:T(8,128)(2,1)S(1)}, bf16[384,256]{1,0:T(8,128)(2,1)S(1)}, u32[]{:S(2)}, u32[]{:S(2)}) collective-permute-start(bf16[384,256]{1,0:T(8,128)(2,1)S(1)} %get-tuple-element.85), channel_id=1, source_target_pairs={{0,24},{4,28},{8,0},{12,4},{16,8},{20,12},{24,16},{28,20},{1,25},{... | collective-permute-start | bytes 589832 | tf_op jit(solution)/shard_map/ppermute | solution.py:409
  83.0 8.3 %attend.5 = (bf16[384,384]{1,0:T(8,128)(2,1)S(1)}, bf16[384,384]{1,0:T(8,128)(2,1)S(1)}, bf16[384,384]{1,0:T(8,128)(2,1)S(1)}, bf16[384,384]{1,0:T(8,128)(2,1)S(...) custom-call(s32[2]{0:T(128)S(1)} %pad_add_fusion.place, ...), custom_call_target="tpu_custom_call" | custom-call | flops 2113929216 | bytes 9437184 | tf_op jit(solution)/shard_map/attend/pallas_call | solution.py:226
  91.8 7.0 %collective-permute-done.32.refs_4_ = bf16[384,256]{1,0:T(8,128)(2,1)S(1)} collective-permute-done((bf16[384,256]{1,0:T(8,128)(2,1)S(1)}, bf16[384,256]{1,0:T(8,128)(2,1)S(1)}, u32[]{:S(2)}, u32[]{:S(2)}) %collective-permute-start.32) | collective-permute-done | bytes 196640 | tf_op jit(solution)/shard_map/ppermute | solution.py:409
  98.8 4.7 %collective-permute-start.24 = (bf16[384,384]{1,0:T(8,128)(2,1)S(1)}, bf16[384,384]{1,0:T(8,128)(2,1)S(1)}, u32[]{:S(2)}, u32[]{:S(2)}) collective-permute-start(bf16[384,384]{1,0:T(8,128)(2,1)S(1)} %get-tuple-element.75), channel_id=1, source_target_pairs={{0,8},{4,12},{8,16},{12,20},{16,24},{20,28},{24,0},{28,4},{1,9},{5... | collective-permute-start | bytes 884744 | tf_op jit(solution)/shard_map/ppermute | solution.py:409
  103.6 10.1 %collective-permute-done.34.refs_6_ = bf16[384,256]{1,0:T(8,128)(2,1)S(1)} collective-permute-done((bf16[384,256]{1,0:T(8,128)(2,1)S(1)}, bf16[384,256]{1,0:T(8,128)(2,1)S(1)}, u32[]{:S(2)}, u32[]{:S(2)}) %collective-permute-start.34) | collective-permute-done | bytes 196640 | tf_op jit(solution)/shard_map/ppermute | solution.py:409
  113.7 8.3 %attend.4 = (bf16[384,384]{1,0:T(8,128)(2,1)S(1)}, bf16[384,384]{1,0:T(8,128)(2,1)S(1)}, bf16[384,384]{1,0:T(8,128)(2,1)S(1)}, bf16[384,384]{1,0:T(8,128)(2,1)S(...) custom-call(s32[2]{0:T(128)S(1)} %pad_add_fusion.place, ...), custom_call_target="tpu_custom_call" | custom-call | flops 2113929216 | bytes 9437184 | tf_op jit(solution)/shard_map/attend/pallas_call | solution.py:226
  122.5 3.0 %collective-permute-start.26 = (bf16[384,384]{1,0:T(8,128)(2,1)S(1)}, bf16[384,384]{1,0:T(8,128)(2,1)S(1)}, u32[]{:S(2)}, u32[]{:S(2)}) collective-permute-start(bf16[384,384]{1,0:T(8,128)(2,1)S(1)} %get-tuple-element.77), channel_id=1, source_target_pairs={{0,24},{4,28},{8,0},{12,4},{16,8},{20,12},{24,16},{28,20},{1,25},{... | collective-permute-start | bytes 884744 | tf_op jit(solution)/shard_map/ppermute | solution.py:409
  125.5 0.8 collective-permute-start.27
  127.1 10.8 %collective-permute-done.24.refs_3_ = bf16[384,384]{1,0:T(8,128)(2,1)S(1)} collective-permute-done((bf16[384,384]{1,0:T(8,128)(2,1)S(1)}, bf16[384,384]{1,0:T(8,128)(2,1)S(1)}, u32[]{:S(2)}, u32[]{:S(2)}) %collective-permute-start.24) | collective-permute-done | bytes 294944 | tf_op jit(solution)/shard_map/ppermute | solution.py:409
  137.8 15.8 %collective-permute-done.25.refs_4_ = bf16[384,384]{1,0:T(8,128)(2,1)S(1)} collective-permute-done((bf16[384,384]{1,0:T(8,128)(2,1)S(1)}, bf16[384,384]{1,0:T(8,128)(2,1)S(1)}, u32[]{:S(2)}, u32[]{:S(2)}) %collective-permute-start.25) | collective-permute-done | bytes 294944 | tf_op jit(solution)/shard_map/ppermute | solution.py:409
  153.7 4.8 %collective-permute-start.14 = (bf16[384,384]{1,0:T(8,128)(2,1)S(1)}, bf16[384,384]{1,0:T(8,128)(2,1)S(1)}, u32[]{:S(2)}, u32[]{:S(2)}) collective-permute-start(bf16[384,384]{1,0:T(8,128)(2,1)S(1)} %get-tuple-element.64), channel_id=1, source_target_pairs={{0,24},{4,28},{8,0},{12,4},{16,8},{20,12},{24,16},{28,20},{1,25},{... | collective-permute-start | bytes 884744 | tf_op jit(solution)/shard_map/ppermute | solution.py:409
  159.1 7.1 %collective-permute-done.17.refs_1_ = bf16[384,384]{1,0:T(8,128)(2,1)S(1)} collective-permute-done((bf16[384,384]{1,0:T(8,128)(2,1)S(1)}, bf16[384,384]{1,0:T(8,128)(2,1)S(1)}, u32[]{:S(2)}, u32[]{:S(2)}) %collective-permute-start.17) | collective-permute-done | bytes 294944 | tf_op jit(solution)/shard_map/ppermute | solution.py:409
  166.2 6.6 %collective-permute-start.15 = (bf16[384,384]{1,0:T(8,128)(2,1)S(1)}, bf16[384,384]{1,0:T(8,128)(2,1)S(1)}, u32[]{:S(2)}, u32[]{:S(2)}) collective-permute-start(bf16[384,384]{1,0:T(8,128)(2,1)S(1)} %get-tuple-element.65), channel_id=1, source_target_pairs={{0,28},{4,24},{8,4},{12,0},{16,12},{20,8},{24,20},{28,16},{1,29},{... | collective-permute-start | bytes 884744 | tf_op jit(solution)/shard_map/ppermute | solution.py:409
  172.8 2.9 %collective-permute-done.18.refs_2_ = bf16[384,384]{1,0:T(8,128)(2,1)S(1)} collective-permute-done((bf16[384,384]{1,0:T(8,128)(2,1)S(1)}, bf16[384,384]{1,0:T(8,128)(2,1)S(1)}, u32[]{:S(2)}, u32[]{:S(2)}) %collective-permute-start.18) | collective-permute-done | bytes 294944 | tf_op jit(solution)/shard_map/ppermute | solution.py:409
  175.7 5.7 %collective-permute-start.16 = (bf16[384,384]{1,0:T(8,128)(2,1)S(1)}, bf16[384,384]{1,0:T(8,128)(2,1)S(1)}, u32[]{:S(2)}, u32[]{:S(2)}) collective-permute-start(bf16[384,384]{1,0:T(8,128)(2,1)S(1)} %get-tuple-element.66), channel_id=1, source_target_pairs={{0,4},{4,0},{8,12},{12,8},{16,20},{20,16},{24,28},{28,24},{1,5},{5... | collective-permute-start | bytes 884744 | tf_op jit(solution)/shard_map/ppermute | solution.py:409
  181.5 2.3 %put.4 = (bf16[3072,1024]{1,0:T(8,128)(2,1)}, s32[2]{0:T(128)}) custom-call(s32[2]{0:T(128)S(1)} %pad_add_fusion.place, s32[1]{0:T(128)} %constant.38.clone.1.low, bf16[384,256]{1,0:T(8,128)(2,1)S(1)} %get-tuple-element.80.refs_0_, bf16[384,256]{1,0:T(8,128)(2,1)S(1)} %collective-permute-done.29.refs_1_, ...), custom_call_target="tpu_custom_call" | custom-call | tf_op jit(solution)/shard_map/put/pallas_call | solution.py:278
  183.7 2.5 %put.5 = (bf16[3072,1024]{1,0:T(8,128)(2,1)}, s32[2]{0:T(128)}) custom-call(s32[2]{0:T(128)S(1)} %pad_add_fusion.place, s32[1]{0:T(128)} %constant.37.clone.1.low, bf16[384,384]{1,0:T(8,128)(2,1)S(1)} %get-tuple-element.72.refs_0_, bf16[384,384]{1,0:T(8,128)(2,1)S(1)} %collective-permute-done.22.refs_1_, ...), custom_call_target="tpu_custom_call", output_to_operand_aliasing={{0}: (10, {})} | custom-call | tf_op jit(solution)/shard_map/put/pallas_call | solution.py:278
  186.3 4.3 %collective-permute-done.20.refs_4_ = bf16[384,384]{1,0:T(8,128)(2,1)S(1)} collective-permute-done((bf16[384,384]{1,0:T(8,128)(2,1)S(1)}, bf16[384,384]{1,0:T(8,128)(2,1)S(1)}, u32[]{:S(2)}, u32[]{:S(2)}) %collective-permute-start.20) | collective-permute-done | bytes 294944 | tf_op jit(solution)/shard_map/ppermute | solution.py:409
  190.5 2.2 %put.6 = (bf16[3072,1024]{1,0:T(8,128)(2,1)}, s32[2]{0:T(128)}) custom-call(s32[2]{0:T(128)S(1)} %pad_add_fusion.place, s32[1]{0:T(128)} %constant.36.clone.1.low, bf16[384,384]{1,0:T(8,128)(2,1)S(1)} %get-tuple-element.67.refs_0_, bf16[384,384]{1,0:T(8,128)(2,1)S(1)} %collective-permute-done.17.refs_1_, ...), custom_call_target="tpu_custom_call", output_to_operand_aliasing={{0}: (7, {})} | custom-call | tf_op jit(solution)/shard_map/put/pallas_call | solution.py:278
  192.8 2.0 %put.7 = (bf16[3072,1024]{1,0:T(8,128)(2,1)}, s32[2]{0:T(128)}) custom-call(s32[2]{0:T(128)S(1)} %pad_add_fusion.place, s32[1]{0:T(128)} %constant.36.clone.1.low, bf16[384,384]{1,0:T(8,128)(2,1)S(1)} %collective-permute-done.14.refs_0_, bf16[384,384]{1,0:T(8,128)(2,1)S(1)} %collective-permute-done.15.refs_1_, ...), custom_call_target="tpu_custom_call", output_to_operand_aliasing={{0}: (5, {})} | custom-call | tf_op jit(solution)/shard_map/put/pallas_call | solution.py:278
  (52 shorter events, 6.1 us)
Async XLA Ops:
  3.5 8.1 %collective-permute-start.2 = (bf16[4,2,128,128]{3,2,1,0:T(8,128)(2,1)S(1)}, bf16[4,2,128,128]{3,2,1,0:T(8,128)(2,1)S(1)}, u32[]{:S(2)}, u32[]{:S(2)}) collective-permute-start(bf16[4,2,128,128]{3,2,1,0:T(8,128)(2,1)S(1)} %get-tuple-element.53), channel_id=1, source_target_pairs={{0,4},{4,0},{8,12},{12,8},{16,20},{20,16},{24,28},{28,24},{1,5},{5... | collective-permute-start | bytes 786440 | tf_op jit(solution)/shard_map/ppermute | solution.py:358
  11.6 12.9 %copy-start.1 = (bf16[4,2,128,128]{3,2,1,0:T(8,128)(2,1)}, bf16[4,2,128,128]{3,2,1,0:T(8,128)(2,1)S(1)}, u32[]{:S(2)}) copy-start(bf16[4,2,128,128]{3,2,1,0:T(8,128)(2,1)S(1)} %collective-permute-done.2) | copy-start | bytes 786436
  11.7 9.1 %collective-permute-start.3 = (bf16[4,2,128,128]{3,2,1,0:T(8,128)(2,1)S(1)}, bf16[4,2,128,128]{3,2,1,0:T(8,128)(2,1)S(1)}, u32[]{:S(2)}, u32[]{:S(2)}) collective-permute-start(bf16[4,2,128,128]{3,2,1,0:T(8,128)(2,1)S(1)} %fusion.8), channel_id=1, source_target_pairs={{0,8},{4,12},{1,9},{5,13},{2,10},{6,14},{3,11},{7,15}} | collective-permute-start | bytes 786440 | tf_op jit(solution)/shard_map/ppermute | solution.py:385
  13.0 10.7 %collective-permute-start.1 = (bf16[4,3,128,128]{3,2,1,0:T(8,128)(2,1)S(1)}, bf16[4,3,128,128]{3,2,1,0:T(8,128)(2,1)S(1)}, u32[]{:S(2)}, u32[]{:S(2)}) collective-permute-start(bf16[4,3,128,128]{3,2,1,0:T(8,128)(2,1)S(1)} %get-tuple-element.51), channel_id=1, source_target_pairs={{0,4},{4,0},{8,12},{12,8},{16,20},{20,16},{24,28},{28,24},{1,5},{5... | collective-permute-start | bytes 1179656 | tf_op jit(solution)/shard_map/ppermute | solution.py:358
  20.8 3.0 %copy-start.2 = (bf16[4,2,128,128]{3,2,1,0:T(8,128)(2,1)}, bf16[4,2,128,128]{3,2,1,0:T(8,128)(2,1)S(1)}, u32[]{:S(2)}) copy-start(bf16[4,2,128,128]{3,2,1,0:T(8,128)(2,1)S(1)} %collective-permute-done.3) | copy-start | bytes 786436
  21.6 28.7 %copy-start = (f32[8192]{0:T(1024)S(1)}, f32[8192]{0:T(1024)}, u32[]{:S(2)}) copy-start(f32[8192]{0:T(1024)} %param.7) | copy-start | bytes 98308
  21.6 5.9 %collective-permute-start.5 = (bf16[4,2,128,128]{3,2,1,0:T(8,128)(2,1)}, bf16[4,2,128,128]{3,2,1,0:T(8,128)(2,1)}, u32[]{:S(2)}, u32[]{:S(2)}) collective-permute-start(bf16[4,2,128,128]{3,2,1,0:T(8,128)(2,1)} %add_convert_fusion.5), channel_id=1, source_target_pairs={{8,16},{12,20},{9,17},{13,21},{10,18},{14,22},{11,19},{15,23}} | collective-permute-start | bytes 786440 | tf_op jit(solution)/shard_map/ppermute | solution.py:385
  24.6 11.3 %collective-permute-start.4 = (bf16[4,3,128,128]{3,2,1,0:T(8,128)(2,1)}, bf16[4,3,128,128]{3,2,1,0:T(8,128)(2,1)}, u32[]{:S(2)}, u32[]{:S(2)}) collective-permute-start(bf16[4,3,128,128]{3,2,1,0:T(8,128)(2,1)} %fusion.7), channel_id=1, source_target_pairs={{0,8},{4,12},{1,9},{5,13},{2,10},{6,14},{3,11},{7,15}} | collective-permute-start | bytes 1179656 | tf_op jit(solution)/shard_map/ppermute | solution.py:385
  25.8 12.5 %collective-permute-start = (bf16[4,3,128,128]{3,2,1,0:T(8,128)(2,1)S(1)}, bf16[4,3,128,128]{3,2,1,0:T(8,128)(2,1)S(1)}, u32[]{:S(2)}, u32[]{:S(2)}) collective-permute-start(bf16[4,3,128,128]{3,2,1,0:T(8,128)(2,1)S(1)} %get-tuple-element.49), channel_id=1, source_target_pairs={{0,4},{4,0},{8,12},{12,8},{16,20},{20,16},{24,28},{28,24},{1,5},{5... | collective-permute-start | bytes 1179656 | tf_op jit(solution)/shard_map/ppermute | solution.py:358
  28.6 11.2 %collective-permute-start.8 = (bf16[4,2,128,128]{3,2,1,0:T(8,128)(2,1)S(1)}, bf16[4,2,128,128]{3,2,1,0:T(8,128)(2,1)S(1)}, u32[]{:S(2)}, u32[]{:S(2)}) collective-permute-start(bf16[4,2,128,128]{3,2,1,0:T(8,128)(2,1)S(1)} %add_convert_fusion.4), channel_id=1, source_target_pairs={{16,24},{20,28},{17,25},{21,29},{18,26},{22,30},{19,27},{23,31}} | collective-permute-start | bytes 786440 | tf_op jit(solution)/shard_map/ppermute | solution.py:385
  37.0 7.2 %collective-permute-start.7 = (bf16[4,3,128,128]{3,2,1,0:T(8,128)(2,1)S(1)}, bf16[4,3,128,128]{3,2,1,0:T(8,128)(2,1)S(1)}, u32[]{:S(2)}, u32[]{:S(2)}) collective-permute-start(bf16[4,3,128,128]{3,2,1,0:T(8,128)(2,1)S(1)} %add_convert_fusion.3), channel_id=1, source_target_pairs={{8,16},{12,20},{9,17},{13,21},{10,18},{14,22},{11,19},{15,23}} | collective-permute-start | bytes 1179656 | tf_op jit(solution)/shard_map/ppermute | solution.py:385
  38.4 10.0 %collective-permute-start.6 = (bf16[4,3,128,128]{3,2,1,0:T(8,128)(2,1)S(1)}, bf16[4,3,128,128]{3,2,1,0:T(8,128)(2,1)S(1)}, u32[]{:S(2)}, u32[]{:S(2)}) collective-permute-start(bf16[4,3,128,128]{3,2,1,0:T(8,128)(2,1)S(1)} %fusion.6), channel_id=1, source_target_pairs={{0,8},{4,12},{1,9},{5,13},{2,10},{6,14},{3,11},{7,15}} | collective-permute-start | bytes 1179656 | tf_op jit(solution)/shard_map/ppermute | solution.py:385
  41.1 9.2 %collective-permute-start.11 = (bf16[4,2,128,128]{3,2,1,0:T(8,128)(2,1)S(1)}, bf16[4,2,128,128]{3,2,1,0:T(8,128)(2,1)S(1)}, u32[]{:S(2)}, u32[]{:S(2)}) collective-permute-start(bf16[4,2,128,128]{3,2,1,0:T(8,128)(2,1)S(1)} %get-tuple-element.96), channel_id=1, source_target_pairs={{0,4},{4,0},{8,12},{12,8},{16,20},{20,16},{24,28},{28,24},{1,5},{5... | collective-permute-start | bytes 786440 | tf_op jit(solution)/shard_map/ppermute | solution.py:385
  44.3 12.3 %collective-permute-start.10 = (bf16[4,3,128,128]{3,2,1,0:T(8,128)(2,1)S(1)}, bf16[4,3,128,128]{3,2,1,0:T(8,128)(2,1)S(1)}, u32[]{:S(2)}, u32[]{:S(2)}) collective-permute-start(bf16[4,3,128,128]{3,2,1,0:T(8,128)(2,1)S(1)} %add_convert_fusion.1), channel_id=1, source_target_pairs={{16,24},{20,28},{17,25},{21,29},{18,26},{22,30},{19,27},{23,31}} | collective-permute-start | bytes 1179656 | tf_op jit(solution)/shard_map/ppermute | solution.py:385
  48.6 9.4 %collective-permute-start.9 = (bf16[4,3,128,128]{3,2,1,0:T(8,128)(2,1)S(1)}, bf16[4,3,128,128]{3,2,1,0:T(8,128)(2,1)S(1)}, u32[]{:S(2)}, u32[]{:S(2)}) collective-permute-start(bf16[4,3,128,128]{3,2,1,0:T(8,128)(2,1)S(1)} %add_convert_fusion.2), channel_id=1, source_target_pairs={{8,16},{12,20},{9,17},{13,21},{10,18},{14,22},{11,19},{15,23}} | collective-permute-start | bytes 1179656 | tf_op jit(solution)/shard_map/ppermute | solution.py:385
  58.2 5.2 %collective-permute-start.12 = (bf16[4,3,128,128]{3,2,1,0:T(8,128)(2,1)S(1)}, bf16[4,3,128,128]{3,2,1,0:T(8,128)(2,1)S(1)}, u32[]{:S(2)}, u32[]{:S(2)}) collective-permute-start(bf16[4,3,128,128]{3,2,1,0:T(8,128)(2,1)S(1)} %add_convert_fusion), channel_id=1, source_target_pairs={{16,24},{20,28},{17,25},{21,29},{18,26},{22,30},{19,27},{23,31}} | collective-permute-start | bytes 1179656 | tf_op jit(solution)/shard_map/ppermute | solution.py:385
  58.9 16.7 %collective-permute-start.29 = (bf16[384,256]{1,0:T(8,128)(2,1)S(1)}, bf16[384,256]{1,0:T(8,128)(2,1)S(1)}, u32[]{:S(2)}, u32[]{:S(2)}) collective-permute-start(bf16[384,256]{1,0:T(8,128)(2,1)S(1)} %get-tuple-element.81), channel_id=1, source_target_pairs={{0,16},{4,20},{8,24},{12,28},{16,0},{20,4},{24,8},{28,12},{1,17},{... | collective-permute-start | bytes 589832 | tf_op jit(solution)/shard_map/ppermute | solution.py:409
  58.9 19.1 %collective-permute-start.30 = (bf16[384,256]{1,0:T(8,128)(2,1)S(1)}, bf16[384,256]{1,0:T(8,128)(2,1)S(1)}, u32[]{:S(2)}, u32[]{:S(2)}) collective-permute-start(bf16[384,256]{1,0:T(8,128)(2,1)S(1)} %get-tuple-element.82), channel_id=1, source_target_pairs={{0,20},{4,16},{8,28},{12,24},{16,4},{20,0},{24,12},{28,8},{1,21},{... | collective-permute-start | bytes 589832 | tf_op jit(solution)/shard_map/ppermute | solution.py:409
  62.8 20.2 %collective-permute-start.21 = (bf16[4,3,128,128]{3,2,1,0:T(8,128)(2,1)S(1)}, bf16[4,3,128,128]{3,2,1,0:T(8,128)(2,1)S(1)}, u32[]{:S(2)}, u32[]{:S(2)}) collective-permute-start(bf16[4,3,128,128]{3,2,1,0:T(8,128)(2,1)S(1)} %get-tuple-element.62), channel_id=1, source_target_pairs={{0,4},{4,0},{8,12},{12,8},{16,20},{20,16},{24,28},{28,24},{1,5},{5... | collective-permute-start | bytes 1179656 | tf_op jit(solution)/shard_map/ppermute | solution.py:385
  63.6 50.0 %collective-permute-start.13 = (bf16[4,3,128,128]{3,2,1,0:T(8,128)(2,1)S(1)}, bf16[4,3,128,128]{3,2,1,0:T(8,128)(2,1)S(1)}, u32[]{:S(2)}, u32[]{:S(2)}) collective-permute-start(bf16[4,3,128,128]{3,2,1,0:T(8,128)(2,1)S(1)} %get-tuple-element.93), channel_id=1, source_target_pairs={{0,4},{4,0},{8,12},{12,8},{16,20},{20,16},{24,28},{28,24},{1,5},{5... | collective-permute-start | bytes 1179656 | tf_op jit(solution)/shard_map/ppermute | solution.py:385
  65.2 26.1 %collective-permute-start.31 = (bf16[384,256]{1,0:T(8,128)(2,1)S(1)}, bf16[384,256]{1,0:T(8,128)(2,1)S(1)}, u32[]{:S(2)}, u32[]{:S(2)}) collective-permute-start(bf16[384,256]{1,0:T(8,128)(2,1)S(1)} %get-tuple-element.83), channel_id=1, source_target_pairs={{0,8},{4,12},{8,16},{12,20},{16,24},{20,28},{24,0},{28,4},{1,9},{5... | collective-permute-start | bytes 589832 | tf_op jit(solution)/shard_map/ppermute | solution.py:409
  75.5 23.3 %collective-permute-start.32 = (bf16[384,256]{1,0:T(8,128)(2,1)S(1)}, bf16[384,256]{1,0:T(8,128)(2,1)S(1)}, u32[]{:S(2)}, u32[]{:S(2)}) collective-permute-start(bf16[384,256]{1,0:T(8,128)(2,1)S(1)} %get-tuple-element.84), channel_id=1, source_target_pairs={{0,12},{4,8},{8,20},{12,16},{16,28},{20,24},{24,4},{28,0},{1,13},{... | collective-permute-start | bytes 589832 | tf_op jit(solution)/shard_map/ppermute | solution.py:409
  78.0 20.8 %collective-permute-start.33 = (bf16[384,256]{1,0:T(8,128)(2,1)S(1)}, bf16[384,256]{1,0:T(8,128)(2,1)S(1)}, u32[]{:S(2)}, u32[]{:S(2)}) collective-permute-start(bf16[384,256]{1,0:T(8,128)(2,1)S(1)} %get-tuple-element.85), channel_id=1, source_target_pairs={{0,24},{4,28},{8,0},{12,4},{16,8},{20,12},{24,16},{28,20},{1,25},{... | collective-permute-start | bytes 589832 | tf_op jit(solution)/shard_map/ppermute | solution.py:409
  83.0 30.7 %collective-permute-start.34 = (bf16[384,256]{1,0:T(8,128)(2,1)S(1)}, bf16[384,256]{1,0:T(8,128)(2,1)S(1)}, u32[]{:S(2)}, u32[]{:S(2)}) collective-permute-start(bf16[384,256]{1,0:T(8,128)(2,1)S(1)} %get-tuple-element.86), channel_id=1, source_target_pairs={{0,28},{4,24},{8,4},{12,0},{16,12},{20,8},{24,20},{28,16},{1,29},{... | collective-permute-start | bytes 589832 | tf_op jit(solution)/shard_map/ppermute | solution.py:409
  91.3 34.2 %collective-permute-start.22 = (bf16[384,384]{1,0:T(8,128)(2,1)S(1)}, bf16[384,384]{1,0:T(8,128)(2,1)S(1)}, u32[]{:S(2)}, u32[]{:S(2)}) collective-permute-start(bf16[384,384]{1,0:T(8,128)(2,1)S(1)} %get-tuple-element.73), channel_id=1, source_target_pairs={{0,16},{4,20},{8,24},{12,28},{16,0},{20,4},{24,8},{28,12},{1,17},{... | collective-permute-start | bytes 884744 | tf_op jit(solution)/shard_map/ppermute | solution.py:409
  98.8 27.5 %collective-permute-start.23 = (bf16[384,384]{1,0:T(8,128)(2,1)S(1)}, bf16[384,384]{1,0:T(8,128)(2,1)S(1)}, u32[]{:S(2)}, u32[]{:S(2)}) collective-permute-start(bf16[384,384]{1,0:T(8,128)(2,1)S(1)} %get-tuple-element.74), channel_id=1, source_target_pairs={{0,20},{4,16},{8,28},{12,24},{16,4},{20,0},{24,12},{28,8},{1,21},{... | collective-permute-start | bytes 884744 | tf_op jit(solution)/shard_map/ppermute | solution.py:409
  98.8 39.0 %collective-permute-start.24 = (bf16[384,384]{1,0:T(8,128)(2,1)S(1)}, bf16[384,384]{1,0:T(8,128)(2,1)S(1)}, u32[]{:S(2)}, u32[]{:S(2)}) collective-permute-start(bf16[384,384]{1,0:T(8,128)(2,1)S(1)} %get-tuple-element.75), channel_id=1, source_target_pairs={{0,8},{4,12},{8,16},{12,20},{16,24},{20,28},{24,0},{28,4},{1,9},{5... | collective-permute-start | bytes 884744 | tf_op jit(solution)/shard_map/ppermute | solution.py:409
  113.7 40.0 %collective-permute-start.25 = (bf16[384,384]{1,0:T(8,128)(2,1)S(1)}, bf16[384,384]{1,0:T(8,128)(2,1)S(1)}, u32[]{:S(2)}, u32[]{:S(2)}) collective-permute-start(bf16[384,384]{1,0:T(8,128)(2,1)S(1)} %get-tuple-element.76), channel_id=1, source_target_pairs={{0,12},{4,8},{8,20},{12,16},{16,28},{20,24},{24,4},{28,0},{1,13},{... | collective-permute-start | bytes 884744 | tf_op jit(solution)/shard_map/ppermute | solution.py:409
  113.7 8.8 %collective-permute-start.35 = (bf16[384,256]{1,0:T(8,128)(2,1)S(1)}, bf16[384,256]{1,0:T(8,128)(2,1)S(1)}, u32[]{:S(2)}, u32[]{:S(2)}) collective-permute-start(bf16[384,256]{1,0:T(8,128)(2,1)S(1)} %get-tuple-element.61), channel_id=1, source_target_pairs={{0,4},{4,0},{8,12},{12,8},{16,20},{20,16},{24,28},{28,24},{1,5},{5... | collective-permute-start | bytes 589832 | tf_op jit(solution)/shard_map/ppermute | solution.py:409
  122.5 31.1 %collective-permute-start.26 = (bf16[384,384]{1,0:T(8,128)(2,1)S(1)}, bf16[384,384]{1,0:T(8,128)(2,1)S(1)}, u32[]{:S(2)}, u32[]{:S(2)}) collective-permute-start(bf16[384,384]{1,0:T(8,128)(2,1)S(1)} %get-tuple-element.77), channel_id=1, source_target_pairs={{0,24},{4,28},{8,0},{12,4},{16,8},{20,12},{24,16},{28,20},{1,25},{... | collective-permute-start | bytes 884744 | tf_op jit(solution)/shard_map/ppermute | solution.py:409
  125.5 33.0 %collective-permute-start.27 = (bf16[384,384]{1,0:T(8,128)(2,1)S(1)}, bf16[384,384]{1,0:T(8,128)(2,1)S(1)}, u32[]{:S(2)}, u32[]{:S(2)}) collective-permute-start(bf16[384,384]{1,0:T(8,128)(2,1)S(1)} %get-tuple-element.78), channel_id=1, source_target_pairs={{0,28},{4,24},{8,4},{12,0},{16,12},{20,8},{24,20},{28,16},{1,29},{... | collective-permute-start | bytes 884744 | tf_op jit(solution)/shard_map/ppermute | solution.py:409
  126.3 32.2 %collective-permute-start.28 = (bf16[384,384]{1,0:T(8,128)(2,1)S(1)}, bf16[384,384]{1,0:T(8,128)(2,1)S(1)}, u32[]{:S(2)}, u32[]{:S(2)}) collective-permute-start(bf16[384,384]{1,0:T(8,128)(2,1)S(1)} %get-tuple-element.79), channel_id=1, source_target_pairs={{0,4},{4,0},{8,12},{12,8},{16,20},{20,16},{24,28},{28,24},{1,5},{5... | collective-permute-start | bytes 884744 | tf_op jit(solution)/shard_map/ppermute | solution.py:409
  137.8 28.4 %collective-permute-start.17 = (bf16[384,384]{1,0:T(8,128)(2,1)S(1)}, bf16[384,384]{1,0:T(8,128)(2,1)S(1)}, u32[]{:S(2)}, u32[]{:S(2)}) collective-permute-start(bf16[384,384]{1,0:T(8,128)(2,1)S(1)} %get-tuple-element.68), channel_id=1, source_target_pairs={{0,16},{4,20},{8,24},{12,28},{16,0},{20,4},{24,8},{28,12},{1,17},{... | collective-permute-start | bytes 884744 | tf_op jit(solution)/shard_map/ppermute | solution.py:409
  153.7 22.1 %collective-permute-start.18 = (bf16[384,384]{1,0:T(8,128)(2,1)S(1)}, bf16[384,384]{1,0:T(8,128)(2,1)S(1)}, u32[]{:S(2)}, u32[]{:S(2)}) collective-permute-start(bf16[384,384]{1,0:T(8,128)(2,1)S(1)} %get-tuple-element.69), channel_id=1, source_target_pairs={{0,20},{4,16},{8,28},{12,24},{16,4},{20,0},{24,12},{28,8},{1,21},{... | collective-permute-start | bytes 884744 | tf_op jit(solution)/shard_map/ppermute | solution.py:409
  153.7 39.1 %collective-permute-start.14 = (bf16[384,384]{1,0:T(8,128)(2,1)S(1)}, bf16[384,384]{1,0:T(8,128)(2,1)S(1)}, u32[]{:S(2)}, u32[]{:S(2)}) collective-permute-start(bf16[384,384]{1,0:T(8,128)(2,1)S(1)} %get-tuple-element.64), channel_id=1, source_target_pairs={{0,24},{4,28},{8,0},{12,4},{16,8},{20,12},{24,16},{28,20},{1,25},{... | collective-permute-start | bytes 884744 | tf_op jit(solution)/shard_map/ppermute | solution.py:409
  158.5 27.8 %collective-permute-start.19 = (bf16[384,384]{1,0:T(8,128)(2,1)S(1)}, bf16[384,384]{1,0:T(8,128)(2,1)S(1)}, u32[]{:S(2)}, u32[]{:S(2)}) collective-permute-start(bf16[384,384]{1,0:T(8,128)(2,1)S(1)} %get-tuple-element.70), channel_id=1, source_target_pairs={{0,8},{4,12},{8,16},{12,20},{16,24},{20,28},{24,0},{28,4},{1,9},{5... | collective-permute-start | bytes 884744 | tf_op jit(solution)/shard_map/ppermute | solution.py:409
  158.5 32.0 %collective-permute-start.20 = (bf16[384,384]{1,0:T(8,128)(2,1)S(1)}, bf16[384,384]{1,0:T(8,128)(2,1)S(1)}, u32[]{:S(2)}, u32[]{:S(2)}) collective-permute-start(bf16[384,384]{1,0:T(8,128)(2,1)S(1)} %get-tuple-element.71), channel_id=1, source_target_pairs={{0,12},{4,8},{8,20},{12,16},{16,28},{20,24},{24,4},{28,0},{1,13},{... | collective-permute-start | bytes 884744 | tf_op jit(solution)/shard_map/ppermute | solution.py:409
  166.2 26.6 %collective-permute-start.15 = (bf16[384,384]{1,0:T(8,128)(2,1)S(1)}, bf16[384,384]{1,0:T(8,128)(2,1)S(1)}, u32[]{:S(2)}, u32[]{:S(2)}) collective-permute-start(bf16[384,384]{1,0:T(8,128)(2,1)S(1)} %get-tuple-element.65), channel_id=1, source_target_pairs={{0,28},{4,24},{8,4},{12,0},{16,12},{20,8},{24,20},{28,16},{1,29},{... | collective-permute-start | bytes 884744 | tf_op jit(solution)/shard_map/ppermute | solution.py:409
  175.7 17.1 %collective-permute-start.16 = (bf16[384,384]{1,0:T(8,128)(2,1)S(1)}, bf16[384,384]{1,0:T(8,128)(2,1)S(1)}, u32[]{:S(2)}, u32[]{:S(2)}) collective-permute-start(bf16[384,384]{1,0:T(8,128)(2,1)S(1)} %get-tuple-element.66), channel_id=1, source_target_pairs={{0,4},{4,0},{8,12},{12,8},{16,20},{20,16},{24,28},{28,24},{1,5},{5... | collective-permute-start | bytes 884744 | tf_op jit(solution)/shard_map/ppermute | solution.py:409
